TPU v7x, 32 devices: a whole 2x2x4 slice. The times are simulated.
32 devices in a mesh: dp: 8 (over y, x, core), ctx: 4 (over z).
Axes of the slice: x: 2, y: 2, z: 4, core: 2. Of those that a mesh axis runs over, the one named last changes fastest.
Arguments:
- tokens: bfloat16 [8, 1536, 8192], P('dp', 'ctx'), may hold values from -24 to 24
- w_query: bfloat16 [8192, 512], P('dp'), may hold values from -0.09375 to 0.09375
- w_key: bfloat16 [8192, 128], P('dp'), may hold values from -0.09375 to 0.09375
- w_value: bfloat16 [8192, 128], P('dp'), may hold values from -0.0625 to 0.0625
- doc_lengths: int32 [8, 16], P('dp'), may hold values from 1 to 768, 1536 in all within a row
Outputs:
- attended: bfloat16 [8, 1536, 512], P('dp', 'ctx')
Inputs may be any that keep to these rules, and one draw needn't show every extreme that they name: `doc_lengths`: each row holds the 16 document lengths of one sequence, summing to 1536, the largest exactly 768.
All inputs are finite; a program needn't handle non-finite values.
Results may differ from a plain program's by a relative error of at most 0.02.
Values may be sent and summed in bfloat16 or wider, within the bound.
No kernel may reach another device: no remote copies, remote signals or barrier semaphores. Data moves between devices by JAX's collectives and lax.ppermute only.
A program may use at most 64 MiB of HBM per device.

v0:
```python
import math

import jax
import jax.numpy as jnp
from jax import lax
from jax.sharding import PartitionSpec as P


def rotate(vectors, positions):
    half_size = vectors.shape[-1] // 2
    exponent = jnp.arange(half_size, dtype=jnp.float32) * (2.0 / vectors.shape[-1])
    inverse = jnp.power(jnp.float32(500000.0), -exponent)
    angles = positions.astype(jnp.float32)[:, None] * inverse[None, :]
    cosine = jnp.cos(angles)
    sine_part = jnp.sin(angles)
    if vectors.ndim == 3:
        cosine = cosine[:, None, :]
        sine_part = sine_part[:, None, :]
    leading = vectors[..., :half_size]
    trailing = vectors[..., half_size:]
    return jnp.concatenate(
        [leading * cosine - trailing * sine_part, trailing * cosine + leading * sine_part], axis=-1
    )


def doc_starts(doc_sizes, positions):
    doc_ends = jnp.cumsum(doc_sizes)
    doc_begin = doc_ends - doc_sizes
    chosen = jnp.where(doc_begin[None, :] <= positions[:, None], doc_begin[None, :], 0)
    return jnp.max(chosen, axis=1)


def shards(tokens, w_query, w_key, w_value, doc_lengths):
    hidden = tokens[0]
    row_count = hidden.shape[0]
    query_width = w_query.shape[1]
    head_size = w_key.shape[1]
    head_count = query_width // head_size
    scaling = 1.0 / math.sqrt(head_size)
    pieces = (
        lax.all_gather(w_query, "dp", axis=0, tiled=True),
        lax.all_gather(w_key, "dp", axis=0, tiled=True),
        lax.all_gather(w_value, "dp", axis=0, tiled=True),
    )
    queries, own_keys, values_here = tuple(
        (jnp.dot(hidden, fetched, preferred_element_type=jnp.float32) for fetched in pieces)
    )
    offset = lax.axis_index("ctx") * row_count
    positions = offset + jnp.arange(row_count, dtype=jnp.int32)
    queries = rotate(queries.reshape(row_count, head_count, head_size), positions).astype(
        jnp.bfloat16
    )
    own_keys = rotate(own_keys, positions).astype(jnp.bfloat16)
    values_here = values_here.astype(jnp.bfloat16)
    doc_first = doc_starts(doc_lengths[0], positions)
    lowest = jnp.min(doc_first)
    last_position = offset + row_count - 1

    def update(softmax_state, key_block, value_block, key_first):
        running_max, denominator, numerator = softmax_state
        scores = (
            jnp.einsum("tgd,kd->tgk", queries, key_block, preferred_element_type=jnp.float32)
            * scaling
        )
        key_pos = key_first + jnp.arange(key_block.shape[0], dtype=jnp.int32)
        allowed = (key_pos[None, :] <= positions[:, None]) & (
            key_pos[None, :] >= doc_first[:, None]
        )
        allowed = allowed[:, None, :]
        scores = jnp.where(allowed, scores, jnp.float32(-1e30))
        new_max = jnp.maximum(running_max, jnp.max(scores, axis=-1))
        factor = jnp.exp(running_max - new_max)
        exponents = jnp.where(allowed, jnp.exp(scores - new_max[..., None]), jnp.float32(0.0))
        denominator = denominator * factor + jnp.sum(exponents, axis=-1)
        weights = exponents.astype(jnp.bfloat16)
        numerator = numerator * factor[..., None] + jnp.einsum(
            "tgk,kd->tgd", weights, value_block, preferred_element_type=jnp.float32
        )
        return (new_max, denominator, numerator)

    start_state = (
        jnp.full((row_count, head_count), -1e30, jnp.float32),
        jnp.zeros((row_count, head_count), jnp.float32),
        jnp.zeros((row_count, head_count, head_size), jnp.float32),
    )
    key_rows_here = lax.all_gather(own_keys, "ctx", axis=0, tiled=True)
    value_rows_here = lax.all_gather(values_here, "ctx", axis=0, tiled=True)
    piece_rows = key_rows_here.shape[0]
    block_rows = math.gcd(piece_rows, 512)

    def key_step(step_index, status):
        key_first = step_index * block_rows
        key_block = lax.dynamic_slice_in_dim(key_rows_here, step_index * block_rows, block_rows, 0)
        value_block = lax.dynamic_slice_in_dim(
            value_rows_here, step_index * block_rows, block_rows, 0
        )
        nothing = (key_first > last_position) | (key_first + block_rows - 1 < lowest)
        return lax.cond(
            nothing,
            lambda kept: kept,
            lambda kept: update(kept, key_block, value_block, key_first),
            status,
        )

    softmax_state = lax.fori_loop(0, piece_rows // block_rows, key_step, start_state)
    running_max, denominator, numerator = softmax_state
    attended = numerator / denominator[..., None]
    return attended.reshape(row_count, query_width).astype(jnp.bfloat16)[None]


def solution(mesh):
    return jax.shard_map(
        shards,
        mesh=mesh,
        in_specs=(P("dp", "ctx", None), P("dp", None), P("dp", None), P("dp", None), P("dp", None)),
        out_specs=P("dp", "ctx", None),
        check_vma=False,
    )
```

profile of v0, /device:TPU:19, one launch (start us, length us, event | category | flops | bytes accessed | tf_op | source)
XLA Modules:
  0.0 165.1 jit_solution(7656147409735562159)
XLA Ops:
  6.5 0.7 all-gather.4.cloned.1.call-update
  7.3 0.7 all-gather.8.cloned.1.call-update
  8.1 0.7 all-gather.6.cloned.1.call-update
  8.7 0.8 reduce-window_clone.1
  9.6 0.7 subtract_bitcast_fusion
  10.3 0.7 reduce_min.9
  11.0 27.6 %all-gather.4.cloned.1.call-done = bf16[8192,128]{1,0:T(8,128)(2,1)} async-done(((bf16[1024,128]{1,0:T(8,128)(2,1)}), bf16[8192,128]{1,0:T(8,128)(2,1)}) %all-gather.4.cloned.1.call-update) | async-done | bytes 2097168 | tf_op jit(solution)/shard_map/all_gather | solution.py:42
  38.6 5.2 %fusion.25 = f32[384,128]{0,1:T(8,128)S(1)} fusion(bf16[8192,128]{1,0:T(8,128)(2,1)} %all-gather.4.cloned.1.call-done, bf16[1,384,8192]{2,1,0:T(8,128)(2,1)} %param.9), kind=kOutput, calls=%fused_computation.28 | convolution fusion | flops 805306368 | bytes 8585216 | tf_op jit(solution)/shard_map/dot_general | solution.py:46
  43.9 0.4 multiply_cosine_fusion
  44.4 11.4 %all_gather.16 = bf16[1536,128]{0,1:T(8,128)(2,1)S(1)} all-gather(bf16[384,128]{0,1:T(8,128)(2,1)S(1)} %pad_maximum_fusion.1), channel_id=1, replica_groups=mesh['dp'=8,'ctx'=4] {'ctx'}, dimensions={0}, use_global_device_ids=true | all-gather | bytes 491520 | tf_op jit(solution)/shard_map/all_gather | solution.py:86
  56.0 12.5 %all-gather.8.cloned.1.call-done = bf16[8192,128]{1,0:T(8,128)(2,1)} async-done(((bf16[1024,128]{1,0:T(8,128)(2,1)}), bf16[8192,128]{1,0:T(8,128)(2,1)}) %all-gather.8.cloned.1.call-update) | async-done | bytes 2097168 | tf_op jit(solution)/shard_map/all_gather | solution.py:43
  68.5 5.2 %fusion.27 = bf16[384,128]{1,0:T(8,128)(2,1)S(1)} fusion(bf16[8192,128]{1,0:T(8,128)(2,1)} %all-gather.8.cloned.1.call-done, bf16[1,384,8192]{2,1,0:T(8,128)(2,1)} %param.9), kind=kOutput, calls=%fused_computation.30 | convolution fusion | flops 805355520 | bytes 8486912 | tf_op jit(solution)/shard_map/dot_general | solution.py:46
  73.7 11.5 %all_gather.19 = bf16[1536,128]{1,0:T(8,128)(2,1)S(1)} all-gather(bf16[384,128]{1,0:T(8,128)(2,1)S(1)} %fusion.27), channel_id=1, replica_groups=mesh['dp'=8,'ctx'=4] {'ctx'}, dimensions={0}, use_global_device_ids=true | all-gather | bytes 491520 | tf_op jit(solution)/shard_map/all_gather | solution.py:87
  85.2 39.6 %all-gather.6.cloned.1.call-done = bf16[8192,512]{1,0:T(8,128)(2,1)} async-done(((bf16[1024,512]{1,0:T(8,128)(2,1)}), bf16[8192,512]{1,0:T(8,128)(2,1)}) %all-gather.6.cloned.1.call-update) | async-done | bytes 8388624 | tf_op jit(solution)/shard_map/all_gather | solution.py:41
  124.8 11.9 %copy.12 = bf16[512,8192]{1,0:T(8,128)(2,1)} copy(bf16[512,8192]{0,1:T(8,128)(2,1)} %bitcast.39) | data formatting | bytes 16777216 | tf_op jit(solution)/shard_map/dot_general | solution.py:46
  136.7 8.8 %fusion.21 = f32[384,4,128]{0,2,1:T(8,128)S(1)} fusion(bf16[4,128,8192]{2,1,0:T(8,128)(2,1)} %bitcast.40, bf16[1,384,8192]{2,1,0:T(8,128)(2,1)} %param.9), kind=kOutput, calls=%fused_computation.24 | convolution fusion | flops 3221225472 | bytes 15466496 | tf_op jit(solution)/shard_map/dot_general | solution.py:46
  146.0 11.1 %while.22 = (s32[]{:T(128)}, f32[384,4]{0,1:T(4,128)S(1)}, f32[384,4]{0,1:T(4,128)S(1)}, f32[384,4,128]{2,0,1:T(8,128)S(1)}, s32[]{:T(128)}, /*index=5*/s32[]{:T...) while((s32[]{:T(128)}, f32[384,4]{0,1:T(4,128)S(1)}, ...), condition=%wide.region_8.9_spmd.clone, body=%wide.region_3.8_spmd.clone.sunk | while | flops 413863808 | bytes 12562281 | solution.py:105
  146.6 3.0 %conditional.3 = (f32[384,4]{0,1:T(4,128)S(1)}, f32[384,4]{0,1:T(4,128)S(1)}, f32[384,4,128]{2,0,1:T(8,128)S(1)}) conditional(s32[]{:T(128)} %convert_element_type.58, (s32[]{:T(128)}, s32[]{:T(128)}, s32[384]{0:T(512)S(1)}, bf16[1536,128]{1,0:T(8,128)(2,1)S(1)}, bf16[384,4,128]{2,0,1:T(8,128)(2,1)S(1)}, /*index=5*/f32[384,4]{0,1:T(4,128)S(1)}, ...), branch_computations={%region_4.6_spmd, %region_7.7_spmd} | conditional | flops 413863808 | bytes 12548170 | solution.py:98
  146.9 0.7 fusion.2
  147.6 0.8 fusion.4
  148.4 1.3 fusion.8
  150.3 3.0 %conditional.3 = (f32[384,4]{0,1:T(4,128)S(1)}, f32[384,4]{0,1:T(4,128)S(1)}, f32[384,4,128]{2,0,1:T(8,128)S(1)}) conditional(s32[]{:T(128)} %convert_element_type.58, (s32[]{:T(128)}, s32[]{:T(128)}, s32[384]{0:T(512)S(1)}, bf16[1536,128]{1,0:T(8,128)(2,1)S(1)}, bf16[384,4,128]{2,0,1:T(8,128)(2,1)S(1)}, /*index=5*/f32[384,4]{0,1:T(4,128)S(1)}, ...), branch_computations={%region_4.6_spmd, %region_7.7_spmd} | conditional | flops 413863808 | bytes 12548170 | solution.py:98
  150.6 0.7 fusion.2
  151.3 0.8 fusion.4
  152.1 1.3 fusion.8
  154.0 3.0 %conditional.3 = (f32[384,4]{0,1:T(4,128)S(1)}, f32[384,4]{0,1:T(4,128)S(1)}, f32[384,4,128]{2,0,1:T(8,128)S(1)}) conditional(s32[]{:T(128)} %convert_element_type.58, (s32[]{:T(128)}, s32[]{:T(128)}, s32[384]{0:T(512)S(1)}, bf16[1536,128]{1,0:T(8,128)(2,1)S(1)}, bf16[384,4,128]{2,0,1:T(8,128)(2,1)S(1)}, /*index=5*/f32[384,4]{0,1:T(4,128)S(1)}, ...), branch_computations={%region_4.6_spmd, %region_7.7_spmd} | conditional | flops 413863808 | bytes 12548170 | solution.py:98
  154.3 0.7 fusion.2
  155.0 0.8 fusion.4
  155.8 1.3 fusion.8
  157.1 0.3 divide_convert_fusion
  157.4 0.3 copy.15
  157.7 0.9 convert_element_type.48
  (36 shorter events, 1.6 us)
Async XLA Ops:
  6.5 32.1 %all-gather.4.cloned.1.call-start = ((), (), s32[]{:S(2)}) async-start(), calls=%async_computation | async-start | bytes 2359296 | tf_op jit(solution)/shard_map/all_gather | solution.py:42
  7.3 61.2 %all-gather.8.cloned.1.call-start = ((), (), s32[]{:S(2)}) async-start(), calls=%async_computation.2 | async-start | bytes 2359296 | tf_op jit(solution)/shard_map/all_gather | solution.py:43
  8.0 116.8 %all-gather.6.cloned.1.call-start = ((), (), s32[]{:S(2)}) async-start(), calls=%async_computation.1 | async-start | bytes 9437184 | tf_op jit(solution)/shard_map/all_gather | solution.py:41
Sparse Core Ops, SparseCore 0:
  9.2 29.3 all-gather.3
  40.5 27.8 all-gather.7
  70.4 54.3 all-gather.5
where the time goes:
time: 166 us; the launch traced here: 165 us
  waiting for transfers between devices  81.8 us (49%)
  matrix products  25 us (15%)
  blocking collectives  22.8 us (14%)
  local copies, waits for them, and re-layouts  13.7 us (8%)
  between operations  13.2 us (8%)
  other arithmetic  6.27 us (4%)
  loops' own time  2.18 us (1%)
    all_gather x1, waiting for transfers between devices, shards(): lax.all_gather(w_query, 'dp', axis=0, tiled=True)  39.6 us
    all_gather x1, waiting for transfers between devices, shards(): lax.all_gather(w_key, 'dp', axis=0, tiled=True)  27.6 us
    dot_general x3, matrix products, shards(): jnp.dot(hidden, fetched, preferred_element_type=jnp.float32)  19.2 us
    all_gather x1, waiting for transfers between devices, shards(): lax.all_gather(w_value, 'dp', axis=0, tiled=True)  12.5 us
    dot_general x1, local copies, waits for them, and re-layouts, shards(): jnp.dot(hidden, fetched, preferred_element_type=jnp.float32)  11.9 us
    all_gather x1, blocking collectives, shards(): value_rows_here = lax.all_gather(values_here, 'ctx', axis=0, tiled=True)  11.5 us
    all_gather x1, blocking collectives, shards(): key_rows_here = lax.all_gather(own_keys, 'ctx', axis=0, tiled=True)  11.4 us
    dot_general x3, matrix products, update(): jnp.einsum('tgk,kd->tgd', weights, value_block, preferred_element_type=jn...  3.78 us
  transfers between devices with their start and end apart: 3, of which 3 were waited for; matrix products, arithmetic and copies ran while one was open for 8% of the time, Pallas kernels for 0%

commit v1 on v0

v1 whole, which is shorter than its diff:
```python
import functools
import math

import jax
import jax.numpy as jnp
from jax import lax
from jax.experimental import pallas as pl
from jax.experimental.pallas import tpu as pltpu
from jax.sharding import PartitionSpec as P

ROW_TILE = 128


def rope_tables(positions, head_size):
    half_size = head_size // 2
    exponent = jnp.arange(half_size, dtype=jnp.float32) * (2.0 / head_size)
    inverse = jnp.power(jnp.float32(500000.0), -exponent)
    angles = positions.astype(jnp.float32)[:, None] * inverse[None, :]
    cosine = jnp.cos(angles)
    sine_part = jnp.sin(angles)
    return (
        jnp.concatenate([cosine, cosine], axis=-1),
        jnp.concatenate([-sine_part, sine_part], axis=-1),
    )


def doc_starts(doc_sizes, positions):
    doc_ends = jnp.cumsum(doc_sizes)
    doc_begin = doc_ends - doc_sizes
    chosen = jnp.where(doc_begin[None, :] <= positions[:, None], doc_begin[None, :], 0)
    return jnp.max(chosen, axis=1)


def attend_kernel(head_count, back, near, far, cosine, sine, first, keys_values, out, rotated):
    rows, head_size = cosine.shape
    base = keys_values.shape[0] - rows
    tiles = rows // ROW_TILE
    for head in range(head_count):
        columns = slice(head * head_size, (head + 1) * head_size)
        query = near[:, columns] + far[:, columns]
        swapped = pltpu.roll(query, head_size // 2, 1)
        turned = (query * cosine[...] + swapped * sine[...]).astype(jnp.bfloat16)
        for tile in range(tiles):
            rotated[tile, head * ROW_TILE : (head + 1) * ROW_TILE, :] = turned[
                tile * ROW_TILE : (tile + 1) * ROW_TILE
            ]
    scale = jnp.float32(math.log2(math.e) / math.sqrt(head_size))
    for tile in range(tiles):
        begin = base + tile * ROW_TILE - back
        window = keys_values[begin : begin + back + ROW_TILE, :]
        scores = lax.dot_general(
            rotated[tile],
            window[:, :head_size],
            (((1,), (1,)), ((), ())),
            preferred_element_type=jnp.float32,
        )
        shape = (ROW_TILE, back + ROW_TILE)
        key_place = lax.broadcasted_iota(jnp.int32, shape, 1) + (tile * ROW_TILE - back)
        row_place = lax.broadcasted_iota(jnp.int32, shape, 0) + tile * ROW_TILE
        lower = first[tile * ROW_TILE : (tile + 1) * ROW_TILE, :]
        allowed = (key_place <= row_place) & (key_place >= lower)
        for head in range(head_count):
            part = scores[head * ROW_TILE : (head + 1) * ROW_TILE]
            part = jnp.where(allowed, part, jnp.float32(-1e30))
            largest = jnp.max(part, axis=-1, keepdims=True)
            exponents = jnp.exp2((part - largest) * scale)
            denominator = jnp.sum(exponents, axis=-1, keepdims=True)
            numerator = jnp.dot(
                exponents.astype(jnp.bfloat16),
                window[:, head_size:],
                preferred_element_type=jnp.float32,
            )
            out[
                tile * ROW_TILE : (tile + 1) * ROW_TILE, head * head_size : (head + 1) * head_size
            ] = (numerator / denominator).astype(out.dtype)


def attend(near, far, cosine, sine, first, keys_values, back):
    rows, width = near.shape
    head_size = cosine.shape[1]
    head_count = width // head_size
    return pl.pallas_call(
        functools.partial(attend_kernel, head_count, back),
        out_shape=jax.ShapeDtypeStruct((rows, width), jnp.bfloat16),
        in_specs=[pl.BlockSpec(memory_space=pltpu.VMEM)] * 6,
        out_specs=pl.BlockSpec(memory_space=pltpu.VMEM),
        scratch_shapes=[
            pltpu.VMEM((rows // ROW_TILE, head_count * ROW_TILE, head_size), jnp.bfloat16)
        ],
        compiler_params=pltpu.CompilerParams(vmem_limit_bytes=48 * 1024 * 1024),
        cost_estimate=pl.CostEstimate(
            flops=4 * rows * width * (back + ROW_TILE),
            bytes_accessed=8 * rows * width,
            transcendentals=rows * head_count * (back + ROW_TILE),
        ),
    )(near, far, cosine, sine, first, keys_values)


def shards(dp_size, ctx_size, tokens, w_query, w_key, w_value, doc_lengths):
    hidden = tokens[0]
    row_count = hidden.shape[0]
    depth = w_query.shape[0]
    head_size = w_key.shape[1]
    chips = dp_size // 2
    bits = chips.bit_length() - 1
    me = lax.axis_index("dp")
    place = lax.axis_index("ctx")

    def swap(array, mask):
        return lax.ppermute(array, "dp", [(i, i ^ mask) for i in range(dp_size)])

    def fetch(array, order):
        held = {0: array}
        for bit in order:
            for chip in sorted(held):
                held[chip | (1 << bit)] = swap(held[chip], 2 << bit)
        return held

    def columns(core):
        return jnp.concatenate(
            [
                lax.dynamic_slice_in_dim(hidden, (me ^ (chip * 2 + core)) * depth, depth, 1)
                for chip in range(chips)
            ],
            axis=1,
        )

    half = depth // 2
    upward, downward = list(range(bits)), list(range(bits))[::-1]
    w_pair = jnp.concatenate([w_key, w_value], axis=1)
    pair_parts = (fetch(w_pair[:half], upward), fetch(w_pair[half:], downward))
    query_parts = (fetch(w_query[:half], upward), fetch(w_query[half:], downward))
    rows_here = jnp.concatenate([columns(0), swap(columns(1), 1)], axis=0)

    def project(parts):
        total = None
        for chip in range(chips):
            for side in range(2):
                begin = chip * depth + side * half
                term = jnp.dot(
                    rows_here[:, begin : begin + half],
                    parts[side][chip],
                    preferred_element_type=jnp.float32,
                )
                total = term if total is None else total + term
        return total[:row_count], swap(total[row_count:], 1)

    offset = place * row_count
    positions = offset + jnp.arange(row_count, dtype=jnp.int32)
    cosine, sine = rope_tables(positions, head_size)
    first = (doc_starts(doc_lengths[0], positions) - offset)[:, None]

    pair_near, pair_far = project(pair_parts)
    pair = pair_near + pair_far
    key = pair[:, :head_size]
    swapped = jnp.concatenate([key[:, head_size // 2 :], key[:, : head_size // 2]], axis=1)
    key = key * cosine + swapped * sine
    pair = jnp.concatenate([key, pair[:, head_size:]], axis=1).astype(jnp.bfloat16)

    longest = ctx_size * row_count // 2
    back = -(-(longest - 1) // ROW_TILE) * ROW_TILE
    hops = min(ctx_size - 1, -(-back // row_count))
    blocks = [
        lax.ppermute(pair, "ctx", [(i, i + hop) for i in range(ctx_size - hop)])
        for hop in range(hops, 0, -1)
    ]
    keys_values = jnp.concatenate(blocks + [pair], axis=0)

    query_near, query_far = project(query_parts)
    return attend(query_near, query_far, cosine, sine, first, keys_values, back)[None]


def solution(mesh):
    return jax.shard_map(
        functools.partial(shards, mesh.shape["dp"], mesh.shape["ctx"]),
        mesh=mesh,
        in_specs=(P("dp", "ctx", None), P("dp", None), P("dp", None), P("dp", None), P("dp", None)),
        out_specs=P("dp", "ctx", None),
        check_vma=False,
    )
```

time: 166 us -> 106 us (0.64)
  the two profiles are of different devices: /device:TPU:19 before, /device:TPU:28 now
where the time goes in v1:
time: 106 us
  waiting for transfers between devices  43.1 us (41%)
  other arithmetic  26.4 us (25%)
  matrix products  12.3 us (12%)
  starting transfers between devices  12.1 us (11%)
  local copies, waits for them, and re-layouts  8 us (8%)
  Pallas kernels  3.65 us (3%)
    ppermute x15, waiting for transfers between devices, swap(): return lax.ppermute(array, 'dp', [(i, i ^ mask) for i in range(dp_size)])  28.2 us
    concatenate x1, other arithmetic, shards(): rows_here = jnp.concatenate([columns(0), swap(columns(1), 1)], axis=0)  23.1 us
    ppermute x2, waiting for transfers between devices, shards(): lax.ppermute(pair, 'ctx', [(i, i + hop) for i in range(ctx_size - hop)])  14.8 us
    dot_general x16, matrix products, project(): jnp.dot(rows_here[:, begin:begin + half], parts[side][chip], preferred_el...  12.3 us
    ppermute x15, starting transfers between devices, swap(): return lax.ppermute(array, 'dp', [(i, i ^ mask) for i in range(dp_size)])  9.5 us
    dynamic_slice x1, local copies, waits for them, and re-layouts, columns(): lax.dynamic_slice_in_dim(hidden, (me ^ chip * 2 + core) * depth, depth, 1)  4.49 us
    pallas_call x1, Pallas kernels, attend(): pl.pallas_call(functools.partial(attend_kernel, head_count, back), out_sh...  3.65 us
    ppermute x2, starting transfers between devices, shards(): lax.ppermute(pair, 'ctx', [(i, i + hop) for i in range(ctx_size - hop)])  2.58 us
  transfers between devices with their start and end apart: 17, of which 9 were waited for; matrix products, arithmetic and copies ran while one was open for 38% of the time, Pallas kernels for 0%

profile of v1, /device:TPU:28, one launch (start us, length us, event | category | flops | bytes accessed | tf_op | source)
XLA Modules:
  0.0 105.8 jit_solution(774870566654169036)
XLA Ops:
  0.0 4.5 %dynamic-slice_bitcast_fusion.7 = (bf16[384,1024]{1,0:T(8,128)(2,1)S(1)}, bf16[384,1024]{1,0:T(8,128)(2,1)S(1)}, bf16[384,1024]{1,0:T(8,128)(2,1)S(1)}, bf16[384...) fusion(bf16[1,384,8192]{2,1,0:T(8,128)(2,1)} %param.5, ...), kind=kLoop, calls=%fused_computation.17 | loop fusion | bytes 12582944 | tf_op jit(solution)/shard_map/dynamic_slice | solution.py:122
  4.5 1.8 %pad_maximum_fusion.1 = bf16[384,4096]{1,0:T(8,128)(2,1)} fusion(bf16[384,1024]{1,0:T(8,128)(2,1)S(1)} %get-tuple-element.13, bf16[384,1024]{1,0:T(8,128)(2,1)S(1)} %get-tuple-element.14, bf16[384,1024]{1,0:T(8,128)(2,1)S(1)} %get-tuple-element.8, bf16[384,1024]{1,0:T(8,128)(2,1)S(1)} %get-tuple-element.9), kind=kLoop, calls=%fused_computation.1 | loop fusion | flops 12582912 | bytes 6291456 | tf_op jit(solution)/shard_map/concatenate | solution.py:120
  6.3 1.1 %fusion.46 = (bf16[512,512]{1,0:T(8,128)(2,1)}, bf16[512,512]{1,0:T(8,128)(2,1)}) fusion(bf16[1024,512]{1,0:T(8,128)(2,1)S(1)} %copy-done), kind=kLoop, calls=%fused_computation.74 | loop fusion | bytes 2097152 | tf_op jit(solution)/shard_map/slice | solution.py:132
  7.4 1.5 %collective-permute-start.1 = (bf16[512,512]{1,0:T(8,128)(2,1)}, bf16[512,512]{1,0:T(8,128)(2,1)}, u32[]{:S(2)}, u32[]{:S(2)}) collective-permute-start(bf16[512,512]{1,0:T(8,128)(2,1)} %get-tuple-element.18), channel_id=1, source_target_pairs={{0,8},{4,12},{8,0},{12,4},{16,24},{20,28},{24,16},{28,20},{1,9},{5... | collective-permute-start | bytes 1572872 | tf_op jit(solution)/shard_map/ppermute | solution.py:110
  9.4 1.5 %collective-permute-start.4 = (bf16[512,512]{1,0:T(8,128)(2,1)}, bf16[512,512]{1,0:T(8,128)(2,1)}, u32[]{:S(2)}, u32[]{:S(2)}) collective-permute-start(bf16[512,512]{1,0:T(8,128)(2,1)} %get-tuple-element.17), channel_id=1, source_target_pairs={{0,16},{4,20},{8,24},{12,28},{16,0},{20,4},{24,8},{28,12},{1,17},{... | collective-permute-start | bytes 1572872 | tf_op jit(solution)/shard_map/ppermute | solution.py:110
  11.8 1.0 constant_dynamic-update-slice_fusion.1
  12.8 1.0 constant_dynamic-update-slice_fusion
  13.8 0.8 fusion.39
  14.6 0.6 collective-permute-start.11
  15.2 23.1 %pad_maximum_fusion = bf16[768,4096]{1,0:T(8,128)(2,1)S(1)} fusion(bf16[384,4096]{1,0:T(8,128)(2,1)} %collective-permute-done, bf16[384,1024]{1,0:T(8,128)(2,1)S(1)} %get-tuple-element.10, bf16[384,1024]{1,0:T(8,128)(2,1)S(1)} %get-tuple-element.11, bf16[384,1024]{1,0:T(8,128)(2,1)} %get-tuple-element.12, bf16[384,1024]{1,0:T(8,128)(2,1)S(1)} %get-tuple-element.7), kind=kLoop, calls=%fused_computation | loop fusion | flops 31457280 | bytes 12582912 | tf_op jit(solution)/shard_map/concatenate | solution.py:133
  38.7 1.3 %collective-permute-done.11 = bf16[512,256]{1,0:T(8,128)(2,1)S(1)} collective-permute-done((bf16[512,256]{1,0:T(8,128)(2,1)S(1)}, bf16[512,256]{1,0:T(8,128)(2,1)S(1)}, u32[]{:S(2)}, u32[]{:S(2)}) %collective-permute-start.11) | collective-permute-done | bytes 262176 | tf_op jit(solution)/shard_map/ppermute | solution.py:110
  40.9 6.7 %collective-permute-done.10 = bf16[512,256]{1,0:T(8,128)(2,1)S(1)} collective-permute-done((bf16[512,256]{1,0:T(8,128)(2,1)S(1)}, bf16[512,256]{1,0:T(8,128)(2,1)S(1)}, u32[]{:S(2)}, u32[]{:S(2)}) %collective-permute-start.10) | collective-permute-done | bytes 262176 | tf_op jit(solution)/shard_map/ppermute | solution.py:110
  48.5 5.8 %collective-permute-done.9 = bf16[512,256]{1,0:T(8,128)(2,1)S(1)} collective-permute-done((bf16[512,256]{1,0:T(8,128)(2,1)S(1)}, bf16[512,256]{1,0:T(8,128)(2,1)S(1)}, u32[]{:S(2)}, u32[]{:S(2)}) %collective-permute-start.9) | collective-permute-done | bytes 262176 | tf_op jit(solution)/shard_map/ppermute | solution.py:110
  55.2 6.4 %collective-permute-done.8 = bf16[512,256]{1,0:T(8,128)(2,1)S(1)} collective-permute-done((bf16[512,256]{1,0:T(8,128)(2,1)S(1)}, bf16[512,256]{1,0:T(8,128)(2,1)S(1)}, u32[]{:S(2)}, u32[]{:S(2)}) %collective-permute-start.8) | collective-permute-done | bytes 262176 | tf_op jit(solution)/shard_map/ppermute | solution.py:110
  63.0 0.6 fusion.35
  63.6 0.6 fusion.32
  64.2 1.2 %collective-permute-start.12 = (bf16[512,256]{1,0:T(8,128)(2,1)S(1)}, bf16[512,256]{1,0:T(8,128)(2,1)S(1)}, u32[]{:S(2)}, u32[]{:S(2)}) collective-permute-start(bf16[512,256]{1,0:T(8,128)(2,1)S(1)} %collective-permute-done.8), channel_id=1, source_target_pairs={{0,16},{4,20},{8,24},{12,28},{16,0},{20,4},{24,8},{28,12},{1,17},{... | collective-permute-start | bytes 786440 | tf_op jit(solution)/shard_map/ppermute | solution.py:110
  65.4 0.9 collective-permute-start.5
  66.3 3.6 %collective-permute-done.13 = bf16[512,256]{1,0:T(8,128)(2,1)S(1)} collective-permute-done((bf16[512,256]{1,0:T(8,128)(2,1)S(1)}, bf16[512,256]{1,0:T(8,128)(2,1)S(1)}, u32[]{:S(2)}, u32[]{:S(2)}) %collective-permute-start.13) | collective-permute-done | bytes 262176 | tf_op jit(solution)/shard_map/ppermute | solution.py:110
  70.8 2.5 %collective-permute-done.12 = bf16[512,256]{1,0:T(8,128)(2,1)S(1)} collective-permute-done((bf16[512,256]{1,0:T(8,128)(2,1)S(1)}, bf16[512,256]{1,0:T(8,128)(2,1)S(1)}, u32[]{:S(2)}, u32[]{:S(2)}) %collective-permute-start.12) | collective-permute-done | bytes 262176 | tf_op jit(solution)/shard_map/ppermute | solution.py:110
  73.8 1.6 %fusion.16 = f32[768,512]{1,0:T(8,128)S(1)} fusion(bf16[512,512]{1,0:T(8,128)(2,1)} %collective-permute-done.4, bf16[768,4096]{1,0:T(8,128)(2,1)S(1)} %pad_maximum_fusion), kind=kOutput, calls=%fused_computation.27 | convolution fusion | flops 402653184 | bytes 2883584 | tf_op jit(solution)/shard_map/dot_general | solution.py:140
  75.4 1.6 %fusion.28 = f32[768,512]{1,0:T(8,128)S(1)} fusion(bf16[512,512]{1,0:T(8,128)(2,1)} %collective-permute-done.1, bf16[768,4096]{1,0:T(8,128)(2,1)S(1)} %pad_maximum_fusion), kind=kOutput, calls=%fused_computation.39 | convolution fusion | flops 402653184 | bytes 2883584 | tf_op jit(solution)/shard_map/dot_general | solution.py:140
  77.0 1.9 %collective-permute-done.5 = bf16[512,512]{1,0:T(8,128)(2,1)S(1)} collective-permute-done((bf16[512,512]{1,0:T(8,128)(2,1)}, bf16[512,512]{1,0:T(8,128)(2,1)S(1)}, u32[]{:S(2)}, u32[]{:S(2)}) %collective-permute-start.5) | collective-permute-done | bytes 524320 | tf_op jit(solution)/shard_map/ppermute | solution.py:110
  78.9 0.6 fusion.12
  79.5 1.6 %fusion.20 = f32[768,512]{1,0:T(8,128)S(1)} fusion(bf16[512,512]{1,0:T(8,128)(2,1)} %collective-permute-done.3, bf16[768,4096]{1,0:T(8,128)(2,1)S(1)} %pad_maximum_fusion), kind=kOutput, calls=%fused_computation.31 | convolution fusion | flops 402653184 | bytes 2883584 | tf_op jit(solution)/shard_map/dot_general | solution.py:140
  81.1 1.6 %fusion.24 = f32[768,512]{1,0:T(8,128)S(1)} fusion(bf16[512,512]{1,0:T(8,128)(2,1)} %collective-permute-done.2, bf16[768,4096]{1,0:T(8,128)(2,1)S(1)} %pad_maximum_fusion), kind=kOutput, calls=%fused_computation.35 | convolution fusion | flops 402653184 | bytes 2883584 | tf_op jit(solution)/shard_map/dot_general | solution.py:140
  82.7 1.1 %add_add_fusion = f32[768,512]{1,0:T(8,128)S(1)} fusion(f32[768,512]{1,0:T(8,128)S(1)} %fusion.12, f32[768,512]{1,0:T(8,128)S(1)} %fusion.16, f32[768,512]{1,0:T(8,128)S(1)} %fusion.20, f32[768,512]{1,0:T(8,128)S(1)} %fusion.24, f32[768,512]{1,0:T(8,128)S(1)} %fusion.28, f32[768,512]{1,0:T(8,128)S(1)} %fusion.35, f32[768,512]{1,0:T(8,128)S(1)} %fusion.32, ...), kind=kOutput, calls=%fused_computation.2 | convolution fusion | flops 405405696 | bytes 13893632 | tf_op jit(solution)/shard_map/dot_general | solution.py:140
  84.5 1.3 %collective-permute-start.16 = (bf16[384,256]{1,0:T(8,128)(2,1)S(1)}, bf16[384,256]{1,0:T(8,128)(2,1)S(1)}, u32[]{:S(2)}, u32[]{:S(2)}) collective-permute-start(bf16[384,256]{1,0:T(8,128)(2,1)S(1)} %pad_maximum_fusion.4), channel_id=1, source_target_pairs={{0,1},{1,2},{2,3},{4,5},{5,6},{6,7},{8,9},{9,10},{10,11},{12,13},{... | collective-permute-start | bytes 589832 | tf_op jit(solution)/shard_map/ppermute | solution.py:164
  85.8 1.3 %collective-permute-start.15 = (bf16[384,256]{1,0:T(8,128)(2,1)S(1)}, bf16[384,256]{1,0:T(8,128)(2,1)S(1)}, u32[]{:S(2)}, u32[]{:S(2)}) collective-permute-start(bf16[384,256]{1,0:T(8,128)(2,1)S(1)} %pad_maximum_fusion.4), channel_id=1, source_target_pairs={{0,2},{1,3},{4,6},{5,7},{8,10},{9,11},{12,14},{13,15},{16,18},{17,... | collective-permute-start | bytes 589832 | tf_op jit(solution)/shard_map/ppermute | solution.py:164
  87.3 6.7 %collective-permute-done.16 = bf16[384,256]{1,0:T(8,128)(2,1)S(1)} collective-permute-done((bf16[384,256]{1,0:T(8,128)(2,1)S(1)}, bf16[384,256]{1,0:T(8,128)(2,1)S(1)}, u32[]{:S(2)}, u32[]{:S(2)}) %collective-permute-start.16) | collective-permute-done | bytes 196640 | tf_op jit(solution)/shard_map/ppermute | solution.py:164
  93.9 8.2 %collective-permute-done.15 = bf16[384,256]{1,0:T(8,128)(2,1)S(1)} collective-permute-done((bf16[384,256]{1,0:T(8,128)(2,1)S(1)}, bf16[384,256]{1,0:T(8,128)(2,1)S(1)}, u32[]{:S(2)}, u32[]{:S(2)}) %collective-permute-start.15) | collective-permute-done | bytes 196640 | tf_op jit(solution)/shard_map/ppermute | solution.py:164
  102.2 3.7 %shard_map.55 = bf16[384,512]{1,0:T(8,128)(2,1)} custom-call(f32[384,512]{1,0:T(8,128)S(1)} %get-tuple-element.16.near, f32[384,512]{1,0:T(8,128)S(1)} %collective-permute-done.7.far, f32[384,128]{1,0:T(8,128)S(1)} %get-tuple-element.23.cosine, f32[384,128]{1,0:T(8,128)S(1)} %get-tuple-element.6.sine, s32[384,1]{1,0:T(8,128)S(1)} %sub.21.first, ...), custom_call_target="tpu_custom_call" | custom-call | flops 704643072 | bytes 1572864 | tf_op jit(solution)/shard_map/pallas_call | solution.py:82
  (46 shorter events, 7.9 us)
Async XLA Ops:
  4.5 1.8 %copy-start = (bf16[1024,512]{1,0:T(8,128)(2,1)S(1)}, bf16[1024,512]{1,0:T(8,128)(2,1)}, u32[]{:S(2)}) copy-start(bf16[1024,512]{1,0:T(8,128)(2,1)} %param.6) | copy-start | bytes 3145732
  4.5 7.0 %copy-start.1 = (s32[1,16]{1,0:T(1,128)S(1)}, s32[1,16]{1,0:T(1,128)}, u32[]{:S(2)}) copy-start(s32[1,16]{1,0:T(1,128)} %param.9) | copy-start | bytes 196
  6.3 8.3 %collective-permute-start = (bf16[384,4096]{1,0:T(8,128)(2,1)}, bf16[384,4096]{1,0:T(8,128)(2,1)}, u32[]{:S(2)}, u32[]{:S(2)}) collective-permute-start(bf16[384,4096]{1,0:T(8,128)(2,1)} %pad_maximum_fusion.1), channel_id=1, source_target_pairs={{0,4},{4,0},{8,12},{12,8},{16,20},{20,16},{24,28},{28,24},{1,5},{5... | collective-permute-start | bytes 9437192 | tf_op jit(solution)/shard_map/ppermute | solution.py:110
  7.4 56.8 %collective-permute-start.1 = (bf16[512,512]{1,0:T(8,128)(2,1)}, bf16[512,512]{1,0:T(8,128)(2,1)}, u32[]{:S(2)}, u32[]{:S(2)}) collective-permute-start(bf16[512,512]{1,0:T(8,128)(2,1)} %get-tuple-element.18), channel_id=1, source_target_pairs={{0,8},{4,12},{8,0},{12,4},{16,24},{20,28},{24,16},{28,20},{1,9},{5... | collective-permute-start | bytes 1572872 | tf_op jit(solution)/shard_map/ppermute | solution.py:110
  8.9 70.6 %collective-permute-start.3 = (bf16[512,512]{1,0:T(8,128)(2,1)}, bf16[512,512]{1,0:T(8,128)(2,1)}, u32[]{:S(2)}, u32[]{:S(2)}) collective-permute-start(bf16[512,512]{1,0:T(8,128)(2,1)} %get-tuple-element.18), channel_id=1, source_target_pairs={{0,16},{4,20},{8,24},{12,28},{16,0},{20,4},{24,8},{28,12},{1,17},{... | collective-permute-start | bytes 1572872 | tf_op jit(solution)/shard_map/ppermute | solution.py:110
  9.4 56.0 %collective-permute-start.4 = (bf16[512,512]{1,0:T(8,128)(2,1)}, bf16[512,512]{1,0:T(8,128)(2,1)}, u32[]{:S(2)}, u32[]{:S(2)}) collective-permute-start(bf16[512,512]{1,0:T(8,128)(2,1)} %get-tuple-element.17), channel_id=1, source_target_pairs={{0,16},{4,20},{8,24},{12,28},{16,0},{20,4},{24,8},{28,12},{1,17},{... | collective-permute-start | bytes 1572872 | tf_op jit(solution)/shard_map/ppermute | solution.py:110
  10.9 70.2 %collective-permute-start.2 = (bf16[512,512]{1,0:T(8,128)(2,1)}, bf16[512,512]{1,0:T(8,128)(2,1)}, u32[]{:S(2)}, u32[]{:S(2)}) collective-permute-start(bf16[512,512]{1,0:T(8,128)(2,1)} %get-tuple-element.17), channel_id=1, source_target_pairs={{0,8},{4,12},{8,0},{12,4},{16,24},{20,28},{24,16},{28,20},{1,9},{5... | collective-permute-start | bytes 1572872 | tf_op jit(solution)/shard_map/ppermute | solution.py:110
  14.6 25.4 %collective-permute-start.11 = (bf16[512,256]{1,0:T(8,128)(2,1)S(1)}, bf16[512,256]{1,0:T(8,128)(2,1)S(1)}, u32[]{:S(2)}, u32[]{:S(2)}) collective-permute-start(bf16[512,256]{1,0:T(8,128)(2,1)S(1)} %get-tuple-element.20), channel_id=1, source_target_pairs={{0,16},{4,20},{8,24},{12,28},{16,0},{20,4},{24,8},{28,12},{1,17},{... | collective-permute-start | bytes 786440 | tf_op jit(solution)/shard_map/ppermute | solution.py:110
  40.0 7.6 %collective-permute-start.10 = (bf16[512,256]{1,0:T(8,128)(2,1)S(1)}, bf16[512,256]{1,0:T(8,128)(2,1)S(1)}, u32[]{:S(2)}, u32[]{:S(2)}) collective-permute-start(bf16[512,256]{1,0:T(8,128)(2,1)S(1)} %get-tuple-element.19), channel_id=1, source_target_pairs={{0,16},{4,20},{8,24},{12,28},{16,0},{20,4},{24,8},{28,12},{1,17},{... | collective-permute-start | bytes 786440 | tf_op jit(solution)/shard_map/ppermute | solution.py:110
  47.6 6.7 %collective-permute-start.9 = (bf16[512,256]{1,0:T(8,128)(2,1)S(1)}, bf16[512,256]{1,0:T(8,128)(2,1)S(1)}, u32[]{:S(2)}, u32[]{:S(2)}) collective-permute-start(bf16[512,256]{1,0:T(8,128)(2,1)S(1)} %get-tuple-element.20), channel_id=1, source_target_pairs={{0,8},{4,12},{8,0},{12,4},{16,24},{20,28},{24,16},{28,20},{1,9},{5... | collective-permute-start | bytes 786440 | tf_op jit(solution)/shard_map/ppermute | solution.py:110
  54.3 7.3 %collective-permute-start.8 = (bf16[512,256]{1,0:T(8,128)(2,1)S(1)}, bf16[512,256]{1,0:T(8,128)(2,1)S(1)}, u32[]{:S(2)}, u32[]{:S(2)}) collective-permute-start(bf16[512,256]{1,0:T(8,128)(2,1)S(1)} %get-tuple-element.19), channel_id=1, source_target_pairs={{0,8},{4,12},{8,0},{12,4},{16,24},{20,28},{24,16},{28,20},{1,9},{5... | collective-permute-start | bytes 786440 | tf_op jit(solution)/shard_map/ppermute | solution.py:110
  61.6 8.2 %collective-permute-start.13 = (bf16[512,256]{1,0:T(8,128)(2,1)S(1)}, bf16[512,256]{1,0:T(8,128)(2,1)S(1)}, u32[]{:S(2)}, u32[]{:S(2)}) collective-permute-start(bf16[512,256]{1,0:T(8,128)(2,1)S(1)} %collective-permute-done.11), channel_id=1, source_target_pairs={{0,8},{4,12},{8,0},{12,4},{16,24},{20,28},{24,16},{28,20},{1,9},{5... | collective-permute-start | bytes 786440 | tf_op jit(solution)/shard_map/ppermute | solution.py:110
  64.2 9.1 %collective-permute-start.12 = (bf16[512,256]{1,0:T(8,128)(2,1)S(1)}, bf16[512,256]{1,0:T(8,128)(2,1)S(1)}, u32[]{:S(2)}, u32[]{:S(2)}) collective-permute-start(bf16[512,256]{1,0:T(8,128)(2,1)S(1)} %collective-permute-done.8), channel_id=1, source_target_pairs={{0,16},{4,20},{8,24},{12,28},{16,0},{20,4},{24,8},{28,12},{1,17},{... | collective-permute-start | bytes 786440 | tf_op jit(solution)/shard_map/ppermute | solution.py:110
  65.4 13.5 %collective-permute-start.5 = (bf16[512,512]{1,0:T(8,128)(2,1)}, bf16[512,512]{1,0:T(8,128)(2,1)S(1)}, u32[]{:S(2)}, u32[]{:S(2)}) collective-permute-start(bf16[512,512]{1,0:T(8,128)(2,1)} %collective-permute-done.1), channel_id=1, source_target_pairs={{0,16},{4,20},{8,24},{12,28},{16,0},{20,4},{24,8},{28,12},{1,17},{... | collective-permute-start | bytes 1572872 | tf_op jit(solution)/shard_map/ppermute | solution.py:110
  69.9 12.8 %collective-permute-start.6 = (bf16[512,512]{1,0:T(8,128)(2,1)}, bf16[512,512]{1,0:T(8,128)(2,1)S(1)}, u32[]{:S(2)}, u32[]{:S(2)}) collective-permute-start(bf16[512,512]{1,0:T(8,128)(2,1)} %collective-permute-done.4), channel_id=1, source_target_pairs={{0,8},{4,12},{8,0},{12,4},{16,24},{20,28},{24,16},{28,20},{1,9},{5... | collective-permute-start | bytes 1572872 | tf_op jit(solution)/shard_map/ppermute | solution.py:110
  73.7 10.4 %collective-permute-start.14 = (f32[384,256]{1,0:T(8,128)S(1)}, f32[384,256]{1,0:T(8,128)S(1)}, u32[]{:S(2)}, u32[]{:S(2)}) collective-permute-start(f32[384,256]{1,0:T(8,128)S(1)} %slice.104), channel_id=1, source_target_pairs={{0,4},{4,0},{8,12},{12,8},{16,20},{20,16},{24,28},{28,24},{1,5},{5... | collective-permute-start | bytes 1179656 | tf_op jit(solution)/shard_map/ppermute | solution.py:110
  84.0 18.2 %collective-permute-start.7 = (f32[384,512]{1,0:T(8,128)S(1)}, f32[384,512]{1,0:T(8,128)S(1)}, u32[]{:S(2)}, u32[]{:S(2)}) collective-permute-start(f32[384,512]{1,0:T(8,128)S(1)} %get-tuple-element.15), channel_id=1, source_target_pairs={{0,4},{4,0},{8,12},{12,8},{16,20},{20,16},{24,28},{28,24},{1,5},{5... | collective-permute-start | bytes 2359304 | tf_op jit(solution)/shard_map/ppermute | solution.py:110
  84.5 9.4 %collective-permute-start.16 = (bf16[384,256]{1,0:T(8,128)(2,1)S(1)}, bf16[384,256]{1,0:T(8,128)(2,1)S(1)}, u32[]{:S(2)}, u32[]{:S(2)}) collective-permute-start(bf16[384,256]{1,0:T(8,128)(2,1)S(1)} %pad_maximum_fusion.4), channel_id=1, source_target_pairs={{0,1},{1,2},{2,3},{4,5},{5,6},{6,7},{8,9},{9,10},{10,11},{12,13},{... | collective-permute-start | bytes 589832 | tf_op jit(solution)/shard_map/ppermute | solution.py:164
  85.8 16.2 %collective-permute-start.15 = (bf16[384,256]{1,0:T(8,128)(2,1)S(1)}, bf16[384,256]{1,0:T(8,128)(2,1)S(1)}, u32[]{:S(2)}, u32[]{:S(2)}) collective-permute-start(bf16[384,256]{1,0:T(8,128)(2,1)S(1)} %pad_maximum_fusion.4), channel_id=1, source_target_pairs={{0,2},{1,3},{4,6},{5,7},{8,10},{9,11},{12,14},{13,15},{16,18},{17,... | collective-permute-start | bytes 589832 | tf_op jit(solution)/shard_map/ppermute | solution.py:164

commit v2 on v1

v2 whole, which is shorter than its diff:
```python
import functools
import math

import jax
import jax.numpy as jnp
from jax import lax
from jax.experimental import pallas as pl
from jax.experimental.pallas import tpu as pltpu
from jax.sharding import PartitionSpec as P

ROW_TILE = 128
VMEM_LIMIT = 48 * 1024 * 1024


def rope_tables(positions, head_size):
    half_size = head_size // 2
    exponent = jnp.arange(half_size, dtype=jnp.float32) * (2.0 / head_size)
    inverse = jnp.power(jnp.float32(500000.0), -exponent)
    angles = positions.astype(jnp.float32)[:, None] * inverse[None, :]
    cosine = jnp.cos(angles)
    sine_part = jnp.sin(angles)
    return (
        jnp.concatenate([cosine, cosine], axis=-1),
        jnp.concatenate([-sine_part, sine_part], axis=-1),
    )


def doc_starts(doc_sizes, positions):
    doc_ends = jnp.cumsum(doc_sizes)
    doc_begin = doc_ends - doc_sizes
    chosen = jnp.where(doc_begin[None, :] <= positions[:, None], doc_begin[None, :], 0)
    return jnp.max(chosen, axis=1)


def vmem(count):
    return [pl.BlockSpec(memory_space=pltpu.VMEM)] * count


def anywhere(count):
    return [pl.BlockSpec(memory_space=pl.ANY)] * count


def after(array, *earlier):
    return lax.optimization_barrier((array, *earlier))[0]


def project_kernel(chips, spots, carried, final, starts, near, far, *refs):
    weights = refs[: len(chips) * len(spots)]
    refs = refs[len(weights) :]
    if carried:
        carry, refs = refs[0], refs[1:]
    outs, (tokens, held, sems) = refs[:-3], refs[-3:]
    rows = near.shape[0]
    depth = held.shape[1]
    copies = []
    for step, chip in enumerate(chips):
        window = pl.ds(pl.multiple_of(starts[chip], 128), depth)
        batch = [
            pltpu.make_async_copy(near.at[:, window], tokens.at[step, :rows], sems.at[step, 0]),
            pltpu.make_async_copy(far.at[:, window], tokens.at[step, rows:], sems.at[step, 1]),
        ]
        for index, spot in enumerate(spots):
            batch.append(
                pltpu.make_async_copy(
                    weights[step * len(spots) + index],
                    held.at[(step, *spot)],
                    sems.at[step, 2 + index],
                )
            )
        for copy in batch:
            copy.start()
        copies.append(batch)
    total = carry[...] if carried else None
    for step, batch in enumerate(copies):
        for copy in batch:
            copy.wait()
        term = jnp.dot(tokens[step], held[step], preferred_element_type=jnp.float32)
        total = term if total is None else total + term
    if final:
        outs[0][...] = total[:rows]
        outs[1][...] = total[rows:]
    else:
        outs[0][...] = total


def project(chips, spots, depth, starts, near, far, weights, carry, final):
    rows = near.shape[0]
    width = sum(w.size for w in weights[: len(spots)]) // depth
    whole = jax.ShapeDtypeStruct((2 * rows, width), jnp.float32)
    part = jax.ShapeDtypeStruct((rows, width), jnp.float32)
    carries = [] if carry is None else [carry]
    return pl.pallas_call(
        functools.partial(project_kernel, chips, spots, carry is not None, final),
        out_shape=(part, part) if final else whole,
        in_specs=[pl.BlockSpec(memory_space=pltpu.SMEM)]
        + anywhere(2 + len(weights))
        + vmem(len(carries)),
        out_specs=tuple(vmem(2)) if final else vmem(1)[0],
        scratch_shapes=[
            pltpu.VMEM((len(chips), 2 * rows, depth), jnp.bfloat16),
            pltpu.VMEM((len(chips), depth, width), jnp.bfloat16),
            pltpu.SemaphoreType.DMA((len(chips), 2 + len(spots))),
        ],
        compiler_params=pltpu.CompilerParams(vmem_limit_bytes=VMEM_LIMIT),
        cost_estimate=pl.CostEstimate(
            flops=4 * rows * width * depth * len(chips),
            bytes_accessed=2 * len(chips) * depth * (2 * rows + width),
            transcendentals=0,
        ),
    )(starts, near, far, *weights, *carries)


def turn(vectors, cosine, sine):
    return vectors * cosine + pltpu.roll(vectors, vectors.shape[1] // 2, 1) * sine


def pair_kernel(near, far, cosine, sine, out):
    head_size = cosine.shape[1]
    pair = near[...] + far[...]
    out[:, :head_size] = turn(pair[:, :head_size], cosine[...], sine[...]).astype(out.dtype)
    out[:, head_size:] = pair[:, head_size:].astype(out.dtype)


def finish_pair(near, far, cosine, sine):
    return pl.pallas_call(
        pair_kernel,
        out_shape=jax.ShapeDtypeStruct(near.shape, jnp.bfloat16),
        in_specs=vmem(4),
        out_specs=vmem(1)[0],
        cost_estimate=pl.CostEstimate(
            flops=6 * near.size, bytes_accessed=14 * near.size, transcendentals=0
        ),
    )(near, far, cosine, sine)


def attend_kernel(back, near, far, cosine, sine, first, keys_values, *refs):
    earlier, (out, rotated) = refs[:-2], refs[-2:]
    rows, head_size = cosine.shape
    head_count = near.shape[1] // head_size
    base = keys_values.shape[0] - rows
    tiles = rows // ROW_TILE
    filled = 0
    for ref in earlier:
        out[:, filled : filled + ref.shape[1]] = ref[...]
        filled += ref.shape[1]
    for head in range(head_count):
        columns = slice(head * head_size, (head + 1) * head_size)
        turned = turn(near[:, columns] + far[:, columns], cosine[...], sine[...])
        turned = turned.astype(jnp.bfloat16)
        for tile in range(tiles):
            rotated[tile, head * ROW_TILE : (head + 1) * ROW_TILE, :] = turned[
                tile * ROW_TILE : (tile + 1) * ROW_TILE
            ]
    scale = jnp.float32(math.log2(math.e) / math.sqrt(head_size))
    for tile in range(tiles):
        begin = base + tile * ROW_TILE - back
        window = keys_values[begin : begin + back + ROW_TILE, :]
        scores = lax.dot_general(
            rotated[tile],
            window[:, :head_size],
            (((1,), (1,)), ((), ())),
            preferred_element_type=jnp.float32,
        )
        shape = (ROW_TILE, back + ROW_TILE)
        key_place = lax.broadcasted_iota(jnp.int32, shape, 1) + (tile * ROW_TILE - back)
        row_place = lax.broadcasted_iota(jnp.int32, shape, 0) + tile * ROW_TILE
        lower = first[tile * ROW_TILE : (tile + 1) * ROW_TILE, :]
        allowed = (key_place <= row_place) & (key_place >= lower)
        for head in range(head_count):
            part = scores[head * ROW_TILE : (head + 1) * ROW_TILE]
            part = jnp.where(allowed, part, jnp.float32(-1e30))
            largest = jnp.max(part, axis=-1, keepdims=True)
            exponents = jnp.exp2((part - largest) * scale)
            denominator = jnp.sum(exponents, axis=-1, keepdims=True)
            numerator = jnp.dot(
                exponents.astype(jnp.bfloat16),
                window[:, head_size:],
                preferred_element_type=jnp.float32,
            )
            left = filled + head * head_size
            out[tile * ROW_TILE : (tile + 1) * ROW_TILE, left : left + head_size] = (
                numerator / denominator
            ).astype(out.dtype)


def attend(near, far, cosine, sine, first, keys_values, back, earlier):
    rows, width = near.shape
    head_size = cosine.shape[1]
    head_count = width // head_size
    full_width = width + sum(array.shape[1] for array in earlier)
    return pl.pallas_call(
        functools.partial(attend_kernel, back),
        out_shape=jax.ShapeDtypeStruct((rows, full_width), jnp.bfloat16),
        in_specs=vmem(6 + len(earlier)),
        out_specs=vmem(1)[0],
        scratch_shapes=[
            pltpu.VMEM((rows // ROW_TILE, head_count * ROW_TILE, head_size), jnp.bfloat16)
        ],
        compiler_params=pltpu.CompilerParams(vmem_limit_bytes=VMEM_LIMIT),
        cost_estimate=pl.CostEstimate(
            flops=4 * rows * width * (back + ROW_TILE),
            bytes_accessed=8 * rows * width,
            transcendentals=rows * head_count * (back + ROW_TILE),
        ),
    )(near, far, cosine, sine, first, keys_values, *earlier)


def shards(dp_size, ctx_size, tokens, w_query, w_key, w_value, doc_lengths):
    hidden = tokens[0]
    row_count = hidden.shape[0]
    depth, query_width = w_query.shape
    head_size = w_key.shape[1]
    chips = dp_size // 2
    bits = chips.bit_length() - 1
    me = lax.axis_index("dp")
    place = lax.axis_index("ctx")

    def swap(array, mask):
        return lax.ppermute(array, "dp", [(i, i ^ mask) for i in range(dp_size)])

    def fetch(pair, gates):
        held = ({0: pair[0]}, {0: pair[1]})
        for step in range(bits):
            axes = (step, bits - 1 - step)
            present = [sorted(held[side]) for side in range(2)]
            for sources in zip(*present):
                for side, source in enumerate(sources):
                    array = held[side][source]
                    if source == 0 and gates:
                        array = after(array, *gates[min(step, len(gates) - 1)])
                    held[side][source | (1 << axes[side])] = swap(array, 2 << axes[side])
        return held

    half = depth // 2
    middle = query_width // 2
    tops = [w_query[:half, :middle], w_query[:half, middle:]]
    bottoms = [w_query[half:, :middle], w_query[half:, middle:]]
    side_by_side = (
        (slice(None), slice(0, head_size)),
        (slice(None), slice(head_size, 2 * head_size)),
    )
    stacked = ((slice(0, half), slice(None)), (slice(half, depth), slice(None)))

    sibling_hidden = swap(hidden, 1)

    offset = place * row_count
    positions = offset + jnp.arange(row_count, dtype=jnp.int32)
    cosine, sine = rope_tables(positions, head_size)
    first = (doc_starts(doc_lengths[0], positions) - offset)[:, None]
    starts = jnp.stack([(me ^ (2 * chip)) * depth for chip in range(chips)]).astype(jnp.int32)

    first_axis, last_axis = 1, 1 << (bits - 1)

    def gates_of(held, *more):
        return (
            (held[0][last_axis], held[1][first_axis], *more),
            (held[0][chips - 1], held[1][chips - 1]),
        )

    def products(held, spots, *gates):
        order = list(range(chips))
        weights = [held[side][chip] for chip in order for side in range(2)]
        split = 2 * (chips - 1)
        carry = project(
            order[:-1], spots, depth, starts, hidden, sibling_hidden, weights[:split], None, False
        )
        if gates:
            carry = after(carry, *gates)
        near, far = project(
            order[-1:], spots, depth, starts, hidden, sibling_hidden, weights[split:], carry, True
        )
        return near, swap(far, 1)

    held_pair = fetch((w_key, w_value), None)
    held_low = fetch((tops[0], bottoms[0]), gates_of(held_pair))
    near, far = products(held_pair, side_by_side)
    pair = finish_pair(near, far, cosine, sine)
    held_high = fetch((tops[1], bottoms[1]), gates_of(held_low, pair))

    longest = ctx_size * row_count // 2
    back = -(-(longest - 1) // ROW_TILE) * ROW_TILE
    hops = min(ctx_size - 1, -(-back // row_count))
    blocks = [
        lax.ppermute(pair, "ctx", [(i, i + hop) for i in range(ctx_size - hop)])
        for hop in range(hops, 0, -1)
    ]
    keys_values = jnp.concatenate(blocks + [pair], axis=0)

    near, far = products(held_low, stacked)
    low = attend(near, far, cosine, sine, first, keys_values, back, [])
    near, far = products(held_high, stacked, low)
    return attend(near, far, cosine, sine, first, keys_values, back, [low])[None]


def solution(mesh):
    return jax.shard_map(
        functools.partial(shards, mesh.shape["dp"], mesh.shape["ctx"]),
        mesh=mesh,
        in_specs=(P("dp", "ctx", None), P("dp", None), P("dp", None), P("dp", None), P("dp", None)),
        out_specs=P("dp", "ctx", None),
        check_vma=False,
    )
```

time: 106 us -> 90.8 us (0.86)
  the two profiles are of different devices: /device:TPU:28 before, /device:TPU:17 now
where the time goes in v2:
time: 90.8 us; the launch traced here: 90.5 us
  waiting for transfers between devices  29.8 us (33%)
  Pallas kernels  28.5 us (31%)
  starting transfers between devices  25.7 us (28%)
  other arithmetic  4.08 us (4%)
  local copies, waits for them, and re-layouts  2.14 us (2%)
    pallas_call x6, Pallas kernels, project(): pl.pallas_call(functools.partial(project_kernel, chips, spots, carry is n...  22.2 us
    ppermute x22, starting transfers between devices, swap(): return lax.ppermute(array, 'dp', [(i, i ^ mask) for i in range(dp_size)])  21 us
    ppermute x22, waiting for transfers between devices, swap(): return lax.ppermute(array, 'dp', [(i, i ^ mask) for i in range(dp_size)])  16.8 us
    ppermute x2, waiting for transfers between devices, shards(): lax.ppermute(pair, 'ctx', [(i, i + hop) for i in range(ctx_size - hop)])  13.1 us
    ppermute x2, starting transfers between devices, shards(): lax.ppermute(pair, 'ctx', [(i, i + hop) for i in range(ctx_size - hop)])  4.67 us
    pallas_call x2, Pallas kernels, attend(): pl.pallas_call(functools.partial(attend_kernel, back), out_shape=jax.Shap...  4.23 us
    pallas_call x1, Pallas kernels, finish_pair(): pl.pallas_call(pair_kernel, out_shape=jax.ShapeDtypeStruct(near.shape, jn...  2.01 us
  transfers between devices with their start and end apart: 24, of which 9 were waited for; matrix products, arithmetic and copies ran while one was open for 6% of the time, Pallas kernels for 26%

profile of v2, /device:TPU:17, one launch (start us, length us, event | category | flops | bytes accessed | tf_op | source)
XLA Modules:
  0.0 90.5 jit_solution(8463604895930508474)
XLA Ops:
  0.7 1.2 %collective-permute-start.8 = (bf16[1024,128]{1,0:T(8,128)(2,1)}, bf16[1024,128]{1,0:T(8,128)(2,1)S(1)}, u32[]{:S(2)}, u32[]{:S(2)}) collective-permute-start(bf16[1024,128]{1,0:T(8,128)(2,1)} %refs_0_.1), channel_id=1, source_target_pairs={{0,16},{4,20},{8,24},{12,28},{16,0},{20,4},{24,8},{28,12},{1,17},{... | collective-permute-start | bytes 786440 | tf_op jit(solution)/shard_map/ppermute | solution.py:219
  1.9 1.2 %collective-permute-start.1 = (bf16[1024,128]{1,0:T(8,128)(2,1)}, bf16[1024,128]{1,0:T(8,128)(2,1)S(1)}, u32[]{:S(2)}, u32[]{:S(2)}) collective-permute-start(bf16[1024,128]{1,0:T(8,128)(2,1)} %refs_0_.1), channel_id=1, source_target_pairs={{0,8},{4,12},{8,0},{12,4},{16,24},{20,28},{24,16},{28,20},{1,9},{5... | collective-permute-start | bytes 786440 | tf_op jit(solution)/shard_map/ppermute | solution.py:219
  5.9 3.8 %collective-permute-done.1.refs_2_ = bf16[1024,128]{1,0:T(8,128)(2,1)S(1)} collective-permute-done((bf16[1024,128]{1,0:T(8,128)(2,1)}, bf16[1024,128]{1,0:T(8,128)(2,1)S(1)}, u32[]{:S(2)}, u32[]{:S(2)}) %collective-permute-start.1) | collective-permute-done | bytes 262176 | tf_op jit(solution)/shard_map/ppermute | solution.py:219
  10.0 4.5 %collective-permute-done.3.refs_5_ = bf16[1024,128]{1,0:T(8,128)(2,1)S(1)} collective-permute-done((bf16[1024,128]{1,0:T(8,128)(2,1)}, bf16[1024,128]{1,0:T(8,128)(2,1)S(1)}, u32[]{:S(2)}, u32[]{:S(2)}) %collective-permute-start.3) | collective-permute-done | bytes 262176 | tf_op jit(solution)/shard_map/ppermute | solution.py:219
  14.4 1.2 %collective-permute-start.4 = (bf16[1024,128]{1,0:T(8,128)(2,1)S(1)}, bf16[1024,128]{1,0:T(8,128)(2,1)S(1)}, u32[]{:S(2)}, u32[]{:S(2)}) collective-permute-start(bf16[1024,128]{1,0:T(8,128)(2,1)S(1)} %collective-permute-done.3.refs_5_), channel_id=1, source_target_pairs={{0,8},{4,12},{8,0},{12,4},{16,24},{20,28},{24,16},{28,20},{1,9},{5... | collective-permute-start | bytes 786440 | tf_op jit(solution)/shard_map/ppermute | solution.py:219
  15.7 1.3 %fusion.2 = (bf16[512,256]{1,0:T(8,128)(2,1)S(1)}, bf16[512,256]{1,0:T(8,128)(2,1)S(1)}, bf16[512,256]{1,0:T(8,128)(2,1)S(1)}, bf16[512,256]{1,0:T(8,128)(2,1)S(1)}) fusion(bf16[1024,512]{1,0:T(8,128)(2,1)} %param.6), kind=kLoop, calls=%fused_computation.13 | loop fusion | bytes 2097152 | tf_op jit(solution)/shard_map/slice | solution.py:237
  17.3 1.2 %collective-permute-start.16 = (bf16[512,256]{1,0:T(8,128)(2,1)S(1)}, bf16[512,256]{1,0:T(8,128)(2,1)S(1)}, u32[]{:S(2)}, u32[]{:S(2)}) collective-permute-start(bf16[512,256]{1,0:T(8,128)(2,1)S(1)} %get-tuple-element.27.refs_1_), channel_id=1, source_target_pairs={{0,16},{4,20},{8,24},{12,28},{16,0},{20,4},{24,8},{28,12},{1,17},{... | collective-permute-start | bytes 786440 | tf_op jit(solution)/shard_map/ppermute | solution.py:219
  18.6 1.5 %collective-permute-done.2.refs_0_ = bf16[1024,128]{1,0:T(8,128)(2,1)S(1)} collective-permute-done((bf16[1024,128]{1,0:T(8,128)(2,1)S(1)}, bf16[1024,128]{1,0:T(8,128)(2,1)S(1)}, u32[]{:S(2)}, u32[]{:S(2)}) %collective-permute-start.2) | collective-permute-done | bytes 262176 | tf_op jit(solution)/shard_map/ppermute | solution.py:219
  20.1 1.0 %collective-permute-done.4.refs_1_ = bf16[1024,128]{1,0:T(8,128)(2,1)S(1)} collective-permute-done((bf16[1024,128]{1,0:T(8,128)(2,1)S(1)}, bf16[1024,128]{1,0:T(8,128)(2,1)S(1)}, u32[]{:S(2)}, u32[]{:S(2)}) %collective-permute-start.4) | collective-permute-done | bytes 262176 | tf_op jit(solution)/shard_map/ppermute | solution.py:219
  21.1 1.2 %collective-permute-start.5 = (bf16[512,256]{1,0:T(8,128)(2,1)S(1)}, bf16[512,256]{1,0:T(8,128)(2,1)S(1)}, u32[]{:S(2)}, u32[]{:S(2)}) collective-permute-start(bf16[512,256]{1,0:T(8,128)(2,1)S(1)} %get-tuple-element.26.refs_0_), channel_id=1, source_target_pairs={{0,16},{4,20},{8,24},{12,28},{16,0},{20,4},{24,8},{28,12},{1,17},{... | collective-permute-start | bytes 786440 | tf_op jit(solution)/shard_map/ppermute | solution.py:219
  22.3 1.2 %collective-permute-start.6 = (bf16[512,256]{1,0:T(8,128)(2,1)S(1)}, bf16[512,256]{1,0:T(8,128)(2,1)S(1)}, u32[]{:S(2)}, u32[]{:S(2)}) collective-permute-start(bf16[512,256]{1,0:T(8,128)(2,1)S(1)} %get-tuple-element.27.refs_1_), channel_id=1, source_target_pairs={{0,8},{4,12},{8,0},{12,4},{16,24},{20,28},{24,16},{28,20},{1,9},{5... | collective-permute-start | bytes 786440 | tf_op jit(solution)/shard_map/ppermute | solution.py:219
  23.5 4.9 %shard_map.55.refs_2_ = f32[768,256]{1,0:T(8,128)S(1)} custom-call(s32[4]{0:T(128)S(1)} %pad_add_fusion.starts, bf16[384,8192]{1,0:T(8,128)(2,1)} %bitcast.9, bf16[384,8192]{1,0:T(8,128)(2,1)} %collective-permute-done.far, bf16[1024,128]{1,0:T(8,128)(2,1)S(1)} %copy-done.3, bf16[1024,128]{1,0:T(8,128)(2,1)S(1)} %copy-done.4, ...), custom_call_target="tpu_custom_call" | custom-call | flops 1207959552 | bytes 6291456 | tf_op jit(solution)/shard_map/pallas_call | solution.py:92
  28.4 2.5 %shard_map.56 = (f32[384,256]{1,0:T(8,128)S(1)}, f32[384,256]{1,0:T(8,128)S(1)}) custom-call(s32[4]{0:T(128)S(1)} %pad_add_fusion.starts, bf16[384,8192]{1,0:T(8,128)(2,1)} %bitcast.10, bf16[384,8192]{1,0:T(8,128)(2,1)} %collective-permute-done.far, bf16[1024,128]{1,0:T(8,128)(2,1)S(1)} %collective-permute-done.2.refs_0_, ...), custom_call_target="tpu_custom_call" | custom-call | flops 402653184 | bytes 2097152 | tf_op jit(solution)/shard_map/pallas_call | solution.py:92
  31.0 4.4 %collective-permute-start.9 = (f32[384,256]{1,0:T(8,128)S(1)}, f32[384,256]{1,0:T(8,128)S(1)}, u32[]{:S(2)}, u32[]{:S(2)}) collective-permute-start(f32[384,256]{1,0:T(8,128)S(1)} %get-tuple-element.23), channel_id=1, source_target_pairs={{0,4},{4,0},{8,12},{12,8},{16,20},{20,16},{24,28},{28,24},{1,5},{5... | collective-permute-start | bytes 1179656 | tf_op jit(solution)/shard_map/ppermute | solution.py:219
  37.6 4.9 %shard_map.59.refs_2_ = f32[768,256]{1,0:T(8,128)S(1)} custom-call(s32[4]{0:T(128)S(1)} %pad_add_fusion.starts, bf16[384,8192]{1,0:T(8,128)(2,1)} %bitcast.11, bf16[384,8192]{1,0:T(8,128)(2,1)} %collective-permute-done.far, bf16[512,256]{1,0:T(8,128)(2,1)S(1)} %get-tuple-element.26.refs_0_, bf16[512,256]{1,0:T(8,128)(2,1)S(1)} %get-tuple-element.27.refs_1_, ...), custom_call_target="tpu_custom_call" | custom-call | flops 1207959552 | bytes 6291456 | tf_op jit(solution)/shard_map/pallas_call | solution.py:92
  43.2 2.0 %shard_map.57 = bf16[384,256]{1,0:T(8,128)(2,1)} custom-call(f32[384,256]{1,0:T(8,128)} %copy-done.2, f32[384,256]{1,0:T(8,128)} %copy-done.6, f32[384,128]{1,0:T(8,128)} %pad_maximum_fusion.1.cosine, f32[384,128]{1,0:T(8,128)} %pad_maximum_fusion.2.sine), custom_call_target="tpu_custom_call" | custom-call | flops 589824 | bytes 1376256 | tf_op jit(solution)/shard_map/pallas_call | solution.py:125
  45.2 1.2 %collective-permute-start.12 = (bf16[512,256]{1,0:T(8,128)(2,1)S(1)}, bf16[512,256]{1,0:T(8,128)(2,1)S(1)}, u32[]{:S(2)}, u32[]{:S(2)}) collective-permute-start(bf16[512,256]{1,0:T(8,128)(2,1)S(1)} %get-tuple-element.28.refs_1_), channel_id=1, source_target_pairs={{0,16},{4,20},{8,24},{12,28},{16,0},{20,4},{24,8},{28,12},{1,17},{... | collective-permute-start | bytes 786440 | tf_op jit(solution)/shard_map/ppermute | solution.py:219
  46.4 1.2 %collective-permute-start.10 = (bf16[512,256]{1,0:T(8,128)(2,1)S(1)}, bf16[512,256]{1,0:T(8,128)(2,1)S(1)}, u32[]{:S(2)}, u32[]{:S(2)}) collective-permute-start(bf16[512,256]{1,0:T(8,128)(2,1)S(1)} %get-tuple-element.29.refs_0_), channel_id=1, source_target_pairs={{0,8},{4,12},{8,0},{12,4},{16,24},{20,28},{24,16},{28,20},{1,9},{5... | collective-permute-start | bytes 786440 | tf_op jit(solution)/shard_map/ppermute | solution.py:219
  47.6 2.5 %shard_map.60 = (f32[384,256]{1,0:T(8,128)S(1)}, f32[384,256]{1,0:T(8,128)S(1)}) custom-call(s32[4]{0:T(128)S(1)} %pad_add_fusion.starts, bf16[384,8192]{1,0:T(8,128)(2,1)} %bitcast.12, bf16[384,8192]{1,0:T(8,128)(2,1)} %collective-permute-done.far, bf16[512,256]{1,0:T(8,128)(2,1)S(1)} %collective-permute-done.15.refs_0_, ...), custom_call_target="tpu_custom_call" | custom-call | flops 402653184 | bytes 2097152 | tf_op jit(solution)/shard_map/pallas_call | solution.py:92
  50.2 1.2 %collective-permute-start.20 = (f32[384,256]{1,0:T(8,128)S(1)}, f32[384,256]{1,0:T(8,128)S(1)}, u32[]{:S(2)}, u32[]{:S(2)}) collective-permute-start(f32[384,256]{1,0:T(8,128)S(1)} %get-tuple-element.31), channel_id=1, source_target_pairs={{0,4},{4,0},{8,12},{12,8},{16,20},{20,16},{24,28},{28,24},{1,5},{5... | collective-permute-start | bytes 1179656 | tf_op jit(solution)/shard_map/ppermute | solution.py:219
  51.4 1.3 %collective-permute-start.21 = (bf16[384,256]{1,0:T(8,128)(2,1)S(1)}, bf16[384,256]{1,0:T(8,128)(2,1)S(1)}, u32[]{:S(2)}, u32[]{:S(2)}) collective-permute-start(bf16[384,256]{1,0:T(8,128)(2,1)S(1)} %copy-done.5), channel_id=1, source_target_pairs={{0,2},{1,3},{4,6},{5,7},{8,10},{9,11},{12,14},{13,15},{16,18},{17,... | collective-permute-start | bytes 589832 | tf_op jit(solution)/shard_map/ppermute | solution.py:284
  52.7 3.4 %collective-permute-start.22 = (bf16[384,256]{1,0:T(8,128)(2,1)S(1)}, bf16[384,256]{1,0:T(8,128)(2,1)S(1)}, u32[]{:S(2)}, u32[]{:S(2)}) collective-permute-start(bf16[384,256]{1,0:T(8,128)(2,1)S(1)} %copy-done.5), channel_id=1, source_target_pairs={{0,1},{1,2},{2,3},{4,5},{5,6},{6,7},{8,9},{9,10},{10,11},{12,13},{... | collective-permute-start | bytes 589832 | tf_op jit(solution)/shard_map/ppermute | solution.py:284
  56.2 4.4 %collective-permute-done.21 = bf16[384,256]{1,0:T(8,128)(2,1)S(1)} collective-permute-done((bf16[384,256]{1,0:T(8,128)(2,1)S(1)}, bf16[384,256]{1,0:T(8,128)(2,1)S(1)}, u32[]{:S(2)}, u32[]{:S(2)}) %collective-permute-start.21) | collective-permute-done | bytes 196640 | tf_op jit(solution)/shard_map/ppermute | solution.py:284
  60.8 8.7 %collective-permute-done.22 = bf16[384,256]{1,0:T(8,128)(2,1)S(1)} collective-permute-done((bf16[384,256]{1,0:T(8,128)(2,1)S(1)}, bf16[384,256]{1,0:T(8,128)(2,1)S(1)}, u32[]{:S(2)}, u32[]{:S(2)}) %collective-permute-start.22) | collective-permute-done | bytes 196640 | tf_op jit(solution)/shard_map/ppermute | solution.py:284
  70.0 1.2 %collective-permute-start.11 = (bf16[512,256]{1,0:T(8,128)(2,1)S(1)}, bf16[512,256]{1,0:T(8,128)(2,1)S(1)}, u32[]{:S(2)}, u32[]{:S(2)}) collective-permute-start(bf16[512,256]{1,0:T(8,128)(2,1)S(1)} %collective-permute-done.10.refs_2_), channel_id=1, source_target_pairs={{0,16},{4,20},{8,24},{12,28},{16,0},{20,4},{24,8},{28,12},{1,17},{... | collective-permute-start | bytes 786440 | tf_op jit(solution)/shard_map/ppermute | solution.py:219
  71.3 1.7 %shard_map.61.refs_0_ = bf16[384,256]{1,0:T(8,128)(2,1)S(1)} custom-call(f32[384,256]{1,0:T(8,128)S(1)} %get-tuple-element.30.near, f32[384,256]{1,0:T(8,128)S(1)} %collective-permute-done.20.far, f32[384,128]{1,0:T(8,128)S(1)} %copy-done, f32[384,128]{1,0:T(8,128)S(1)} %copy-done.1, s32[384,1]{1,0:T(8,128)S(1)} %sub.21.first, ...), custom_call_target="tpu_custom_call" | custom-call | flops 352321536 | bytes 786432 | tf_op jit(solution)/shard_map/pallas_call | solution.py:191
  73.1 3.9 %collective-permute-done.19.refs_4_ = bf16[512,256]{1,0:T(8,128)(2,1)S(1)} collective-permute-done((bf16[512,256]{1,0:T(8,128)(2,1)S(1)}, bf16[512,256]{1,0:T(8,128)(2,1)S(1)}, u32[]{:S(2)}, u32[]{:S(2)}) %collective-permute-start.19) | collective-permute-done | bytes 262176 | tf_op jit(solution)/shard_map/ppermute | solution.py:219
  77.0 4.9 %shard_map.58.refs_2_ = f32[768,256]{1,0:T(8,128)S(1)} custom-call(s32[4]{0:T(128)S(1)} %pad_add_fusion.starts, bf16[384,8192]{1,0:T(8,128)(2,1)} %bitcast.13, bf16[384,8192]{1,0:T(8,128)(2,1)} %collective-permute-done.far, bf16[512,256]{1,0:T(8,128)(2,1)S(1)} %get-tuple-element.29.refs_0_, bf16[512,256]{1,0:T(8,128)(2,1)S(1)} %get-tuple-element.28.refs_1_, ...), custom_call_target="tpu_custom_call" | custom-call | flops 1207959552 | bytes 6291456 | tf_op jit(solution)/shard_map/pallas_call | solution.py:92
  82.6 2.5 %shard_map.62 = (f32[384,256]{1,0:T(8,128)S(1)}, f32[384,256]{1,0:T(8,128)S(1)}) custom-call(s32[4]{0:T(128)S(1)} %pad_add_fusion.starts, bf16[384,8192]{1,0:T(8,128)(2,1)} %bitcast.14, bf16[384,8192]{1,0:T(8,128)(2,1)} %collective-permute-done.far, bf16[512,256]{1,0:T(8,128)(2,1)S(1)} %collective-permute-done.11.refs_0_, ...), custom_call_target="tpu_custom_call" | custom-call | flops 402653184 | bytes 2097152 | tf_op jit(solution)/shard_map/pallas_call | solution.py:92
  85.1 1.5 %collective-permute-start.23 = (f32[384,256]{1,0:T(8,128)S(1)}, f32[384,256]{1,0:T(8,128)S(1)}, u32[]{:S(2)}, u32[]{:S(2)}) collective-permute-start(f32[384,256]{1,0:T(8,128)S(1)} %get-tuple-element.34), channel_id=1, source_target_pairs={{0,4},{4,0},{8,12},{12,8},{16,20},{20,16},{24,28},{28,24},{1,5},{5... | collective-permute-start | bytes 1179656 | tf_op jit(solution)/shard_map/ppermute | solution.py:219
  86.6 1.3 %collective-permute-done.23.far = f32[384,256]{1,0:T(8,128)S(1)} collective-permute-done((f32[384,256]{1,0:T(8,128)S(1)}, f32[384,256]{1,0:T(8,128)S(1)}, u32[]{:S(2)}, u32[]{:S(2)}) %collective-permute-start.23) | collective-permute-done | bytes 393248 | tf_op jit(solution)/shard_map/ppermute | solution.py:219
  88.0 2.5 %shard_map.63 = bf16[384,512]{1,0:T(8,128)(2,1)} custom-call(f32[384,256]{1,0:T(8,128)S(1)} %get-tuple-element.33.near, f32[384,256]{1,0:T(8,128)S(1)} %collective-permute-done.23.far, f32[384,128]{1,0:T(8,128)S(1)} %copy-done, f32[384,128]{1,0:T(8,128)S(1)} %copy-done.1, s32[384,1]{1,0:T(8,128)S(1)} %sub.21.first, ...), custom_call_target="tpu_custom_call" | custom-call | flops 352321536 | bytes 786432 | tf_op jit(solution)/shard_map/pallas_call | solution.py:191
  (52 shorter events, 8.6 us)
Async XLA Ops:
  0.0 23.5 %collective-permute-start = (bf16[384,8192]{1,0:T(8,128)(2,1)}, bf16[384,8192]{1,0:T(8,128)(2,1)}, u32[]{:S(2)}, u32[]{:S(2)}) collective-permute-start(bf16[384,8192]{1,0:T(8,128)(2,1)} %bitcast.8), channel_id=1, source_target_pairs={{0,4},{4,0},{8,12},{12,8},{16,20},{20,16},{24,28},{28,24},{1,5},{5... | collective-permute-start | bytes 18874376 | tf_op jit(solution)/shard_map/ppermute | solution.py:219
  0.7 16.3 %collective-permute-start.8 = (bf16[1024,128]{1,0:T(8,128)(2,1)}, bf16[1024,128]{1,0:T(8,128)(2,1)S(1)}, u32[]{:S(2)}, u32[]{:S(2)}) collective-permute-start(bf16[1024,128]{1,0:T(8,128)(2,1)} %refs_0_.1), channel_id=1, source_target_pairs={{0,16},{4,20},{8,24},{12,28},{16,0},{20,4},{24,8},{28,12},{1,17},{... | collective-permute-start | bytes 786440 | tf_op jit(solution)/shard_map/ppermute | solution.py:219
  1.9 7.8 %collective-permute-start.1 = (bf16[1024,128]{1,0:T(8,128)(2,1)}, bf16[1024,128]{1,0:T(8,128)(2,1)S(1)}, u32[]{:S(2)}, u32[]{:S(2)}) collective-permute-start(bf16[1024,128]{1,0:T(8,128)(2,1)} %refs_0_.1), channel_id=1, source_target_pairs={{0,8},{4,12},{8,0},{12,4},{16,24},{20,28},{24,16},{28,20},{1,9},{5... | collective-permute-start | bytes 786440 | tf_op jit(solution)/shard_map/ppermute | solution.py:219
  3.1 13.9 %collective-permute-start.7 = (bf16[1024,128]{1,0:T(8,128)(2,1)}, bf16[1024,128]{1,0:T(8,128)(2,1)S(1)}, u32[]{:S(2)}, u32[]{:S(2)}) collective-permute-start(bf16[1024,128]{1,0:T(8,128)(2,1)} %refs_1_.1), channel_id=1, source_target_pairs={{0,8},{4,12},{8,0},{12,4},{16,24},{20,28},{24,16},{28,20},{1,9},{5... | collective-permute-start | bytes 786440 | tf_op jit(solution)/shard_map/ppermute | solution.py:219
  3.4 11.1 %collective-permute-start.3 = (bf16[1024,128]{1,0:T(8,128)(2,1)}, bf16[1024,128]{1,0:T(8,128)(2,1)S(1)}, u32[]{:S(2)}, u32[]{:S(2)}) collective-permute-start(bf16[1024,128]{1,0:T(8,128)(2,1)} %refs_1_.1), channel_id=1, source_target_pairs={{0,16},{4,20},{8,24},{12,28},{16,0},{20,4},{24,8},{28,12},{1,17},{... | collective-permute-start | bytes 786440 | tf_op jit(solution)/shard_map/ppermute | solution.py:219
  5.9 17.6 %copy-start.3 = (bf16[1024,128]{1,0:T(8,128)(2,1)S(1)}, bf16[1024,128]{1,0:T(8,128)(2,1)}, u32[]{:S(2)}) copy-start(bf16[1024,128]{1,0:T(8,128)(2,1)} %refs_0_.1) | copy-start | bytes 786436
  5.9 17.6 %copy-start.4 = (bf16[1024,128]{1,0:T(8,128)(2,1)S(1)}, bf16[1024,128]{1,0:T(8,128)(2,1)}, u32[]{:S(2)}) copy-start(bf16[1024,128]{1,0:T(8,128)(2,1)} %refs_1_.1) | copy-start | bytes 786436
  9.7 10.3 %collective-permute-start.2 = (bf16[1024,128]{1,0:T(8,128)(2,1)S(1)}, bf16[1024,128]{1,0:T(8,128)(2,1)S(1)}, u32[]{:S(2)}, u32[]{:S(2)}) collective-permute-start(bf16[1024,128]{1,0:T(8,128)(2,1)S(1)} %collective-permute-done.1.refs_2_), channel_id=1, source_target_pairs={{0,16},{4,20},{8,24},{12,28},{16,0},{20,4},{24,8},{28,12},{1,17},{... | collective-permute-start | bytes 786440 | tf_op jit(solution)/shard_map/ppermute | solution.py:219
  14.4 6.6 %collective-permute-start.4 = (bf16[1024,128]{1,0:T(8,128)(2,1)S(1)}, bf16[1024,128]{1,0:T(8,128)(2,1)S(1)}, u32[]{:S(2)}, u32[]{:S(2)}) collective-permute-start(bf16[1024,128]{1,0:T(8,128)(2,1)S(1)} %collective-permute-done.3.refs_5_), channel_id=1, source_target_pairs={{0,8},{4,12},{8,0},{12,4},{16,24},{20,28},{24,16},{28,20},{1,9},{5... | collective-permute-start | bytes 786440 | tf_op jit(solution)/shard_map/ppermute | solution.py:219
  17.0 19.2 %collective-permute-start.14 = (bf16[512,256]{1,0:T(8,128)(2,1)S(1)}, bf16[512,256]{1,0:T(8,128)(2,1)S(1)}, u32[]{:S(2)}, u32[]{:S(2)}) collective-permute-start(bf16[512,256]{1,0:T(8,128)(2,1)S(1)} %get-tuple-element.26.refs_0_), channel_id=1, source_target_pairs={{0,8},{4,12},{8,0},{12,4},{16,24},{20,28},{24,16},{28,20},{1,9},{5... | collective-permute-start | bytes 786440 | tf_op jit(solution)/shard_map/ppermute | solution.py:219
  17.3 19.1 %collective-permute-start.16 = (bf16[512,256]{1,0:T(8,128)(2,1)S(1)}, bf16[512,256]{1,0:T(8,128)(2,1)S(1)}, u32[]{:S(2)}, u32[]{:S(2)}) collective-permute-start(bf16[512,256]{1,0:T(8,128)(2,1)S(1)} %get-tuple-element.27.refs_1_), channel_id=1, source_target_pairs={{0,16},{4,20},{8,24},{12,28},{16,0},{20,4},{24,8},{28,12},{1,17},{... | collective-permute-start | bytes 786440 | tf_op jit(solution)/shard_map/ppermute | solution.py:219
  21.1 16.5 %collective-permute-start.5 = (bf16[512,256]{1,0:T(8,128)(2,1)S(1)}, bf16[512,256]{1,0:T(8,128)(2,1)S(1)}, u32[]{:S(2)}, u32[]{:S(2)}) collective-permute-start(bf16[512,256]{1,0:T(8,128)(2,1)S(1)} %get-tuple-element.26.refs_0_), channel_id=1, source_target_pairs={{0,16},{4,20},{8,24},{12,28},{16,0},{20,4},{24,8},{28,12},{1,17},{... | collective-permute-start | bytes 786440 | tf_op jit(solution)/shard_map/ppermute | solution.py:219
  22.3 15.2 %collective-permute-start.6 = (bf16[512,256]{1,0:T(8,128)(2,1)S(1)}, bf16[512,256]{1,0:T(8,128)(2,1)S(1)}, u32[]{:S(2)}, u32[]{:S(2)}) collective-permute-start(bf16[512,256]{1,0:T(8,128)(2,1)S(1)} %get-tuple-element.27.refs_1_), channel_id=1, source_target_pairs={{0,8},{4,12},{8,0},{12,4},{16,24},{20,28},{24,16},{28,20},{1,9},{5... | collective-permute-start | bytes 786440 | tf_op jit(solution)/shard_map/ppermute | solution.py:219
  31.0 6.6 %copy-start.2 = (f32[384,256]{1,0:T(8,128)}, f32[384,256]{1,0:T(8,128)S(1)}, u32[]{:S(2)}) copy-start(f32[384,256]{1,0:T(8,128)S(1)} %get-tuple-element.22.near) | copy-start | bytes 1179652
  31.0 11.5 %collective-permute-start.9 = (f32[384,256]{1,0:T(8,128)S(1)}, f32[384,256]{1,0:T(8,128)S(1)}, u32[]{:S(2)}, u32[]{:S(2)}) collective-permute-start(f32[384,256]{1,0:T(8,128)S(1)} %get-tuple-element.23), channel_id=1, source_target_pairs={{0,4},{4,0},{8,12},{12,8},{16,20},{20,16},{24,28},{28,24},{1,5},{5... | collective-permute-start | bytes 1179656 | tf_op jit(solution)/shard_map/ppermute | solution.py:219
  36.2 11.5 %collective-permute-start.15 = (bf16[512,256]{1,0:T(8,128)(2,1)S(1)}, bf16[512,256]{1,0:T(8,128)(2,1)S(1)}, u32[]{:S(2)}, u32[]{:S(2)}) collective-permute-start(bf16[512,256]{1,0:T(8,128)(2,1)S(1)} %collective-permute-done.14.refs_2_), channel_id=1, source_target_pairs={{0,16},{4,20},{8,24},{12,28},{16,0},{20,4},{24,8},{28,12},{1,17},{... | collective-permute-start | bytes 786440 | tf_op jit(solution)/shard_map/ppermute | solution.py:219
  36.4 11.2 %collective-permute-start.17 = (bf16[512,256]{1,0:T(8,128)(2,1)S(1)}, bf16[512,256]{1,0:T(8,128)(2,1)S(1)}, u32[]{:S(2)}, u32[]{:S(2)}) collective-permute-start(bf16[512,256]{1,0:T(8,128)(2,1)S(1)} %collective-permute-done.16.refs_5_), channel_id=1, source_target_pairs={{0,8},{4,12},{8,0},{12,4},{16,24},{20,28},{24,16},{28,20},{1,9},{5... | collective-permute-start | bytes 786440 | tf_op jit(solution)/shard_map/ppermute | solution.py:219
  42.5 0.8 copy-start.6
  45.2 24.5 %collective-permute-start.12 = (bf16[512,256]{1,0:T(8,128)(2,1)S(1)}, bf16[512,256]{1,0:T(8,128)(2,1)S(1)}, u32[]{:S(2)}, u32[]{:S(2)}) collective-permute-start(bf16[512,256]{1,0:T(8,128)(2,1)S(1)} %get-tuple-element.28.refs_1_), channel_id=1, source_target_pairs={{0,16},{4,20},{8,24},{12,28},{16,0},{20,4},{24,8},{28,12},{1,17},{... | collective-permute-start | bytes 786440 | tf_op jit(solution)/shard_map/ppermute | solution.py:219
  46.4 5.0 %copy-start.5 = (bf16[384,256]{1,0:T(8,128)(2,1)S(1)}, bf16[384,256]{1,0:T(8,128)(2,1)}, u32[]{:S(2)}) copy-start(bf16[384,256]{1,0:T(8,128)(2,1)} %shard_map.57) | copy-start | bytes 589828
  46.4 23.6 %collective-permute-start.10 = (bf16[512,256]{1,0:T(8,128)(2,1)S(1)}, bf16[512,256]{1,0:T(8,128)(2,1)S(1)}, u32[]{:S(2)}, u32[]{:S(2)}) collective-permute-start(bf16[512,256]{1,0:T(8,128)(2,1)S(1)} %get-tuple-element.29.refs_0_), channel_id=1, source_target_pairs={{0,8},{4,12},{8,0},{12,4},{16,24},{20,28},{24,16},{28,20},{1,9},{5... | collective-permute-start | bytes 786440 | tf_op jit(solution)/shard_map/ppermute | solution.py:219
  50.2 21.1 %copy-start = (f32[384,128]{1,0:T(8,128)S(1)}, f32[384,128]{1,0:T(8,128)}, u32[]{:S(2)}) copy-start(f32[384,128]{1,0:T(8,128)} %pad_maximum_fusion.1.cosine) | copy-start | bytes 589828
  50.2 21.1 %copy-start.1 = (f32[384,128]{1,0:T(8,128)S(1)}, f32[384,128]{1,0:T(8,128)}, u32[]{:S(2)}) copy-start(f32[384,128]{1,0:T(8,128)} %pad_maximum_fusion.2.sine) | copy-start | bytes 589828
  50.2 21.1 %collective-permute-start.20 = (f32[384,256]{1,0:T(8,128)S(1)}, f32[384,256]{1,0:T(8,128)S(1)}, u32[]{:S(2)}, u32[]{:S(2)}) collective-permute-start(f32[384,256]{1,0:T(8,128)S(1)} %get-tuple-element.31), channel_id=1, source_target_pairs={{0,4},{4,0},{8,12},{12,8},{16,20},{20,16},{24,28},{28,24},{1,5},{5... | collective-permute-start | bytes 1179656 | tf_op jit(solution)/shard_map/ppermute | solution.py:219
  51.4 9.2 %collective-permute-start.21 = (bf16[384,256]{1,0:T(8,128)(2,1)S(1)}, bf16[384,256]{1,0:T(8,128)(2,1)S(1)}, u32[]{:S(2)}, u32[]{:S(2)}) collective-permute-start(bf16[384,256]{1,0:T(8,128)(2,1)S(1)} %copy-done.5), channel_id=1, source_target_pairs={{0,2},{1,3},{4,6},{5,7},{8,10},{9,11},{12,14},{13,15},{16,18},{17,... | collective-permute-start | bytes 589832 | tf_op jit(solution)/shard_map/ppermute | solution.py:284
  52.7 16.8 %collective-permute-start.22 = (bf16[384,256]{1,0:T(8,128)(2,1)S(1)}, bf16[384,256]{1,0:T(8,128)(2,1)S(1)}, u32[]{:S(2)}, u32[]{:S(2)}) collective-permute-start(bf16[384,256]{1,0:T(8,128)(2,1)S(1)} %copy-done.5), channel_id=1, source_target_pairs={{0,1},{1,2},{2,3},{4,5},{5,6},{6,7},{8,9},{9,10},{10,11},{12,13},{... | collective-permute-start | bytes 589832 | tf_op jit(solution)/shard_map/ppermute | solution.py:284
  60.6 12.5 %collective-permute-start.18 = (bf16[512,256]{1,0:T(8,128)(2,1)S(1)}, bf16[512,256]{1,0:T(8,128)(2,1)S(1)}, u32[]{:S(2)}, u32[]{:S(2)}) collective-permute-start(bf16[512,256]{1,0:T(8,128)(2,1)S(1)} %get-tuple-element.28.refs_1_), channel_id=1, source_target_pairs={{0,8},{4,12},{8,0},{12,4},{16,24},{20,28},{24,16},{28,20},{1,9},{5... | collective-permute-start | bytes 786440 | tf_op jit(solution)/shard_map/ppermute | solution.py:219
  69.5 7.4 %collective-permute-start.19 = (bf16[512,256]{1,0:T(8,128)(2,1)S(1)}, bf16[512,256]{1,0:T(8,128)(2,1)S(1)}, u32[]{:S(2)}, u32[]{:S(2)}) collective-permute-start(bf16[512,256]{1,0:T(8,128)(2,1)S(1)} %get-tuple-element.29.refs_0_), channel_id=1, source_target_pairs={{0,16},{4,20},{8,24},{12,28},{16,0},{20,4},{24,8},{28,12},{1,17},{... | collective-permute-start | bytes 786440 | tf_op jit(solution)/shard_map/ppermute | solution.py:219
  69.7 12.1 %collective-permute-start.13 = (bf16[512,256]{1,0:T(8,128)(2,1)S(1)}, bf16[512,256]{1,0:T(8,128)(2,1)S(1)}, u32[]{:S(2)}, u32[]{:S(2)}) collective-permute-start(bf16[512,256]{1,0:T(8,128)(2,1)S(1)} %collective-permute-done.12.refs_5_), channel_id=1, source_target_pairs={{0,8},{4,12},{8,0},{12,4},{16,24},{20,28},{24,16},{28,20},{1,9},{5... | collective-permute-start | bytes 786440 | tf_op jit(solution)/shard_map/ppermute | solution.py:219
  70.0 12.6 %collective-permute-start.11 = (bf16[512,256]{1,0:T(8,128)(2,1)S(1)}, bf16[512,256]{1,0:T(8,128)(2,1)S(1)}, u32[]{:S(2)}, u32[]{:S(2)}) collective-permute-start(bf16[512,256]{1,0:T(8,128)(2,1)S(1)} %collective-permute-done.10.refs_2_), channel_id=1, source_target_pairs={{0,16},{4,20},{8,24},{12,28},{16,0},{20,4},{24,8},{28,12},{1,17},{... | collective-permute-start | bytes 786440 | tf_op jit(solution)/shard_map/ppermute | solution.py:219
  85.1 2.9 %collective-permute-start.23 = (f32[384,256]{1,0:T(8,128)S(1)}, f32[384,256]{1,0:T(8,128)S(1)}, u32[]{:S(2)}, u32[]{:S(2)}) collective-permute-start(f32[384,256]{1,0:T(8,128)S(1)} %get-tuple-element.34), channel_id=1, source_target_pairs={{0,4},{4,0},{8,12},{12,8},{16,20},{20,16},{24,28},{28,24},{1,5},{5... | collective-permute-start | bytes 1179656 | tf_op jit(solution)/shard_map/ppermute | solution.py:219

commit v3 on v2

v3 whole, which is shorter than its diff:
```python
import functools
import math

import jax
import jax.numpy as jnp
from jax import lax
from jax.experimental import pallas as pl
from jax.experimental.pallas import tpu as pltpu
from jax.sharding import PartitionSpec as P

ROW_TILE = 128
MIB = 1024 * 1024


def rope_tables(positions, head_size):
    half_size = head_size // 2
    exponent = jnp.arange(half_size, dtype=jnp.float32) * (2.0 / head_size)
    inverse = jnp.power(jnp.float32(500000.0), -exponent)
    angles = positions.astype(jnp.float32)[:, None] * inverse[None, :]
    cosine = jnp.cos(angles)
    sine_part = jnp.sin(angles)
    return (
        jnp.concatenate([cosine, cosine], axis=-1),
        jnp.concatenate([-sine_part, sine_part], axis=-1),
    )


def doc_starts(doc_sizes, positions):
    doc_ends = jnp.cumsum(doc_sizes)
    doc_begin = doc_ends - doc_sizes
    chosen = jnp.where(doc_begin[None, :] <= positions[:, None], doc_begin[None, :], 0)
    return jnp.max(chosen, axis=1)


def vmem(count):
    return [pl.BlockSpec(memory_space=pltpu.VMEM)] * count


def anywhere(count):
    return [pl.BlockSpec(memory_space=pl.ANY)] * count


def after(array, *earlier):
    return lax.optimization_barrier((array, *earlier))[0]


def project_kernel(steps, carried, final, starts, near, far, *refs):
    count = sum(len(spots) for _, spots in steps)
    weights, refs = refs[:count], refs[count:]
    if carried:
        carry, refs = refs[0], refs[1:]
    outs = refs[: 2 if final else 1]
    refs = refs[len(outs) :]
    tokens, held, sems = refs[: len(steps)], refs[len(steps) : 2 * len(steps)], refs[-1]
    rows = near.shape[0]
    copies = []
    used = 0
    for step, (depth, spots) in enumerate(steps):
        window = pl.ds(pl.multiple_of(starts[step], 128), depth)
        batch = [
            pltpu.make_async_copy(near.at[:, window], tokens[step].at[:rows], sems.at[step, 0]),
            pltpu.make_async_copy(far.at[:, window], tokens[step].at[rows:], sems.at[step, 1]),
        ]
        for index, columns in enumerate(spots):
            batch.append(
                pltpu.make_async_copy(
                    weights[used], held[step].at[:, columns], sems.at[step, 2 + index]
                )
            )
            used += 1
        for copy in batch:
            copy.start()
        copies.append(batch)
    total = carry[...] if carried else None
    for step, batch in enumerate(copies):
        for copy in batch:
            copy.wait()
        term = jnp.dot(tokens[step][...], held[step][...], preferred_element_type=jnp.float32)
        total = term if total is None else total + term
    if final:
        outs[0][...] = total[:rows]
        outs[1][...] = total[rows:]
    else:
        outs[0][...] = total


def project(terms, near, far, carry=None, final=False):
    rows = near.shape[0]
    width = sum(array.shape[1] for array in terms[0][1])
    steps = []
    for _, arrays in terms:
        edges = [sum(array.shape[1] for array in arrays[:i]) for i in range(len(arrays) + 1)]
        spots = [slice(*edge) for edge in zip(edges[:-1], edges[1:])]
        steps.append((arrays[0].shape[0], spots))
    depth = sum(step[0] for step in steps)
    starts = jnp.stack([start for start, _ in terms]).astype(jnp.int32)
    weights = [array for _, arrays in terms for array in arrays]
    whole = jax.ShapeDtypeStruct((2 * rows, width), jnp.float32)
    part = jax.ShapeDtypeStruct((rows, width), jnp.float32)
    carries = [] if carry is None else [carry]
    need = 2 * depth * (2 * rows + width) + 16 * rows * width
    return pl.pallas_call(
        functools.partial(project_kernel, steps, carry is not None, final),
        out_shape=(part, part) if final else whole,
        in_specs=[pl.BlockSpec(memory_space=pltpu.SMEM)]
        + anywhere(2 + len(weights))
        + vmem(len(carries)),
        out_specs=tuple(vmem(2)) if final else vmem(1)[0],
        scratch_shapes=[pltpu.VMEM((2 * rows, step[0]), jnp.bfloat16) for step in steps]
        + [pltpu.VMEM((step[0], width), jnp.bfloat16) for step in steps]
        + [pltpu.SemaphoreType.DMA((len(steps), 4))],
        compiler_params=pltpu.CompilerParams(vmem_limit_bytes=need + 8 * MIB),
        cost_estimate=pl.CostEstimate(
            flops=4 * rows * width * depth,
            bytes_accessed=2 * depth * (2 * rows + width),
            transcendentals=0,
        ),
    )(starts, near, far, *weights, *carries)


def turn(vectors, cosine, sine):
    return vectors * cosine + pltpu.roll(vectors, vectors.shape[1] // 2, 1) * sine


def pair_kernel(near, far, cosine, sine, out):
    head_size = cosine.shape[1]
    pair = near[...] + far[...]
    out[:, :head_size] = turn(pair[:, :head_size], cosine[...], sine[...]).astype(out.dtype)
    out[:, head_size:] = pair[:, head_size:].astype(out.dtype)


def finish_pair(near, far, cosine, sine):
    return pl.pallas_call(
        pair_kernel,
        out_shape=jax.ShapeDtypeStruct(near.shape, jnp.bfloat16),
        in_specs=vmem(4),
        out_specs=vmem(1)[0],
        compiler_params=pltpu.CompilerParams(vmem_limit_bytes=8 * MIB),
        cost_estimate=pl.CostEstimate(
            flops=6 * near.size, bytes_accessed=14 * near.size, transcendentals=0
        ),
    )(near, far, cosine, sine)


def attend_kernel(back, near, far, cosine, sine, first, keys_values, out, rotated):
    rows, head_size = cosine.shape
    head_count = near.shape[1] // head_size
    base = keys_values.shape[0] - rows
    tiles = rows // ROW_TILE
    for head in range(head_count):
        columns = slice(head * head_size, (head + 1) * head_size)
        turned = turn(near[:, columns] + far[:, columns], cosine[...], sine[...])
        turned = turned.astype(jnp.bfloat16)
        for tile in range(tiles):
            rotated[tile, head * ROW_TILE : (head + 1) * ROW_TILE, :] = turned[
                tile * ROW_TILE : (tile + 1) * ROW_TILE
            ]
    scale = jnp.float32(math.log2(math.e) / math.sqrt(head_size))
    for tile in range(tiles):
        begin = base + tile * ROW_TILE - back
        window = keys_values[begin : begin + back + ROW_TILE, :]
        scores = lax.dot_general(
            rotated[tile],
            window[:, :head_size],
            (((1,), (1,)), ((), ())),
            preferred_element_type=jnp.float32,
        )
        shape = (ROW_TILE, back + ROW_TILE)
        key_place = lax.broadcasted_iota(jnp.int32, shape, 1) + (tile * ROW_TILE - back)
        row_place = lax.broadcasted_iota(jnp.int32, shape, 0) + tile * ROW_TILE
        lower = first[tile * ROW_TILE : (tile + 1) * ROW_TILE, :]
        allowed = (key_place <= row_place) & (key_place >= lower)
        for head in range(head_count):
            part = scores[head * ROW_TILE : (head + 1) * ROW_TILE]
            part = jnp.where(allowed, part, jnp.float32(-1e30))
            largest = jnp.max(part, axis=-1, keepdims=True)
            exponents = jnp.exp2((part - largest) * scale)
            denominator = jnp.sum(exponents, axis=-1, keepdims=True)
            numerator = jnp.dot(
                exponents.astype(jnp.bfloat16),
                window[:, head_size:],
                preferred_element_type=jnp.float32,
            )
            left = head * head_size
            out[tile * ROW_TILE : (tile + 1) * ROW_TILE, left : left + head_size] = (
                numerator / denominator
            ).astype(out.dtype)


def attend(near, far, cosine, sine, first, keys_values, back):
    rows, width = near.shape
    head_size = cosine.shape[1]
    head_count = width // head_size
    window = back + ROW_TILE
    return pl.pallas_call(
        functools.partial(attend_kernel, back),
        out_shape=jax.ShapeDtypeStruct((rows, width), jnp.bfloat16),
        in_specs=vmem(6),
        out_specs=vmem(1)[0],
        scratch_shapes=[
            pltpu.VMEM((rows // ROW_TILE, head_count * ROW_TILE, head_size), jnp.bfloat16)
        ],
        compiler_params=pltpu.CompilerParams(
            vmem_limit_bytes=8 * MIB + 24 * head_count * ROW_TILE * window
        ),
        cost_estimate=pl.CostEstimate(
            flops=4 * rows * width * window,
            bytes_accessed=8 * rows * width,
            transcendentals=rows * head_count * window,
        ),
    )(near, far, cosine, sine, first, keys_values)


def shards(dp_size, ctx_size, tokens, w_query, w_key, w_value, doc_lengths):
    hidden = tokens[0]
    row_count = hidden.shape[0]
    depth, query_width = w_query.shape
    head_size = w_key.shape[1]
    chips = dp_size // 2
    bits = chips.bit_length() - 1
    me = lax.axis_index("dp")
    place = lax.axis_index("ctx")

    def swap(array, mask):
        return lax.ppermute(array, "dp", [(i, i ^ mask) for i in range(dp_size)])

    def fetch(pair, gates, assisted):
        held = [{0: [(0, array)]} for array in pair]
        for step in range(bits):
            axes = (step, bits - 1 - step)
            for sources in zip(*[sorted(side) for side in held]):
                for side, source in enumerate(sources):
                    array = held[side][source][0][1]
                    mask = 2 << axes[side]
                    if source == 0 and gates:
                        array = after(array, *gates[min(step, len(gates) - 1)])
                    if source == 0 and assisted and step == bits - 1:
                        some = array.shape[0] // 2
                        begin = (place % 2) * some
                        mine = swap(lax.dynamic_slice_in_dim(array, begin, some, 0), mask)
                        other = lax.ppermute(mine, "ctx", [(i, i ^ 1) for i in range(ctx_size)])
                        got = [(begin, mine), (some - begin, other)]
                    else:
                        got = [(0, swap(array, mask))]
                    held[side][source | (1 << axes[side])] = got
        return held

    sibling_hidden = swap(hidden, 1)

    offset = place * row_count
    positions = offset + jnp.arange(row_count, dtype=jnp.int32)
    cosine, sine = rope_tables(positions, head_size)
    first = (doc_starts(doc_lengths[0], positions) - offset)[:, None]

    def begins(chip):
        return (me ^ (2 * chip)) * depth

    first_axis, last_axis = 1, 1 << (bits - 1)
    last = chips - 1

    pair_held = fetch((w_key, w_value), None, False)
    pair_terms = [
        (begins(chip), [pair_held[side][chip][0][1] for side in range(2)]) for chip in range(chips)
    ]
    carry = project(pair_terms[:-1], hidden, sibling_hidden)
    gates = (
        [pair_held[0][last_axis][0][1], pair_held[1][first_axis][0][1]],
        [pair_held[0][last][0][1], pair_held[1][last][0][1], carry],
    )
    half = depth // 2
    query_held = fetch((w_query[:half], w_query[half:]), gates, ctx_size % 2 == 0)

    near, far = project(pair_terms[-1:], hidden, sibling_hidden, carry, True)
    pair = finish_pair(near, swap(far, 1), cosine, sine)
    longest = ctx_size * row_count // 2
    back = -(-(longest - 1) // ROW_TILE) * ROW_TILE
    hops = min(ctx_size - 1, -(-back // row_count))
    blocks = [
        lax.ppermute(pair, "ctx", [(i, i + hop) for i in range(ctx_size - hop)])
        for hop in range(hops, 0, -1)
    ]
    keys_values = jnp.concatenate(blocks + [pair], axis=0)

    def query_terms(wanted):
        return [
            (begins(chip) + side * half + begin, [array])
            for side, chip in wanted
            for begin, array in query_held[side][chip]
        ]

    early = [(0, 0), (1, 0), (0, first_axis), (1, last_axis)]
    late = [(0, last), (1, last)]
    rest = [
        (side, chip)
        for chip in range(chips)
        for side in range(2)
        if (side, chip) not in early + late
    ]
    carry = after(project(query_terms(early), hidden, sibling_hidden), pair)
    carry = project(query_terms(rest), hidden, sibling_hidden, carry)
    near, far = project(query_terms(late), hidden, sibling_hidden, carry, True)
    return attend(near, swap(far, 1), cosine, sine, first, keys_values, back)[None]


def solution(mesh):
    return jax.shard_map(
        functools.partial(shards, mesh.shape["dp"], mesh.shape["ctx"]),
        mesh=mesh,
        in_specs=(P("dp", "ctx", None), P("dp", None), P("dp", None), P("dp", None), P("dp", None)),
        out_specs=P("dp", "ctx", None),
        check_vma=False,
    )
```

time: 90.8 us -> 94.7 us (1.043)
  local copies, waits for them, and re-layouts: 2.14 us -> 11.3 us
  Pallas kernels: 28.5 us -> 21.9 us
  waiting for transfers between devices: 29.8 us -> 36.2 us
  starting transfers between devices: 25.7 us -> 20.8 us
    unnamed x14 -> x32, local copies, waits for them, and re-layouts: 0.78 us -> 8.28 us
    ppermute x22 -> x15, starting transfers between devices: 21 us -> 14.8 us  [swap(): return lax.ppermute(array, 'dp', [(i, i ^ mask) for i in range(dp_size)])]
    pallas_call x6 -> x5, Pallas kernels: 22.2 us -> 17.1 us  [project(): pl.pallas_call(functools.partial(project_kernel, steps, carry is not None...]
    ppermute x0 -> x2, waiting for transfers between devices: none -> 3.9 us  [fetch(): other = lax.ppermute(mine, 'ctx', [(i, i ^ 1) for i in range(ctx_size)])]
    ppermute x22 -> x15, waiting for transfers between devices: 16.8 us -> 18.8 us  [swap(): return lax.ppermute(array, 'dp', [(i, i ^ mask) for i in range(dp_size)])]
    dynamic_slice x0 -> x2, local copies, waits for them, and re-layouts: none -> 1.54 us  [fetch(): mine = swap(lax.dynamic_slice_in_dim(array, begin, some, 0), mask)]
    ppermute x0 -> x2, starting transfers between devices: none -> 1.53 us  [fetch(): other = lax.ppermute(mine, 'ctx', [(i, i ^ 1) for i in range(ctx_size)])]
    pallas_call x2 -> x1, Pallas kernels: 4.23 us -> 3.69 us  [attend(): pl.pallas_call(functools.partial(attend_kernel, back), out_shape=jax.Shap...]
  transfers between devices with their start and end apart: 24 -> 19, of which waited for: 9 -> 7; matrix products, arithmetic and copies ran while one was open for 6% -> 7% of each run, Pallas kernels for 26% -> 16%
where the time goes in v3:
time: 94.7 us; the launch traced here: 94.3 us
  waiting for transfers between devices  36.2 us (38%)
  Pallas kernels  21.9 us (23%)
  starting transfers between devices  20.8 us (22%)
  local copies, waits for them, and re-layouts  11.3 us (12%)
  other arithmetic  3.89 us (4%)
    ppermute x15, waiting for transfers between devices, swap(): return lax.ppermute(array, 'dp', [(i, i ^ mask) for i in range(dp_size)])  18.8 us
    pallas_call x5, Pallas kernels, project(): pl.pallas_call(functools.partial(project_kernel, steps, carry is not None...  17.1 us
    ppermute x15, starting transfers between devices, swap(): return lax.ppermute(array, 'dp', [(i, i ^ mask) for i in range(dp_size)])  14.8 us
    ppermute x2, waiting for transfers between devices, shards(): lax.ppermute(pair, 'ctx', [(i, i + hop) for i in range(ctx_size - hop)])  13.5 us
    unnamed x32, local copies, waits for them, and re-layouts  8.28 us
    ppermute x2, starting transfers between devices, shards(): lax.ppermute(pair, 'ctx', [(i, i + hop) for i in range(ctx_size - hop)])  4.49 us
    ppermute x2, waiting for transfers between devices, fetch(): other = lax.ppermute(mine, 'ctx', [(i, i ^ 1) for i in range(ctx_size)])  3.9 us
    pallas_call x1, Pallas kernels, attend(): pl.pallas_call(functools.partial(attend_kernel, back), out_shape=jax.Shap...  3.69 us
  transfers between devices with their start and end apart: 19, of which 7 were waited for; matrix products, arithmetic and copies ran while one was open for 7% of the time, Pallas kernels for 16%

profile of v3, /device:TPU:17, one launch (start us, length us, event | category | flops | bytes accessed | tf_op | source)
XLA Modules:
  0.0 94.3 jit_solution(5673791781761267505)
XLA Ops:
  0.7 1.2 %collective-permute-start.1 = (bf16[1024,128]{1,0:T(8,128)(2,1)}, bf16[1024,128]{1,0:T(8,128)(2,1)S(1)}, u32[]{:S(2)}, u32[]{:S(2)}) collective-permute-start(bf16[1024,128]{1,0:T(8,128)(2,1)} %refs_0_.1), channel_id=1, source_target_pairs={{0,16},{4,20},{8,24},{12,28},{16,0},{20,4},{24,8},{28,12},{1,17},{... | collective-permute-start | bytes 786440 | tf_op jit(solution)/shard_map/ppermute | solution.py:225
  1.9 1.2 %collective-permute-start.7 = (bf16[1024,128]{1,0:T(8,128)(2,1)}, bf16[1024,128]{1,0:T(8,128)(2,1)S(1)}, u32[]{:S(2)}, u32[]{:S(2)}) collective-permute-start(bf16[1024,128]{1,0:T(8,128)(2,1)} %refs_0_.1), channel_id=1, source_target_pairs={{0,8},{4,12},{8,0},{12,4},{16,24},{20,28},{24,16},{28,20},{1,9},{5... | collective-permute-start | bytes 786440 | tf_op jit(solution)/shard_map/ppermute | solution.py:225
  3.6 1.3 %fusion.2 = (bf16[512,512]{1,0:T(8,128)(2,1)S(1)}, bf16[512,512]{1,0:T(8,128)(2,1)S(1)}) fusion(bf16[1024,512]{1,0:T(8,128)(2,1)} %param.6), kind=kLoop, calls=%fused_computation.18 | loop fusion | bytes 2097152 | tf_op jit(solution)/shard_map/slice | solution.py:271
  5.0 3.8 %collective-permute-done.1.refs_4_ = bf16[1024,128]{1,0:T(8,128)(2,1)S(1)} collective-permute-done((bf16[1024,128]{1,0:T(8,128)(2,1)}, bf16[1024,128]{1,0:T(8,128)(2,1)S(1)}, u32[]{:S(2)}, u32[]{:S(2)}) %collective-permute-start.1) | collective-permute-done | bytes 262176 | tf_op jit(solution)/shard_map/ppermute | solution.py:225
  8.8 6.5 %collective-permute-done.2.refs_3_ = bf16[1024,128]{1,0:T(8,128)(2,1)S(1)} collective-permute-done((bf16[1024,128]{1,0:T(8,128)(2,1)}, bf16[1024,128]{1,0:T(8,128)(2,1)S(1)}, u32[]{:S(2)}, u32[]{:S(2)}) %collective-permute-start.2) | collective-permute-done | bytes 262176 | tf_op jit(solution)/shard_map/ppermute | solution.py:225
  15.4 1.2 %collective-permute-start.3 = (bf16[512,512]{1,0:T(8,128)(2,1)S(1)}, bf16[512,512]{1,0:T(8,128)(2,1)}, u32[]{:S(2)}, u32[]{:S(2)}) collective-permute-start(bf16[512,512]{1,0:T(8,128)(2,1)S(1)} %get-tuple-element.17.refs_0_), channel_id=1, source_target_pairs={{0,8},{4,12},{8,0},{12,4},{16,24},{20,28},{24,16},{28,20},{1,9},{5... | collective-permute-start | bytes 1572872 | tf_op jit(solution)/shard_map/ppermute | solution.py:225
  16.9 1.5 %fusion = (f32[384,64]{1,0:T(8,128)}, f32[384,64]{1,0:T(8,128)}, f32[384,64]{1,0:T(8,128)S(1)}) fusion(f32[64]{0:T(128)S(1)} %negate_power_fusion, f32[384]{0:T(512)S(1)} %get-tuple-element.29), kind=kLoop, calls=%fused_computation.5 | loop fusion | flops 49152 | bytes 296704 | tf_op jit(solution)/shard_map/neg | solution.py:24
  18.7 1.2 %collective-permute-start.8 = (bf16[1024,128]{1,0:T(8,128)(2,1)S(1)}, bf16[1024,128]{1,0:T(8,128)(2,1)S(1)}, u32[]{:S(2)}, u32[]{:S(2)}) collective-permute-start(bf16[1024,128]{1,0:T(8,128)(2,1)S(1)} %collective-permute-done.7.refs_2_), channel_id=1, source_target_pairs={{0,16},{4,20},{8,24},{12,28},{16,0},{20,4},{24,8},{28,12},{1,17},{... | collective-permute-start | bytes 786440 | tf_op jit(solution)/shard_map/ppermute | solution.py:225
  20.1 7.7 %collective-permute-done.3.refs_2_ = bf16[512,512]{1,0:T(8,128)(2,1)} collective-permute-done((bf16[512,512]{1,0:T(8,128)(2,1)S(1)}, bf16[512,512]{1,0:T(8,128)(2,1)}, u32[]{:S(2)}, u32[]{:S(2)}) %collective-permute-start.3) | collective-permute-done | bytes 524320 | tf_op jit(solution)/shard_map/ppermute | solution.py:225
  29.2 2.8 %copy-done = bf16[1,384,8192]{2,1,0:T(8,128)(2,1)S(1)} copy-done((bf16[1,384,8192]{2,1,0:T(8,128)(2,1)S(1)}, bf16[1,384,8192]{2,1,0:T(8,128)(2,1)}, u32[]{:S(2)}) %copy-start) | copy-done | bytes 6291480
  32.0 4.7 %shard_map.55.refs_2_ = f32[768,256]{1,0:T(8,128)S(1)} custom-call(s32[3]{0:T(128)S(1)} %pad_add_fusion.2.starts, bf16[384,8192]{1,0:T(8,128)(2,1)S(1)} %bitcast.16, bf16[384,8192]{1,0:T(8,128)(2,1)} %collective-permute-done.far, bf16[1024,128]{1,0:T(8,128)(2,1)S(1)} %copy-done.5, bf16[1024,128]{1,0:T(8,128)(2,1)S(1)} %copy-done.6, ...), custom_call_target="tpu_custom_call" | custom-call | flops 1207959552 | bytes 6291456 | tf_op jit(solution)/shard_map/pallas_call | solution.py:102
  36.8 0.8 constant_dynamic-slice_fusion.1
  37.6 1.0 %collective-permute-start.11 = (bf16[256,512]{1,0:T(8,128)(2,1)}, bf16[256,512]{1,0:T(8,128)(2,1)}, u32[]{:S(2)}, u32[]{:S(2)}) collective-permute-start(bf16[256,512]{1,0:T(8,128)(2,1)} %constant_dynamic-slice_fusion.1), channel_id=1, source_target_pairs={{0,8},{4,12},{8,0},{12,4},{16,24},{20,28},{24,16},{28,20},{1,9},{5... | collective-permute-start | bytes 786440 | tf_op jit(solution)/shard_map/ppermute | solution.py:225
  39.8 0.9 %copy-done.8 = bf16[1024,128]{1,0:T(8,128)(2,1)S(1)} copy-done((bf16[1024,128]{1,0:T(8,128)(2,1)S(1)}, bf16[1024,128]{1,0:T(8,128)(2,1)}, u32[]{:S(2)}) %copy-start.8) | copy-done | bytes 262168
  40.8 0.9 %copy-done.10 = bf16[1024,128]{1,0:T(8,128)(2,1)S(1)} copy-done((bf16[1024,128]{1,0:T(8,128)(2,1)S(1)}, bf16[1024,128]{1,0:T(8,128)(2,1)}, u32[]{:S(2)}) %copy-start.10) | copy-done | bytes 262168
  41.7 2.7 %shard_map.57 = (f32[384,256]{1,0:T(8,128)S(1)}, f32[384,256]{1,0:T(8,128)}) custom-call(s32[1]{0:T(128)} %bitcast.starts, bf16[384,8192]{1,0:T(8,128)(2,1)S(1)} %bitcast.17, bf16[384,8192]{1,0:T(8,128)(2,1)} %collective-permute-done.far, bf16[1024,128]{1,0:T(8,128)(2,1)S(1)} %copy-done.10, bf16[1024,128]{1,0:T(8,128)(2,1)S(1)} %copy-done.8, ...), custom_call_target="tpu_custom_call" | custom-call | flops 402653184 | bytes 2097152 | tf_op jit(solution)/shard_map/pallas_call | solution.py:102
  44.5 0.8 copy-done.3
  45.2 4.8 %collective-permute-start.15 = (f32[384,256]{1,0:T(8,128)}, f32[384,256]{1,0:T(8,128)}, u32[]{:S(2)}, u32[]{:S(2)}) collective-permute-start(f32[384,256]{1,0:T(8,128)} %get-tuple-element.19), channel_id=1, source_target_pairs={{0,4},{4,0},{8,12},{12,8},{16,20},{20,16},{24,28},{28,24},{1,5},{5... | collective-permute-start | bytes 1179656 | tf_op jit(solution)/shard_map/ppermute | solution.py:225
  50.8 1.0 %pad_maximum_fusion.2.sine = f32[384,128]{1,0:T(8,128)S(1)} fusion(f32[384,64]{1,0:T(8,128)} %get-tuple-element.26, f32[384,64]{1,0:T(8,128)S(1)} %copy-done.11), kind=kLoop, calls=%fused_computation.4 | loop fusion | flops 49152 | bytes 393216 | tf_op jit(solution)/shard_map/concatenate | solution.py:24
  51.9 1.4 %collective-permute-start.12 = (bf16[256,512]{1,0:T(8,128)(2,1)}, bf16[256,512]{1,0:T(8,128)(2,1)S(1)}, u32[]{:S(2)}, u32[]{:S(2)}) collective-permute-start(bf16[256,512]{1,0:T(8,128)(2,1)} %collective-permute-done.11.refs_0_), channel_id=1, source_target_pairs={{0,1},{1,0},{2,3},{3,2},{4,5},{5,4},{6,7},{7,6},{8,9},{9,8},{10,11... | collective-permute-start | bytes 786440 | tf_op jit(solution)/shard_map/ppermute | solution.py:241
  53.5 2.8 %copy-done.2 = bf16[1,384,8192]{2,1,0:T(8,128)(2,1)S(1)} copy-done((bf16[1,384,8192]{2,1,0:T(8,128)(2,1)S(1)}, bf16[1,384,8192]{2,1,0:T(8,128)(2,1)}, u32[]{:S(2)}) %copy-start.2) | copy-done | bytes 6291480
  56.3 3.9 %shard_map.56.refs_4_ = f32[768,512]{1,0:T(8,128)S(1)} custom-call(s32[4]{0:T(128)S(1)} %pad_add_fusion.3.starts, bf16[384,8192]{1,0:T(8,128)(2,1)S(1)} %bitcast.18, bf16[384,8192]{1,0:T(8,128)(2,1)} %collective-permute-done.far, bf16[512,512]{1,0:T(8,128)(2,1)S(1)} %get-tuple-element.17.refs_0_, bf16[512,512]{1,0:T(8,128)(2,1)S(1)} %get-tuple-element.16.refs_1_, ...), custom_call_target="tpu_custom_call" | custom-call | flops 1610612736 | bytes 5242880 | tf_op jit(solution)/shard_map/pallas_call | solution.py:102
  60.2 1.1 %shard_map.58 = bf16[384,256]{1,0:T(8,128)(2,1)S(1)} custom-call(f32[384,256]{1,0:T(8,128)S(1)} %copy-done.4, f32[384,256]{1,0:T(8,128)} %collective-permute-done.15.far, f32[384,128]{1,0:T(8,128)S(1)} %pad_maximum_fusion.1.cosine, f32[384,128]{1,0:T(8,128)S(1)} %pad_maximum_fusion.2.sine), custom_call_target="tpu_custom_call" | custom-call | flops 589824 | bytes 1376256 | tf_op jit(solution)/shard_map/pallas_call | solution.py:133
  61.4 3.9 %collective-permute-done.14.refs_3_ = bf16[256,512]{1,0:T(8,128)(2,1)S(1)} collective-permute-done((bf16[256,512]{1,0:T(8,128)(2,1)}, bf16[256,512]{1,0:T(8,128)(2,1)S(1)}, u32[]{:S(2)}, u32[]{:S(2)}) %collective-permute-start.14) | collective-permute-done | bytes 262176 | tf_op jit(solution)/shard_map/ppermute | solution.py:241
  65.3 2.9 %shard_map.59.refs_2_ = f32[768,512]{1,0:T(8,128)S(1)} custom-call(s32[4]{0:T(128)S(1)} %pad_add_fusion.1.starts, bf16[384,8192]{1,0:T(8,128)(2,1)S(1)} %bitcast.21, bf16[384,8192]{1,0:T(8,128)(2,1)} %collective-permute-done.far, bf16[256,512]{1,0:T(8,128)(2,1)} %collective-permute-done.11.refs_0_, bf16[256,512]{1,0:T(8,128)(2,1)S(1)} %collective-permute-done.12.refs_1_, ...), custom_call_target="tpu_custom_call" | custom-call | flops 805306368 | bytes 2621440 | tf_op jit(solution)/shard_map/pallas_call | solution.py:102
  68.2 2.8 %shard_map.60 = (f32[384,512]{1,0:T(8,128)S(1)}, f32[384,512]{1,0:T(8,128)S(1)}) custom-call(s32[2]{0:T(128)S(1)} %pad_add_fusion.starts, bf16[384,8192]{1,0:T(8,128)(2,1)S(1)} %bitcast.22, bf16[384,8192]{1,0:T(8,128)(2,1)} %collective-permute-done.far, bf16[512,512]{1,0:T(8,128)(2,1)} %collective-permute-done.4.refs_0_, ...), custom_call_target="tpu_custom_call" | custom-call | flops 805306368 | bytes 2621440 | tf_op jit(solution)/shard_map/pallas_call | solution.py:102
  71.1 1.2 %collective-permute-start.16 = (f32[384,512]{1,0:T(8,128)S(1)}, f32[384,512]{1,0:T(8,128)S(1)}, u32[]{:S(2)}, u32[]{:S(2)}) collective-permute-start(f32[384,512]{1,0:T(8,128)S(1)} %get-tuple-element.22), channel_id=1, source_target_pairs={{0,4},{4,0},{8,12},{12,8},{16,20},{20,16},{24,28},{28,24},{1,5},{5... | collective-permute-start | bytes 2359304 | tf_op jit(solution)/shard_map/ppermute | solution.py:225
  72.4 1.3 %collective-permute-start.17 = (bf16[384,256]{1,0:T(8,128)(2,1)S(1)}, bf16[384,256]{1,0:T(8,128)(2,1)S(1)}, u32[]{:S(2)}, u32[]{:S(2)}) collective-permute-start(bf16[384,256]{1,0:T(8,128)(2,1)S(1)} %shard_map.58), channel_id=1, source_target_pairs={{0,2},{1,3},{4,6},{5,7},{8,10},{9,11},{12,14},{13,15},{16,18},{17,... | collective-permute-start | bytes 589832 | tf_op jit(solution)/shard_map/ppermute | solution.py:279
  73.7 3.2 %collective-permute-start.18 = (bf16[384,256]{1,0:T(8,128)(2,1)S(1)}, bf16[384,256]{1,0:T(8,128)(2,1)S(1)}, u32[]{:S(2)}, u32[]{:S(2)}) collective-permute-start(bf16[384,256]{1,0:T(8,128)(2,1)S(1)} %shard_map.58), channel_id=1, source_target_pairs={{0,1},{1,2},{2,3},{4,5},{5,6},{6,7},{8,9},{9,10},{10,11},{12,13},{... | collective-permute-start | bytes 589832 | tf_op jit(solution)/shard_map/ppermute | solution.py:279
  77.1 4.7 %collective-permute-done.17 = bf16[384,256]{1,0:T(8,128)(2,1)S(1)} collective-permute-done((bf16[384,256]{1,0:T(8,128)(2,1)S(1)}, bf16[384,256]{1,0:T(8,128)(2,1)S(1)}, u32[]{:S(2)}, u32[]{:S(2)}) %collective-permute-start.17) | collective-permute-done | bytes 196640 | tf_op jit(solution)/shard_map/ppermute | solution.py:279
  81.8 8.8 %collective-permute-done.18 = bf16[384,256]{1,0:T(8,128)(2,1)S(1)} collective-permute-done((bf16[384,256]{1,0:T(8,128)(2,1)S(1)}, bf16[384,256]{1,0:T(8,128)(2,1)S(1)}, u32[]{:S(2)}, u32[]{:S(2)}) %collective-permute-start.18) | collective-permute-done | bytes 196640 | tf_op jit(solution)/shard_map/ppermute | solution.py:279
  90.6 3.7 %shard_map.61 = bf16[384,512]{1,0:T(8,128)(2,1)} custom-call(f32[384,512]{1,0:T(8,128)S(1)} %get-tuple-element.21.near, f32[384,512]{1,0:T(8,128)S(1)} %collective-permute-done.16.far, f32[384,128]{1,0:T(8,128)S(1)} %pad_maximum_fusion.1.cosine, f32[384,128]{1,0:T(8,128)S(1)} %pad_maximum_fusion.2.sine, s32[384,1]{1,0:T(8,128)S(1)} %sub.26.first, ...), custom_call_target="tpu_custom_call" | custom-call | flops 704643072 | bytes 1572864 | tf_op jit(solution)/shard_map/pallas_call | solution.py:195
  (64 shorter events, 6.0 us)
Async XLA Ops:
  0.0 29.2 %collective-permute-start = (bf16[384,8192]{1,0:T(8,128)(2,1)}, bf16[384,8192]{1,0:T(8,128)(2,1)}, u32[]{:S(2)}, u32[]{:S(2)}) collective-permute-start(bf16[384,8192]{1,0:T(8,128)(2,1)} %bitcast.15), channel_id=1, source_target_pairs={{0,4},{4,0},{8,12},{12,8},{16,20},{20,16},{24,28},{28,24},{1,5},{5... | collective-permute-start | bytes 18874376 | tf_op jit(solution)/shard_map/ppermute | solution.py:225
  0.7 8.1 %collective-permute-start.1 = (bf16[1024,128]{1,0:T(8,128)(2,1)}, bf16[1024,128]{1,0:T(8,128)(2,1)S(1)}, u32[]{:S(2)}, u32[]{:S(2)}) collective-permute-start(bf16[1024,128]{1,0:T(8,128)(2,1)} %refs_0_.1), channel_id=1, source_target_pairs={{0,16},{4,20},{8,24},{12,28},{16,0},{20,4},{24,8},{28,12},{1,17},{... | collective-permute-start | bytes 786440 | tf_op jit(solution)/shard_map/ppermute | solution.py:225
  1.9 16.8 %collective-permute-start.7 = (bf16[1024,128]{1,0:T(8,128)(2,1)}, bf16[1024,128]{1,0:T(8,128)(2,1)S(1)}, u32[]{:S(2)}, u32[]{:S(2)}) collective-permute-start(bf16[1024,128]{1,0:T(8,128)(2,1)} %refs_0_.1), channel_id=1, source_target_pairs={{0,8},{4,12},{8,0},{12,4},{16,24},{20,28},{24,16},{28,20},{1,9},{5... | collective-permute-start | bytes 786440 | tf_op jit(solution)/shard_map/ppermute | solution.py:225
  3.1 12.2 %collective-permute-start.2 = (bf16[1024,128]{1,0:T(8,128)(2,1)}, bf16[1024,128]{1,0:T(8,128)(2,1)S(1)}, u32[]{:S(2)}, u32[]{:S(2)}) collective-permute-start(bf16[1024,128]{1,0:T(8,128)(2,1)} %refs_1_.1), channel_id=1, source_target_pairs={{0,8},{4,12},{8,0},{12,4},{16,24},{20,28},{24,16},{28,20},{1,9},{5... | collective-permute-start | bytes 786440 | tf_op jit(solution)/shard_map/ppermute | solution.py:225
  3.4 15.0 %collective-permute-start.9 = (bf16[1024,128]{1,0:T(8,128)(2,1)}, bf16[1024,128]{1,0:T(8,128)(2,1)S(1)}, u32[]{:S(2)}, u32[]{:S(2)}) collective-permute-start(bf16[1024,128]{1,0:T(8,128)(2,1)} %refs_1_.1), channel_id=1, source_target_pairs={{0,16},{4,20},{8,24},{12,28},{16,0},{20,4},{24,8},{28,12},{1,17},{... | collective-permute-start | bytes 786440 | tf_op jit(solution)/shard_map/ppermute | solution.py:225
  3.6 25.6 %copy-start.5 = (bf16[1024,128]{1,0:T(8,128)(2,1)S(1)}, bf16[1024,128]{1,0:T(8,128)(2,1)}, u32[]{:S(2)}) copy-start(bf16[1024,128]{1,0:T(8,128)(2,1)} %refs_0_.1) | copy-start | bytes 786436
  3.6 25.6 %copy-start.6 = (bf16[1024,128]{1,0:T(8,128)(2,1)S(1)}, bf16[1024,128]{1,0:T(8,128)(2,1)}, u32[]{:S(2)}) copy-start(bf16[1024,128]{1,0:T(8,128)(2,1)} %refs_1_.1) | copy-start | bytes 786436
  15.4 12.4 %collective-permute-start.3 = (bf16[512,512]{1,0:T(8,128)(2,1)S(1)}, bf16[512,512]{1,0:T(8,128)(2,1)}, u32[]{:S(2)}, u32[]{:S(2)}) collective-permute-start(bf16[512,512]{1,0:T(8,128)(2,1)S(1)} %get-tuple-element.17.refs_0_), channel_id=1, source_target_pairs={{0,8},{4,12},{8,0},{12,4},{16,24},{20,28},{24,16},{28,20},{1,9},{5... | collective-permute-start | bytes 1572872 | tf_op jit(solution)/shard_map/ppermute | solution.py:225
  16.6 12.1 %collective-permute-start.5 = (bf16[512,512]{1,0:T(8,128)(2,1)S(1)}, bf16[512,512]{1,0:T(8,128)(2,1)}, u32[]{:S(2)}, u32[]{:S(2)}) collective-permute-start(bf16[512,512]{1,0:T(8,128)(2,1)S(1)} %get-tuple-element.16.refs_1_), channel_id=1, source_target_pairs={{0,16},{4,20},{8,24},{12,28},{16,0},{20,4},{24,8},{28,12},{1,17},{... | collective-permute-start | bytes 1572872 | tf_op jit(solution)/shard_map/ppermute | solution.py:225
  18.4 18.3 %collective-permute-start.10 = (bf16[1024,128]{1,0:T(8,128)(2,1)S(1)}, bf16[1024,128]{1,0:T(8,128)(2,1)S(1)}, u32[]{:S(2)}, u32[]{:S(2)}) collective-permute-start(bf16[1024,128]{1,0:T(8,128)(2,1)S(1)} %collective-permute-done.9.refs_5_), channel_id=1, source_target_pairs={{0,8},{4,12},{8,0},{12,4},{16,24},{20,28},{24,16},{28,20},{1,9},{5... | collective-permute-start | bytes 786440 | tf_op jit(solution)/shard_map/ppermute | solution.py:225
  18.7 18.1 %collective-permute-start.8 = (bf16[1024,128]{1,0:T(8,128)(2,1)S(1)}, bf16[1024,128]{1,0:T(8,128)(2,1)S(1)}, u32[]{:S(2)}, u32[]{:S(2)}) collective-permute-start(bf16[1024,128]{1,0:T(8,128)(2,1)S(1)} %collective-permute-done.7.refs_2_), channel_id=1, source_target_pairs={{0,16},{4,20},{8,24},{12,28},{16,0},{20,4},{24,8},{28,12},{1,17},{... | collective-permute-start | bytes 786440 | tf_op jit(solution)/shard_map/ppermute | solution.py:225
  27.8 40.4 %collective-permute-start.4 = (bf16[512,512]{1,0:T(8,128)(2,1)}, bf16[512,512]{1,0:T(8,128)(2,1)}, u32[]{:S(2)}, u32[]{:S(2)}) collective-permute-start(bf16[512,512]{1,0:T(8,128)(2,1)} %collective-permute-done.3.refs_2_), channel_id=1, source_target_pairs={{0,16},{4,20},{8,24},{12,28},{16,0},{20,4},{24,8},{28,12},{1,17},{... | collective-permute-start | bytes 1572872 | tf_op jit(solution)/shard_map/ppermute | solution.py:225
  28.7 39.5 %collective-permute-start.6 = (bf16[512,512]{1,0:T(8,128)(2,1)}, bf16[512,512]{1,0:T(8,128)(2,1)}, u32[]{:S(2)}, u32[]{:S(2)}) collective-permute-start(bf16[512,512]{1,0:T(8,128)(2,1)} %collective-permute-done.5.refs_3_), channel_id=1, source_target_pairs={{0,8},{4,12},{8,0},{12,4},{16,24},{20,28},{24,16},{28,20},{1,9},{5... | collective-permute-start | bytes 1572872 | tf_op jit(solution)/shard_map/ppermute | solution.py:225
  29.2 2.8 %copy-start = (bf16[1,384,8192]{2,1,0:T(8,128)(2,1)S(1)}, bf16[1,384,8192]{2,1,0:T(8,128)(2,1)}, u32[]{:S(2)}) copy-start(bf16[1,384,8192]{2,1,0:T(8,128)(2,1)} %param.5) | copy-start | bytes 18874372
  32.0 7.8 %copy-start.1 = (bf16[1,384,8192]{2,1,0:T(8,128)(2,1)S(1)}, bf16[1,384,8192]{2,1,0:T(8,128)(2,1)}, u32[]{:S(2)}) copy-start(bf16[1,384,8192]{2,1,0:T(8,128)(2,1)} %param.5) | copy-start | bytes 18874372
  36.7 2.5 %copy-start.7 = (bf16[1024,128]{1,0:T(8,128)(2,1)}, bf16[1024,128]{1,0:T(8,128)(2,1)S(1)}, u32[]{:S(2)}) copy-start(bf16[1024,128]{1,0:T(8,128)(2,1)S(1)} %collective-permute-done.10.refs_1_) | copy-start | bytes 786436
  36.8 2.5 %copy-start.9 = (bf16[1024,128]{1,0:T(8,128)(2,1)}, bf16[1024,128]{1,0:T(8,128)(2,1)S(1)}, u32[]{:S(2)}) copy-start(bf16[1024,128]{1,0:T(8,128)(2,1)S(1)} %collective-permute-done.8.refs_0_) | copy-start | bytes 786436
  37.6 14.3 %collective-permute-start.11 = (bf16[256,512]{1,0:T(8,128)(2,1)}, bf16[256,512]{1,0:T(8,128)(2,1)}, u32[]{:S(2)}, u32[]{:S(2)}) collective-permute-start(bf16[256,512]{1,0:T(8,128)(2,1)} %constant_dynamic-slice_fusion.1), channel_id=1, source_target_pairs={{0,8},{4,12},{8,0},{12,4},{16,24},{20,28},{24,16},{28,20},{1,9},{5... | collective-permute-start | bytes 786440 | tf_op jit(solution)/shard_map/ppermute | solution.py:225
  39.3 13.9 %collective-permute-start.13 = (bf16[256,512]{1,0:T(8,128)(2,1)}, bf16[256,512]{1,0:T(8,128)(2,1)}, u32[]{:S(2)}, u32[]{:S(2)}) collective-permute-start(bf16[256,512]{1,0:T(8,128)(2,1)} %constant_dynamic-slice_fusion), channel_id=1, source_target_pairs={{0,16},{4,20},{8,24},{12,28},{16,0},{20,4},{24,8},{28,12},{1,17},{... | collective-permute-start | bytes 786440 | tf_op jit(solution)/shard_map/ppermute | solution.py:225
  41.7 8.4 %copy-start.12 = (s32[1,16]{1,0:T(1,128)S(1)}, s32[1,16]{1,0:T(1,128)}, u32[]{:S(2)}) copy-start(s32[1,16]{1,0:T(1,128)} %param.9) | copy-start | bytes 196
  41.7 9.1 %copy-start.11 = (f32[384,64]{1,0:T(8,128)S(1)}, f32[384,64]{1,0:T(8,128)}, u32[]{:S(2)}) copy-start(f32[384,64]{1,0:T(8,128)} %get-tuple-element.25) | copy-start | bytes 294916
  41.7 23.6 %slice-start = ((s8[6291456]{0:T(1024)(128)(4,1)}), s8[2097152]{0:T(1024)(128)(4,1)S(1)}, s32[]{:S(2)}) async-start(s8[6291456]{0:T(1024)(128)(4,1)} %bitcast.19), calls=%async_computation | async-start | bytes 4194304
  45.2 15.0 %collective-permute-start.15 = (f32[384,256]{1,0:T(8,128)}, f32[384,256]{1,0:T(8,128)}, u32[]{:S(2)}, u32[]{:S(2)}) collective-permute-start(f32[384,256]{1,0:T(8,128)} %get-tuple-element.19), channel_id=1, source_target_pairs={{0,4},{4,0},{8,12},{12,8},{16,20},{20,16},{24,28},{28,24},{1,5},{5... | collective-permute-start | bytes 1179656 | tf_op jit(solution)/shard_map/ppermute | solution.py:225
  51.9 9.5 %collective-permute-start.12 = (bf16[256,512]{1,0:T(8,128)(2,1)}, bf16[256,512]{1,0:T(8,128)(2,1)S(1)}, u32[]{:S(2)}, u32[]{:S(2)}) collective-permute-start(bf16[256,512]{1,0:T(8,128)(2,1)} %collective-permute-done.11.refs_0_), channel_id=1, source_target_pairs={{0,1},{1,0},{2,3},{3,2},{4,5},{5,4},{6,7},{7,6},{8,9},{9,8},{10,11... | collective-permute-start | bytes 786440 | tf_op jit(solution)/shard_map/ppermute | solution.py:241
  53.2 12.1 %collective-permute-start.14 = (bf16[256,512]{1,0:T(8,128)(2,1)}, bf16[256,512]{1,0:T(8,128)(2,1)S(1)}, u32[]{:S(2)}, u32[]{:S(2)}) collective-permute-start(bf16[256,512]{1,0:T(8,128)(2,1)} %collective-permute-done.13.refs_2_), channel_id=1, source_target_pairs={{0,1},{1,0},{2,3},{3,2},{4,5},{5,4},{6,7},{7,6},{8,9},{9,8},{10,11... | collective-permute-start | bytes 786440 | tf_op jit(solution)/shard_map/ppermute | solution.py:241
  53.5 2.8 %copy-start.2 = (bf16[1,384,8192]{2,1,0:T(8,128)(2,1)S(1)}, bf16[1,384,8192]{2,1,0:T(8,128)(2,1)}, u32[]{:S(2)}) copy-start(bf16[1,384,8192]{2,1,0:T(8,128)(2,1)} %param.5) | copy-start | bytes 18874372
  56.3 4.0 %copy-start.4 = (f32[384,256]{1,0:T(8,128)S(1)}, f32[384,256]{1,0:T(8,128)}, u32[]{:S(2)}) copy-start(f32[384,256]{1,0:T(8,128)} %copy-done.3) | copy-start | bytes 1179652
  56.3 9.0 %slice-start.1 = ((s8[6291456]{0:T(1024)(128)(4,1)}), s8[4194304]{0:T(1024)(128)(4,1)S(1)}, s32[]{:S(2)}) async-start(s8[6291456]{0:T(1024)(128)(4,1)} %bitcast.19), calls=%async_computation.1 | async-start | bytes 8388608
  68.2 4.1 %copy-start.13 = (s32[1,16]{1,0:T(1,128)S(1)}, s32[1,16]{1,0:T(1,128)}, u32[]{:S(2)}) copy-start(s32[1,16]{1,0:T(1,128)} %reduce-window_clone.1) | copy-start | bytes 196
  71.1 19.5 %collective-permute-start.16 = (f32[384,512]{1,0:T(8,128)S(1)}, f32[384,512]{1,0:T(8,128)S(1)}, u32[]{:S(2)}, u32[]{:S(2)}) collective-permute-start(f32[384,512]{1,0:T(8,128)S(1)} %get-tuple-element.22), channel_id=1, source_target_pairs={{0,4},{4,0},{8,12},{12,8},{16,20},{20,16},{24,28},{28,24},{1,5},{5... | collective-permute-start | bytes 2359304 | tf_op jit(solution)/shard_map/ppermute | solution.py:225
  72.4 9.3 %collective-permute-start.17 = (bf16[384,256]{1,0:T(8,128)(2,1)S(1)}, bf16[384,256]{1,0:T(8,128)(2,1)S(1)}, u32[]{:S(2)}, u32[]{:S(2)}) collective-permute-start(bf16[384,256]{1,0:T(8,128)(2,1)S(1)} %shard_map.58), channel_id=1, source_target_pairs={{0,2},{1,3},{4,6},{5,7},{8,10},{9,11},{12,14},{13,15},{16,18},{17,... | collective-permute-start | bytes 589832 | tf_op jit(solution)/shard_map/ppermute | solution.py:279
  73.7 16.8 %collective-permute-start.18 = (bf16[384,256]{1,0:T(8,128)(2,1)S(1)}, bf16[384,256]{1,0:T(8,128)(2,1)S(1)}, u32[]{:S(2)}, u32[]{:S(2)}) collective-permute-start(bf16[384,256]{1,0:T(8,128)(2,1)S(1)} %shard_map.58), channel_id=1, source_target_pairs={{0,1},{1,2},{2,3},{4,5},{5,6},{6,7},{8,9},{9,10},{10,11},{12,13},{... | collective-permute-start | bytes 589832 | tf_op jit(solution)/shard_map/ppermute | solution.py:279
  (3 other events, 2.7 us)

commit v4 on v3

--- a/solution.py
+++ b/solution.py
@@ -49,39 +49,43 @@
     weights, refs = refs[:count], refs[count:]
     if carried:
         carry, refs = refs[0], refs[1:]
-    outs = refs[: 2 if final else 1]
-    refs = refs[len(outs) :]
-    tokens, held, sems = refs[: len(steps)], refs[len(steps) : 2 * len(steps)], refs[-1]
+    outs, (tokens, held, sems) = refs[:-3], refs[-3:]
     rows = near.shape[0]
-    copies = []
-    used = 0
+    batches = ([], [], [])
+    used = row = 0
     for step, (depth, spots) in enumerate(steps):
+        here = slice(row, row + depth)
+        row += depth
         window = pl.ds(pl.multiple_of(starts[step], 128), depth)
-        batch = [
-            pltpu.make_async_copy(near.at[:, window], tokens[step].at[:rows], sems.at[step, 0]),
-            pltpu.make_async_copy(far.at[:, window], tokens[step].at[rows:], sems.at[step, 1]),
-        ]
         for index, columns in enumerate(spots):
-            batch.append(
+            batches[0].append(
                 pltpu.make_async_copy(
-                    weights[used], held[step].at[:, columns], sems.at[step, 2 + index]
+                    weights[used], held.at[here, columns], sems.at[step, 2 + index]
                 )
             )
             used += 1
+        for side, ref in enumerate((far, near)):
+            batches[1 + side].append(
+                pltpu.make_async_copy(
+                    ref.at[:, window], tokens.at[side, :, here], sems.at[step, side]
+                )
+            )
+    for batch in batches:
         for copy in batch:
             copy.start()
-        copies.append(batch)
-    total = carry[...] if carried else None
-    for step, batch in enumerate(copies):
-        for copy in batch:
+    for copy in batches[0]:
+        copy.wait()
+    for side in range(2):
+        for copy in batches[1 + side]:
             copy.wait()
-        term = jnp.dot(tokens[step][...], held[step][...], preferred_element_type=jnp.float32)
-        total = term if total is None else total + term
-    if final:
-        outs[0][...] = total[:rows]
-        outs[1][...] = total[rows:]
-    else:
-        outs[0][...] = total
+        total = jnp.dot(tokens[side], held[...], preferred_element_type=jnp.float32)
+        place = slice((1 - side) * rows, (2 - side) * rows)
+        if carried:
+            total = total + carry[place, :]
+        if final:
+            outs[1 - side][...] = total
+        else:
+            outs[0][place, :] = total
 
 
 def project(terms, near, far, carry=None, final=False):
@@ -98,7 +102,6 @@
     whole = jax.ShapeDtypeStruct((2 * rows, width), jnp.float32)
     part = jax.ShapeDtypeStruct((rows, width), jnp.float32)
     carries = [] if carry is None else [carry]
-    need = 2 * depth * (2 * rows + width) + 16 * rows * width
     return pl.pallas_call(
         functools.partial(project_kernel, steps, carry is not None, final),
         out_shape=(part, part) if final else whole,
@@ -106,10 +109,12 @@
         + anywhere(2 + len(weights))
         + vmem(len(carries)),
         out_specs=tuple(vmem(2)) if final else vmem(1)[0],
-        scratch_shapes=[pltpu.VMEM((2 * rows, step[0]), jnp.bfloat16) for step in steps]
-        + [pltpu.VMEM((step[0], width), jnp.bfloat16) for step in steps]
-        + [pltpu.SemaphoreType.DMA((len(steps), 4))],
-        compiler_params=pltpu.CompilerParams(vmem_limit_bytes=need + 8 * MIB),
+        scratch_shapes=[
+            pltpu.VMEM((2, rows, depth), jnp.bfloat16),
+            pltpu.VMEM((depth, width), jnp.bfloat16),
+            pltpu.SemaphoreType.DMA((len(steps), 4)),
+        ],
+        compiler_params=pltpu.CompilerParams(vmem_limit_bytes=48 * MIB),
         cost_estimate=pl.CostEstimate(
             flops=4 * rows * width * depth,
             bytes_accessed=2 * depth * (2 * rows + width),
@@ -224,7 +229,7 @@
     def swap(array, mask):
         return lax.ppermute(array, "dp", [(i, i ^ mask) for i in range(dp_size)])
 
-    def fetch(pair, gates, assisted):
+    def fetch(pair, gate, later, seconds):
         held = [{0: [(0, array)]} for array in pair]
         for step in range(bits):
             axes = (step, bits - 1 - step)
@@ -232,15 +237,10 @@
                 for side, source in enumerate(sources):
                     array = held[side][source][0][1]
                     mask = 2 << axes[side]
-                    if source == 0 and gates:
-                        array = after(array, *gates[min(step, len(gates) - 1)])
-                    if source == 0 and assisted and step == bits - 1:
-                        some = array.shape[0] // 2
-                        begin = (place % 2) * some
-                        mine = swap(lax.dynamic_slice_in_dim(array, begin, some, 0), mask)
-                        other = lax.ppermute(mine, "ctx", [(i, i ^ 1) for i in range(ctx_size)])
-                        got = [(begin, mine), (some - begin, other)]
+                    if source == 0 and step == bits - 1 and seconds:
+                        got = seconds[side]
                     else:
+                        array = after(array, *(gate if source == 0 else later))
                         got = [(0, swap(array, mask))]
                     held[side][source | (1 << axes[side])] = got
         return held
@@ -258,47 +258,52 @@
     first_axis, last_axis = 1, 1 << (bits - 1)
     last = chips - 1
 
-    pair_held = fetch((w_key, w_value), None, False)
+    half = depth // 2
+    halves = [w_query[:half], w_query[half:]]
+    parts = []
+    if ctx_size % 2 == 0:
+        begin = (place % 2) * (half // 2)
+        parts = [
+            lax.dynamic_slice_in_dim(w_query, side * half + begin, half // 2, 0)
+            for side in range(2)
+        ]
+
+    pair_held = fetch((w_key, w_value), [], [], [])
     pair_terms = [
         (begins(chip), [pair_held[side][chip][0][1] for side in range(2)]) for chip in range(chips)
     ]
     carry = project(pair_terms[:-1], hidden, sibling_hidden)
-    gates = (
-        [pair_held[0][last_axis][0][1], pair_held[1][first_axis][0][1]],
-        [pair_held[0][last][0][1], pair_held[1][last][0][1], carry],
-    )
-    half = depth // 2
-    query_held = fetch((w_query[:half], w_query[half:]), gates, ctx_size % 2 == 0)
-
     near, far = project(pair_terms[-1:], hidden, sibling_hidden, carry, True)
+    gate = [pair_held[0][last_axis][0][1], pair_held[1][first_axis][0][1]]
+    gate += [cosine, sine, first, *halves, *parts]
+    mine = [swap(after(part, *gate), 2 << axis) for part, axis in zip(parts, (bits - 1, 0))]
+    other = [lax.ppermute(part, "ctx", [(i, i ^ 1) for i in range(ctx_size)]) for part in mine]
+    seconds = [
+        [(begin, here), (half // 2 - begin, there)] for here, there in zip(mine, other)
+    ]
+    query_held = fetch(halves, gate, [near, *mine], seconds)
+
     pair = finish_pair(near, swap(far, 1), cosine, sine)
     longest = ctx_size * row_count // 2
     back = -(-(longest - 1) // ROW_TILE) * ROW_TILE
     hops = min(ctx_size - 1, -(-back // row_count))
     blocks = [
-        lax.ppermute(pair, "ctx", [(i, i + hop) for i in range(ctx_size - hop)])
+        lax.ppermute(after(pair, *other), "ctx", [(i, i + hop) for i in range(ctx_size - hop)])
         for hop in range(hops, 0, -1)
     ]
     keys_values = jnp.concatenate(blocks + [pair], axis=0)
 
-    def query_terms(wanted):
+    def query_terms(wanted, *gate):
         return [
-            (begins(chip) + side * half + begin, [array])
+            (begins(chip) + side * half + begin, [after(array, *gate)])
             for side, chip in wanted
             for begin, array in query_held[side][chip]
         ]
 
-    early = [(0, 0), (1, 0), (0, first_axis), (1, last_axis)]
     late = [(0, last), (1, last)]
-    rest = [
-        (side, chip)
-        for chip in range(chips)
-        for side in range(2)
-        if (side, chip) not in early + late
-    ]
-    carry = after(project(query_terms(early), hidden, sibling_hidden), pair)
-    carry = project(query_terms(rest), hidden, sibling_hidden, carry)
-    near, far = project(query_terms(late), hidden, sibling_hidden, carry, True)
+    early = [(side, chip) for chip in range(last) for side in range(2)]
+    carry = project(query_terms(early, pair), hidden, sibling_hidden)
+    near, far = project(query_terms(late, keys_values), hidden, sibling_hidden, carry, True)
     return attend(near, swap(far, 1), cosine, sine, first, keys_values, back)[None]
 
 

time: 94.7 us -> 78.1 us (0.82); the launches traced: 94.3 us -> 76.7 us
  waiting for transfers between devices: 36.2 us -> 23.4 us
  local copies, waits for them, and re-layouts: 11.3 us -> 6.85 us
  other arithmetic: 3.89 us -> 2.79 us
    ppermute x15, waiting for transfers between devices: 18.8 us -> 11.5 us  [swap(): return lax.ppermute(array, 'dp', [(i, i ^ mask) for i in range(dp_size)])]
    ppermute x4, waiting for transfers between devices: 17.4 us -> 11.9 us  [the longest x2 7.36 us: shards(): lax.ppermute(after(pair, *other), 'ctx', [(i, i + hop) for i in range(ctx...]
    unnamed x32 -> x12, local copies, waits for them, and re-layouts: 8.28 us -> 3.41 us
    ppermute x4, starting transfers between devices: 6.03 us -> 7.08 us  [the longest x2 4.49 us: shards(): lax.ppermute(after(pair, *other), 'ctx', [(i, i + hop) for i in range(ctx...]
    dynamic_slice x2 -> x1, local copies, waits for them, and re-layouts: 1.54 us -> 1.95 us  [shards(): lax.dynamic_slice_in_dim(w_query, side * half + begin, half // 2, 0)]
    pallas_call x5 -> x4, Pallas kernels: 17.1 us -> 16.9 us  [project(): pl.pallas_call(functools.partial(project_kernel, steps, carry is not None...]
  transfers between devices with their start and end apart: 19 -> 19, of which waited for: 7 -> 8; matrix products, arithmetic and copies ran while one was open for 7% -> 8% of each run, Pallas kernels for 16% -> 19%
where the time goes in v4:
time: 78.1 us; the launch traced here: 76.7 us
  waiting for transfers between devices  23.4 us (30%)
  starting transfers between devices  21.7 us (28%)
  Pallas kernels  21.7 us (28%)
  local copies, waits for them, and re-layouts  6.85 us (9%)
  other arithmetic  2.79 us (4%)
    pallas_call x4, Pallas kernels, project(): pl.pallas_call(functools.partial(project_kernel, steps, carry is not None...  16.9 us
    ppermute x15, starting transfers between devices, swap(): return lax.ppermute(array, 'dp', [(i, i ^ mask) for i in range(dp_size)])  14.7 us
    ppermute x15, waiting for transfers between devices, swap(): return lax.ppermute(array, 'dp', [(i, i ^ mask) for i in range(dp_size)])  11.5 us
    ppermute x2, waiting for transfers between devices, shards(): lax.ppermute(after(pair, *other), 'ctx', [(i, i + hop) for i in range(ctx...  7.36 us
    ppermute x2, waiting for transfers between devices, shards(): lax.ppermute(part, 'ctx', [(i, i ^ 1) for i in range(ctx_size)])  4.58 us
    ppermute x2, starting transfers between devices, shards(): lax.ppermute(after(pair, *other), 'ctx', [(i, i + hop) for i in range(ctx...  4.49 us
    pallas_call x1, Pallas kernels, attend(): pl.pallas_call(functools.partial(attend_kernel, back), out_shape=jax.Shap...  3.65 us
    unnamed x12, local copies, waits for them, and re-layouts  3.41 us
  transfers between devices with their start and end apart: 19, of which 8 were waited for; matrix products, arithmetic and copies ran while one was open for 8% of the time, Pallas kernels for 19%

profile of v4, /device:TPU:17, one launch (start us, length us, event | category | flops | bytes accessed | tf_op | source)
XLA Modules:
  0.0 76.7 jit_solution(10059402259839089183)
XLA Ops:
  0.7 1.2 %collective-permute-start.1 = (bf16[1024,128]{1,0:T(8,128)(2,1)}, bf16[1024,128]{1,0:T(8,128)(2,1)S(1)}, u32[]{:S(2)}, u32[]{:S(2)}) collective-permute-start(bf16[1024,128]{1,0:T(8,128)(2,1)} %refs_0_.1), channel_id=1, source_target_pairs={{0,16},{4,20},{8,24},{12,28},{16,0},{20,4},{24,8},{28,12},{1,17},{... | collective-permute-start | bytes 786440 | tf_op jit(solution)/shard_map/ppermute | solution.py:230
  1.9 1.2 %collective-permute-start.4 = (bf16[1024,128]{1,0:T(8,128)(2,1)}, bf16[1024,128]{1,0:T(8,128)(2,1)S(1)}, u32[]{:S(2)}, u32[]{:S(2)}) collective-permute-start(bf16[1024,128]{1,0:T(8,128)(2,1)} %refs_0_.1), channel_id=1, source_target_pairs={{0,8},{4,12},{8,0},{12,4},{16,24},{20,28},{24,16},{28,20},{1,9},{5... | collective-permute-start | bytes 786440 | tf_op jit(solution)/shard_map/ppermute | solution.py:230
  3.6 0.8 %reduce-window_clone.1 = s32[1,16]{1,0:T(1,128)S(1)} reduce-window(s32[1,16]{1,0:T(1,128)} %param.9, s32[]{:T(128)} %constant.39.clone.1), window={size=1x16 pad=0_0x15_0}, to_apply=%region_0.0 | reduce-window | flops 240 | bytes 132 | tf_op jit(solution)/shard_map/reduce-window.clone
  5.2 0.8 fusion
  6.0 1.3 %fusion.2 = (bf16[512,512]{1,0:T(8,128)(2,1)S(1)}, bf16[512,512]{1,0:T(8,128)(2,1)S(1)}) fusion(bf16[1024,512]{1,0:T(8,128)(2,1)} %param.6), kind=kLoop, calls=%fused_computation.16 | loop fusion | bytes 2097152 | tf_op jit(solution)/shard_map/slice | solution.py:262
  7.3 2.0 %constant_dynamic-slice_fusion = (bf16[256,512]{1,0:T(8,128)(2,1)}, bf16[256,512]{1,0:T(8,128)(2,1)}) fusion(bf16[1024,512]{1,0:T(8,128)(2,1)} %param.6, s32[]{:T(128)S(6)} %select_n.20, s32[]{:T(128)S(6)} %select_n.19), kind=kLoop, calls=%fused_computation.13 | loop fusion | bytes 1048584 | tf_op jit(solution)/shard_map/dynamic_slice | solution.py:267
  10.6 3.9 %collective-permute-done.6.refs_5_ = bf16[1024,128]{1,0:T(8,128)(2,1)} collective-permute-done((bf16[1024,128]{1,0:T(8,128)(2,1)}, bf16[1024,128]{1,0:T(8,128)(2,1)}, u32[]{:S(2)}, u32[]{:S(2)}) %collective-permute-start.6) | collective-permute-done | bytes 262176 | tf_op jit(solution)/shard_map/ppermute | solution.py:230
  14.5 1.2 %collective-permute-start.7 = (bf16[1024,128]{1,0:T(8,128)(2,1)}, bf16[1024,128]{1,0:T(8,128)(2,1)}, u32[]{:S(2)}, u32[]{:S(2)}) collective-permute-start(bf16[1024,128]{1,0:T(8,128)(2,1)} %collective-permute-done.6.refs_5_), channel_id=1, source_target_pairs={{0,8},{4,12},{8,0},{12,4},{16,24},{20,28},{24,16},{28,20},{1,9},{5... | collective-permute-start | bytes 786440 | tf_op jit(solution)/shard_map/ppermute | solution.py:230
  16.6 1.2 %collective-permute-start.16 = (bf16[512,512]{1,0:T(8,128)(2,1)S(1)}, bf16[512,512]{1,0:T(8,128)(2,1)S(1)}, u32[]{:S(2)}, u32[]{:S(2)}) collective-permute-start(bf16[512,512]{1,0:T(8,128)(2,1)S(1)} %get-tuple-element.38.refs_1_), channel_id=1, source_target_pairs={{0,16},{4,20},{8,24},{12,28},{16,0},{20,4},{24,8},{28,12},{1,17},{... | collective-permute-start | bytes 1572872 | tf_op jit(solution)/shard_map/ppermute | solution.py:230
  18.2 2.0 %collective-permute-done.5.refs_0_ = bf16[1024,128]{1,0:T(8,128)(2,1)} collective-permute-done((bf16[1024,128]{1,0:T(8,128)(2,1)S(1)}, bf16[1024,128]{1,0:T(8,128)(2,1)}, u32[]{:S(2)}, u32[]{:S(2)}) %collective-permute-start.5) | collective-permute-done | bytes 262176 | tf_op jit(solution)/shard_map/ppermute | solution.py:230
  20.2 1.2 %collective-permute-start.8 = (bf16[256,512]{1,0:T(8,128)(2,1)}, bf16[256,512]{1,0:T(8,128)(2,1)}, u32[]{:S(2)}, u32[]{:S(2)}) collective-permute-start(bf16[256,512]{1,0:T(8,128)(2,1)} %get-tuple-element.28), channel_id=1, source_target_pairs={{0,16},{4,20},{8,24},{12,28},{16,0},{20,4},{24,8},{28,12},{1,17},{... | collective-permute-start | bytes 786440 | tf_op jit(solution)/shard_map/ppermute | solution.py:230
  21.4 1.2 %collective-permute-start.9 = (bf16[256,512]{1,0:T(8,128)(2,1)}, bf16[256,512]{1,0:T(8,128)(2,1)}, u32[]{:S(2)}, u32[]{:S(2)}) collective-permute-start(bf16[256,512]{1,0:T(8,128)(2,1)} %get-tuple-element.29), channel_id=1, source_target_pairs={{0,8},{4,12},{8,0},{12,4},{16,24},{20,28},{24,16},{28,20},{1,9},{5... | collective-permute-start | bytes 786440 | tf_op jit(solution)/shard_map/ppermute | solution.py:230
  22.6 0.9 %copy-done.5 = bf16[1024,128]{1,0:T(8,128)(2,1)S(1)} copy-done((bf16[1024,128]{1,0:T(8,128)(2,1)S(1)}, bf16[1024,128]{1,0:T(8,128)(2,1)}, u32[]{:S(2)}) %copy-start.5) | copy-done | bytes 262168
  23.6 5.3 %shard_map.55.refs_2_ = f32[768,256]{1,0:T(8,128)S(1)} custom-call(s32[3]{0:T(128)S(1)} %pad_add_fusion.1.starts, bf16[384,8192]{1,0:T(8,128)(2,1)} %bitcast.16, bf16[384,8192]{1,0:T(8,128)(2,1)} %collective-permute-done.far, bf16[1024,128]{1,0:T(8,128)(2,1)S(1)} %copy-done.2, bf16[1024,128]{1,0:T(8,128)(2,1)S(1)} %copy-done.3, ...), custom_call_target="tpu_custom_call" | custom-call | flops 1207959552 | bytes 6291456 | tf_op jit(solution)/shard_map/pallas_call | solution.py:105
  28.9 2.6 %shard_map.56 = (f32[384,256]{1,0:T(8,128)S(1)}, f32[384,256]{1,0:T(8,128)}) custom-call(s32[1]{0:T(128)} %bitcast.starts, bf16[384,8192]{1,0:T(8,128)(2,1)} %bitcast.17, bf16[384,8192]{1,0:T(8,128)(2,1)} %collective-permute-done.far, bf16[1024,128]{1,0:T(8,128)(2,1)} %collective-permute-done.5.refs_0_, bf16[1024,128]{1,0:T(8,128)(2,1)} %collective-permute-done.7.refs_1_, ...), custom_call_target="tpu_custom_call" | custom-call | flops 402653184 | bytes 2097152 | tf_op jit(solution)/shard_map/pallas_call | solution.py:105
  32.3 1.7 %collective-permute-start.11 = (f32[384,256]{1,0:T(8,128)}, f32[384,256]{1,0:T(8,128)}, u32[]{:S(2)}, u32[]{:S(2)}) collective-permute-start(f32[384,256]{1,0:T(8,128)} %get-tuple-element.31), channel_id=1, source_target_pairs={{0,4},{4,0},{8,12},{12,8},{16,20},{20,16},{24,28},{28,24},{1,5},{5... | collective-permute-start | bytes 1179656 | tf_op jit(solution)/shard_map/ppermute | solution.py:230
  34.0 2.5 %collective-permute-done.8.refs_5_ = bf16[256,512]{1,0:T(8,128)(2,1)} collective-permute-done((bf16[256,512]{1,0:T(8,128)(2,1)}, bf16[256,512]{1,0:T(8,128)(2,1)}, u32[]{:S(2)}, u32[]{:S(2)}) %collective-permute-start.8) | collective-permute-done | bytes 262176 | tf_op jit(solution)/shard_map/ppermute | solution.py:230
  36.5 1.3 %collective-permute-start.12 = (bf16[256,512]{1,0:T(8,128)(2,1)}, bf16[256,512]{1,0:T(8,128)(2,1)}, u32[]{:S(2)}, u32[]{:S(2)}) collective-permute-start(bf16[256,512]{1,0:T(8,128)(2,1)} %collective-permute-done.8.refs_5_), channel_id=1, source_target_pairs={{0,1},{1,0},{2,3},{3,2},{4,5},{5,4},{6,7},{7,6},{8,9},{9,8},{10,11... | collective-permute-start | bytes 786440 | tf_op jit(solution)/shard_map/ppermute | solution.py:280
  38.3 1.3 %collective-permute-start.13 = (bf16[256,512]{1,0:T(8,128)(2,1)}, bf16[256,512]{1,0:T(8,128)(2,1)}, u32[]{:S(2)}, u32[]{:S(2)}) collective-permute-start(bf16[256,512]{1,0:T(8,128)(2,1)} %collective-permute-done.9.refs_3_), channel_id=1, source_target_pairs={{0,1},{1,0},{2,3},{3,2},{4,5},{5,4},{6,7},{7,6},{8,9},{9,8},{10,11... | collective-permute-start | bytes 786440 | tf_op jit(solution)/shard_map/ppermute | solution.py:280
  39.6 1.2 %collective-permute-start.17 = (bf16[512,512]{1,0:T(8,128)(2,1)S(1)}, bf16[512,512]{1,0:T(8,128)(2,1)S(1)}, u32[]{:S(2)}, u32[]{:S(2)}) collective-permute-start(bf16[512,512]{1,0:T(8,128)(2,1)S(1)} %collective-permute-done.16.refs_7_), channel_id=1, source_target_pairs={{0,8},{4,12},{8,0},{12,4},{16,24},{20,28},{24,16},{28,20},{1,9},{5... | collective-permute-start | bytes 1572872 | tf_op jit(solution)/shard_map/ppermute | solution.py:230
  40.9 1.2 %collective-permute-start.10 = (bf16[512,512]{1,0:T(8,128)(2,1)S(1)}, bf16[512,512]{1,0:T(8,128)(2,1)S(1)}, u32[]{:S(2)}, u32[]{:S(2)}) collective-permute-start(bf16[512,512]{1,0:T(8,128)(2,1)S(1)} %collective-permute-done.3.refs_2_), channel_id=1, source_target_pairs={{0,16},{4,20},{8,24},{12,28},{16,0},{20,4},{24,8},{28,12},{1,17},{... | collective-permute-start | bytes 1572872 | tf_op jit(solution)/shard_map/ppermute | solution.py:230
  42.3 1.0 %copy-done.1 = f32[384,256]{1,0:T(8,128)S(1)} copy-done((f32[384,256]{1,0:T(8,128)S(1)}, f32[384,256]{1,0:T(8,128)}, u32[]{:S(2)}) %copy-start.1) | copy-done | bytes 393240
  43.3 1.1 %shard_map.57 = bf16[384,256]{1,0:T(8,128)(2,1)S(1)} custom-call(f32[384,256]{1,0:T(8,128)S(1)} %copy-done.1, f32[384,256]{1,0:T(8,128)} %collective-permute-done.11.far, f32[384,128]{1,0:T(8,128)S(1)} %pad_maximum_fusion.1.cosine, f32[384,128]{1,0:T(8,128)S(1)} %pad_maximum_fusion.2.sine), custom_call_target="tpu_custom_call" | custom-call | flops 589824 | bytes 1376256 | tf_op jit(solution)/shard_map/pallas_call | solution.py:138
  44.4 4.6 %collective-permute-done.13.refs_4_ = bf16[256,512]{1,0:T(8,128)(2,1)} collective-permute-done((bf16[256,512]{1,0:T(8,128)(2,1)}, bf16[256,512]{1,0:T(8,128)(2,1)}, u32[]{:S(2)}, u32[]{:S(2)}) %collective-permute-start.13) | collective-permute-done | bytes 262176 | tf_op jit(solution)/shard_map/ppermute | solution.py:280
  49.0 1.3 %collective-permute-start.14 = (bf16[384,256]{1,0:T(8,128)(2,1)S(1)}, bf16[384,256]{1,0:T(8,128)(2,1)S(1)}, u32[]{:S(2)}, u32[]{:S(2)}) collective-permute-start(bf16[384,256]{1,0:T(8,128)(2,1)S(1)} %shard_map.57), channel_id=1, source_target_pairs={{0,2},{1,3},{4,6},{5,7},{8,10},{9,11},{12,14},{13,15},{16,18},{17,... | collective-permute-start | bytes 589832 | tf_op jit(solution)/shard_map/ppermute | solution.py:291
  50.3 3.2 %collective-permute-start.15 = (bf16[384,256]{1,0:T(8,128)(2,1)S(1)}, bf16[384,256]{1,0:T(8,128)(2,1)S(1)}, u32[]{:S(2)}, u32[]{:S(2)}) collective-permute-start(bf16[384,256]{1,0:T(8,128)(2,1)S(1)} %shard_map.57), channel_id=1, source_target_pairs={{0,1},{1,2},{2,3},{4,5},{5,6},{6,7},{8,9},{9,10},{10,11},{12,13},{... | collective-permute-start | bytes 589832 | tf_op jit(solution)/shard_map/ppermute | solution.py:291
  53.5 5.6 %shard_map.58.refs_2_ = f32[768,512]{1,0:T(8,128)S(1)} custom-call(s32[8]{0:T(128)S(1)} %stack.58.starts, bf16[384,8192]{1,0:T(8,128)(2,1)} %bitcast.18, bf16[384,8192]{1,0:T(8,128)(2,1)} %collective-permute-done.far, bf16[512,512]{1,0:T(8,128)(2,1)S(1)} %get-tuple-element.37.refs_0_, bf16[512,512]{1,0:T(8,128)(2,1)S(1)} %get-tuple-element.38.refs_1_, ...), custom_call_target="tpu_custom_call" | custom-call | flops 2415919104 | bytes 7864320 | tf_op jit(solution)/shard_map/pallas_call | solution.py:105
  59.2 7.4 %collective-permute-done.15 = bf16[384,256]{1,0:T(8,128)(2,1)S(1)} collective-permute-done((bf16[384,256]{1,0:T(8,128)(2,1)S(1)}, bf16[384,256]{1,0:T(8,128)(2,1)S(1)}, u32[]{:S(2)}, u32[]{:S(2)}) %collective-permute-start.15) | collective-permute-done | bytes 196640 | tf_op jit(solution)/shard_map/ppermute | solution.py:291
  66.6 3.3 %shard_map.59 = (f32[384,512]{1,0:T(8,128)S(1)}, f32[384,512]{1,0:T(8,128)}) custom-call(s32[2]{0:T(128)S(1)} %pad_add_fusion.starts, bf16[384,8192]{1,0:T(8,128)(2,1)} %bitcast.19, bf16[384,8192]{1,0:T(8,128)(2,1)} %collective-permute-done.far, bf16[512,512]{1,0:T(8,128)(2,1)S(1)} %collective-permute-done.10.refs_0_, ...), custom_call_target="tpu_custom_call" | custom-call | flops 805306368 | bytes 2621440 | tf_op jit(solution)/shard_map/pallas_call | solution.py:105
  69.9 1.1 %collective-permute-start.18 = (f32[384,512]{1,0:T(8,128)}, f32[384,512]{1,0:T(8,128)S(1)}, u32[]{:S(2)}, u32[]{:S(2)}) collective-permute-start(f32[384,512]{1,0:T(8,128)} %get-tuple-element.46), channel_id=1, source_target_pairs={{0,4},{4,0},{8,12},{12,8},{16,20},{20,16},{24,28},{28,24},{1,5},{5... | collective-permute-start | bytes 2359304 | tf_op jit(solution)/shard_map/ppermute | solution.py:230
  71.1 2.0 %collective-permute-done.18.far = f32[384,512]{1,0:T(8,128)S(1)} collective-permute-done((f32[384,512]{1,0:T(8,128)}, f32[384,512]{1,0:T(8,128)S(1)}, u32[]{:S(2)}, u32[]{:S(2)}) %collective-permute-start.18) | collective-permute-done | bytes 786464 | tf_op jit(solution)/shard_map/ppermute | solution.py:230
  73.1 3.6 %shard_map.60 = bf16[384,512]{1,0:T(8,128)(2,1)} custom-call(f32[384,512]{1,0:T(8,128)S(1)} %get-tuple-element.45.near, f32[384,512]{1,0:T(8,128)S(1)} %collective-permute-done.18.far, f32[384,128]{1,0:T(8,128)S(1)} %pad_maximum_fusion.1.cosine, f32[384,128]{1,0:T(8,128)S(1)} %pad_maximum_fusion.2.sine, s32[384,1]{1,0:T(8,128)S(1)} %copy.7.first, ...), custom_call_target="tpu_custom_call" | custom-call | flops 704643072 | bytes 1572864 | tf_op jit(solution)/shard_map/pallas_call | solution.py:200
  (41 shorter events, 6.1 us)
Async XLA Ops:
  0.0 21.4 %collective-permute-start = (bf16[384,8192]{1,0:T(8,128)(2,1)}, bf16[384,8192]{1,0:T(8,128)(2,1)}, u32[]{:S(2)}, u32[]{:S(2)}) collective-permute-start(bf16[384,8192]{1,0:T(8,128)(2,1)} %bitcast.15), channel_id=1, source_target_pairs={{0,4},{4,0},{8,12},{12,8},{16,20},{20,16},{24,28},{28,24},{1,5},{5... | collective-permute-start | bytes 18874376 | tf_op jit(solution)/shard_map/ppermute | solution.py:230
  0.7 15.2 %collective-permute-start.1 = (bf16[1024,128]{1,0:T(8,128)(2,1)}, bf16[1024,128]{1,0:T(8,128)(2,1)S(1)}, u32[]{:S(2)}, u32[]{:S(2)}) collective-permute-start(bf16[1024,128]{1,0:T(8,128)(2,1)} %refs_0_.1), channel_id=1, source_target_pairs={{0,16},{4,20},{8,24},{12,28},{16,0},{20,4},{24,8},{28,12},{1,17},{... | collective-permute-start | bytes 786440 | tf_op jit(solution)/shard_map/ppermute | solution.py:230
  1.9 7.9 %collective-permute-start.4 = (bf16[1024,128]{1,0:T(8,128)(2,1)}, bf16[1024,128]{1,0:T(8,128)(2,1)S(1)}, u32[]{:S(2)}, u32[]{:S(2)}) collective-permute-start(bf16[1024,128]{1,0:T(8,128)(2,1)} %refs_0_.1), channel_id=1, source_target_pairs={{0,8},{4,12},{8,0},{12,4},{16,24},{20,28},{24,16},{28,20},{1,9},{5... | collective-permute-start | bytes 786440 | tf_op jit(solution)/shard_map/ppermute | solution.py:230
  3.1 12.8 %collective-permute-start.2 = (bf16[1024,128]{1,0:T(8,128)(2,1)}, bf16[1024,128]{1,0:T(8,128)(2,1)S(1)}, u32[]{:S(2)}, u32[]{:S(2)}) collective-permute-start(bf16[1024,128]{1,0:T(8,128)(2,1)} %refs_1_.1), channel_id=1, source_target_pairs={{0,8},{4,12},{8,0},{12,4},{16,24},{20,28},{24,16},{28,20},{1,9},{5... | collective-permute-start | bytes 786440 | tf_op jit(solution)/shard_map/ppermute | solution.py:230
  3.4 11.2 %collective-permute-start.6 = (bf16[1024,128]{1,0:T(8,128)(2,1)}, bf16[1024,128]{1,0:T(8,128)(2,1)}, u32[]{:S(2)}, u32[]{:S(2)}) collective-permute-start(bf16[1024,128]{1,0:T(8,128)(2,1)} %refs_1_.1), channel_id=1, source_target_pairs={{0,16},{4,20},{8,24},{12,28},{16,0},{20,4},{24,8},{28,12},{1,17},{... | collective-permute-start | bytes 786440 | tf_op jit(solution)/shard_map/ppermute | solution.py:230
  7.3 15.4 %copy-start.2 = (bf16[1024,128]{1,0:T(8,128)(2,1)S(1)}, bf16[1024,128]{1,0:T(8,128)(2,1)}, u32[]{:S(2)}) copy-start(bf16[1024,128]{1,0:T(8,128)(2,1)} %refs_0_.1) | copy-start | bytes 786436
  7.3 15.4 %copy-start.3 = (bf16[1024,128]{1,0:T(8,128)(2,1)S(1)}, bf16[1024,128]{1,0:T(8,128)(2,1)}, u32[]{:S(2)}) copy-start(bf16[1024,128]{1,0:T(8,128)(2,1)} %refs_1_.1) | copy-start | bytes 786436
  9.9 10.3 %collective-permute-start.5 = (bf16[1024,128]{1,0:T(8,128)(2,1)S(1)}, bf16[1024,128]{1,0:T(8,128)(2,1)}, u32[]{:S(2)}, u32[]{:S(2)}) collective-permute-start(bf16[1024,128]{1,0:T(8,128)(2,1)S(1)} %collective-permute-done.4.refs_2_), channel_id=1, source_target_pairs={{0,16},{4,20},{8,24},{12,28},{16,0},{20,4},{24,8},{28,12},{1,17},{... | collective-permute-start | bytes 786440 | tf_op jit(solution)/shard_map/ppermute | solution.py:230
  14.5 14.3 %collective-permute-start.7 = (bf16[1024,128]{1,0:T(8,128)(2,1)}, bf16[1024,128]{1,0:T(8,128)(2,1)}, u32[]{:S(2)}, u32[]{:S(2)}) collective-permute-start(bf16[1024,128]{1,0:T(8,128)(2,1)} %collective-permute-done.6.refs_5_), channel_id=1, source_target_pairs={{0,8},{4,12},{8,0},{12,4},{16,24},{20,28},{24,16},{28,20},{1,9},{5... | collective-permute-start | bytes 786440 | tf_op jit(solution)/shard_map/ppermute | solution.py:230
  15.9 0.7 copy-start.4
  16.6 23.0 %collective-permute-start.16 = (bf16[512,512]{1,0:T(8,128)(2,1)S(1)}, bf16[512,512]{1,0:T(8,128)(2,1)S(1)}, u32[]{:S(2)}, u32[]{:S(2)}) collective-permute-start(bf16[512,512]{1,0:T(8,128)(2,1)S(1)} %get-tuple-element.38.refs_1_), channel_id=1, source_target_pairs={{0,16},{4,20},{8,24},{12,28},{16,0},{20,4},{24,8},{28,12},{1,17},{... | collective-permute-start | bytes 1572872 | tf_op jit(solution)/shard_map/ppermute | solution.py:230
  17.9 23.0 %collective-permute-start.3 = (bf16[512,512]{1,0:T(8,128)(2,1)S(1)}, bf16[512,512]{1,0:T(8,128)(2,1)S(1)}, u32[]{:S(2)}, u32[]{:S(2)}) collective-permute-start(bf16[512,512]{1,0:T(8,128)(2,1)S(1)} %get-tuple-element.37.refs_0_), channel_id=1, source_target_pairs={{0,8},{4,12},{8,0},{12,4},{16,24},{20,28},{24,16},{28,20},{1,9},{5... | collective-permute-start | bytes 1572872 | tf_op jit(solution)/shard_map/ppermute | solution.py:230
  20.2 16.4 %collective-permute-start.8 = (bf16[256,512]{1,0:T(8,128)(2,1)}, bf16[256,512]{1,0:T(8,128)(2,1)}, u32[]{:S(2)}, u32[]{:S(2)}) collective-permute-start(bf16[256,512]{1,0:T(8,128)(2,1)} %get-tuple-element.28), channel_id=1, source_target_pairs={{0,16},{4,20},{8,24},{12,28},{16,0},{20,4},{24,8},{28,12},{1,17},{... | collective-permute-start | bytes 786440 | tf_op jit(solution)/shard_map/ppermute | solution.py:230
  21.4 16.9 %collective-permute-start.9 = (bf16[256,512]{1,0:T(8,128)(2,1)}, bf16[256,512]{1,0:T(8,128)(2,1)}, u32[]{:S(2)}, u32[]{:S(2)}) collective-permute-start(bf16[256,512]{1,0:T(8,128)(2,1)} %get-tuple-element.29), channel_id=1, source_target_pairs={{0,8},{4,12},{8,0},{12,4},{16,24},{20,28},{24,16},{28,20},{1,9},{5... | collective-permute-start | bytes 786440 | tf_op jit(solution)/shard_map/ppermute | solution.py:230
  22.6 1.0 %copy-start.5 = (bf16[1024,128]{1,0:T(8,128)(2,1)S(1)}, bf16[1024,128]{1,0:T(8,128)(2,1)}, u32[]{:S(2)}) copy-start(bf16[1024,128]{1,0:T(8,128)(2,1)} %copy-done.4) | copy-start | bytes 786436
  31.5 0.8 copy-start
  32.3 10.0 %collective-permute-start.11 = (f32[384,256]{1,0:T(8,128)}, f32[384,256]{1,0:T(8,128)}, u32[]{:S(2)}, u32[]{:S(2)}) collective-permute-start(f32[384,256]{1,0:T(8,128)} %get-tuple-element.31), channel_id=1, source_target_pairs={{0,4},{4,0},{8,12},{12,8},{16,20},{20,16},{24,28},{28,24},{1,5},{5... | collective-permute-start | bytes 1179656 | tf_op jit(solution)/shard_map/ppermute | solution.py:230
  36.5 7.9 %collective-permute-start.12 = (bf16[256,512]{1,0:T(8,128)(2,1)}, bf16[256,512]{1,0:T(8,128)(2,1)}, u32[]{:S(2)}, u32[]{:S(2)}) collective-permute-start(bf16[256,512]{1,0:T(8,128)(2,1)} %collective-permute-done.8.refs_5_), channel_id=1, source_target_pairs={{0,1},{1,0},{2,3},{3,2},{4,5},{5,4},{6,7},{7,6},{8,9},{9,8},{10,11... | collective-permute-start | bytes 786440 | tf_op jit(solution)/shard_map/ppermute | solution.py:280
  38.3 10.7 %collective-permute-start.13 = (bf16[256,512]{1,0:T(8,128)(2,1)}, bf16[256,512]{1,0:T(8,128)(2,1)}, u32[]{:S(2)}, u32[]{:S(2)}) collective-permute-start(bf16[256,512]{1,0:T(8,128)(2,1)} %collective-permute-done.9.refs_3_), channel_id=1, source_target_pairs={{0,1},{1,0},{2,3},{3,2},{4,5},{5,4},{6,7},{7,6},{8,9},{9,8},{10,11... | collective-permute-start | bytes 786440 | tf_op jit(solution)/shard_map/ppermute | solution.py:280
  39.6 26.9 %collective-permute-start.17 = (bf16[512,512]{1,0:T(8,128)(2,1)S(1)}, bf16[512,512]{1,0:T(8,128)(2,1)S(1)}, u32[]{:S(2)}, u32[]{:S(2)}) collective-permute-start(bf16[512,512]{1,0:T(8,128)(2,1)S(1)} %collective-permute-done.16.refs_7_), channel_id=1, source_target_pairs={{0,8},{4,12},{8,0},{12,4},{16,24},{20,28},{24,16},{28,20},{1,9},{5... | collective-permute-start | bytes 1572872 | tf_op jit(solution)/shard_map/ppermute | solution.py:230
  40.9 25.7 %collective-permute-start.10 = (bf16[512,512]{1,0:T(8,128)(2,1)S(1)}, bf16[512,512]{1,0:T(8,128)(2,1)S(1)}, u32[]{:S(2)}, u32[]{:S(2)}) collective-permute-start(bf16[512,512]{1,0:T(8,128)(2,1)S(1)} %collective-permute-done.3.refs_2_), channel_id=1, source_target_pairs={{0,16},{4,20},{8,24},{12,28},{16,0},{20,4},{24,8},{28,12},{1,17},{... | collective-permute-start | bytes 1572872 | tf_op jit(solution)/shard_map/ppermute | solution.py:230
  42.3 1.0 %copy-start.1 = (f32[384,256]{1,0:T(8,128)S(1)}, f32[384,256]{1,0:T(8,128)}, u32[]{:S(2)}) copy-start(f32[384,256]{1,0:T(8,128)} %copy-done) | copy-start | bytes 1179652
  49.0 10.2 %collective-permute-start.14 = (bf16[384,256]{1,0:T(8,128)(2,1)S(1)}, bf16[384,256]{1,0:T(8,128)(2,1)S(1)}, u32[]{:S(2)}, u32[]{:S(2)}) collective-permute-start(bf16[384,256]{1,0:T(8,128)(2,1)S(1)} %shard_map.57), channel_id=1, source_target_pairs={{0,2},{1,3},{4,6},{5,7},{8,10},{9,11},{12,14},{13,15},{16,18},{17,... | collective-permute-start | bytes 589832 | tf_op jit(solution)/shard_map/ppermute | solution.py:291
  50.3 16.2 %collective-permute-start.15 = (bf16[384,256]{1,0:T(8,128)(2,1)S(1)}, bf16[384,256]{1,0:T(8,128)(2,1)S(1)}, u32[]{:S(2)}, u32[]{:S(2)}) collective-permute-start(bf16[384,256]{1,0:T(8,128)(2,1)S(1)} %shard_map.57), channel_id=1, source_target_pairs={{0,1},{1,2},{2,3},{4,5},{5,6},{6,7},{8,9},{9,10},{10,11},{12,13},{... | collective-permute-start | bytes 589832 | tf_op jit(solution)/shard_map/ppermute | solution.py:291
  69.9 3.2 %collective-permute-start.18 = (f32[384,512]{1,0:T(8,128)}, f32[384,512]{1,0:T(8,128)S(1)}, u32[]{:S(2)}, u32[]{:S(2)}) collective-permute-start(f32[384,512]{1,0:T(8,128)} %get-tuple-element.46), channel_id=1, source_target_pairs={{0,4},{4,0},{8,12},{12,8},{16,20},{20,16},{24,28},{28,24},{1,5},{5... | collective-permute-start | bytes 2359304 | tf_op jit(solution)/shard_map/ppermute | solution.py:230

commit v5 on v4

--- a/solution.py
+++ b/solution.py
@@ -44,26 +44,60 @@
     return lax.optimization_barrier((array, *earlier))[0]
 
 
+def pack_kernel(begin, key, value, query, *refs):
+    pair, top, bottom = refs[:3]
+    parts, sems = refs[3:-1], refs[-1]
+    head_size = key.shape[1]
+    half = top.shape[0]
+    copies = []
+    for side, part in enumerate(parts):
+        rows = pl.ds(pl.multiple_of(side * half + begin[0], 16), part.shape[0])
+        copies.append((query.at[rows], part))
+    copies += [
+        (key, pair.at[:, :head_size]),
+        (value, pair.at[:, head_size:]),
+        (query.at[:half], top),
+        (query.at[half:], bottom),
+    ]
+    copies = [pltpu.make_async_copy(*copy, sems.at[i]) for i, copy in enumerate(copies)]
+    for copy in copies:
+        copy.start()
+    for copy in copies:
+        copy.wait()
+
+
+def pack(begin, key, value, query, halved):
+    depth, width = query.shape
+    shapes = [(depth, 2 * key.shape[1])] + [(depth // 2, width)] * 2
+    shapes += [(depth // 4, width)] * (2 if halved else 0)
+    return pl.pallas_call(
+        pack_kernel,
+        out_shape=[jax.ShapeDtypeStruct(shape, query.dtype) for shape in shapes],
+        in_specs=[pl.BlockSpec(memory_space=pltpu.SMEM)] + anywhere(3),
+        out_specs=anywhere(len(shapes)),
+        scratch_shapes=[pltpu.SemaphoreType.DMA((6,))],
+        compiler_params=pltpu.CompilerParams(vmem_limit_bytes=48 * MIB),
+        cost_estimate=pl.CostEstimate(
+            flops=0, bytes_accessed=8 * query.size, transcendentals=0
+        ),
+    )(begin, key, value, query)
+
+
 def project_kernel(steps, carried, final, starts, near, far, *refs):
-    count = sum(len(spots) for _, spots in steps)
-    weights, refs = refs[:count], refs[count:]
+    weights, refs = refs[: len(steps)], refs[len(steps) :]
     if carried:
         carry, refs = refs[0], refs[1:]
     outs, (tokens, held, sems) = refs[:-3], refs[-3:]
     rows = near.shape[0]
     batches = ([], [], [])
-    used = row = 0
-    for step, (depth, spots) in enumerate(steps):
+    row = 0
+    for step, depth in enumerate(steps):
         here = slice(row, row + depth)
         row += depth
         window = pl.ds(pl.multiple_of(starts[step], 128), depth)
-        for index, columns in enumerate(spots):
-            batches[0].append(
-                pltpu.make_async_copy(
-                    weights[used], held.at[here, columns], sems.at[step, 2 + index]
-                )
-            )
-            used += 1
+        batches[0].append(
+            pltpu.make_async_copy(weights[step], held.at[here], sems.at[step, 2])
+        )
         for side, ref in enumerate((far, near)):
             batches[1 + side].append(
                 pltpu.make_async_copy(
@@ -90,15 +124,10 @@
 
 def project(terms, near, far, carry=None, final=False):
     rows = near.shape[0]
-    width = sum(array.shape[1] for array in terms[0][1])
-    steps = []
-    for _, arrays in terms:
-        edges = [sum(array.shape[1] for array in arrays[:i]) for i in range(len(arrays) + 1)]
-        spots = [slice(*edge) for edge in zip(edges[:-1], edges[1:])]
-        steps.append((arrays[0].shape[0], spots))
-    depth = sum(step[0] for step in steps)
+    width = terms[0][1].shape[1]
+    steps = [array.shape[0] for _, array in terms]
+    depth = sum(steps)
     starts = jnp.stack([start for start, _ in terms]).astype(jnp.int32)
-    weights = [array for _, arrays in terms for array in arrays]
     whole = jax.ShapeDtypeStruct((2 * rows, width), jnp.float32)
     part = jax.ShapeDtypeStruct((rows, width), jnp.float32)
     carries = [] if carry is None else [carry]
@@ -106,13 +135,13 @@
         functools.partial(project_kernel, steps, carry is not None, final),
         out_shape=(part, part) if final else whole,
         in_specs=[pl.BlockSpec(memory_space=pltpu.SMEM)]
-        + anywhere(2 + len(weights))
+        + anywhere(2 + len(terms))
         + vmem(len(carries)),
         out_specs=tuple(vmem(2)) if final else vmem(1)[0],
         scratch_shapes=[
             pltpu.VMEM((2, rows, depth), jnp.bfloat16),
             pltpu.VMEM((depth, width), jnp.bfloat16),
-            pltpu.SemaphoreType.DMA((len(steps), 4)),
+            pltpu.SemaphoreType.DMA((len(steps), 3)),
         ],
         compiler_params=pltpu.CompilerParams(vmem_limit_bytes=48 * MIB),
         cost_estimate=pl.CostEstimate(
@@ -120,7 +149,7 @@
             bytes_accessed=2 * depth * (2 * rows + width),
             transcendentals=0,
         ),
-    )(starts, near, far, *weights, *carries)
+    )(starts, near, far, *[array for _, array in terms], *carries)
 
 
 def turn(vectors, cosine, sine):
@@ -229,20 +258,19 @@
     def swap(array, mask):
         return lax.ppermute(array, "dp", [(i, i ^ mask) for i in range(dp_size)])
 
-    def fetch(pair, gate, later, seconds):
-        held = [{0: [(0, array)]} for array in pair]
-        for step in range(bits):
-            axes = (step, bits - 1 - step)
-            for sources in zip(*[sorted(side) for side in held]):
-                for side, source in enumerate(sources):
-                    array = held[side][source][0][1]
-                    mask = 2 << axes[side]
-                    if source == 0 and step == bits - 1 and seconds:
-                        got = seconds[side]
-                    else:
-                        array = after(array, *(gate if source == 0 else later))
-                        got = [(0, swap(array, mask))]
-                    held[side][source | (1 << axes[side])] = got
+    def fetch(pair, given, gate, later):
+        held = []
+        for side, array in enumerate(pair):
+            pieces = {0: [(0, array)], **given[side]}
+            reached = [0]
+            for axis in list(range(bits))[:: 1 - 2 * side]:
+                for source in list(reached):
+                    target = source | (1 << axis)
+                    reached.append(target)
+                    if target not in pieces:
+                        sent = after(pieces[source][0][1], *(later if source else gate))
+                        pieces[target] = [(0, swap(sent, 2 << axis))]
+            held.append(pieces)
         return held
 
     sibling_hidden = swap(hidden, 1)
@@ -252,56 +280,66 @@
     cosine, sine = rope_tables(positions, head_size)
     first = (doc_starts(doc_lengths[0], positions) - offset)[:, None]
 
+    axes = [1 << axis for axis in range(bits)]
+
     def begins(chip):
         return (me ^ (2 * chip)) * depth
 
-    first_axis, last_axis = 1, 1 << (bits - 1)
-    last = chips - 1
-
     half = depth // 2
-    halves = [w_query[:half], w_query[half:]]
-    parts = []
-    if ctx_size % 2 == 0:
-        begin = (place % 2) * (half // 2)
-        parts = [
-            lax.dynamic_slice_in_dim(w_query, side * half + begin, half // 2, 0)
-            for side in range(2)
+    halved = ctx_size % 2 == 0
+    some = half // 2
+    begin = (place % 2) * some
+    packed = pack(begin[None], w_key, w_value, w_query, halved)
+    pair_here, halves, parts = packed[0], packed[1:3], packed[3:]
+
+    given = [{}, {}]
+    mine = [swap(part, 2 << axis) for part, axis in zip(parts, (bits - 1, 0))]
+    if halved:
+        both = jnp.concatenate(mine, axis=0)
+        both = lax.ppermute(both, "ctx", [(i, i ^ 1) for i in range(ctx_size)])
+        given = [
+            {1 << axis: [(begin, mine[side]), (some - begin, both[side * some : side * some + some])]}
+            for side, axis in enumerate((bits - 1, 0))
         ]
-
-    pair_held = fetch((w_key, w_value), [], [], [])
+    pairs = [pair_here] + [swap(pair_here, 2 << axis) for axis in range(bits)]
+    sides = [slice(0, half), slice(half, depth)]
+    pair_held = fetch(
+        [pair_here[rows] for rows in sides],
+        [{1 << axis: [(0, pairs[1 + axis][rows])] for axis in range(bits)} for rows in sides],
+        [],
+        [],
+    )
+    pair_terms = [(begins(chip), array) for chip, array in zip([0] + axes, pairs)]
+    carry = project(pair_terms, hidden, sibling_hidden)
     pair_terms = [
-        (begins(chip), [pair_held[side][chip][0][1] for side in range(2)]) for chip in range(chips)
+        (begins(chip) + side * half, pair_held[side][chip][0][1])
+        for chip in range(chips)
+        if chip not in [0] + axes
+        for side in range(2)
     ]
-    carry = project(pair_terms[:-1], hidden, sibling_hidden)
-    near, far = project(pair_terms[-1:], hidden, sibling_hidden, carry, True)
-    gate = [pair_held[0][last_axis][0][1], pair_held[1][first_axis][0][1]]
-    gate += [cosine, sine, first, *halves, *parts]
-    mine = [swap(after(part, *gate), 2 << axis) for part, axis in zip(parts, (bits - 1, 0))]
-    other = [lax.ppermute(part, "ctx", [(i, i ^ 1) for i in range(ctx_size)]) for part in mine]
-    seconds = [
-        [(begin, here), (half // 2 - begin, there)] for here, there in zip(mine, other)
-    ]
-    query_held = fetch(halves, gate, [near, *mine], seconds)
+    near, far = project(pair_terms, hidden, sibling_hidden, carry, True)
+    query_held = fetch(halves, given, [*mine, cosine, sine, first], [near])
 
     pair = finish_pair(near, swap(far, 1), cosine, sine)
     longest = ctx_size * row_count // 2
     back = -(-(longest - 1) // ROW_TILE) * ROW_TILE
     hops = min(ctx_size - 1, -(-back // row_count))
     blocks = [
-        lax.ppermute(after(pair, *other), "ctx", [(i, i + hop) for i in range(ctx_size - hop)])
+        lax.ppermute(after(pair, both) if halved else pair, "ctx", [(i, i + hop) for i in range(ctx_size - hop)])
         for hop in range(hops, 0, -1)
     ]
     keys_values = jnp.concatenate(blocks + [pair], axis=0)
 
     def query_terms(wanted, *gate):
         return [
-            (begins(chip) + side * half + begin, [after(array, *gate)])
+            (begins(chip) + side * half + row, after(array, *gate))
             for side, chip in wanted
-            for begin, array in query_held[side][chip]
+            for row, array in query_held[side][chip]
         ]
 
-    late = [(0, last), (1, last)]
-    early = [(side, chip) for chip in range(last) for side in range(2)]
+    everything = [(side, chip) for chip in range(chips) for side in range(2)]
+    early = [(side, chip) for side, chip in everything if chip in [0] + axes]
+    late = [wanted for wanted in everything if wanted not in early]
     carry = project(query_terms(early, pair), hidden, sibling_hidden)
     near, far = project(query_terms(late, keys_values), hidden, sibling_hidden, carry, True)
     return attend(near, swap(far, 1), cosine, sine, first, keys_values, back)[None]

time: 78.1 us -> 80.8 us (1.035); the launches traced: 76.7 us -> 80.4 us
  waiting for transfers between devices: 23.4 us -> 33.2 us
  starting transfers between devices: 21.7 us -> 16.1 us
  local copies, waits for them, and re-layouts: 6.85 us -> 5.15 us
  other arithmetic: 2.79 us -> 3.94 us
    ppermute x15 -> x13, waiting for transfers between devices: 11.5 us -> 26.1 us  [swap(): return lax.ppermute(array, 'dp', [(i, i ^ mask) for i in range(dp_size)])]
    ppermute x4 -> x3, waiting for transfers between devices: 11.9 us -> 7.14 us  [the longest x2 7.13 us: shards(): lax.ppermute(after(pair, both) if halved else pair, 'ctx', [(i, i + hop)...]
    ppermute x15 -> x13, starting transfers between devices: 14.7 us -> 11.4 us  [swap(): return lax.ppermute(array, 'dp', [(i, i ^ mask) for i in range(dp_size)])]
    ppermute x4 -> x3, starting transfers between devices: 7.08 us -> 4.67 us  [the longest x2 3.37 us: shards(): lax.ppermute(after(pair, both) if halved else pair, 'ctx', [(i, i + hop)...]
    dynamic_slice x1 -> x0, local copies, waits for them, and re-layouts: 1.95 us -> none  [shards(): lax.dynamic_slice_in_dim(w_query, side * half + begin, half // 2, 0)]
    pallas_call x1, Pallas kernels: 1.14 us -> 0.12 us  [finish_pair(): pl.pallas_call(pair_kernel, out_shape=jax.ShapeDtypeStruct(near.shape, jn...]
    pallas_call x0 -> x1, Pallas kernels: none -> 1 us  [pack(): pl.pallas_call(pack_kernel, out_shape=[jax.ShapeDtypeStruct(shape, query....]
    concatenate x1, other arithmetic: 0.12 us -> 1.05 us  [rope_tables(): jnp.concatenate([-sine_part, sine_part], axis=-1)]
  transfers between devices with their start and end apart: 19 -> 16, of which waited for: 8 -> 5; matrix products, arithmetic and copies ran while one was open for 8% -> 7% of each run, Pallas kernels for 19% -> 19%
where the time goes in v5:
time: 80.8 us; the launch traced here: 80.4 us
  waiting for transfers between devices  33.2 us (41%)
  Pallas kernels  21.9 us (27%)
  starting transfers between devices  16.1 us (20%)
  local copies, waits for them, and re-layouts  5.15 us (6%)
  other arithmetic  3.94 us (5%)
    ppermute x13, waiting for transfers between devices, swap(): return lax.ppermute(array, 'dp', [(i, i ^ mask) for i in range(dp_size)])  26.1 us
    pallas_call x4, Pallas kernels, project(): pl.pallas_call(functools.partial(project_kernel, steps, carry is not None...  17.1 us
    ppermute x13, starting transfers between devices, swap(): return lax.ppermute(array, 'dp', [(i, i ^ mask) for i in range(dp_size)])  11.4 us
    ppermute x2, waiting for transfers between devices, shards(): lax.ppermute(after(pair, both) if halved else pair, 'ctx', [(i, i + hop)...  7.13 us
    pallas_call x1, Pallas kernels, attend(): pl.pallas_call(functools.partial(attend_kernel, back), out_shape=jax.Shap...  3.65 us
    ppermute x2, starting transfers between devices, shards(): lax.ppermute(after(pair, both) if halved else pair, 'ctx', [(i, i + hop)...  3.37 us
    unnamed x8, local copies, waits for them, and re-layouts  3.13 us
  transfers between devices with their start and end apart: 16, of which 5 were waited for; matrix products, arithmetic and copies ran while one was open for 7% of the time, Pallas kernels for 19%

profile of v5, /device:TPU:17, one launch (start us, length us, event | category | flops | bytes accessed | tf_op | source)
XLA Modules:
  0.0 80.4 jit_solution(5152730538074805060)
XLA Ops:
  0.0 0.7 collective-permute-start
  0.7 1.2 %copy-done = bf16[1024,512]{1,0:T(8,128)(2,1)S(1)} copy-done((bf16[1024,512]{1,0:T(8,128)(2,1)S(1)}, bf16[1024,512]{1,0:T(8,128)(2,1)}, u32[]{:S(2)}) %copy-start) | copy-done | bytes 1048600
  1.9 0.9 %copy-done.1 = bf16[1024,128]{1,0:T(8,128)(2,1)S(1)} copy-done((bf16[1024,128]{1,0:T(8,128)(2,1)S(1)}, bf16[1024,128]{1,0:T(8,128)(2,1)}, u32[]{:S(2)}) %copy-start.1) | copy-done | bytes 262168
  2.9 0.9 %copy-done.2 = bf16[1024,128]{1,0:T(8,128)(2,1)S(1)} copy-done((bf16[1024,128]{1,0:T(8,128)(2,1)S(1)}, bf16[1024,128]{1,0:T(8,128)(2,1)}, u32[]{:S(2)}) %copy-start.2) | copy-done | bytes 262168
  3.8 1.0 %shard_map.55 = (bf16[1024,256]{1,0:T(8,128)(2,1)}, bf16[512,512]{1,0:T(8,128)(2,1)S(1)}, bf16[512,512]{1,0:T(8,128)(2,1)S(1)}, bf16[256,512]{1,0:T(8,128)(2,1)}, bf16[256,512]{1,0:T(8,128)(2,1)S(1)}) custom-call(s32[1]{0:T(128)} %bitcast.3.begin, bf16[1024,128]{1,0:T(8,128)(2,1)S(1)} %copy-done.1, bf16[1024,128]{1,0:T(8,128)(2,1)S(1)} %copy-done.2, ...), custom_call_target="tpu_custom_call" | custom-call | bytes 4194304 | tf_op jit(solution)/shard_map/pallas_call | solution.py:73
  4.8 1.3 %collective-permute-start.4 = (bf16[1024,256]{1,0:T(8,128)(2,1)}, bf16[1024,256]{1,0:T(8,128)(2,1)S(1)}, u32[]{:S(2)}, u32[]{:S(2)}) collective-permute-start(bf16[1024,256]{1,0:T(8,128)(2,1)} %get-tuple-element.33.refs_0_), channel_id=1, source_target_pairs={{0,8},{4,12},{8,0},{12,4},{16,24},{20,28},{24,16},{28,20},{1,9},{5... | collective-permute-start | bytes 1572872 | tf_op jit(solution)/shard_map/ppermute | solution.py:259
  6.1 1.2 %collective-permute-start.6 = (bf16[1024,256]{1,0:T(8,128)(2,1)}, bf16[1024,256]{1,0:T(8,128)(2,1)S(1)}, u32[]{:S(2)}, u32[]{:S(2)}) collective-permute-start(bf16[1024,256]{1,0:T(8,128)(2,1)} %get-tuple-element.33.refs_0_), channel_id=1, source_target_pairs={{0,16},{4,20},{8,24},{12,28},{16,0},{20,4},{24,8},{28,12},{1,17},{... | collective-permute-start | bytes 1572872 | tf_op jit(solution)/shard_map/ppermute | solution.py:259
  8.1 1.4 %fusion = (f32[384,64]{1,0:T(8,128)S(1)}, f32[384,64]{1,0:T(8,128)}, f32[384,64]{1,0:T(8,128)S(1)}) fusion(f32[64]{0:T(128)S(1)} %negate_power_fusion, f32[384]{0:T(512)S(1)} %get-tuple-element.59), kind=kLoop, calls=%fused_computation.6 | loop fusion | flops 49152 | bytes 296704 | tf_op jit(solution)/shard_map/neg | solution.py:24
  9.7 1.0 %pad_maximum_fusion.3.sine = f32[384,128]{1,0:T(8,128)S(1)} fusion(f32[384,64]{1,0:T(8,128)} %get-tuple-element.56, f32[384,64]{1,0:T(8,128)S(1)} %get-tuple-element.55), kind=kLoop, calls=%fused_computation.5 | loop fusion | flops 49152 | bytes 393216 | tf_op jit(solution)/shard_map/concatenate | solution.py:24
  10.8 14.4 %collective-permute-done.1.refs_5_ = bf16[256,512]{1,0:T(8,128)(2,1)S(1)} collective-permute-done((bf16[256,512]{1,0:T(8,128)(2,1)}, bf16[256,512]{1,0:T(8,128)(2,1)S(1)}, u32[]{:S(2)}, u32[]{:S(2)}) %collective-permute-start.1) | collective-permute-done | bytes 262176 | tf_op jit(solution)/shard_map/ppermute | solution.py:259
  25.2 1.2 %collective-permute-start.13 = (bf16[512,512]{1,0:T(8,128)(2,1)S(1)}, bf16[512,512]{1,0:T(8,128)(2,1)}, u32[]{:S(2)}, u32[]{:S(2)}) collective-permute-start(bf16[512,512]{1,0:T(8,128)(2,1)S(1)} %get-tuple-element.44.refs_1_), channel_id=1, source_target_pairs={{0,16},{4,20},{8,24},{12,28},{16,0},{20,4},{24,8},{28,12},{1,17},{... | collective-permute-start | bytes 1572872 | tf_op jit(solution)/shard_map/ppermute | solution.py:259
  26.4 0.8 %pad_maximum_fusion.1 = bf16[512,512]{1,0:T(8,128)(2,1)} fusion(bf16[256,512]{1,0:T(8,128)(2,1)S(1)} %collective-permute-done.2.refs_3_, bf16[256,512]{1,0:T(8,128)(2,1)S(1)} %collective-permute-done.1.refs_5_), kind=kLoop, calls=%fused_computation.1 | loop fusion | flops 1048576 | bytes 1048576 | tf_op jit(solution)/shard_map/concatenate | solution.py:298
  27.2 1.3 %collective-permute-start.10 = (bf16[512,512]{1,0:T(8,128)(2,1)}, bf16[512,512]{1,0:T(8,128)(2,1)}, u32[]{:S(2)}, u32[]{:S(2)}) collective-permute-start(bf16[512,512]{1,0:T(8,128)(2,1)} %pad_maximum_fusion.1), channel_id=1, source_target_pairs={{0,1},{1,0},{2,3},{3,2},{4,5},{5,4},{6,7},{7,6},{8,9},{9,8},{10,11... | collective-permute-start | bytes 1572872 | tf_op jit(solution)/shard_map/ppermute | solution.py:299
  28.5 0.3 collective-permute-start.3
  28.9 0.3 collective-permute-start.5
  29.2 0.7 slice.17
  29.9 1.2 %collective-permute-start.7 = (bf16[512,256]{1,0:T(8,128)(2,1)}, bf16[512,256]{1,0:T(8,128)(2,1)}, u32[]{:S(2)}, u32[]{:S(2)}) collective-permute-start(bf16[512,256]{1,0:T(8,128)(2,1)} %slice.17), channel_id=1, source_target_pairs={{0,8},{4,12},{8,0},{12,4},{16,24},{20,28},{24,16},{28,20},{1,9},{5... | collective-permute-start | bytes 786440 | tf_op jit(solution)/shard_map/ppermute | solution.py:259
  31.2 5.1 %shard_map.56.refs_2_ = f32[768,256]{1,0:T(8,128)S(1)} custom-call(s32[3]{0:T(128)S(1)} %pad_add_fusion.1.starts, bf16[384,8192]{1,0:T(8,128)(2,1)} %bitcast.17, bf16[384,8192]{1,0:T(8,128)(2,1)} %collective-permute-done.far, bf16[1024,256]{1,0:T(8,128)(2,1)} %get-tuple-element.33.refs_0_, bf16[1024,256]{1,0:T(8,128)(2,1)S(1)} %collective-permute-done.4.refs_1_, ...), custom_call_target="tpu_custom_call" | custom-call | flops 1207959552 | bytes 6291456 | tf_op jit(solution)/shard_map/pallas_call | solution.py:134
  36.4 6.8 %collective-permute-done.5.refs_0_ = bf16[512,256]{1,0:T(8,128)(2,1)S(1)} collective-permute-done((bf16[512,256]{1,0:T(8,128)(2,1)S(1)}, bf16[512,256]{1,0:T(8,128)(2,1)S(1)}, u32[]{:S(2)}, u32[]{:S(2)}) %collective-permute-start.5) | collective-permute-done | bytes 262176 | tf_op jit(solution)/shard_map/ppermute | solution.py:259
  43.2 2.8 %collective-permute-done.7.refs_1_ = bf16[512,256]{1,0:T(8,128)(2,1)} collective-permute-done((bf16[512,256]{1,0:T(8,128)(2,1)}, bf16[512,256]{1,0:T(8,128)(2,1)}, u32[]{:S(2)}, u32[]{:S(2)}) %collective-permute-start.7) | collective-permute-done | bytes 262176 | tf_op jit(solution)/shard_map/ppermute | solution.py:259
  46.0 3.1 %shard_map.57 = (f32[384,256]{1,0:T(8,128)S(1)}, f32[384,256]{1,0:T(8,128)}) custom-call(s32[2]{0:T(128)S(1)} %pad_add_fusion.starts, bf16[384,8192]{1,0:T(8,128)(2,1)} %bitcast.18, bf16[384,8192]{1,0:T(8,128)(2,1)} %collective-permute-done.far, bf16[512,256]{1,0:T(8,128)(2,1)S(1)} %collective-permute-done.5.refs_0_, ...), custom_call_target="tpu_custom_call" | custom-call | flops 402653184 | bytes 2097152 | tf_op jit(solution)/shard_map/pallas_call | solution.py:134
  49.1 2.7 %collective-permute-start.9 = (f32[384,256]{1,0:T(8,128)}, f32[384,256]{1,0:T(8,128)S(1)}, u32[]{:S(2)}, u32[]{:S(2)}) collective-permute-start(f32[384,256]{1,0:T(8,128)} %get-tuple-element.36), channel_id=1, source_target_pairs={{0,4},{4,0},{8,12},{12,8},{16,20},{20,16},{24,28},{28,24},{1,5},{5... | collective-permute-start | bytes 1179656 | tf_op jit(solution)/shard_map/ppermute | solution.py:259
  51.9 0.4 collective-permute-start.14
  52.5 1.1 %fusion.2 = (bf16[256,512]{1,0:T(8,128)(2,1)S(1)}, bf16[256,512]{1,0:T(8,128)(2,1)S(1)}) fusion(bf16[512,512]{1,0:T(8,128)(2,1)} %collective-permute-done.10), kind=kLoop, calls=%fused_computation.15 | loop fusion | bytes 1048576 | tf_op jit(solution)/shard_map/slice | solution.py:301
  53.7 1.3 %collective-permute-start.11 = (bf16[384,256]{1,0:T(8,128)(2,1)S(1)}, bf16[384,256]{1,0:T(8,128)(2,1)S(1)}, u32[]{:S(2)}, u32[]{:S(2)}) collective-permute-start(bf16[384,256]{1,0:T(8,128)(2,1)S(1)} %shard_map.58), channel_id=1, source_target_pairs={{0,2},{1,3},{4,6},{5,7},{8,10},{9,11},{12,14},{13,15},{16,18},{17,... | collective-permute-start | bytes 589832 | tf_op jit(solution)/shard_map/ppermute | solution.py:328
  55.0 2.1 %collective-permute-start.12 = (bf16[384,256]{1,0:T(8,128)(2,1)S(1)}, bf16[384,256]{1,0:T(8,128)(2,1)S(1)}, u32[]{:S(2)}, u32[]{:S(2)}) collective-permute-start(bf16[384,256]{1,0:T(8,128)(2,1)S(1)} %shard_map.58), channel_id=1, source_target_pairs={{0,1},{1,2},{2,3},{4,5},{5,6},{6,7},{8,9},{9,10},{10,11},{12,13},{... | collective-permute-start | bytes 589832 | tf_op jit(solution)/shard_map/ppermute | solution.py:328
  57.1 5.5 %shard_map.59.refs_2_ = f32[768,512]{1,0:T(8,128)S(1)} custom-call(s32[8]{0:T(128)S(1)} %stack.60.starts, bf16[384,8192]{1,0:T(8,128)(2,1)} %bitcast.19, bf16[384,8192]{1,0:T(8,128)(2,1)} %collective-permute-done.far, bf16[512,512]{1,0:T(8,128)(2,1)S(1)} %get-tuple-element.43.refs_0_, bf16[512,512]{1,0:T(8,128)(2,1)S(1)} %get-tuple-element.44.refs_1_, ...), custom_call_target="tpu_custom_call" | custom-call | flops 2415919104 | bytes 7864320 | tf_op jit(solution)/shard_map/pallas_call | solution.py:134
  62.6 7.1 %collective-permute-done.12 = bf16[384,256]{1,0:T(8,128)(2,1)S(1)} collective-permute-done((bf16[384,256]{1,0:T(8,128)(2,1)S(1)}, bf16[384,256]{1,0:T(8,128)(2,1)S(1)}, u32[]{:S(2)}, u32[]{:S(2)}) %collective-permute-start.12) | collective-permute-done | bytes 196640 | tf_op jit(solution)/shard_map/ppermute | solution.py:328
  69.8 3.3 %shard_map.60 = (f32[384,512]{1,0:T(8,128)S(1)}, f32[384,512]{1,0:T(8,128)}) custom-call(s32[2]{0:T(128)S(1)} %pad_add_fusion.starts, bf16[384,8192]{1,0:T(8,128)(2,1)} %bitcast.20, bf16[384,8192]{1,0:T(8,128)(2,1)} %collective-permute-done.far, bf16[512,512]{1,0:T(8,128)(2,1)S(1)} %collective-permute-done.8.refs_0_, ...), custom_call_target="tpu_custom_call" | custom-call | flops 805306368 | bytes 2621440 | tf_op jit(solution)/shard_map/pallas_call | solution.py:134
  73.1 1.5 %collective-permute-start.15 = (f32[384,512]{1,0:T(8,128)}, f32[384,512]{1,0:T(8,128)S(1)}, u32[]{:S(2)}, u32[]{:S(2)}) collective-permute-start(f32[384,512]{1,0:T(8,128)} %get-tuple-element.52), channel_id=1, source_target_pairs={{0,4},{4,0},{8,12},{12,8},{16,20},{20,16},{24,28},{28,24},{1,5},{5... | collective-permute-start | bytes 2359304 | tf_op jit(solution)/shard_map/ppermute | solution.py:259
  74.8 2.0 %collective-permute-done.15.far = f32[384,512]{1,0:T(8,128)S(1)} collective-permute-done((f32[384,512]{1,0:T(8,128)}, f32[384,512]{1,0:T(8,128)S(1)}, u32[]{:S(2)}, u32[]{:S(2)}) %collective-permute-start.15) | collective-permute-done | bytes 786464 | tf_op jit(solution)/shard_map/ppermute | solution.py:259
  76.8 3.6 %shard_map.61 = bf16[384,512]{1,0:T(8,128)(2,1)} custom-call(f32[384,512]{1,0:T(8,128)S(1)} %get-tuple-element.51.near, f32[384,512]{1,0:T(8,128)S(1)} %collective-permute-done.15.far, f32[384,128]{1,0:T(8,128)S(1)} %pad_maximum_fusion.2.cosine, f32[384,128]{1,0:T(8,128)S(1)} %pad_maximum_fusion.3.sine, s32[384,1]{1,0:T(8,128)S(1)} %copy.7.first, ...), custom_call_target="tpu_custom_call" | custom-call | flops 704643072 | bytes 1572864 | tf_op jit(solution)/shard_map/pallas_call | solution.py:229
  (34 shorter events, 1.7 us)
Async XLA Ops:
  0.0 7.8 %copy-start.3 = (s32[1,16]{1,0:T(1,128)S(1)}, s32[1,16]{1,0:T(1,128)}, u32[]{:S(2)}) copy-start(s32[1,16]{1,0:T(1,128)} %param.9) | copy-start | bytes 196
  0.0 29.9 %collective-permute-start = (bf16[384,8192]{1,0:T(8,128)(2,1)}, bf16[384,8192]{1,0:T(8,128)(2,1)}, u32[]{:S(2)}, u32[]{:S(2)}) collective-permute-start(bf16[384,8192]{1,0:T(8,128)(2,1)} %bitcast.16), channel_id=1, source_target_pairs={{0,4},{4,0},{8,12},{12,8},{16,20},{20,16},{24,28},{28,24},{1,5},{5... | collective-permute-start | bytes 18874376 | tf_op jit(solution)/shard_map/ppermute | solution.py:259
  0.7 1.2 %copy-start = (bf16[1024,512]{1,0:T(8,128)(2,1)S(1)}, bf16[1024,512]{1,0:T(8,128)(2,1)}, u32[]{:S(2)}) copy-start(bf16[1024,512]{1,0:T(8,128)(2,1)} %query.1) | copy-start | bytes 3145732
  1.9 0.9 %copy-start.1 = (bf16[1024,128]{1,0:T(8,128)(2,1)S(1)}, bf16[1024,128]{1,0:T(8,128)(2,1)}, u32[]{:S(2)}) copy-start(bf16[1024,128]{1,0:T(8,128)(2,1)} %key.1) | copy-start | bytes 786436
  2.9 0.9 %copy-start.2 = (bf16[1024,128]{1,0:T(8,128)(2,1)S(1)}, bf16[1024,128]{1,0:T(8,128)(2,1)}, u32[]{:S(2)}) copy-start(bf16[1024,128]{1,0:T(8,128)(2,1)} %value.1) | copy-start | bytes 786436
  4.8 23.7 %collective-permute-start.4 = (bf16[1024,256]{1,0:T(8,128)(2,1)}, bf16[1024,256]{1,0:T(8,128)(2,1)S(1)}, u32[]{:S(2)}, u32[]{:S(2)}) collective-permute-start(bf16[1024,256]{1,0:T(8,128)(2,1)} %get-tuple-element.33.refs_0_), channel_id=1, source_target_pairs={{0,8},{4,12},{8,0},{12,4},{16,24},{20,28},{24,16},{28,20},{1,9},{5... | collective-permute-start | bytes 1572872 | tf_op jit(solution)/shard_map/ppermute | solution.py:259
  6.1 22.8 %collective-permute-start.6 = (bf16[1024,256]{1,0:T(8,128)(2,1)}, bf16[1024,256]{1,0:T(8,128)(2,1)S(1)}, u32[]{:S(2)}, u32[]{:S(2)}) collective-permute-start(bf16[1024,256]{1,0:T(8,128)(2,1)} %get-tuple-element.33.refs_0_), channel_id=1, source_target_pairs={{0,16},{4,20},{8,24},{12,28},{16,0},{20,4},{24,8},{28,12},{1,17},{... | collective-permute-start | bytes 1572872 | tf_op jit(solution)/shard_map/ppermute | solution.py:259
  7.3 17.8 %collective-permute-start.1 = (bf16[256,512]{1,0:T(8,128)(2,1)}, bf16[256,512]{1,0:T(8,128)(2,1)S(1)}, u32[]{:S(2)}, u32[]{:S(2)}) collective-permute-start(bf16[256,512]{1,0:T(8,128)(2,1)} %get-tuple-element.30), channel_id=1, source_target_pairs={{0,16},{4,20},{8,24},{12,28},{16,0},{20,4},{24,8},{28,12},{1,17},{... | collective-permute-start | bytes 786440 | tf_op jit(solution)/shard_map/ppermute | solution.py:259
  7.6 17.6 %collective-permute-start.2 = (bf16[256,512]{1,0:T(8,128)(2,1)S(1)}, bf16[256,512]{1,0:T(8,128)(2,1)S(1)}, u32[]{:S(2)}, u32[]{:S(2)}) collective-permute-start(bf16[256,512]{1,0:T(8,128)(2,1)S(1)} %get-tuple-element.31), channel_id=1, source_target_pairs={{0,8},{4,12},{8,0},{12,4},{16,24},{20,28},{24,16},{28,20},{1,9},{5... | collective-permute-start | bytes 786440 | tf_op jit(solution)/shard_map/ppermute | solution.py:259
  25.2 26.7 %collective-permute-start.13 = (bf16[512,512]{1,0:T(8,128)(2,1)S(1)}, bf16[512,512]{1,0:T(8,128)(2,1)}, u32[]{:S(2)}, u32[]{:S(2)}) collective-permute-start(bf16[512,512]{1,0:T(8,128)(2,1)S(1)} %get-tuple-element.44.refs_1_), channel_id=1, source_target_pairs={{0,16},{4,20},{8,24},{12,28},{16,0},{20,4},{24,8},{28,12},{1,17},{... | collective-permute-start | bytes 1572872 | tf_op jit(solution)/shard_map/ppermute | solution.py:259
  27.2 25.3 %collective-permute-start.10 = (bf16[512,512]{1,0:T(8,128)(2,1)}, bf16[512,512]{1,0:T(8,128)(2,1)}, u32[]{:S(2)}, u32[]{:S(2)}) collective-permute-start(bf16[512,512]{1,0:T(8,128)(2,1)} %pad_maximum_fusion.1), channel_id=1, source_target_pairs={{0,1},{1,0},{2,3},{3,2},{4,5},{5,4},{6,7},{7,6},{8,9},{9,8},{10,11... | collective-permute-start | bytes 1572872 | tf_op jit(solution)/shard_map/ppermute | solution.py:299
  28.5 23.7 %collective-permute-start.3 = (bf16[512,512]{1,0:T(8,128)(2,1)S(1)}, bf16[512,512]{1,0:T(8,128)(2,1)}, u32[]{:S(2)}, u32[]{:S(2)}) collective-permute-start(bf16[512,512]{1,0:T(8,128)(2,1)S(1)} %get-tuple-element.43.refs_0_), channel_id=1, source_target_pairs={{0,8},{4,12},{8,0},{12,4},{16,24},{20,28},{24,16},{28,20},{1,9},{5... | collective-permute-start | bytes 1572872 | tf_op jit(solution)/shard_map/ppermute | solution.py:259
  28.9 14.3 %collective-permute-start.5 = (bf16[512,256]{1,0:T(8,128)(2,1)S(1)}, bf16[512,256]{1,0:T(8,128)(2,1)S(1)}, u32[]{:S(2)}, u32[]{:S(2)}) collective-permute-start(bf16[512,256]{1,0:T(8,128)(2,1)S(1)} %slice.16), channel_id=1, source_target_pairs={{0,16},{4,20},{8,24},{12,28},{16,0},{20,4},{24,8},{28,12},{1,17},{... | collective-permute-start | bytes 786440 | tf_op jit(solution)/shard_map/ppermute | solution.py:259
  29.9 16.1 %collective-permute-start.7 = (bf16[512,256]{1,0:T(8,128)(2,1)}, bf16[512,256]{1,0:T(8,128)(2,1)}, u32[]{:S(2)}, u32[]{:S(2)}) collective-permute-start(bf16[512,256]{1,0:T(8,128)(2,1)} %slice.17), channel_id=1, source_target_pairs={{0,8},{4,12},{8,0},{12,4},{16,24},{20,28},{24,16},{28,20},{1,9},{5... | collective-permute-start | bytes 786440 | tf_op jit(solution)/shard_map/ppermute | solution.py:259
  49.1 4.4 %collective-permute-start.9 = (f32[384,256]{1,0:T(8,128)}, f32[384,256]{1,0:T(8,128)S(1)}, u32[]{:S(2)}, u32[]{:S(2)}) collective-permute-start(f32[384,256]{1,0:T(8,128)} %get-tuple-element.36), channel_id=1, source_target_pairs={{0,4},{4,0},{8,12},{12,8},{16,20},{20,16},{24,28},{28,24},{1,5},{5... | collective-permute-start | bytes 1179656 | tf_op jit(solution)/shard_map/ppermute | solution.py:259
  51.9 17.9 %collective-permute-start.14 = (bf16[512,512]{1,0:T(8,128)(2,1)}, bf16[512,512]{1,0:T(8,128)(2,1)S(1)}, u32[]{:S(2)}, u32[]{:S(2)}) collective-permute-start(bf16[512,512]{1,0:T(8,128)(2,1)} %collective-permute-done.13.refs_7_), channel_id=1, source_target_pairs={{0,8},{4,12},{8,0},{12,4},{16,24},{20,28},{24,16},{28,20},{1,9},{5... | collective-permute-start | bytes 1572872 | tf_op jit(solution)/shard_map/ppermute | solution.py:259
  52.3 17.6 %collective-permute-start.8 = (bf16[512,512]{1,0:T(8,128)(2,1)}, bf16[512,512]{1,0:T(8,128)(2,1)S(1)}, u32[]{:S(2)}, u32[]{:S(2)}) collective-permute-start(bf16[512,512]{1,0:T(8,128)(2,1)} %collective-permute-done.3.refs_2_), channel_id=1, source_target_pairs={{0,16},{4,20},{8,24},{12,28},{16,0},{20,4},{24,8},{28,12},{1,17},{... | collective-permute-start | bytes 1572872 | tf_op jit(solution)/shard_map/ppermute | solution.py:259
  53.7 8.9 %collective-permute-start.11 = (bf16[384,256]{1,0:T(8,128)(2,1)S(1)}, bf16[384,256]{1,0:T(8,128)(2,1)S(1)}, u32[]{:S(2)}, u32[]{:S(2)}) collective-permute-start(bf16[384,256]{1,0:T(8,128)(2,1)S(1)} %shard_map.58), channel_id=1, source_target_pairs={{0,2},{1,3},{4,6},{5,7},{8,10},{9,11},{12,14},{13,15},{16,18},{17,... | collective-permute-start | bytes 589832 | tf_op jit(solution)/shard_map/ppermute | solution.py:328
  55.0 14.8 %collective-permute-start.12 = (bf16[384,256]{1,0:T(8,128)(2,1)S(1)}, bf16[384,256]{1,0:T(8,128)(2,1)S(1)}, u32[]{:S(2)}, u32[]{:S(2)}) collective-permute-start(bf16[384,256]{1,0:T(8,128)(2,1)S(1)} %shard_map.58), channel_id=1, source_target_pairs={{0,1},{1,2},{2,3},{4,5},{5,6},{6,7},{8,9},{9,10},{10,11},{12,13},{... | collective-permute-start | bytes 589832 | tf_op jit(solution)/shard_map/ppermute | solution.py:328
  73.1 3.6 %collective-permute-start.15 = (f32[384,512]{1,0:T(8,128)}, f32[384,512]{1,0:T(8,128)S(1)}, u32[]{:S(2)}, u32[]{:S(2)}) collective-permute-start(f32[384,512]{1,0:T(8,128)} %get-tuple-element.52), channel_id=1, source_target_pairs={{0,4},{4,0},{8,12},{12,8},{16,20},{20,16},{24,28},{28,24},{1,5},{5... | collective-permute-start | bytes 2359304 | tf_op jit(solution)/shard_map/ppermute | solution.py:259

commit v6 on v5

--- a/solution.py
+++ b/solution.py
@@ -36,51 +36,60 @@
     return [pl.BlockSpec(memory_space=pltpu.VMEM)] * count
 
 
-def anywhere(count):
-    return [pl.BlockSpec(memory_space=pl.ANY)] * count
+def in_hbm(count):
+    return [pl.BlockSpec(memory_space=pltpu.HBM)] * count
 
 
 def after(array, *earlier):
     return lax.optimization_barrier((array, *earlier))[0]
 
 
-def pack_kernel(begin, key, value, query, *refs):
-    pair, top, bottom = refs[:3]
-    parts, sems = refs[3:-1], refs[-1]
-    head_size = key.shape[1]
-    half = top.shape[0]
+def copy_all(copies, sems):
+    copies = [pltpu.make_async_copy(*copy, sems.at[i]) for i, copy in enumerate(copies)]
+    for copy in copies:
+        copy.start()
+    for copy in copies:
+        copy.wait()
+
+
+def halves_kernel(begin, query, *refs):
+    parts, sems = refs[:-1], refs[-1]
     copies = []
     for side, part in enumerate(parts):
-        rows = pl.ds(pl.multiple_of(side * half + begin[0], 16), part.shape[0])
-        copies.append((query.at[rows], part))
-    copies += [
+        row = side * query.shape[0] // 2 + begin[0]
+        copies.append((query.at[pl.ds(pl.multiple_of(row, 16), part.shape[0])], part))
+    copy_all(copies, sems)
+
+
+def pack_kernel(starts, key, value, query, tokens, pair, top, bottom, columns, sems):
+    head_size = key.shape[1]
+    half, depth = top.shape[0], query.shape[0]
+    copies = [
         (key, pair.at[:, :head_size]),
         (value, pair.at[:, head_size:]),
         (query.at[:half], top),
         (query.at[half:], bottom),
     ]
-    copies = [pltpu.make_async_copy(*copy, sems.at[i]) for i, copy in enumerate(copies)]
-    for copy in copies:
-        copy.start()
-    for copy in copies:
-        copy.wait()
-
-
-def pack(begin, key, value, query, halved):
-    depth, width = query.shape
-    shapes = [(depth, 2 * key.shape[1])] + [(depth // 2, width)] * 2
-    shapes += [(depth // 4, width)] * (2 if halved else 0)
+    for chip in range(columns.shape[1] // depth):
+        window = pl.ds(pl.multiple_of(starts[chip], 128), depth)
+        copies.append((tokens.at[:, window], columns.at[:, chip * depth : (chip + 1) * depth]))
+    copy_all(copies, sems)
+
+
+def copy_call(kernel, places, arrays, shapes, count):
     return pl.pallas_call(
-        pack_kernel,
-        out_shape=[jax.ShapeDtypeStruct(shape, query.dtype) for shape in shapes],
-        in_specs=[pl.BlockSpec(memory_space=pltpu.SMEM)] + anywhere(3),
-        out_specs=anywhere(len(shapes)),
-        scratch_shapes=[pltpu.SemaphoreType.DMA((6,))],
-        compiler_params=pltpu.CompilerParams(vmem_limit_bytes=48 * MIB),
+        kernel,
+        out_shape=[jax.ShapeDtypeStruct(shape, jnp.bfloat16) for shape in shapes],
+        in_specs=[pl.BlockSpec(memory_space=pltpu.SMEM)] + in_hbm(len(arrays)),
+        out_specs=in_hbm(len(shapes)),
+        scratch_shapes=[pltpu.SemaphoreType.DMA((count,))],
+        compiler_params=pltpu.CompilerParams(vmem_limit_bytes=63 * MIB),
         cost_estimate=pl.CostEstimate(
-            flops=0, bytes_accessed=8 * query.size, transcendentals=0
-        ),
-    )(begin, key, value, query)
+            flops=0,
+            bytes_accessed=4 * sum(math.prod(shape) for shape in shapes),
+            transcendentals=0,
+        ),
+    )(places, *arrays)
 
 
 def project_kernel(steps, carried, final, starts, near, far, *refs):
@@ -94,11 +103,11 @@
     for step, depth in enumerate(steps):
         here = slice(row, row + depth)
         row += depth
-        window = pl.ds(pl.multiple_of(starts[step], 128), depth)
         batches[0].append(
             pltpu.make_async_copy(weights[step], held.at[here], sems.at[step, 2])
         )
         for side, ref in enumerate((far, near)):
+            window = pl.ds(pl.multiple_of(starts[side, step], 128), depth)
             batches[1 + side].append(
                 pltpu.make_async_copy(
                     ref.at[:, window], tokens.at[side, :, here], sems.at[step, side]
@@ -124,10 +133,12 @@
 
 def project(terms, near, far, carry=None, final=False):
     rows = near.shape[0]
-    width = terms[0][1].shape[1]
-    steps = [array.shape[0] for _, array in terms]
+    width = terms[0][0].shape[1]
+    steps = [array.shape[0] for array, *_ in terms]
     depth = sum(steps)
-    starts = jnp.stack([start for start, _ in terms]).astype(jnp.int32)
+    starts = jnp.stack(
+        [jnp.stack([jnp.int32(term[1 + side]) for term in terms]) for side in range(2)]
+    )
     whole = jax.ShapeDtypeStruct((2 * rows, width), jnp.float32)
     part = jax.ShapeDtypeStruct((rows, width), jnp.float32)
     carries = [] if carry is None else [carry]
@@ -135,7 +146,7 @@
         functools.partial(project_kernel, steps, carry is not None, final),
         out_shape=(part, part) if final else whole,
         in_specs=[pl.BlockSpec(memory_space=pltpu.SMEM)]
-        + anywhere(2 + len(terms))
+        + in_hbm(2 + len(terms))
         + vmem(len(carries)),
         out_specs=tuple(vmem(2)) if final else vmem(1)[0],
         scratch_shapes=[
@@ -149,7 +160,7 @@
             bytes_accessed=2 * depth * (2 * rows + width),
             transcendentals=0,
         ),
-    )(starts, near, far, *[array for _, array in terms], *carries)
+    )(starts, near, far, *[array for array, *_ in terms], *carries)
 
 
 def turn(vectors, cosine, sine):
@@ -273,24 +284,27 @@
             held.append(pieces)
         return held
 
-    sibling_hidden = swap(hidden, 1)
-
     offset = place * row_count
     positions = offset + jnp.arange(row_count, dtype=jnp.int32)
     cosine, sine = rope_tables(positions, head_size)
     first = (doc_starts(doc_lengths[0], positions) - offset)[:, None]
 
     axes = [1 << axis for axis in range(bits)]
-
-    def begins(chip):
-        return (me ^ (2 * chip)) * depth
-
     half = depth // 2
+    some = half // 2
     halved = ctx_size % 2 == 0
-    some = half // 2
     begin = (place % 2) * some
-    packed = pack(begin[None], w_key, w_value, w_query, halved)
-    pair_here, halves, parts = packed[0], packed[1:3], packed[3:]
+    parts = []
+    if halved:
+        shapes = [(some, query_width)] * 2
+        parts = copy_call(halves_kernel, begin[None], [w_query], shapes, 2)
+    theirs = jnp.stack([(me ^ (2 * chip + 1)) * depth for chip in range(chips)])
+    shapes = [(depth, 2 * head_size)] + [(half, query_width)] * 2 + [(row_count, chips * depth)]
+    arrays = [after(w_key, *parts), w_value, w_query, hidden]
+    pair_here, *halves, sent = copy_call(pack_kernel, theirs, arrays, shapes, 4 + chips)
+
+    def term(array, chip, row):
+        return (array, chip * depth + row, (me ^ (2 * chip)) * depth + row)
 
     given = [{}, {}]
     mine = [swap(part, 2 << axis) for part, axis in zip(parts, (bits - 1, 0))]
@@ -302,6 +316,7 @@
             for side, axis in enumerate((bits - 1, 0))
         ]
     pairs = [pair_here] + [swap(pair_here, 2 << axis) for axis in range(bits)]
+    far_tokens = swap(sent, 1)
     sides = [slice(0, half), slice(half, depth)]
     pair_held = fetch(
         [pair_here[rows] for rows in sides],
@@ -309,30 +324,29 @@
         [],
         [],
     )
-    pair_terms = [(begins(chip), array) for chip, array in zip([0] + axes, pairs)]
-    carry = project(pair_terms, hidden, sibling_hidden)
+    pair_terms = [term(array, chip, 0) for chip, array in zip([0] + axes, pairs)]
+    carry = project(pair_terms, hidden, far_tokens)
     pair_terms = [
-        (begins(chip) + side * half, pair_held[side][chip][0][1])
+        term(pair_held[side][chip][0][1], chip, side * half)
         for chip in range(chips)
         if chip not in [0] + axes
         for side in range(2)
     ]
-    near, far = project(pair_terms, hidden, sibling_hidden, carry, True)
-    query_held = fetch(halves, given, [*mine, cosine, sine, first], [near])
+    near, far = project(pair_terms, hidden, far_tokens, carry, True)
+    query_held = fetch(halves, given, [*pairs, cosine, sine, first], [near])
 
     pair = finish_pair(near, swap(far, 1), cosine, sine)
     longest = ctx_size * row_count // 2
     back = -(-(longest - 1) // ROW_TILE) * ROW_TILE
     hops = min(ctx_size - 1, -(-back // row_count))
-    blocks = [
-        lax.ppermute(after(pair, both) if halved else pair, "ctx", [(i, i + hop) for i in range(ctx_size - hop)])
-        for hop in range(hops, 0, -1)
-    ]
-    keys_values = jnp.concatenate(blocks + [pair], axis=0)
+    blocks = [after(pair, both) if halved else pair]
+    for _ in range(hops):
+        blocks.insert(0, lax.ppermute(blocks[0], "ctx", [(i, i + 1) for i in range(ctx_size - 1)]))
+    keys_values = jnp.concatenate(blocks, axis=0)
 
     def query_terms(wanted, *gate):
         return [
-            (begins(chip) + side * half + row, after(array, *gate))
+            term(after(array, *gate), chip, side * half + row)
             for side, chip in wanted
             for row, array in query_held[side][chip]
         ]
@@ -340,8 +354,8 @@
     everything = [(side, chip) for chip in range(chips) for side in range(2)]
     early = [(side, chip) for side, chip in everything if chip in [0] + axes]
     late = [wanted for wanted in everything if wanted not in early]
-    carry = project(query_terms(early, pair), hidden, sibling_hidden)
-    near, far = project(query_terms(late, keys_values), hidden, sibling_hidden, carry, True)
+    carry = project(query_terms(early, pair), hidden, far_tokens)
+    near, far = project(query_terms(late, keys_values), hidden, far_tokens, carry, True)
     return attend(near, swap(far, 1), cosine, sine, first, keys_values, back)[None]
 
 

time: 80.8 us -> 237 us (2.93)
  Pallas kernels: 21.9 us -> 183 us
  waiting for transfers between devices: 33.2 us -> 25.4 us
  starting transfers between devices: 16.1 us -> 19.1 us
    pallas_call x1 -> x2, Pallas kernels: 1 us -> 162 us  [copy_call(): pl.pallas_call(kernel, out_shape=[jax.ShapeDtypeStruct(shape, jnp.bfloat1...]
    ppermute x2, waiting for transfers between devices: 7.13 us -> 0.01 us  [shards(): lax.ppermute(blocks[0], 'ctx', [(i, i + 1) for i in range(ctx_size - 1)])]
  transfers between devices with their start and end apart: 16 -> 16, of which waited for: 5 -> 7; matrix products, arithmetic and copies ran while one was open for 7% -> 3% of each run, Pallas kernels for 19% -> 6%
where the time goes in v6:
time: 237 us; the launch traced here: 236 us
  Pallas kernels  183 us (77%)
  waiting for transfers between devices  25.4 us (11%)
  starting transfers between devices  19.1 us (8%)
  local copies, waits for them, and re-layouts  4.36 us (2%)
  other arithmetic  4.02 us (2%)
    pallas_call x2, Pallas kernels, copy_call(): pl.pallas_call(kernel, out_shape=[jax.ShapeDtypeStruct(shape, jnp.bfloat1...  162 us
    ppermute x13, waiting for transfers between devices, swap(): return lax.ppermute(array, 'dp', [(i, i ^ mask) for i in range(dp_size)])  25.4 us
    pallas_call x4, Pallas kernels, project(): pl.pallas_call(functools.partial(project_kernel, steps, carry is not None...  16.6 us
    ppermute x13, starting transfers between devices, swap(): return lax.ppermute(array, 'dp', [(i, i ^ mask) for i in range(dp_size)])  13.7 us
  transfers between devices with their start and end apart: 16, of which 7 were waited for; matrix products, arithmetic and copies ran while one was open for 3% of the time, Pallas kernels for 6%

profile of v6, /device:TPU:17, one launch (start us, length us, event | category | flops | bytes accessed | tf_op | source)
XLA Modules:
  0.0 235.7 jit_solution(5880009193585057713)
XLA Ops:
  0.0 17.0 %shard_map.55 = (bf16[256,512]{1,0:T(8,128)(2,1)}, bf16[256,512]{1,0:T(8,128)(2,1)}) custom-call(s32[1]{0:T(128)} %bitcast.8.begin, bf16[1024,512]{1,0:T(8,128)(2,1)} %query.3), custom_call_target="tpu_custom_call" | custom-call | bytes 1048576 | tf_op jit(solution)/shard_map/pallas_call | solution.py:80
  17.7 144.9 %shard_map.56 = (bf16[1024,256]{1,0:T(8,128)(2,1)}, bf16[512,512]{1,0:T(8,128)(2,1)}, bf16[512,512]{1,0:T(8,128)(2,1)}, bf16[384,4096]{1,0:T(8,128)(2,1)}) custom-call(s32[4]{0:T(128)} %pad_add_fusion.3.starts, bf16[1024,128]{1,0:T(8,128)(2,1)} %key, bf16[1024,128]{1,0:T(8,128)(2,1)} %value.1, bf16[1024,512]{1,0:T(8,128)(2,1)} %query.3, ...), custom_call_target="tpu_custom_call" | custom-call | bytes 9437184 | tf_op jit(solution)/shard_map/pallas_call | solution.py:80
  162.6 0.7 collective-permute-start
  163.3 1.2 collective-permute-start.1
  164.6 1.2 collective-permute-start.2
  166.7 0.8 fusion
  167.7 9.5 %collective-permute-done.1.refs_1_ = bf16[1024,256]{1,0:T(8,128)(2,1)} collective-permute-done((bf16[1024,256]{1,0:T(8,128)(2,1)}, bf16[1024,256]{1,0:T(8,128)(2,1)}, u32[]{:S(2)}, u32[]{:S(2)}) %collective-permute-start.1) | collective-permute-done | bytes 524320 | tf_op jit(solution)/shard_map/ppermute | solution.py:270
  177.2 1.0 slice.16
  178.1 1.3 collective-permute-start.4
  179.4 1.0 slice.17
  180.4 1.3 collective-permute-start.5
  181.7 1.1 collective-permute-done.9.refs_3_
  182.8 0.9 collective-permute-done.8.refs_5_
  183.7 1.9 pad_maximum_fusion
  185.5 1.3 collective-permute-start.10
  186.8 5.1 %shard_map.57.refs_2_ = f32[768,256]{1,0:T(8,128)S(1)} custom-call(s32[2,3]{1,0:T(2,128)S(1)} %pad_add_fusion.1.starts, bf16[384,8192]{1,0:T(8,128)(2,1)} %bitcast.31, bf16[384,4096]{1,0:T(8,128)(2,1)S(1)} %collective-permute-done.far, bf16[1024,256]{1,0:T(8,128)(2,1)S(1)} %copy-done.1, bf16[1024,256]{1,0:T(8,128)(2,1)} %collective-permute-done.1.refs_1_, ...), custom_call_target="tpu_custom_call" | custom-call | flops 1207959552 | bytes 6291456 | tf_op jit(solution)/shard_map/pallas_call | solution.py:145
  192.0 2.6 %shard_map.58 = (f32[384,256]{1,0:T(8,128)S(1)}, f32[384,256]{1,0:T(8,128)}) custom-call(s32[2,2]{1,0:T(2,128)S(1)} %pad_add_fusion.starts, bf16[384,8192]{1,0:T(8,128)(2,1)} %bitcast.32, bf16[384,4096]{1,0:T(8,128)(2,1)S(1)} %collective-permute-done.far, bf16[512,256]{1,0:T(8,128)(2,1)S(1)} %collective-permute-done.4.refs_0_, ...), custom_call_target="tpu_custom_call" | custom-call | flops 402653184 | bytes 2097152 | tf_op jit(solution)/shard_map/pallas_call | solution.py:145
  194.6 2.3 collective-permute-start.7
  197.3 1.2 collective-permute-start.13
  198.8 1.0 copy-done.3
  199.9 2.1 collective-permute-start.11
  202.0 1.1 fusion.2
  203.1 7.8 %collective-permute-done.3.refs_2_ = bf16[512,512]{1,0:T(8,128)(2,1)S(1)} collective-permute-done((bf16[512,512]{1,0:T(8,128)(2,1)}, bf16[512,512]{1,0:T(8,128)(2,1)S(1)}, u32[]{:S(2)}, u32[]{:S(2)}) %collective-permute-start.3) | collective-permute-done | bytes 524320 | tf_op jit(solution)/shard_map/ppermute | solution.py:270
  210.8 1.2 collective-permute-start.6
  212.3 2.1 collective-permute-start.12
  214.4 5.7 %shard_map.60.refs_2_ = f32[768,512]{1,0:T(8,128)S(1)} custom-call(s32[2,8]{1,0:T(2,128)S(1)} %pad_add_fusion.2.starts, bf16[384,8192]{1,0:T(8,128)(2,1)} %bitcast.33, bf16[384,4096]{1,0:T(8,128)(2,1)} %copy-done, bf16[512,512]{1,0:T(8,128)(2,1)} %get-tuple-element.47.refs_0_, bf16[512,512]{1,0:T(8,128)(2,1)} %get-tuple-element.48.refs_1_, ...), custom_call_target="tpu_custom_call" | custom-call | flops 2415919104 | bytes 7864320 | tf_op jit(solution)/shard_map/pallas_call | solution.py:145
  220.1 3.3 %collective-permute-done.6.refs_0_ = bf16[512,512]{1,0:T(8,128)(2,1)S(1)} collective-permute-done((bf16[512,512]{1,0:T(8,128)(2,1)S(1)}, bf16[512,512]{1,0:T(8,128)(2,1)S(1)}, u32[]{:S(2)}, u32[]{:S(2)}) %collective-permute-start.6) | collective-permute-done | bytes 524320 | tf_op jit(solution)/shard_map/ppermute | solution.py:270
  223.5 0.9 collective-permute-done.14.refs_1_
  224.4 3.3 %shard_map.61 = (f32[384,512]{1,0:T(8,128)S(1)}, f32[384,512]{1,0:T(8,128)}) custom-call(s32[2,2]{1,0:T(2,128)S(1)} %pad_add_fusion.starts, bf16[384,8192]{1,0:T(8,128)(2,1)} %bitcast.34, bf16[384,4096]{1,0:T(8,128)(2,1)} %copy-done, bf16[512,512]{1,0:T(8,128)(2,1)S(1)} %collective-permute-done.6.refs_0_, ...), custom_call_target="tpu_custom_call" | custom-call | flops 805306368 | bytes 2621440 | tf_op jit(solution)/shard_map/pallas_call | solution.py:145
  227.7 2.1 collective-permute-start.15
  229.9 2.0 collective-permute-done.15.far
  231.9 3.9 %shard_map.62 = bf16[384,512]{1,0:T(8,128)(2,1)} custom-call(f32[384,512]{1,0:T(8,128)S(1)} %get-tuple-element.55.near, f32[384,512]{1,0:T(8,128)S(1)} %collective-permute-done.15.far, f32[384,128]{1,0:T(8,128)S(1)} %pad_maximum_fusion.1.cosine, f32[384,128]{1,0:T(8,128)S(1)} %pad_maximum_fusion.2.sine, s32[384,1]{1,0:T(8,128)S(1)} %copy.7.first, ...), custom_call_target="tpu_custom_call" | custom-call | flops 704643072 | bytes 1572864 | tf_op jit(solution)/shard_map/pallas_call | solution.py:240
  (48 shorter events, 3.0 us)
Async XLA Ops:
  17.7 148.6 %copy-start.6 = (s32[1,16]{1,0:T(1,128)S(1)}, s32[1,16]{1,0:T(1,128)}, u32[]{:S(2)}) copy-start(s32[1,16]{1,0:T(1,128)} %param.9) | copy-start | bytes 196
  17.7 148.9 %copy-start.5 = (s32[1,2]{1,0:T(1,128)S(1)}, s32[1,2]{1,0:T(1,128)}, u32[]{:S(2)}) copy-start(s32[1,2]{1,0:T(1,128)} %constant.16.clone.1) | copy-start | bytes 28
  17.7 164.0 %copy-start.4 = (s32[1,3]{1,0:T(1,128)S(1)}, s32[1,3]{1,0:T(1,128)}, u32[]{:S(2)}) copy-start(s32[1,3]{1,0:T(1,128)} %constant.62.clone.1) | copy-start | bytes 40
  162.6 24.2 %collective-permute-start = (bf16[384,4096]{1,0:T(8,128)(2,1)}, bf16[384,4096]{1,0:T(8,128)(2,1)S(1)}, u32[]{:S(2)}, u32[]{:S(2)}) collective-permute-start(bf16[384,4096]{1,0:T(8,128)(2,1)} %get-tuple-element.34), channel_id=1, source_target_pairs={{0,4},{4,0},{8,12},{12,8},{16,20},{20,16},{24,28},{28,24},{1,5},{5... | collective-permute-start | bytes 9437192 | tf_op jit(solution)/shard_map/ppermute | solution.py:270
  163.3 13.8 %collective-permute-start.1 = (bf16[1024,256]{1,0:T(8,128)(2,1)}, bf16[1024,256]{1,0:T(8,128)(2,1)}, u32[]{:S(2)}, u32[]{:S(2)}) collective-permute-start(bf16[1024,256]{1,0:T(8,128)(2,1)} %get-tuple-element.36.refs_0_), channel_id=1, source_target_pairs={{0,8},{4,12},{8,0},{12,4},{16,24},{20,28},{24,16},{28,20},{1,9},{5... | collective-permute-start | bytes 1572872 | tf_op jit(solution)/shard_map/ppermute | solution.py:270
  164.6 14.9 %collective-permute-start.2 = (bf16[1024,256]{1,0:T(8,128)(2,1)}, bf16[1024,256]{1,0:T(8,128)(2,1)}, u32[]{:S(2)}, u32[]{:S(2)}) collective-permute-start(bf16[1024,256]{1,0:T(8,128)(2,1)} %get-tuple-element.36.refs_0_), channel_id=1, source_target_pairs={{0,16},{4,20},{8,24},{12,28},{16,0},{20,4},{24,8},{28,12},{1,17},{... | collective-permute-start | bytes 1572872 | tf_op jit(solution)/shard_map/ppermute | solution.py:270
  165.8 17.0 %collective-permute-start.9 = (bf16[256,512]{1,0:T(8,128)(2,1)}, bf16[256,512]{1,0:T(8,128)(2,1)}, u32[]{:S(2)}, u32[]{:S(2)}) collective-permute-start(bf16[256,512]{1,0:T(8,128)(2,1)} %get-tuple-element.32), channel_id=1, source_target_pairs={{0,8},{4,12},{8,0},{12,4},{16,24},{20,28},{24,16},{28,20},{1,9},{5... | collective-permute-start | bytes 786440 | tf_op jit(solution)/shard_map/ppermute | solution.py:270
  166.1 17.6 %collective-permute-start.8 = (bf16[256,512]{1,0:T(8,128)(2,1)}, bf16[256,512]{1,0:T(8,128)(2,1)}, u32[]{:S(2)}, u32[]{:S(2)}) collective-permute-start(bf16[256,512]{1,0:T(8,128)(2,1)} %get-tuple-element.31), channel_id=1, source_target_pairs={{0,16},{4,20},{8,24},{12,28},{16,0},{20,4},{24,8},{28,12},{1,17},{... | collective-permute-start | bytes 786440 | tf_op jit(solution)/shard_map/ppermute | solution.py:270
  166.7 20.1 %copy-start.1 = (bf16[1024,256]{1,0:T(8,128)(2,1)S(1)}, bf16[1024,256]{1,0:T(8,128)(2,1)}, u32[]{:S(2)}) copy-start(bf16[1024,256]{1,0:T(8,128)(2,1)} %get-tuple-element.36.refs_0_) | copy-start | bytes 1572868
  178.1 13.8 %collective-permute-start.4 = (bf16[512,256]{1,0:T(8,128)(2,1)S(1)}, bf16[512,256]{1,0:T(8,128)(2,1)S(1)}, u32[]{:S(2)}, u32[]{:S(2)}) collective-permute-start(bf16[512,256]{1,0:T(8,128)(2,1)S(1)} %slice.16), channel_id=1, source_target_pairs={{0,16},{4,20},{8,24},{12,28},{16,0},{20,4},{24,8},{28,12},{1,17},{... | collective-permute-start | bytes 786440 | tf_op jit(solution)/shard_map/ppermute | solution.py:270
  180.4 11.6 %collective-permute-start.5 = (bf16[512,256]{1,0:T(8,128)(2,1)S(1)}, bf16[512,256]{1,0:T(8,128)(2,1)S(1)}, u32[]{:S(2)}, u32[]{:S(2)}) collective-permute-start(bf16[512,256]{1,0:T(8,128)(2,1)S(1)} %slice.17), channel_id=1, source_target_pairs={{0,8},{4,12},{8,0},{12,4},{16,24},{20,28},{24,16},{28,20},{1,9},{5... | collective-permute-start | bytes 786440 | tf_op jit(solution)/shard_map/ppermute | solution.py:270
  185.5 14.4 %collective-permute-start.10 = (bf16[512,512]{1,0:T(8,128)(2,1)}, bf16[512,512]{1,0:T(8,128)(2,1)}, u32[]{:S(2)}, u32[]{:S(2)}) collective-permute-start(bf16[512,512]{1,0:T(8,128)(2,1)} %pad_maximum_fusion), channel_id=1, source_target_pairs={{0,1},{1,0},{2,3},{3,2},{4,5},{5,4},{6,7},{7,6},{8,9},{9,8},{10,11... | collective-permute-start | bytes 1572872 | tf_op jit(solution)/shard_map/ppermute | solution.py:313
  186.8 5.1 %copy-start = (bf16[384,4096]{1,0:T(8,128)(2,1)}, bf16[384,4096]{1,0:T(8,128)(2,1)S(1)}, u32[]{:S(2)}) copy-start(bf16[384,4096]{1,0:T(8,128)(2,1)S(1)} %collective-permute-done.far) | copy-start | bytes 9437188
  194.6 2.7 %copy-start.2 = (f32[384,256]{1,0:T(8,128)}, f32[384,256]{1,0:T(8,128)S(1)}, u32[]{:S(2)}) copy-start(f32[384,256]{1,0:T(8,128)S(1)} %get-tuple-element.38.near) | copy-start | bytes 1179652
  194.6 4.2 %collective-permute-start.7 = (f32[384,256]{1,0:T(8,128)}, f32[384,256]{1,0:T(8,128)S(1)}, u32[]{:S(2)}, u32[]{:S(2)}) collective-permute-start(f32[384,256]{1,0:T(8,128)} %get-tuple-element.40), channel_id=1, source_target_pairs={{0,4},{4,0},{8,12},{12,8},{16,20},{20,16},{24,28},{28,24},{1,5},{5... | collective-permute-start | bytes 1179656 | tf_op jit(solution)/shard_map/ppermute | solution.py:270
  197.0 13.8 %collective-permute-start.3 = (bf16[512,512]{1,0:T(8,128)(2,1)}, bf16[512,512]{1,0:T(8,128)(2,1)S(1)}, u32[]{:S(2)}, u32[]{:S(2)}) collective-permute-start(bf16[512,512]{1,0:T(8,128)(2,1)} %get-tuple-element.47.refs_0_), channel_id=1, source_target_pairs={{0,8},{4,12},{8,0},{12,4},{16,24},{20,28},{24,16},{28,20},{1,9},{5... | collective-permute-start | bytes 1572872 | tf_op jit(solution)/shard_map/ppermute | solution.py:270
  197.3 14.7 %collective-permute-start.13 = (bf16[512,512]{1,0:T(8,128)(2,1)}, bf16[512,512]{1,0:T(8,128)(2,1)S(1)}, u32[]{:S(2)}, u32[]{:S(2)}) collective-permute-start(bf16[512,512]{1,0:T(8,128)(2,1)} %get-tuple-element.48.refs_1_), channel_id=1, source_target_pairs={{0,16},{4,20},{8,24},{12,28},{16,0},{20,4},{24,8},{28,12},{1,17},{... | collective-permute-start | bytes 1572872 | tf_op jit(solution)/shard_map/ppermute | solution.py:270
  198.8 1.0 copy-start.3
  199.9 12.4 %collective-permute-start.11 = (bf16[384,256]{1,0:T(8,128)(2,1)S(1)}, bf16[384,256]{1,0:T(8,128)(2,1)S(1)}, u32[]{:S(2)}, u32[]{:S(2)}) collective-permute-start(bf16[384,256]{1,0:T(8,128)(2,1)S(1)} %shard_map.59), channel_id=1, source_target_pairs={{0,1},{1,2},{2,3},{4,5},{5,6},{6,7},{8,9},{9,10},{10,11},{12,13},{... | collective-permute-start | bytes 589832 | tf_op jit(solution)/shard_map/ppermute | solution.py:344
  210.8 12.7 %collective-permute-start.6 = (bf16[512,512]{1,0:T(8,128)(2,1)S(1)}, bf16[512,512]{1,0:T(8,128)(2,1)S(1)}, u32[]{:S(2)}, u32[]{:S(2)}) collective-permute-start(bf16[512,512]{1,0:T(8,128)(2,1)S(1)} %collective-permute-done.3.refs_2_), channel_id=1, source_target_pairs={{0,16},{4,20},{8,24},{12,28},{16,0},{20,4},{24,8},{28,12},{1,17},{... | collective-permute-start | bytes 1572872 | tf_op jit(solution)/shard_map/ppermute | solution.py:270
  212.1 12.3 %collective-permute-start.14 = (bf16[512,512]{1,0:T(8,128)(2,1)S(1)}, bf16[512,512]{1,0:T(8,128)(2,1)S(1)}, u32[]{:S(2)}, u32[]{:S(2)}) collective-permute-start(bf16[512,512]{1,0:T(8,128)(2,1)S(1)} %collective-permute-done.13.refs_7_), channel_id=1, source_target_pairs={{0,8},{4,12},{8,0},{12,4},{16,24},{20,28},{24,16},{28,20},{1,9},{5... | collective-permute-start | bytes 1572872 | tf_op jit(solution)/shard_map/ppermute | solution.py:270
  212.3 7.7 %collective-permute-start.12 = (bf16[384,256]{1,0:T(8,128)(2,1)S(1)}, bf16[384,256]{1,0:T(8,128)(2,1)S(1)}, u32[]{:S(2)}, u32[]{:S(2)}) collective-permute-start(bf16[384,256]{1,0:T(8,128)(2,1)S(1)} %collective-permute-done.11), channel_id=1, source_target_pairs={{0,1},{1,2},{2,3},{4,5},{5,6},{6,7},{8,9},{9,10},{10,11},{12,13},{... | collective-permute-start | bytes 589832 | tf_op jit(solution)/shard_map/ppermute | solution.py:344
  227.7 4.2 %collective-permute-start.15 = (f32[384,512]{1,0:T(8,128)}, f32[384,512]{1,0:T(8,128)S(1)}, u32[]{:S(2)}, u32[]{:S(2)}) collective-permute-start(f32[384,512]{1,0:T(8,128)} %get-tuple-element.56), channel_id=1, source_target_pairs={{0,4},{4,0},{8,12},{12,8},{16,20},{20,16},{24,28},{28,24},{1,5},{5... | collective-permute-start | bytes 2359304 | tf_op jit(solution)/shard_map/ppermute | solution.py:270

commit v7 on v6

--- a/solution.py
+++ b/solution.py
@@ -44,45 +44,49 @@
     return lax.optimization_barrier((array, *earlier))[0]
 
 
-def copy_all(copies, sems):
-    copies = [pltpu.make_async_copy(*copy, sems.at[i]) for i, copy in enumerate(copies)]
-    for copy in copies:
-        copy.start()
-    for copy in copies:
-        copy.wait()
-
-
-def halves_kernel(begin, query, *refs):
-    parts, sems = refs[:-1], refs[-1]
-    copies = []
+def copy_all(copies, buffers, sems):
+    loads = []
+    stores = []
+    for i, ((source, target), buffer) in enumerate(zip(copies, buffers)):
+        loads.append(pltpu.make_async_copy(source, buffer, sems.at[0, i]))
+        stores.append(pltpu.make_async_copy(buffer, target, sems.at[1, i]))
+    for load in loads:
+        load.start()
+    for load, store in zip(loads, stores):
+        load.wait()
+        store.start()
+    for store in stores:
+        store.wait()
+
+
+def first_kernel(begin, key, value, query, pair, *refs):
+    parts, buffers, sems = refs[: (len(refs) - 3) // 2], refs[(len(refs) - 3) // 2 : -1], refs[-1]
+    head_size = key.shape[1]
+    copies = [(key, pair.at[:, :head_size]), (value, pair.at[:, head_size:])]
     for side, part in enumerate(parts):
-        row = side * query.shape[0] // 2 + begin[0]
+        row = side * (query.shape[0] // 2) + begin[0]
         copies.append((query.at[pl.ds(pl.multiple_of(row, 16), part.shape[0])], part))
-    copy_all(copies, sems)
-
-
-def pack_kernel(starts, key, value, query, tokens, pair, top, bottom, columns, sems):
-    head_size = key.shape[1]
+    copy_all(copies, buffers, sems)
+
+
+def second_kernel(starts, query, tokens, top, bottom, columns, *refs):
+    buffers, sems = refs[:-1], refs[-1]
     half, depth = top.shape[0], query.shape[0]
-    copies = [
-        (key, pair.at[:, :head_size]),
-        (value, pair.at[:, head_size:]),
-        (query.at[:half], top),
-        (query.at[half:], bottom),
-    ]
+    copies = [(query.at[:half], top), (query.at[half:], bottom)]
     for chip in range(columns.shape[1] // depth):
         window = pl.ds(pl.multiple_of(starts[chip], 128), depth)
         copies.append((tokens.at[:, window], columns.at[:, chip * depth : (chip + 1) * depth]))
-    copy_all(copies, sems)
-
-
-def copy_call(kernel, places, arrays, shapes, count):
+    copy_all(copies, buffers, sems)
+
+
+def copy_call(kernel, places, arrays, shapes, buffers):
     return pl.pallas_call(
         kernel,
         out_shape=[jax.ShapeDtypeStruct(shape, jnp.bfloat16) for shape in shapes],
         in_specs=[pl.BlockSpec(memory_space=pltpu.SMEM)] + in_hbm(len(arrays)),
         out_specs=in_hbm(len(shapes)),
-        scratch_shapes=[pltpu.SemaphoreType.DMA((count,))],
+        scratch_shapes=[pltpu.VMEM(shape, jnp.bfloat16) for shape in buffers]
+        + [pltpu.SemaphoreType.DMA((2, len(buffers)))],
         compiler_params=pltpu.CompilerParams(vmem_limit_bytes=63 * MIB),
         cost_estimate=pl.CostEstimate(
             flops=0,
@@ -294,14 +298,23 @@
     some = half // 2
     halved = ctx_size % 2 == 0
     begin = (place % 2) * some
-    parts = []
-    if halved:
-        shapes = [(some, query_width)] * 2
-        parts = copy_call(halves_kernel, begin[None], [w_query], shapes, 2)
+    part_shapes = [(some, query_width)] * (2 if halved else 0)
+    pair_here, *parts = copy_call(
+        first_kernel,
+        begin[None],
+        [w_key, w_value, w_query],
+        [(depth, 2 * head_size)] + part_shapes,
+        [(depth, head_size)] * 2 + part_shapes,
+    )
     theirs = jnp.stack([(me ^ (2 * chip + 1)) * depth for chip in range(chips)])
-    shapes = [(depth, 2 * head_size)] + [(half, query_width)] * 2 + [(row_count, chips * depth)]
-    arrays = [after(w_key, *parts), w_value, w_query, hidden]
-    pair_here, *halves, sent = copy_call(pack_kernel, theirs, arrays, shapes, 4 + chips)
+    half_shapes = [(half, query_width)] * 2
+    *halves, sent = copy_call(
+        second_kernel,
+        theirs,
+        [after(w_query, pair_here), hidden],
+        half_shapes + [(row_count, chips * depth)],
+        half_shapes + [(row_count, depth)] * chips,
+    )
 
     def term(array, chip, row):
         return (array, chip * depth + row, (me ^ (2 * chip)) * depth + row)
@@ -324,15 +337,13 @@
         [],
         [],
     )
-    pair_terms = [term(array, chip, 0) for chip, array in zip([0] + axes, pairs)]
-    carry = project(pair_terms, hidden, far_tokens)
-    pair_terms = [
+    pair_terms = [term(array, chip, 0) for chip, array in zip([0] + axes, pairs)] + [
         term(pair_held[side][chip][0][1], chip, side * half)
         for chip in range(chips)
         if chip not in [0] + axes
         for side in range(2)
     ]
-    near, far = project(pair_terms, hidden, far_tokens, carry, True)
+    near, far = project(pair_terms, hidden, far_tokens, None, True)
     query_held = fetch(halves, given, [*pairs, cosine, sine, first], [near])
 
     pair = finish_pair(near, swap(far, 1), cosine, sine)
@@ -355,7 +366,7 @@
     early = [(side, chip) for side, chip in everything if chip in [0] + axes]
     late = [wanted for wanted in everything if wanted not in early]
     carry = project(query_terms(early, pair), hidden, far_tokens)
-    near, far = project(query_terms(late, keys_values), hidden, far_tokens, carry, True)
+    near, far = project(query_terms(late, blocks[-2]), hidden, far_tokens, carry, True)
     return attend(near, swap(far, 1), cosine, sine, first, keys_values, back)[None]
 
 

time: 237 us -> 79.9 us (0.34)
  Pallas kernels: 183 us -> 25.5 us
  waiting for transfers between devices: 25.4 us -> 19.2 us
  other arithmetic: 4.02 us -> 6.65 us
    pallas_call x2, Pallas kernels: 162 us -> 6.52 us  [copy_call(): pl.pallas_call(kernel, out_shape=[jax.ShapeDtypeStruct(shape, jnp.bfloat1...]
    ppermute x13, waiting for transfers between devices: 25.4 us -> 14 us  [swap(): return lax.ppermute(array, 'dp', [(i, i ^ mask) for i in range(dp_size)])]
    ppermute x2, waiting for transfers between devices: 0.01 us -> 5.26 us  [shards(): lax.ppermute(blocks[0], 'ctx', [(i, i + 1) for i in range(ctx_size - 1)])]
    pallas_call x4 -> x3, Pallas kernels: 16.6 us -> 15.1 us  [project(): pl.pallas_call(functools.partial(project_kernel, steps, carry is not None...]
  transfers between devices with their start and end apart: 16 -> 16, of which waited for: 7 -> 5; matrix products, arithmetic and copies ran while one was open for 3% -> 14% of each run, Pallas kernels for 6% -> 15%
where the time goes in v7:
time: 79.9 us; the launch traced here: 78.7 us
  Pallas kernels  25.5 us (32%)
  starting transfers between devices  21.1 us (26%)
  waiting for transfers between devices  19.2 us (24%)
  other arithmetic  6.65 us (8%)
  local copies, waits for them, and re-layouts  5.94 us (7%)
    pallas_call x3, Pallas kernels, project(): pl.pallas_call(functools.partial(project_kernel, steps, carry is not None...  15.1 us
    ppermute x13, waiting for transfers between devices, swap(): return lax.ppermute(array, 'dp', [(i, i ^ mask) for i in range(dp_size)])  14 us
    ppermute x13, starting transfers between devices, swap(): return lax.ppermute(array, 'dp', [(i, i ^ mask) for i in range(dp_size)])  13.4 us
    pallas_call x2, Pallas kernels, copy_call(): pl.pallas_call(kernel, out_shape=[jax.ShapeDtypeStruct(shape, jnp.bfloat1...  6.52 us
    ppermute x2, starting transfers between devices, shards(): lax.ppermute(blocks[0], 'ctx', [(i, i + 1) for i in range(ctx_size - 1)])  6.4 us
    ppermute x2, waiting for transfers between devices, shards(): lax.ppermute(blocks[0], 'ctx', [(i, i + 1) for i in range(ctx_size - 1)])  5.26 us
    pallas_call x1, Pallas kernels, attend(): pl.pallas_call(functools.partial(attend_kernel, back), out_shape=jax.Shap...  3.78 us
    slice x2, local copies, waits for them, and re-layouts, shards(): pairs[1 + axis][rows]  3.34 us
  transfers between devices with their start and end apart: 16, of which 5 were waited for; matrix products, arithmetic and copies ran while one was open for 14% of the time, Pallas kernels for 15%

profile of v7, /device:TPU:17, one launch (start us, length us, event | category | flops | bytes accessed | tf_op | source)
XLA Modules:
  0.0 78.7 jit_solution(3958126234423194486)
XLA Ops:
  0.0 2.0 %shard_map.55 = (bf16[1024,256]{1,0:T(8,128)(2,1)}, bf16[256,512]{1,0:T(8,128)(2,1)}, bf16[256,512]{1,0:T(8,128)(2,1)}) custom-call(s32[1]{0:T(128)} %bitcast.8.begin, bf16[1024,128]{1,0:T(8,128)(2,1)} %key.1, bf16[1024,128]{1,0:T(8,128)(2,1)} %value.1, bf16[1024,512]{1,0:T(8,128)(2,1)} %query.2), custom_call_target="tpu_custom_call" | custom-call | bytes 2097152 | tf_op jit(solution)/shard_map/pallas_call | solution.py:83
  2.0 0.7 pad_add_fusion.3.starts
  2.7 4.5 %shard_map.56 = (bf16[512,512]{1,0:T(8,128)(2,1)}, bf16[512,512]{1,0:T(8,128)(2,1)}, bf16[384,4096]{1,0:T(8,128)(2,1)}) custom-call(s32[4]{0:T(128)} %pad_add_fusion.3.starts, bf16[1024,512]{1,0:T(8,128)(2,1)} %query.2, bf16[384,8192]{1,0:T(8,128)(2,1)} %bitcast.29), custom_call_target="tpu_custom_call" | custom-call | bytes 8388608 | tf_op jit(solution)/shard_map/pallas_call | solution.py:83
  7.2 0.7 collective-permute-start
  7.9 1.2 %collective-permute-start.1 = (bf16[1024,256]{1,0:T(8,128)(2,1)}, bf16[1024,256]{1,0:T(8,128)(2,1)}, u32[]{:S(2)}, u32[]{:S(2)}) collective-permute-start(bf16[1024,256]{1,0:T(8,128)(2,1)} %get-tuple-element.31.refs_0_), channel_id=1, source_target_pairs={{0,8},{4,12},{8,0},{12,4},{16,24},{20,28},{24,16},{28,20},{1,9},{5... | collective-permute-start | bytes 1572872 | tf_op jit(solution)/shard_map/ppermute | solution.py:274
  9.2 1.2 %collective-permute-start.2 = (bf16[1024,256]{1,0:T(8,128)(2,1)}, bf16[1024,256]{1,0:T(8,128)(2,1)}, u32[]{:S(2)}, u32[]{:S(2)}) collective-permute-start(bf16[1024,256]{1,0:T(8,128)(2,1)} %get-tuple-element.31.refs_0_), channel_id=1, source_target_pairs={{0,16},{4,20},{8,24},{12,28},{16,0},{20,4},{24,8},{28,12},{1,17},{... | collective-permute-start | bytes 1572872 | tf_op jit(solution)/shard_map/ppermute | solution.py:274
  11.1 1.5 %fusion = (f32[384,64]{1,0:T(8,128)}, f32[384,64]{1,0:T(8,128)}, f32[384,64]{1,0:T(8,128)S(1)}) fusion(f32[64]{0:T(128)S(1)} %negate_power_fusion, f32[384]{0:T(512)S(1)} %get-tuple-element.63), kind=kLoop, calls=%fused_computation.6 | loop fusion | flops 49152 | bytes 296704 | tf_op jit(solution)/shard_map/neg | solution.py:24
  12.7 9.0 %collective-permute-done.1.refs_1_ = bf16[1024,256]{1,0:T(8,128)(2,1)} collective-permute-done((bf16[1024,256]{1,0:T(8,128)(2,1)}, bf16[1024,256]{1,0:T(8,128)(2,1)}, u32[]{:S(2)}, u32[]{:S(2)}) %collective-permute-start.1) | collective-permute-done | bytes 524320 | tf_op jit(solution)/shard_map/ppermute | solution.py:274
  21.8 1.7 %slice.16 = bf16[512,256]{1,0:T(8,128)(2,1)} slice(bf16[1024,256]{1,0:T(8,128)(2,1)} %collective-permute-done.1.refs_1_), slice={[0:512], [0:256]} | slice | bytes 524288 | tf_op jit(solution)/shard_map/slice | solution.py:336
  23.4 1.2 %collective-permute-start.4 = (bf16[512,256]{1,0:T(8,128)(2,1)}, bf16[512,256]{1,0:T(8,128)(2,1)}, u32[]{:S(2)}, u32[]{:S(2)}) collective-permute-start(bf16[512,256]{1,0:T(8,128)(2,1)} %slice.16), channel_id=1, source_target_pairs={{0,16},{4,20},{8,24},{12,28},{16,0},{20,4},{24,8},{28,12},{1,17},{... | collective-permute-start | bytes 786440 | tf_op jit(solution)/shard_map/ppermute | solution.py:274
  24.9 1.1 %pad_maximum_fusion.3.sine = f32[384,128]{1,0:T(8,128)S(1)} fusion(f32[384,64]{1,0:T(8,128)} %get-tuple-element.60, f32[384,64]{1,0:T(8,128)} %get-tuple-element.59), kind=kLoop, calls=%fused_computation.5 | loop fusion | flops 49152 | bytes 393216 | tf_op jit(solution)/shard_map/concatenate | solution.py:24
  26.1 1.7 %slice.17 = bf16[512,256]{1,0:T(8,128)(2,1)} slice(bf16[1024,256]{1,0:T(8,128)(2,1)} %collective-permute-done.2.refs_2_), slice={[512:1024], [0:256]} | slice | bytes 524288 | tf_op jit(solution)/shard_map/slice | solution.py:336
  27.7 1.2 %collective-permute-start.5 = (bf16[512,256]{1,0:T(8,128)(2,1)}, bf16[512,256]{1,0:T(8,128)(2,1)}, u32[]{:S(2)}, u32[]{:S(2)}) collective-permute-start(bf16[512,256]{1,0:T(8,128)(2,1)} %slice.17), channel_id=1, source_target_pairs={{0,8},{4,12},{8,0},{12,4},{16,24},{20,28},{24,16},{28,20},{1,9},{5... | collective-permute-start | bytes 786440 | tf_op jit(solution)/shard_map/ppermute | solution.py:274
  29.0 0.5 collective-permute-start.12
  29.7 1.8 %pad_maximum_fusion.1 = bf16[512,512]{1,0:T(8,128)(2,1)} fusion(bf16[256,512]{1,0:T(8,128)(2,1)} %collective-permute-done.9.refs_3_, bf16[256,512]{1,0:T(8,128)(2,1)} %collective-permute-done.8.refs_5_), kind=kLoop, calls=%fused_computation.1 | loop fusion | flops 1048576 | bytes 1048576 | tf_op jit(solution)/shard_map/concatenate | solution.py:325
  31.6 2.3 %collective-permute-done.4.refs_3_ = bf16[512,256]{1,0:T(8,128)(2,1)} collective-permute-done((bf16[512,256]{1,0:T(8,128)(2,1)}, bf16[512,256]{1,0:T(8,128)(2,1)}, u32[]{:S(2)}, u32[]{:S(2)}) %collective-permute-start.4) | collective-permute-done | bytes 262176 | tf_op jit(solution)/shard_map/ppermute | solution.py:274
  33.9 1.3 %collective-permute-start.10 = (bf16[512,512]{1,0:T(8,128)(2,1)}, bf16[512,512]{1,0:T(8,128)(2,1)}, u32[]{:S(2)}, u32[]{:S(2)}) collective-permute-start(bf16[512,512]{1,0:T(8,128)(2,1)} %pad_maximum_fusion.1), channel_id=1, source_target_pairs={{0,1},{1,0},{2,3},{3,2},{4,5},{5,4},{6,7},{7,6},{8,9},{9,8},{10,11... | collective-permute-start | bytes 1572872 | tf_op jit(solution)/shard_map/ppermute | solution.py:326
  35.4 1.0 %copy-done.3 = bf16[1024,256]{1,0:T(8,128)(2,1)S(1)} copy-done((bf16[1024,256]{1,0:T(8,128)(2,1)S(1)}, bf16[1024,256]{1,0:T(8,128)(2,1)}, u32[]{:S(2)}) %copy-start.3) | copy-done | bytes 524312
  36.5 6.1 %shard_map.57 = (f32[384,256]{1,0:T(8,128)S(1)}, f32[384,256]{1,0:T(8,128)S(1)}) custom-call(s32[2,5]{1,0:T(2,128)S(1)} %pad_add_fusion.1.starts, bf16[384,8192]{1,0:T(8,128)(2,1)} %bitcast.30, bf16[384,4096]{1,0:T(8,128)(2,1)S(1)} %collective-permute-done.far, bf16[1024,256]{1,0:T(8,128)(2,1)S(1)} %copy-done.3, ...), custom_call_target="tpu_custom_call" | custom-call | flops 1610612736 | bytes 8388608 | tf_op jit(solution)/shard_map/pallas_call | solution.py:149
  42.6 3.5 %collective-permute-start.7 = (f32[384,256]{1,0:T(8,128)S(1)}, f32[384,256]{1,0:T(8,128)S(1)}, u32[]{:S(2)}, u32[]{:S(2)}) collective-permute-start(f32[384,256]{1,0:T(8,128)S(1)} %get-tuple-element.38), channel_id=1, source_target_pairs={{0,4},{4,0},{8,12},{12,8},{16,20},{20,16},{24,28},{28,24},{1,5},{5... | collective-permute-start | bytes 1179656 | tf_op jit(solution)/shard_map/ppermute | solution.py:274
  46.2 1.2 %collective-permute-start.13 = (bf16[512,512]{1,0:T(8,128)(2,1)}, bf16[512,512]{1,0:T(8,128)(2,1)S(1)}, u32[]{:S(2)}, u32[]{:S(2)}) collective-permute-start(bf16[512,512]{1,0:T(8,128)(2,1)} %collective-permute-done.12.refs_7_), channel_id=1, source_target_pairs={{0,8},{4,12},{8,0},{12,4},{16,24},{20,28},{24,16},{28,20},{1,9},{5... | collective-permute-start | bytes 1572872 | tf_op jit(solution)/shard_map/ppermute | solution.py:274
  47.7 1.1 %fusion.2 = (bf16[256,512]{1,0:T(8,128)(2,1)S(1)}, bf16[256,512]{1,0:T(8,128)(2,1)S(1)}) fusion(bf16[512,512]{1,0:T(8,128)(2,1)} %collective-permute-done.10), kind=kLoop, calls=%fused_computation.18 | loop fusion | bytes 1048576 | tf_op jit(solution)/shard_map/slice | solution.py:328
  49.0 3.2 %collective-permute-start.11 = (bf16[384,256]{1,0:T(8,128)(2,1)S(1)}, bf16[384,256]{1,0:T(8,128)(2,1)}, u32[]{:S(2)}, u32[]{:S(2)}) collective-permute-start(bf16[384,256]{1,0:T(8,128)(2,1)S(1)} %shard_map.58), channel_id=1, source_target_pairs={{0,1},{1,2},{2,3},{4,5},{5,6},{6,7},{8,9},{9,10},{10,11},{12,13},{... | collective-permute-start | bytes 589832 | tf_op jit(solution)/shard_map/ppermute | solution.py:355
  52.2 5.7 %shard_map.59.refs_2_ = f32[768,512]{1,0:T(8,128)S(1)} custom-call(s32[2,8]{1,0:T(2,128)S(1)} %pad_add_fusion.2.starts, bf16[384,8192]{1,0:T(8,128)(2,1)} %bitcast.31, bf16[384,4096]{1,0:T(8,128)(2,1)} %copy-done, bf16[512,512]{1,0:T(8,128)(2,1)S(1)} %copy-done.1, bf16[512,512]{1,0:T(8,128)(2,1)S(1)} %copy-done.2, ...), custom_call_target="tpu_custom_call" | custom-call | flops 2415919104 | bytes 7864320 | tf_op jit(solution)/shard_map/pallas_call | solution.py:149
  57.9 2.0 %collective-permute-done.13.refs_1_ = bf16[512,512]{1,0:T(8,128)(2,1)S(1)} collective-permute-done((bf16[512,512]{1,0:T(8,128)(2,1)}, bf16[512,512]{1,0:T(8,128)(2,1)S(1)}, u32[]{:S(2)}, u32[]{:S(2)}) %collective-permute-start.13) | collective-permute-done | bytes 524320 | tf_op jit(solution)/shard_map/ppermute | solution.py:274
  59.9 0.6 collective-permute-done.6.refs_0_
  60.5 3.3 %shard_map.60 = (f32[384,512]{1,0:T(8,128)S(1)}, f32[384,512]{1,0:T(8,128)}) custom-call(s32[2,2]{1,0:T(2,128)S(1)} %pad_add_fusion.starts, bf16[384,8192]{1,0:T(8,128)(2,1)} %bitcast.32, bf16[384,4096]{1,0:T(8,128)(2,1)} %copy-done, bf16[512,512]{1,0:T(8,128)(2,1)S(1)} %collective-permute-done.6.refs_0_, ...), custom_call_target="tpu_custom_call" | custom-call | flops 805306368 | bytes 2621440 | tf_op jit(solution)/shard_map/pallas_call | solution.py:149
  63.8 1.5 %collective-permute-start.14 = (f32[384,512]{1,0:T(8,128)}, f32[384,512]{1,0:T(8,128)S(1)}, u32[]{:S(2)}, u32[]{:S(2)}) collective-permute-start(f32[384,512]{1,0:T(8,128)} %get-tuple-element.56), channel_id=1, source_target_pairs={{0,4},{4,0},{8,12},{12,8},{16,20},{20,16},{24,28},{28,24},{1,5},{5... | collective-permute-start | bytes 2359304 | tf_op jit(solution)/shard_map/ppermute | solution.py:274
  65.3 3.2 %collective-permute-start.15 = (bf16[384,256]{1,0:T(8,128)(2,1)}, bf16[384,256]{1,0:T(8,128)(2,1)S(1)}, u32[]{:S(2)}, u32[]{:S(2)}) collective-permute-start(bf16[384,256]{1,0:T(8,128)(2,1)} %collective-permute-done.11), channel_id=1, source_target_pairs={{0,1},{1,2},{2,3},{4,5},{5,6},{6,7},{8,9},{9,10},{10,11},{12,13},{... | collective-permute-start | bytes 589832 | tf_op jit(solution)/shard_map/ppermute | solution.py:355
  68.7 5.3 %collective-permute-done.15 = bf16[384,256]{1,0:T(8,128)(2,1)S(1)} collective-permute-done((bf16[384,256]{1,0:T(8,128)(2,1)}, bf16[384,256]{1,0:T(8,128)(2,1)S(1)}, u32[]{:S(2)}, u32[]{:S(2)}) %collective-permute-start.15) | collective-permute-done | bytes 196640 | tf_op jit(solution)/shard_map/ppermute | solution.py:355
  73.9 1.0 %pad_maximum_fusion.keys_values = bf16[1152,256]{1,0:T(8,128)(2,1)S(1)} fusion(bf16[384,256]{1,0:T(8,128)(2,1)S(1)} %shard_map.58, bf16[384,256]{1,0:T(8,128)(2,1)} %collective-permute-done.11, bf16[384,256]{1,0:T(8,128)(2,1)S(1)} %collective-permute-done.15), kind=kLoop, calls=%fused_computation | loop fusion | flops 1769472 | bytes 1179648 | tf_op jit(solution)/shard_map/concatenate | solution.py:356
  74.9 3.8 %shard_map.61 = bf16[384,512]{1,0:T(8,128)(2,1)} custom-call(f32[384,512]{1,0:T(8,128)S(1)} %get-tuple-element.55.near, f32[384,512]{1,0:T(8,128)S(1)} %collective-permute-done.14.far, f32[384,128]{1,0:T(8,128)S(1)} %pad_maximum_fusion.2.cosine, f32[384,128]{1,0:T(8,128)S(1)} %pad_maximum_fusion.3.sine, s32[384,1]{1,0:T(8,128)S(1)} %copy.7.first, ...), custom_call_target="tpu_custom_call" | custom-call | flops 704643072 | bytes 1572864 | tf_op jit(solution)/shard_map/pallas_call | solution.py:244
  (45 shorter events, 2.1 us)
Async XLA Ops:
  2.7 8.2 %copy-start.6 = (s32[1,16]{1,0:T(1,128)S(1)}, s32[1,16]{1,0:T(1,128)}, u32[]{:S(2)}) copy-start(s32[1,16]{1,0:T(1,128)} %param.9) | copy-start | bytes 196
  7.2 28.2 %collective-permute-start = (bf16[384,4096]{1,0:T(8,128)(2,1)}, bf16[384,4096]{1,0:T(8,128)(2,1)S(1)}, u32[]{:S(2)}, u32[]{:S(2)}) collective-permute-start(bf16[384,4096]{1,0:T(8,128)(2,1)} %get-tuple-element.33), channel_id=1, source_target_pairs={{0,4},{4,0},{8,12},{12,8},{16,20},{20,16},{24,28},{28,24},{1,5},{5... | collective-permute-start | bytes 9437192 | tf_op jit(solution)/shard_map/ppermute | solution.py:274
  7.9 13.8 %collective-permute-start.1 = (bf16[1024,256]{1,0:T(8,128)(2,1)}, bf16[1024,256]{1,0:T(8,128)(2,1)}, u32[]{:S(2)}, u32[]{:S(2)}) collective-permute-start(bf16[1024,256]{1,0:T(8,128)(2,1)} %get-tuple-element.31.refs_0_), channel_id=1, source_target_pairs={{0,8},{4,12},{8,0},{12,4},{16,24},{20,28},{24,16},{28,20},{1,9},{5... | collective-permute-start | bytes 1572872 | tf_op jit(solution)/shard_map/ppermute | solution.py:274
  9.2 16.9 %collective-permute-start.2 = (bf16[1024,256]{1,0:T(8,128)(2,1)}, bf16[1024,256]{1,0:T(8,128)(2,1)}, u32[]{:S(2)}, u32[]{:S(2)}) collective-permute-start(bf16[1024,256]{1,0:T(8,128)(2,1)} %get-tuple-element.31.refs_0_), channel_id=1, source_target_pairs={{0,16},{4,20},{8,24},{12,28},{16,0},{20,4},{24,8},{28,12},{1,17},{... | collective-permute-start | bytes 1572872 | tf_op jit(solution)/shard_map/ppermute | solution.py:274
  10.4 18.5 %collective-permute-start.8 = (bf16[256,512]{1,0:T(8,128)(2,1)}, bf16[256,512]{1,0:T(8,128)(2,1)}, u32[]{:S(2)}, u32[]{:S(2)}) collective-permute-start(bf16[256,512]{1,0:T(8,128)(2,1)} %get-tuple-element.39), channel_id=1, source_target_pairs={{0,16},{4,20},{8,24},{12,28},{16,0},{20,4},{24,8},{28,12},{1,17},{... | collective-permute-start | bytes 786440 | tf_op jit(solution)/shard_map/ppermute | solution.py:274
  10.6 18.8 %collective-permute-start.9 = (bf16[256,512]{1,0:T(8,128)(2,1)}, bf16[256,512]{1,0:T(8,128)(2,1)}, u32[]{:S(2)}, u32[]{:S(2)}) collective-permute-start(bf16[256,512]{1,0:T(8,128)(2,1)} %get-tuple-element.40), channel_id=1, source_target_pairs={{0,8},{4,12},{8,0},{12,4},{16,24},{20,28},{24,16},{28,20},{1,9},{5... | collective-permute-start | bytes 786440 | tf_op jit(solution)/shard_map/ppermute | solution.py:274
  23.4 10.5 %collective-permute-start.4 = (bf16[512,256]{1,0:T(8,128)(2,1)}, bf16[512,256]{1,0:T(8,128)(2,1)}, u32[]{:S(2)}, u32[]{:S(2)}) collective-permute-start(bf16[512,256]{1,0:T(8,128)(2,1)} %slice.16), channel_id=1, source_target_pairs={{0,16},{4,20},{8,24},{12,28},{16,0},{20,4},{24,8},{28,12},{1,17},{... | collective-permute-start | bytes 786440 | tf_op jit(solution)/shard_map/ppermute | solution.py:274
  24.8 10.4 %copy-start.5 = (s32[1,5]{1,0:T(1,128)S(1)}, s32[1,5]{1,0:T(1,128)}, u32[]{:S(2)}) copy-start(s32[1,5]{1,0:T(1,128)} %constant.62.clone.1) | copy-start | bytes 64
  27.7 7.7 %collective-permute-start.5 = (bf16[512,256]{1,0:T(8,128)(2,1)}, bf16[512,256]{1,0:T(8,128)(2,1)}, u32[]{:S(2)}, u32[]{:S(2)}) collective-permute-start(bf16[512,256]{1,0:T(8,128)(2,1)} %slice.17), channel_id=1, source_target_pairs={{0,8},{4,12},{8,0},{12,4},{16,24},{20,28},{24,16},{28,20},{1,9},{5... | collective-permute-start | bytes 786440 | tf_op jit(solution)/shard_map/ppermute | solution.py:274
  29.0 17.3 %collective-permute-start.12 = (bf16[512,512]{1,0:T(8,128)(2,1)}, bf16[512,512]{1,0:T(8,128)(2,1)}, u32[]{:S(2)}, u32[]{:S(2)}) collective-permute-start(bf16[512,512]{1,0:T(8,128)(2,1)} %get-tuple-element.48.refs_1_), channel_id=1, source_target_pairs={{0,16},{4,20},{8,24},{12,28},{16,0},{20,4},{24,8},{28,12},{1,17},{... | collective-permute-start | bytes 1572872 | tf_op jit(solution)/shard_map/ppermute | solution.py:274
  29.5 17.9 %collective-permute-start.3 = (bf16[512,512]{1,0:T(8,128)(2,1)}, bf16[512,512]{1,0:T(8,128)(2,1)}, u32[]{:S(2)}, u32[]{:S(2)}) collective-permute-start(bf16[512,512]{1,0:T(8,128)(2,1)} %get-tuple-element.47.refs_0_), channel_id=1, source_target_pairs={{0,8},{4,12},{8,0},{12,4},{16,24},{20,28},{24,16},{28,20},{1,9},{5... | collective-permute-start | bytes 1572872 | tf_op jit(solution)/shard_map/ppermute | solution.py:274
  33.9 13.8 %collective-permute-start.10 = (bf16[512,512]{1,0:T(8,128)(2,1)}, bf16[512,512]{1,0:T(8,128)(2,1)}, u32[]{:S(2)}, u32[]{:S(2)}) collective-permute-start(bf16[512,512]{1,0:T(8,128)(2,1)} %pad_maximum_fusion.1), channel_id=1, source_target_pairs={{0,1},{1,0},{2,3},{3,2},{4,5},{5,4},{6,7},{7,6},{8,9},{9,8},{10,11... | collective-permute-start | bytes 1572872 | tf_op jit(solution)/shard_map/ppermute | solution.py:326
  35.4 12.3 %copy-start.4 = (s32[1,2]{1,0:T(1,128)S(1)}, s32[1,2]{1,0:T(1,128)}, u32[]{:S(2)}) copy-start(s32[1,2]{1,0:T(1,128)} %constant.16.clone.1) | copy-start | bytes 28
  35.4 1.0 %copy-start.3 = (bf16[1024,256]{1,0:T(8,128)(2,1)S(1)}, bf16[1024,256]{1,0:T(8,128)(2,1)}, u32[]{:S(2)}) copy-start(bf16[1024,256]{1,0:T(8,128)(2,1)} %get-tuple-element.31.refs_0_) | copy-start | bytes 1572868
  36.5 6.1 %copy-start = (bf16[384,4096]{1,0:T(8,128)(2,1)}, bf16[384,4096]{1,0:T(8,128)(2,1)S(1)}, u32[]{:S(2)}) copy-start(bf16[384,4096]{1,0:T(8,128)(2,1)S(1)} %collective-permute-done.far) | copy-start | bytes 9437188
  42.6 6.2 %collective-permute-start.7 = (f32[384,256]{1,0:T(8,128)S(1)}, f32[384,256]{1,0:T(8,128)S(1)}, u32[]{:S(2)}, u32[]{:S(2)}) collective-permute-start(f32[384,256]{1,0:T(8,128)S(1)} %get-tuple-element.38), channel_id=1, source_target_pairs={{0,4},{4,0},{8,12},{12,8},{16,20},{20,16},{24,28},{28,24},{1,5},{5... | collective-permute-start | bytes 1179656 | tf_op jit(solution)/shard_map/ppermute | solution.py:274
  46.2 13.7 %collective-permute-start.13 = (bf16[512,512]{1,0:T(8,128)(2,1)}, bf16[512,512]{1,0:T(8,128)(2,1)S(1)}, u32[]{:S(2)}, u32[]{:S(2)}) collective-permute-start(bf16[512,512]{1,0:T(8,128)(2,1)} %collective-permute-done.12.refs_7_), channel_id=1, source_target_pairs={{0,8},{4,12},{8,0},{12,4},{16,24},{20,28},{24,16},{28,20},{1,9},{5... | collective-permute-start | bytes 1572872 | tf_op jit(solution)/shard_map/ppermute | solution.py:274
  47.4 13.1 %collective-permute-start.6 = (bf16[512,512]{1,0:T(8,128)(2,1)}, bf16[512,512]{1,0:T(8,128)(2,1)S(1)}, u32[]{:S(2)}, u32[]{:S(2)}) collective-permute-start(bf16[512,512]{1,0:T(8,128)(2,1)} %collective-permute-done.3.refs_2_), channel_id=1, source_target_pairs={{0,16},{4,20},{8,24},{12,28},{16,0},{20,4},{24,8},{28,12},{1,17},{... | collective-permute-start | bytes 1572872 | tf_op jit(solution)/shard_map/ppermute | solution.py:274
  47.7 4.5 %copy-start.1 = (bf16[512,512]{1,0:T(8,128)(2,1)S(1)}, bf16[512,512]{1,0:T(8,128)(2,1)}, u32[]{:S(2)}) copy-start(bf16[512,512]{1,0:T(8,128)(2,1)} %get-tuple-element.47.refs_0_) | copy-start | bytes 1572868
  47.7 4.5 %copy-start.2 = (bf16[512,512]{1,0:T(8,128)(2,1)S(1)}, bf16[512,512]{1,0:T(8,128)(2,1)}, u32[]{:S(2)}) copy-start(bf16[512,512]{1,0:T(8,128)(2,1)} %get-tuple-element.48.refs_1_) | copy-start | bytes 1572868
  49.0 10.9 %collective-permute-start.11 = (bf16[384,256]{1,0:T(8,128)(2,1)S(1)}, bf16[384,256]{1,0:T(8,128)(2,1)}, u32[]{:S(2)}, u32[]{:S(2)}) collective-permute-start(bf16[384,256]{1,0:T(8,128)(2,1)S(1)} %shard_map.58), channel_id=1, source_target_pairs={{0,1},{1,2},{2,3},{4,5},{5,6},{6,7},{8,9},{9,10},{10,11},{12,13},{... | collective-permute-start | bytes 589832 | tf_op jit(solution)/shard_map/ppermute | solution.py:355
  63.8 11.1 %collective-permute-start.14 = (f32[384,512]{1,0:T(8,128)}, f32[384,512]{1,0:T(8,128)S(1)}, u32[]{:S(2)}, u32[]{:S(2)}) collective-permute-start(f32[384,512]{1,0:T(8,128)} %get-tuple-element.56), channel_id=1, source_target_pairs={{0,4},{4,0},{8,12},{12,8},{16,20},{20,16},{24,28},{28,24},{1,5},{5... | collective-permute-start | bytes 2359304 | tf_op jit(solution)/shard_map/ppermute | solution.py:274
  65.3 8.6 %collective-permute-start.15 = (bf16[384,256]{1,0:T(8,128)(2,1)}, bf16[384,256]{1,0:T(8,128)(2,1)S(1)}, u32[]{:S(2)}, u32[]{:S(2)}) collective-permute-start(bf16[384,256]{1,0:T(8,128)(2,1)} %collective-permute-done.11), channel_id=1, source_target_pairs={{0,1},{1,2},{2,3},{4,5},{5,6},{6,7},{8,9},{9,10},{10,11},{12,13},{... | collective-permute-start | bytes 589832 | tf_op jit(solution)/shard_map/ppermute | solution.py:355

commit v8 on v7

--- a/solution.py
+++ b/solution.py
@@ -59,23 +59,12 @@
         store.wait()
 
 
-def first_kernel(begin, key, value, query, pair, *refs):
-    parts, buffers, sems = refs[: (len(refs) - 3) // 2], refs[(len(refs) - 3) // 2 : -1], refs[-1]
-    head_size = key.shape[1]
-    copies = [(key, pair.at[:, :head_size]), (value, pair.at[:, head_size:])]
-    for side, part in enumerate(parts):
-        row = side * (query.shape[0] // 2) + begin[0]
-        copies.append((query.at[pl.ds(pl.multiple_of(row, 16), part.shape[0])], part))
-    copy_all(copies, buffers, sems)
-
-
-def second_kernel(starts, query, tokens, top, bottom, columns, *refs):
-    buffers, sems = refs[:-1], refs[-1]
-    half, depth = top.shape[0], query.shape[0]
-    copies = [(query.at[:half], top), (query.at[half:], bottom)]
-    for chip in range(columns.shape[1] // depth):
-        window = pl.ds(pl.multiple_of(starts[chip], 128), depth)
-        copies.append((tokens.at[:, window], columns.at[:, chip * depth : (chip + 1) * depth]))
+def cut_kernel(places, query, *refs):
+    pieces, buffers, sems = refs[: len(refs) // 2], refs[len(refs) // 2 : -1], refs[-1]
+    copies = []
+    for i, piece in enumerate(pieces):
+        rows = pl.ds(pl.multiple_of(places[i], 16), piece.shape[0])
+        copies.append((query.at[rows], piece))
     copy_all(copies, buffers, sems)
 
 
@@ -96,22 +85,25 @@
     )(places, *arrays)
 
 
-def project_kernel(steps, carried, final, starts, near, far, *refs):
-    weights, refs = refs[: len(steps)], refs[len(steps) :]
-    if carried:
-        carry, refs = refs[0], refs[1:]
-    outs, (tokens, held, sems) = refs[:-3], refs[-3:]
+def project_kernel(steps, starts, near, far, *refs):
+    count = sum(len(spots) for _, spots in steps)
+    weights, refs = refs[:count], refs[count:]
+    *carry, far_out, near_out, tokens, held, sems = refs
     rows = near.shape[0]
     batches = ([], [], [])
-    row = 0
-    for step, depth in enumerate(steps):
+    used = row = 0
+    for step, (depth, spots) in enumerate(steps):
         here = slice(row, row + depth)
         row += depth
-        batches[0].append(
-            pltpu.make_async_copy(weights[step], held.at[here], sems.at[step, 2])
-        )
+        for index, columns in enumerate(spots):
+            batches[0].append(
+                pltpu.make_async_copy(
+                    weights[used], held.at[here, columns], sems.at[step, 2 + index]
+                )
+            )
+            used += 1
+        window = pl.ds(pl.multiple_of(starts[step], 128), depth)
         for side, ref in enumerate((far, near)):
-            window = pl.ds(pl.multiple_of(starts[side, step], 128), depth)
             batches[1 + side].append(
                 pltpu.make_async_copy(
                     ref.at[:, window], tokens.at[side, :, here], sems.at[step, side]
@@ -122,41 +114,35 @@
             copy.start()
     for copy in batches[0]:
         copy.wait()
-    for side in range(2):
+    for side, out in enumerate((far_out, near_out)):
         for copy in batches[1 + side]:
             copy.wait()
         total = jnp.dot(tokens[side], held[...], preferred_element_type=jnp.float32)
-        place = slice((1 - side) * rows, (2 - side) * rows)
-        if carried:
-            total = total + carry[place, :]
-        if final:
-            outs[1 - side][...] = total
-        else:
-            outs[0][place, :] = total
-
-
-def project(terms, near, far, carry=None, final=False):
+        out[...] = total + carry[side][...] if carry else total
+
+
+def project(terms, near, far, carry=()):
     rows = near.shape[0]
-    width = terms[0][0].shape[1]
-    steps = [array.shape[0] for array, *_ in terms]
-    depth = sum(steps)
-    starts = jnp.stack(
-        [jnp.stack([jnp.int32(term[1 + side]) for term in terms]) for side in range(2)]
-    )
-    whole = jax.ShapeDtypeStruct((2 * rows, width), jnp.float32)
-    part = jax.ShapeDtypeStruct((rows, width), jnp.float32)
-    carries = [] if carry is None else [carry]
+    width = sum(array.shape[1] for array in terms[0][0])
+    steps = []
+    for arrays, _ in terms:
+        edges = [sum(array.shape[1] for array in arrays[:i]) for i in range(len(arrays) + 1)]
+        spots = [slice(*edge) for edge in zip(edges[:-1], edges[1:])]
+        steps.append((arrays[0].shape[0], spots))
+    depth = sum(step[0] for step in steps)
+    starts = jnp.stack([jnp.int32(start) for _, start in terms])
+    weights = [array for arrays, _ in terms for array in arrays]
     return pl.pallas_call(
-        functools.partial(project_kernel, steps, carry is not None, final),
-        out_shape=(part, part) if final else whole,
+        functools.partial(project_kernel, steps),
+        out_shape=[jax.ShapeDtypeStruct((rows, width), jnp.float32)] * 2,
         in_specs=[pl.BlockSpec(memory_space=pltpu.SMEM)]
-        + in_hbm(2 + len(terms))
-        + vmem(len(carries)),
-        out_specs=tuple(vmem(2)) if final else vmem(1)[0],
+        + in_hbm(2 + len(weights))
+        + vmem(len(carry)),
+        out_specs=vmem(2),
         scratch_shapes=[
             pltpu.VMEM((2, rows, depth), jnp.bfloat16),
             pltpu.VMEM((depth, width), jnp.bfloat16),
-            pltpu.SemaphoreType.DMA((len(steps), 3)),
+            pltpu.SemaphoreType.DMA((len(steps), 4)),
         ],
         compiler_params=pltpu.CompilerParams(vmem_limit_bytes=48 * MIB),
         cost_estimate=pl.CostEstimate(
@@ -164,7 +150,7 @@
             bytes_accessed=2 * depth * (2 * rows + width),
             transcendentals=0,
         ),
-    )(starts, near, far, *[array for array, *_ in terms], *carries)
+    )(starts, near, far, *weights, *carry)
 
 
 def turn(vectors, cosine, sine):
@@ -298,75 +284,55 @@
     some = half // 2
     halved = ctx_size % 2 == 0
     begin = (place % 2) * some
-    part_shapes = [(some, query_width)] * (2 if halved else 0)
-    pair_here, *parts = copy_call(
-        first_kernel,
-        begin[None],
-        [w_key, w_value, w_query],
-        [(depth, 2 * head_size)] + part_shapes,
-        [(depth, head_size)] * 2 + part_shapes,
-    )
-    theirs = jnp.stack([(me ^ (2 * chip + 1)) * depth for chip in range(chips)])
-    half_shapes = [(half, query_width)] * 2
-    *halves, sent = copy_call(
-        second_kernel,
-        theirs,
-        [after(w_query, pair_here), hidden],
-        half_shapes + [(row_count, chips * depth)],
-        half_shapes + [(row_count, depth)] * chips,
-    )
-
-    def term(array, chip, row):
-        return (array, chip * depth + row, (me ^ (2 * chip)) * depth + row)
-
-    given = [{}, {}]
+
+    pair_held = fetch((w_key, w_value), [{}, {}], [], [])
+    far_tokens = swap(hidden, 1)
+    rows = [0, half] + ([begin, half + begin] if halved else [])
+    shapes = [(half, query_width)] * 2 + [(some, query_width)] * (len(rows) - 2)
+    places = jnp.stack([jnp.int32(row) for row in rows])
+    halves = copy_call(cut_kernel, places, [w_query], shapes, shapes)
+    parts = halves[2:]
+
+    def term(arrays, chip, row):
+        return (arrays, (me ^ (2 * chip)) * depth + row)
+
+    direct = [pair_held[side][chip][0][1] for side in range(2) for chip in axes]
+    gate = [*direct, cosine, sine, first]
+    given, other = [{}, {}], []
     mine = [swap(part, 2 << axis) for part, axis in zip(parts, (bits - 1, 0))]
     if halved:
-        both = jnp.concatenate(mine, axis=0)
-        both = lax.ppermute(both, "ctx", [(i, i ^ 1) for i in range(ctx_size)])
+        other = [lax.ppermute(part, "ctx", [(i, i ^ 1) for i in range(ctx_size)]) for part in mine]
         given = [
-            {1 << axis: [(begin, mine[side]), (some - begin, both[side * some : side * some + some])]}
+            {1 << axis: [(begin, mine[side]), (some - begin, other[side])]}
             for side, axis in enumerate((bits - 1, 0))
         ]
-    pairs = [pair_here] + [swap(pair_here, 2 << axis) for axis in range(bits)]
-    far_tokens = swap(sent, 1)
-    sides = [slice(0, half), slice(half, depth)]
-    pair_held = fetch(
-        [pair_here[rows] for rows in sides],
-        [{1 << axis: [(0, pairs[1 + axis][rows])] for axis in range(bits)} for rows in sides],
-        [],
-        [],
-    )
-    pair_terms = [term(array, chip, 0) for chip, array in zip([0] + axes, pairs)] + [
-        term(pair_held[side][chip][0][1], chip, side * half)
-        for chip in range(chips)
-        if chip not in [0] + axes
-        for side in range(2)
+    pair_terms = [
+        term([pair_held[side][chip][0][1] for side in range(2)], chip, 0) for chip in range(chips)
     ]
-    near, far = project(pair_terms, hidden, far_tokens, None, True)
-    query_held = fetch(halves, given, [*pairs, cosine, sine, first], [near])
+    far, near = project(pair_terms, hidden, far_tokens)
+    query_held = fetch(halves[:2], given, [*gate, *mine], [near, *other])
 
     pair = finish_pair(near, swap(far, 1), cosine, sine)
     longest = ctx_size * row_count // 2
     back = -(-(longest - 1) // ROW_TILE) * ROW_TILE
     hops = min(ctx_size - 1, -(-back // row_count))
-    blocks = [after(pair, both) if halved else pair]
+    blocks = [pair]
     for _ in range(hops):
         blocks.insert(0, lax.ppermute(blocks[0], "ctx", [(i, i + 1) for i in range(ctx_size - 1)]))
     keys_values = jnp.concatenate(blocks, axis=0)
 
     def query_terms(wanted, *gate):
         return [
-            term(after(array, *gate), chip, side * half + row)
+            term([after(array, *gate)], chip, side * half + row)
             for side, chip in wanted
             for row, array in query_held[side][chip]
         ]
 
     everything = [(side, chip) for chip in range(chips) for side in range(2)]
-    early = [(side, chip) for side, chip in everything if chip in [0] + axes]
+    early = [(0, 0), (1, 0), (0, axes[0]), (1, axes[-1])]
     late = [wanted for wanted in everything if wanted not in early]
     carry = project(query_terms(early, pair), hidden, far_tokens)
-    near, far = project(query_terms(late, blocks[-2]), hidden, far_tokens, carry, True)
+    far, near = project(query_terms(late, blocks[-2]), hidden, far_tokens, carry)
     return attend(near, swap(far, 1), cosine, sine, first, keys_values, back)[None]
 
 

time: 79.9 us -> 80.1 us (level)
  waiting for transfers between devices: 19.2 us -> 23.2 us
  Pallas kernels: 25.5 us -> 22.2 us
  other arithmetic: 6.65 us -> 4.32 us
  local copies, waits for them, and re-layouts: 5.94 us -> 7.75 us
    unnamed x14 -> x32, local copies, waits for them, and re-layouts: 1.06 us -> 7.53 us
    slice x3 -> x0, local copies, waits for them, and re-layouts: 4.48 us -> none  [the longest x2 3.34 us: shards(): pairs[1 + axis][rows]]
    ppermute x13 -> x15, waiting for transfers between devices: 14 us -> 18 us  [swap(): return lax.ppermute(array, 'dp', [(i, i ^ mask) for i in range(dp_size)])]
    pallas_call x2 -> x1, Pallas kernels: 6.52 us -> 3.31 us  [copy_call(): pl.pallas_call(kernel, out_shape=[jax.ShapeDtypeStruct(shape, jnp.bfloat1...]
    concatenate x1 -> x0, other arithmetic: 1.85 us -> none  [shards(): both = jnp.concatenate(mine, axis=0)]
    concatenate x1, other arithmetic: 1.14 us -> 0.12 us  [rope_tables(): jnp.concatenate([-sine_part, sine_part], axis=-1)]
    ppermute x13 -> x15, starting transfers between devices: 13.4 us -> 13.4 us  [swap(): return lax.ppermute(array, 'dp', [(i, i ^ mask) for i in range(dp_size)])]
  transfers between devices with their start and end apart: 16 -> 19, of which waited for: 5 -> 6; matrix products, arithmetic and copies ran while one was open for 14% -> 6% of each run, Pallas kernels for 15% -> 18%
where the time goes in v8:
time: 80.1 us; the launch traced here: 78.9 us
  waiting for transfers between devices  23.2 us (29%)
  Pallas kernels  22.2 us (28%)
  starting transfers between devices  21.3 us (27%)
  local copies, waits for them, and re-layouts  7.75 us (10%)
  other arithmetic  4.32 us (5%)
    ppermute x15, waiting for transfers between devices, swap(): return lax.ppermute(array, 'dp', [(i, i ^ mask) for i in range(dp_size)])  18 us
    pallas_call x3, Pallas kernels, project(): pl.pallas_call(functools.partial(project_kernel, steps), out_shape=[jax.S...  15.1 us
    ppermute x15, starting transfers between devices, swap(): return lax.ppermute(array, 'dp', [(i, i ^ mask) for i in range(dp_size)])  13.4 us
    unnamed x32, local copies, waits for them, and re-layouts  7.53 us
    ppermute x2, starting transfers between devices, shards(): lax.ppermute(blocks[0], 'ctx', [(i, i + 1) for i in range(ctx_size - 1)])  6.4 us
    ppermute x2, waiting for transfers between devices, shards(): lax.ppermute(blocks[0], 'ctx', [(i, i + 1) for i in range(ctx_size - 1)])  5.26 us
    pallas_call x1, Pallas kernels, attend(): pl.pallas_call(functools.partial(attend_kernel, back), out_shape=jax.Shap...  3.65 us
    pallas_call x1, Pallas kernels, copy_call(): pl.pallas_call(kernel, out_shape=[jax.ShapeDtypeStruct(shape, jnp.bfloat1...  3.31 us
  transfers between devices with their start and end apart: 19, of which 6 were waited for; matrix products, arithmetic and copies ran while one was open for 6% of the time, Pallas kernels for 18%

profile of v8, /device:TPU:17, one launch (start us, length us, event | category | flops | bytes accessed | tf_op | source)
XLA Modules:
  0.0 78.9 jit_solution(16662893918891113265)
XLA Ops:
  0.7 1.2 %collective-permute-start.5 = (bf16[1024,128]{1,0:T(8,128)(2,1)}, bf16[1024,128]{1,0:T(8,128)(2,1)}, u32[]{:S(2)}, u32[]{:S(2)}) collective-permute-start(bf16[1024,128]{1,0:T(8,128)(2,1)} %refs_1_.1), channel_id=1, source_target_pairs={{0,16},{4,20},{8,24},{12,28},{16,0},{20,4},{24,8},{28,12},{1,17},{... | collective-permute-start | bytes 786440 | tf_op jit(solution)/shard_map/ppermute | solution.py:260
  1.9 1.2 %collective-permute-start.3 = (bf16[1024,128]{1,0:T(8,128)(2,1)}, bf16[1024,128]{1,0:T(8,128)(2,1)S(1)}, u32[]{:S(2)}, u32[]{:S(2)}) collective-permute-start(bf16[1024,128]{1,0:T(8,128)(2,1)} %refs_1_.1), channel_id=1, source_target_pairs={{0,8},{4,12},{8,0},{12,4},{16,24},{20,28},{24,16},{28,20},{1,9},{5... | collective-permute-start | bytes 786440 | tf_op jit(solution)/shard_map/ppermute | solution.py:260
  3.6 0.8 %reduce-window_clone.1 = s32[1,16]{1,0:T(1,128)S(1)} reduce-window(s32[1,16]{1,0:T(1,128)} %param.9, s32[]{:T(128)} %constant.16.clone.1), window={size=1x16 pad=0_0x15_0}, to_apply=%region_0.0 | reduce-window | flops 240 | bytes 132 | tf_op jit(solution)/shard_map/reduce-window.clone
  5.8 3.3 %shard_map.55 = (bf16[512,512]{1,0:T(8,128)(2,1)}, bf16[512,512]{1,0:T(8,128)(2,1)}, bf16[256,512]{1,0:T(8,128)(2,1)}, bf16[256,512]{1,0:T(8,128)(2,1)}) custom-call(s32[4]{0:T(128)} %pad_add_fusion.places, bf16[1024,512]{1,0:T(8,128)(2,1)} %query.1), custom_call_target="tpu_custom_call" | custom-call | bytes 3145728 | tf_op jit(solution)/shard_map/pallas_call | solution.py:72
  9.2 0.8 fusion
  9.9 5.5 %collective-permute-done.2.refs_2_ = bf16[1024,128]{1,0:T(8,128)(2,1)} collective-permute-done((bf16[1024,128]{1,0:T(8,128)(2,1)}, bf16[1024,128]{1,0:T(8,128)(2,1)}, u32[]{:S(2)}, u32[]{:S(2)}) %collective-permute-start.2) | collective-permute-done | bytes 262176 | tf_op jit(solution)/shard_map/ppermute | solution.py:260
  15.5 1.2 %collective-permute-start.1 = (bf16[256,512]{1,0:T(8,128)(2,1)}, bf16[256,512]{1,0:T(8,128)(2,1)}, u32[]{:S(2)}, u32[]{:S(2)}) collective-permute-start(bf16[256,512]{1,0:T(8,128)(2,1)} %get-tuple-element.29), channel_id=1, source_target_pairs={{0,8},{4,12},{8,0},{12,4},{16,24},{20,28},{24,16},{28,20},{1,9},{5... | collective-permute-start | bytes 786440 | tf_op jit(solution)/shard_map/ppermute | solution.py:260
  17.1 1.3 %collective-permute-start.6 = (bf16[1024,128]{1,0:T(8,128)(2,1)}, bf16[1024,128]{1,0:T(8,128)(2,1)S(1)}, u32[]{:S(2)}, u32[]{:S(2)}) collective-permute-start(bf16[1024,128]{1,0:T(8,128)(2,1)} %collective-permute-done.2.refs_2_), channel_id=1, source_target_pairs={{0,16},{4,20},{8,24},{12,28},{16,0},{20,4},{24,8},{28,12},{1,17},{... | collective-permute-start | bytes 786440 | tf_op jit(solution)/shard_map/ppermute | solution.py:260
  18.8 3.7 %collective-permute-done.1.refs_0_ = bf16[256,512]{1,0:T(8,128)(2,1)} collective-permute-done((bf16[256,512]{1,0:T(8,128)(2,1)}, bf16[256,512]{1,0:T(8,128)(2,1)}, u32[]{:S(2)}, u32[]{:S(2)}) %collective-permute-start.1) | collective-permute-done | bytes 262176 | tf_op jit(solution)/shard_map/ppermute | solution.py:260
  22.5 0.9 %collective-permute-done.11.refs_2_ = bf16[256,512]{1,0:T(8,128)(2,1)} collective-permute-done((bf16[256,512]{1,0:T(8,128)(2,1)}, bf16[256,512]{1,0:T(8,128)(2,1)}, u32[]{:S(2)}, u32[]{:S(2)}) %collective-permute-start.11) | collective-permute-done | bytes 262176 | tf_op jit(solution)/shard_map/ppermute | solution.py:260
  24.1 5.0 %collective-permute-done.6.refs_6_ = bf16[1024,128]{1,0:T(8,128)(2,1)S(1)} collective-permute-done((bf16[1024,128]{1,0:T(8,128)(2,1)}, bf16[1024,128]{1,0:T(8,128)(2,1)S(1)}, u32[]{:S(2)}, u32[]{:S(2)}) %collective-permute-start.6) | collective-permute-done | bytes 262176 | tf_op jit(solution)/shard_map/ppermute | solution.py:260
  29.0 0.7 copy-done.14
  29.7 1.3 %collective-permute-start.10 = (bf16[256,512]{1,0:T(8,128)(2,1)}, bf16[256,512]{1,0:T(8,128)(2,1)S(1)}, u32[]{:S(2)}, u32[]{:S(2)}) collective-permute-start(bf16[256,512]{1,0:T(8,128)(2,1)} %collective-permute-done.1.refs_0_), channel_id=1, source_target_pairs={{0,1},{1,0},{2,3},{3,2},{4,5},{5,4},{6,7},{7,6},{8,9},{9,8},{10,11... | collective-permute-start | bytes 786440 | tf_op jit(solution)/shard_map/ppermute | solution.py:304
  31.2 0.9 %copy-done.9 = bf16[1024,128]{1,0:T(8,128)(2,1)S(1)} copy-done((bf16[1024,128]{1,0:T(8,128)(2,1)S(1)}, bf16[1024,128]{1,0:T(8,128)(2,1)}, u32[]{:S(2)}) %copy-start.9) | copy-done | bytes 262168
  32.2 0.9 %copy-done.15 = bf16[1024,128]{1,0:T(8,128)(2,1)S(1)} copy-done((bf16[1024,128]{1,0:T(8,128)(2,1)S(1)}, bf16[1024,128]{1,0:T(8,128)(2,1)}, u32[]{:S(2)}) %copy-start.15) | copy-done | bytes 262168
  33.1 6.5 %shard_map.56 = (f32[384,256]{1,0:T(8,128)}, f32[384,256]{1,0:T(8,128)S(1)}) custom-call(s32[4]{0:T(128)S(1)} %pad_add_fusion.1.starts, bf16[384,8192]{1,0:T(8,128)(2,1)} %bitcast.18, bf16[384,8192]{1,0:T(8,128)(2,1)} %collective-permute-done.far, bf16[1024,128]{1,0:T(8,128)(2,1)S(1)} %copy-done.6, bf16[1024,128]{1,0:T(8,128)(2,1)S(1)} %copy-done.7, ...), custom_call_target="tpu_custom_call" | custom-call | flops 1610612736 | bytes 8388608 | tf_op jit(solution)/shard_map/pallas_call | solution.py:135
  39.6 0.7 copy-done.2
  40.4 4.7 %collective-permute-start.8 = (f32[384,256]{1,0:T(8,128)}, f32[384,256]{1,0:T(8,128)S(1)}, u32[]{:S(2)}, u32[]{:S(2)}) collective-permute-start(f32[384,256]{1,0:T(8,128)} %get-tuple-element.31), channel_id=1, source_target_pairs={{0,4},{4,0},{8,12},{12,8},{16,20},{20,16},{24,28},{28,24},{1,5},{5... | collective-permute-start | bytes 1179656 | tf_op jit(solution)/shard_map/ppermute | solution.py:260
  45.1 0.7 copy-done.10
  45.8 0.7 copy-done.12
  47.0 0.7 copy-done.4
  47.7 1.0 %copy-done.3 = f32[384,256]{1,0:T(8,128)S(1)} copy-done((f32[384,256]{1,0:T(8,128)S(1)}, f32[384,256]{1,0:T(8,128)}, u32[]{:S(2)}) %copy-start.3) | copy-done | bytes 393240
  48.7 1.0 %copy-done.5 = f32[384,256]{1,0:T(8,128)S(1)} copy-done((f32[384,256]{1,0:T(8,128)S(1)}, f32[384,256]{1,0:T(8,128)}, u32[]{:S(2)}) %copy-start.5) | copy-done | bytes 393240
  49.8 3.2 %collective-permute-start.9 = (bf16[384,256]{1,0:T(8,128)(2,1)S(1)}, bf16[384,256]{1,0:T(8,128)(2,1)}, u32[]{:S(2)}, u32[]{:S(2)}) collective-permute-start(bf16[384,256]{1,0:T(8,128)(2,1)S(1)} %shard_map.57), channel_id=1, source_target_pairs={{0,1},{1,2},{2,3},{4,5},{5,6},{6,7},{8,9},{9,10},{10,11},{12,13},{... | collective-permute-start | bytes 589832 | tf_op jit(solution)/shard_map/ppermute | solution.py:321
  53.2 4.1 %shard_map.58 = (f32[384,512]{1,0:T(8,128)S(1)}, f32[384,512]{1,0:T(8,128)S(1)}) custom-call(s32[4]{0:T(128)S(1)} %pad_add_fusion.2.starts, bf16[384,8192]{1,0:T(8,128)(2,1)} %bitcast.19, bf16[384,8192]{1,0:T(8,128)(2,1)} %collective-permute-done.far, bf16[512,512]{1,0:T(8,128)(2,1)S(1)} %copy-done, bf16[512,512]{1,0:T(8,128)(2,1)S(1)} %copy-done.1, ...), custom_call_target="tpu_custom_call" | custom-call | flops 1610612736 | bytes 5242880 | tf_op jit(solution)/shard_map/pallas_call | solution.py:135
  57.4 2.8 %collective-permute-done.16.refs_5_ = bf16[512,512]{1,0:T(8,128)(2,1)S(1)} collective-permute-done((bf16[512,512]{1,0:T(8,128)(2,1)S(1)}, bf16[512,512]{1,0:T(8,128)(2,1)S(1)}, u32[]{:S(2)}, u32[]{:S(2)}) %collective-permute-start.16) | collective-permute-done | bytes 524320 | tf_op jit(solution)/shard_map/ppermute | solution.py:260
  60.2 4.4 %shard_map.59 = (f32[384,512]{1,0:T(8,128)}, f32[384,512]{1,0:T(8,128)S(1)}) custom-call(s32[6]{0:T(128)S(1)} %stack.60.starts, bf16[384,8192]{1,0:T(8,128)(2,1)} %bitcast.20, bf16[384,8192]{1,0:T(8,128)(2,1)} %collective-permute-done.far, bf16[256,512]{1,0:T(8,128)(2,1)} %collective-permute-done.1.refs_0_, bf16[256,512]{1,0:T(8,128)(2,1)S(1)} %copy-done.11, ...), custom_call_target="tpu_custom_call" | custom-call | flops 1610612736 | bytes 5242880 | tf_op jit(solution)/shard_map/pallas_call | solution.py:135
  64.6 1.1 %collective-permute-start.17 = (f32[384,512]{1,0:T(8,128)}, f32[384,512]{1,0:T(8,128)S(1)}, u32[]{:S(2)}, u32[]{:S(2)}) collective-permute-start(f32[384,512]{1,0:T(8,128)} %get-tuple-element.52), channel_id=1, source_target_pairs={{0,4},{4,0},{8,12},{12,8},{16,20},{20,16},{24,28},{28,24},{1,5},{5... | collective-permute-start | bytes 2359304 | tf_op jit(solution)/shard_map/ppermute | solution.py:260
  65.7 3.2 %collective-permute-start.18 = (bf16[384,256]{1,0:T(8,128)(2,1)}, bf16[384,256]{1,0:T(8,128)(2,1)S(1)}, u32[]{:S(2)}, u32[]{:S(2)}) collective-permute-start(bf16[384,256]{1,0:T(8,128)(2,1)} %collective-permute-done.9), channel_id=1, source_target_pairs={{0,1},{1,2},{2,3},{4,5},{5,6},{6,7},{8,9},{9,10},{10,11},{12,13},{... | collective-permute-start | bytes 589832 | tf_op jit(solution)/shard_map/ppermute | solution.py:321
  69.0 5.3 %collective-permute-done.18 = bf16[384,256]{1,0:T(8,128)(2,1)S(1)} collective-permute-done((bf16[384,256]{1,0:T(8,128)(2,1)}, bf16[384,256]{1,0:T(8,128)(2,1)S(1)}, u32[]{:S(2)}, u32[]{:S(2)}) %collective-permute-start.18) | collective-permute-done | bytes 196640 | tf_op jit(solution)/shard_map/ppermute | solution.py:321
  74.3 1.0 %pad_maximum_fusion.keys_values = bf16[1152,256]{1,0:T(8,128)(2,1)S(1)} fusion(bf16[384,256]{1,0:T(8,128)(2,1)S(1)} %shard_map.57, bf16[384,256]{1,0:T(8,128)(2,1)} %collective-permute-done.9, bf16[384,256]{1,0:T(8,128)(2,1)S(1)} %collective-permute-done.18), kind=kLoop, calls=%fused_computation | loop fusion | flops 1769472 | bytes 1179648 | tf_op jit(solution)/shard_map/concatenate | solution.py:322
  75.3 3.6 %shard_map.60 = bf16[384,512]{1,0:T(8,128)(2,1)} custom-call(f32[384,512]{1,0:T(8,128)S(1)} %get-tuple-element.51.near, f32[384,512]{1,0:T(8,128)S(1)} %collective-permute-done.17.far, f32[384,128]{1,0:T(8,128)S(1)} %pad_maximum_fusion.1.cosine, f32[384,128]{1,0:T(8,128)S(1)} %pad_maximum_fusion.2.sine, s32[384,1]{1,0:T(8,128)S(1)} %copy.7.first, ...), custom_call_target="tpu_custom_call" | custom-call | flops 704643072 | bytes 1572864 | tf_op jit(solution)/shard_map/pallas_call | solution.py:230
  (60 shorter events, 5.0 us)
Async XLA Ops:
  0.0 31.2 %collective-permute-start = (bf16[384,8192]{1,0:T(8,128)(2,1)}, bf16[384,8192]{1,0:T(8,128)(2,1)}, u32[]{:S(2)}, u32[]{:S(2)}) collective-permute-start(bf16[384,8192]{1,0:T(8,128)(2,1)} %bitcast.17), channel_id=1, source_target_pairs={{0,4},{4,0},{8,12},{12,8},{16,20},{20,16},{24,28},{28,24},{1,5},{5... | collective-permute-start | bytes 18874376 | tf_op jit(solution)/shard_map/ppermute | solution.py:260
  0.7 16.0 %collective-permute-start.5 = (bf16[1024,128]{1,0:T(8,128)(2,1)}, bf16[1024,128]{1,0:T(8,128)(2,1)}, u32[]{:S(2)}, u32[]{:S(2)}) collective-permute-start(bf16[1024,128]{1,0:T(8,128)(2,1)} %refs_1_.1), channel_id=1, source_target_pairs={{0,16},{4,20},{8,24},{12,28},{16,0},{20,4},{24,8},{28,12},{1,17},{... | collective-permute-start | bytes 786440 | tf_op jit(solution)/shard_map/ppermute | solution.py:260
  1.9 15.1 %collective-permute-start.3 = (bf16[1024,128]{1,0:T(8,128)(2,1)}, bf16[1024,128]{1,0:T(8,128)(2,1)S(1)}, u32[]{:S(2)}, u32[]{:S(2)}) collective-permute-start(bf16[1024,128]{1,0:T(8,128)(2,1)} %refs_1_.1), channel_id=1, source_target_pairs={{0,8},{4,12},{8,0},{12,4},{16,24},{20,28},{24,16},{28,20},{1,9},{5... | collective-permute-start | bytes 786440 | tf_op jit(solution)/shard_map/ppermute | solution.py:260
  3.1 12.3 %collective-permute-start.2 = (bf16[1024,128]{1,0:T(8,128)(2,1)}, bf16[1024,128]{1,0:T(8,128)(2,1)}, u32[]{:S(2)}, u32[]{:S(2)}) collective-permute-start(bf16[1024,128]{1,0:T(8,128)(2,1)} %refs_0_.1), channel_id=1, source_target_pairs={{0,8},{4,12},{8,0},{12,4},{16,24},{20,28},{24,16},{28,20},{1,9},{5... | collective-permute-start | bytes 786440 | tf_op jit(solution)/shard_map/ppermute | solution.py:260
  3.4 15.0 %collective-permute-start.4 = (bf16[1024,128]{1,0:T(8,128)(2,1)}, bf16[1024,128]{1,0:T(8,128)(2,1)}, u32[]{:S(2)}, u32[]{:S(2)}) collective-permute-start(bf16[1024,128]{1,0:T(8,128)(2,1)} %refs_0_.1), channel_id=1, source_target_pairs={{0,16},{4,20},{8,24},{12,28},{16,0},{20,4},{24,8},{28,12},{1,17},{... | collective-permute-start | bytes 786440 | tf_op jit(solution)/shard_map/ppermute | solution.py:260
  5.8 25.4 %copy-start.6 = (bf16[1024,128]{1,0:T(8,128)(2,1)S(1)}, bf16[1024,128]{1,0:T(8,128)(2,1)}, u32[]{:S(2)}) copy-start(bf16[1024,128]{1,0:T(8,128)(2,1)} %refs_0_.1) | copy-start | bytes 786436
  5.8 25.4 %copy-start.7 = (bf16[1024,128]{1,0:T(8,128)(2,1)S(1)}, bf16[1024,128]{1,0:T(8,128)(2,1)}, u32[]{:S(2)}) copy-start(bf16[1024,128]{1,0:T(8,128)(2,1)} %refs_1_.1) | copy-start | bytes 786436
  9.1 14.3 %copy-start.1 = (bf16[512,512]{1,0:T(8,128)(2,1)S(1)}, bf16[512,512]{1,0:T(8,128)(2,1)}, u32[]{:S(2)}) copy-start(bf16[512,512]{1,0:T(8,128)(2,1)} %get-tuple-element.46.refs_1_) | copy-start | bytes 1572868
  9.1 14.5 %copy-start = (bf16[512,512]{1,0:T(8,128)(2,1)S(1)}, bf16[512,512]{1,0:T(8,128)(2,1)}, u32[]{:S(2)}) copy-start(bf16[512,512]{1,0:T(8,128)(2,1)} %get-tuple-element.45.refs_0_) | copy-start | bytes 1572868
  15.5 7.0 %collective-permute-start.1 = (bf16[256,512]{1,0:T(8,128)(2,1)}, bf16[256,512]{1,0:T(8,128)(2,1)}, u32[]{:S(2)}, u32[]{:S(2)}) collective-permute-start(bf16[256,512]{1,0:T(8,128)(2,1)} %get-tuple-element.29), channel_id=1, source_target_pairs={{0,8},{4,12},{8,0},{12,4},{16,24},{20,28},{24,16},{28,20},{1,9},{5... | collective-permute-start | bytes 786440 | tf_op jit(solution)/shard_map/ppermute | solution.py:260
  16.7 6.7 %collective-permute-start.11 = (bf16[256,512]{1,0:T(8,128)(2,1)}, bf16[256,512]{1,0:T(8,128)(2,1)}, u32[]{:S(2)}, u32[]{:S(2)}) collective-permute-start(bf16[256,512]{1,0:T(8,128)(2,1)} %get-tuple-element.34), channel_id=1, source_target_pairs={{0,16},{4,20},{8,24},{12,28},{16,0},{20,4},{24,8},{28,12},{1,17},{... | collective-permute-start | bytes 786440 | tf_op jit(solution)/shard_map/ppermute | solution.py:260
  17.0 6.4 %copy-start.8 = (bf16[1024,128]{1,0:T(8,128)(2,1)}, bf16[1024,128]{1,0:T(8,128)(2,1)S(1)}, u32[]{:S(2)}) copy-start(bf16[1024,128]{1,0:T(8,128)(2,1)S(1)} %collective-permute-done.3.refs_3_) | copy-start | bytes 786436
  17.1 12.0 %collective-permute-start.6 = (bf16[1024,128]{1,0:T(8,128)(2,1)}, bf16[1024,128]{1,0:T(8,128)(2,1)S(1)}, u32[]{:S(2)}, u32[]{:S(2)}) collective-permute-start(bf16[1024,128]{1,0:T(8,128)(2,1)} %collective-permute-done.2.refs_2_), channel_id=1, source_target_pairs={{0,16},{4,20},{8,24},{12,28},{16,0},{20,4},{24,8},{28,12},{1,17},{... | collective-permute-start | bytes 786440 | tf_op jit(solution)/shard_map/ppermute | solution.py:260
  18.4 12.7 %collective-permute-start.7 = (bf16[1024,128]{1,0:T(8,128)(2,1)}, bf16[1024,128]{1,0:T(8,128)(2,1)}, u32[]{:S(2)}, u32[]{:S(2)}) collective-permute-start(bf16[1024,128]{1,0:T(8,128)(2,1)} %collective-permute-done.5.refs_5_), channel_id=1, source_target_pairs={{0,8},{4,12},{8,0},{12,4},{16,24},{20,28},{24,16},{28,20},{1,9},{5... | collective-permute-start | bytes 786440 | tf_op jit(solution)/shard_map/ppermute | solution.py:260
  23.4 23.1 %collective-permute-start.15 = (bf16[512,512]{1,0:T(8,128)(2,1)S(1)}, bf16[512,512]{1,0:T(8,128)(2,1)S(1)}, u32[]{:S(2)}, u32[]{:S(2)}) collective-permute-start(bf16[512,512]{1,0:T(8,128)(2,1)S(1)} %copy-done.1), channel_id=1, source_target_pairs={{0,16},{4,20},{8,24},{12,28},{16,0},{20,4},{24,8},{28,12},{1,17},{... | collective-permute-start | bytes 1572872 | tf_op jit(solution)/shard_map/ppermute | solution.py:260
  23.7 23.1 %collective-permute-start.13 = (bf16[512,512]{1,0:T(8,128)(2,1)S(1)}, bf16[512,512]{1,0:T(8,128)(2,1)S(1)}, u32[]{:S(2)}, u32[]{:S(2)}) collective-permute-start(bf16[512,512]{1,0:T(8,128)(2,1)S(1)} %copy-done), channel_id=1, source_target_pairs={{0,8},{4,12},{8,0},{12,4},{16,24},{20,28},{24,16},{28,20},{1,9},{5... | collective-permute-start | bytes 1572872 | tf_op jit(solution)/shard_map/ppermute | solution.py:260
  29.7 15.3 %collective-permute-start.10 = (bf16[256,512]{1,0:T(8,128)(2,1)}, bf16[256,512]{1,0:T(8,128)(2,1)S(1)}, u32[]{:S(2)}, u32[]{:S(2)}) collective-permute-start(bf16[256,512]{1,0:T(8,128)(2,1)} %collective-permute-done.1.refs_0_), channel_id=1, source_target_pairs={{0,1},{1,0},{2,3},{3,2},{4,5},{5,4},{6,7},{7,6},{8,9},{9,8},{10,11... | collective-permute-start | bytes 786440 | tf_op jit(solution)/shard_map/ppermute | solution.py:304
  31.0 14.7 %collective-permute-start.12 = (bf16[256,512]{1,0:T(8,128)(2,1)}, bf16[256,512]{1,0:T(8,128)(2,1)S(1)}, u32[]{:S(2)}, u32[]{:S(2)}) collective-permute-start(bf16[256,512]{1,0:T(8,128)(2,1)} %collective-permute-done.11.refs_2_), channel_id=1, source_target_pairs={{0,1},{1,0},{2,3},{3,2},{4,5},{5,4},{6,7},{7,6},{8,9},{9,8},{10,11... | collective-permute-start | bytes 786440 | tf_op jit(solution)/shard_map/ppermute | solution.py:304
  31.2 1.0 %copy-start.9 = (bf16[1024,128]{1,0:T(8,128)(2,1)S(1)}, bf16[1024,128]{1,0:T(8,128)(2,1)}, u32[]{:S(2)}) copy-start(bf16[1024,128]{1,0:T(8,128)(2,1)} %copy-done.8) | copy-start | bytes 786436
  32.2 0.9 %copy-start.15 = (bf16[1024,128]{1,0:T(8,128)(2,1)S(1)}, bf16[1024,128]{1,0:T(8,128)(2,1)}, u32[]{:S(2)}) copy-start(bf16[1024,128]{1,0:T(8,128)(2,1)} %copy-done.14) | copy-start | bytes 786436
  39.6 0.8 copy-start.2
  40.4 6.6 %collective-permute-start.8 = (f32[384,256]{1,0:T(8,128)}, f32[384,256]{1,0:T(8,128)S(1)}, u32[]{:S(2)}, u32[]{:S(2)}) collective-permute-start(f32[384,256]{1,0:T(8,128)} %get-tuple-element.31), channel_id=1, source_target_pairs={{0,4},{4,0},{8,12},{12,8},{16,20},{20,16},{24,28},{28,24},{1,5},{5... | collective-permute-start | bytes 1179656 | tf_op jit(solution)/shard_map/ppermute | solution.py:260
  46.5 13.7 %collective-permute-start.16 = (bf16[512,512]{1,0:T(8,128)(2,1)S(1)}, bf16[512,512]{1,0:T(8,128)(2,1)S(1)}, u32[]{:S(2)}, u32[]{:S(2)}) collective-permute-start(bf16[512,512]{1,0:T(8,128)(2,1)S(1)} %collective-permute-done.15.refs_3_), channel_id=1, source_target_pairs={{0,8},{4,12},{8,0},{12,4},{16,24},{20,28},{24,16},{28,20},{1,9},{5... | collective-permute-start | bytes 1572872 | tf_op jit(solution)/shard_map/ppermute | solution.py:260
  46.7 13.4 %collective-permute-start.14 = (bf16[512,512]{1,0:T(8,128)(2,1)S(1)}, bf16[512,512]{1,0:T(8,128)(2,1)}, u32[]{:S(2)}, u32[]{:S(2)}) collective-permute-start(bf16[512,512]{1,0:T(8,128)(2,1)S(1)} %collective-permute-done.13.refs_2_), channel_id=1, source_target_pairs={{0,16},{4,20},{8,24},{12,28},{16,0},{20,4},{24,8},{28,12},{1,17},{... | collective-permute-start | bytes 1572872 | tf_op jit(solution)/shard_map/ppermute | solution.py:260
  47.0 0.7 copy-start.4
  47.7 1.0 %copy-start.3 = (f32[384,256]{1,0:T(8,128)S(1)}, f32[384,256]{1,0:T(8,128)}, u32[]{:S(2)}) copy-start(f32[384,256]{1,0:T(8,128)} %copy-done.2) | copy-start | bytes 1179652
  48.7 1.0 %copy-start.5 = (f32[384,256]{1,0:T(8,128)S(1)}, f32[384,256]{1,0:T(8,128)}, u32[]{:S(2)}) copy-start(f32[384,256]{1,0:T(8,128)} %copy-done.4) | copy-start | bytes 1179652
  49.8 10.3 %collective-permute-start.9 = (bf16[384,256]{1,0:T(8,128)(2,1)S(1)}, bf16[384,256]{1,0:T(8,128)(2,1)}, u32[]{:S(2)}, u32[]{:S(2)}) collective-permute-start(bf16[384,256]{1,0:T(8,128)(2,1)S(1)} %shard_map.57), channel_id=1, source_target_pairs={{0,1},{1,2},{2,3},{4,5},{5,6},{6,7},{8,9},{9,10},{10,11},{12,13},{... | collective-permute-start | bytes 589832 | tf_op jit(solution)/shard_map/ppermute | solution.py:321
  53.2 6.9 %copy-start.11 = (bf16[256,512]{1,0:T(8,128)(2,1)S(1)}, bf16[256,512]{1,0:T(8,128)(2,1)}, u32[]{:S(2)}) copy-start(bf16[256,512]{1,0:T(8,128)(2,1)} %copy-done.10) | copy-start | bytes 786436
  53.2 6.9 %copy-start.13 = (bf16[256,512]{1,0:T(8,128)(2,1)S(1)}, bf16[256,512]{1,0:T(8,128)(2,1)}, u32[]{:S(2)}) copy-start(bf16[256,512]{1,0:T(8,128)(2,1)} %copy-done.12) | copy-start | bytes 786436
  64.6 10.7 %collective-permute-start.17 = (f32[384,512]{1,0:T(8,128)}, f32[384,512]{1,0:T(8,128)S(1)}, u32[]{:S(2)}, u32[]{:S(2)}) collective-permute-start(f32[384,512]{1,0:T(8,128)} %get-tuple-element.52), channel_id=1, source_target_pairs={{0,4},{4,0},{8,12},{12,8},{16,20},{20,16},{24,28},{28,24},{1,5},{5... | collective-permute-start | bytes 2359304 | tf_op jit(solution)/shard_map/ppermute | solution.py:260
  65.7 8.6 %collective-permute-start.18 = (bf16[384,256]{1,0:T(8,128)(2,1)}, bf16[384,256]{1,0:T(8,128)(2,1)S(1)}, u32[]{:S(2)}, u32[]{:S(2)}) collective-permute-start(bf16[384,256]{1,0:T(8,128)(2,1)} %collective-permute-done.9), channel_id=1, source_target_pairs={{0,1},{1,2},{2,3},{4,5},{5,6},{6,7},{8,9},{9,10},{10,11},{12,13},{... | collective-permute-start | bytes 589832 | tf_op jit(solution)/shard_map/ppermute | solution.py:321
  (3 other events, 2.1 us)

commit v9 on v8

--- a/solution.py
+++ b/solution.py
@@ -36,115 +36,112 @@
     return [pl.BlockSpec(memory_space=pltpu.VMEM)] * count
 
 
-def in_hbm(count):
-    return [pl.BlockSpec(memory_space=pltpu.HBM)] * count
+def anywhere(count):
+    return [pl.BlockSpec(memory_space=pl.ANY)] * count
 
 
 def after(array, *earlier):
     return lax.optimization_barrier((array, *earlier))[0]
 
 
-def copy_all(copies, buffers, sems):
-    loads = []
-    stores = []
-    for i, ((source, target), buffer) in enumerate(zip(copies, buffers)):
-        loads.append(pltpu.make_async_copy(source, buffer, sems.at[0, i]))
-        stores.append(pltpu.make_async_copy(buffer, target, sems.at[1, i]))
-    for load in loads:
-        load.start()
-    for load, store in zip(loads, stores):
-        load.wait()
-        store.start()
-    for store in stores:
-        store.wait()
-
-
-def cut_kernel(places, query, *refs):
-    pieces, buffers, sems = refs[: len(refs) // 2], refs[len(refs) // 2 : -1], refs[-1]
+def cut_kernel(chips, places, query, tokens, *refs):
+    *pieces, columns, sems = refs
+    depth = query.shape[0]
     copies = []
     for i, piece in enumerate(pieces):
-        rows = pl.ds(pl.multiple_of(places[i], 16), piece.shape[0])
+        rows = pl.ds(pl.multiple_of(places[chips + i], 16), piece.shape[0])
         copies.append((query.at[rows], piece))
-    copy_all(copies, buffers, sems)
-
-
-def copy_call(kernel, places, arrays, shapes, buffers):
+    for chip in range(chips):
+        window = pl.ds(pl.multiple_of(places[chip], 128), depth)
+        copies.append((tokens.at[:, window], columns.at[:, chip * depth : (chip + 1) * depth]))
+    copies = [pltpu.make_async_copy(*copy, sems.at[i]) for i, copy in enumerate(copies)]
+    for copy in copies:
+        copy.start()
+    for copy in copies:
+        copy.wait()
+
+
+def cut(places, query, tokens, shapes):
+    depth = query.shape[0]
+    chips = len(places) - len(shapes)
+    shapes = shapes + [(tokens.shape[0], chips * depth)]
     return pl.pallas_call(
-        kernel,
-        out_shape=[jax.ShapeDtypeStruct(shape, jnp.bfloat16) for shape in shapes],
-        in_specs=[pl.BlockSpec(memory_space=pltpu.SMEM)] + in_hbm(len(arrays)),
-        out_specs=in_hbm(len(shapes)),
-        scratch_shapes=[pltpu.VMEM(shape, jnp.bfloat16) for shape in buffers]
-        + [pltpu.SemaphoreType.DMA((2, len(buffers)))],
-        compiler_params=pltpu.CompilerParams(vmem_limit_bytes=63 * MIB),
+        functools.partial(cut_kernel, chips),
+        out_shape=[jax.ShapeDtypeStruct(shape, query.dtype) for shape in shapes],
+        in_specs=[pl.BlockSpec(memory_space=pltpu.SMEM)] + anywhere(2),
+        out_specs=vmem(len(shapes)),
+        scratch_shapes=[pltpu.SemaphoreType.DMA((len(places),))],
+        compiler_params=pltpu.CompilerParams(vmem_limit_bytes=40 * MIB),
         cost_estimate=pl.CostEstimate(
             flops=0,
             bytes_accessed=4 * sum(math.prod(shape) for shape in shapes),
             transcendentals=0,
         ),
-    )(places, *arrays)
+    )(jnp.stack([jnp.int32(place) for place in places]), query, tokens)
 
 
 def project_kernel(steps, starts, near, far, *refs):
     count = sum(len(spots) for _, spots in steps)
     weights, refs = refs[:count], refs[count:]
-    *carry, far_out, near_out, tokens, held, sems = refs
-    rows = near.shape[0]
-    batches = ([], [], [])
+    *carry, far_out, near_out, held, sems = refs
+    batches = []
     used = row = 0
     for step, (depth, spots) in enumerate(steps):
-        here = slice(row, row + depth)
-        row += depth
+        batch = []
         for index, columns in enumerate(spots):
-            batches[0].append(
+            batch.append(
                 pltpu.make_async_copy(
-                    weights[used], held.at[here, columns], sems.at[step, 2 + index]
+                    weights[used], held.at[row : row + depth, columns], sems.at[step, index]
                 )
             )
+            batch[-1].start()
             used += 1
-        window = pl.ds(pl.multiple_of(starts[step], 128), depth)
+        batches.append((row, depth, batch))
+        row += depth
+    totals = [ref[...] for ref in carry]
+    for step, (row, depth, batch) in enumerate(batches):
+        for copy in batch:
+            copy.wait()
+        terms = []
         for side, ref in enumerate((far, near)):
-            batches[1 + side].append(
-                pltpu.make_async_copy(
-                    ref.at[:, window], tokens.at[side, :, here], sems.at[step, side]
+            window = pl.ds(pl.multiple_of(starts[side, step], 128), depth)
+            terms.append(
+                jnp.dot(
+                    ref[:, window],
+                    held[row : row + depth, :],
+                    preferred_element_type=jnp.float32,
                 )
             )
-    for batch in batches:
-        for copy in batch:
-            copy.start()
-    for copy in batches[0]:
-        copy.wait()
-    for side, out in enumerate((far_out, near_out)):
-        for copy in batches[1 + side]:
-            copy.wait()
-        total = jnp.dot(tokens[side], held[...], preferred_element_type=jnp.float32)
-        out[...] = total + carry[side][...] if carry else total
+        totals = [total + term for total, term in zip(totals, terms)] if totals else terms
+    far_out[...], near_out[...] = totals
 
 
 def project(terms, near, far, carry=()):
     rows = near.shape[0]
     width = sum(array.shape[1] for array in terms[0][0])
     steps = []
-    for arrays, _ in terms:
+    for arrays, *_ in terms:
         edges = [sum(array.shape[1] for array in arrays[:i]) for i in range(len(arrays) + 1)]
         spots = [slice(*edge) for edge in zip(edges[:-1], edges[1:])]
         steps.append((arrays[0].shape[0], spots))
     depth = sum(step[0] for step in steps)
-    starts = jnp.stack([jnp.int32(start) for _, start in terms])
-    weights = [array for arrays, _ in terms for array in arrays]
+    starts = jnp.stack(
+        [jnp.stack([jnp.int32(term[1 + side]) for term in terms]) for side in range(2)]
+    )
+    weights = [array for arrays, *_ in terms for array in arrays]
     return pl.pallas_call(
         functools.partial(project_kernel, steps),
         out_shape=[jax.ShapeDtypeStruct((rows, width), jnp.float32)] * 2,
         in_specs=[pl.BlockSpec(memory_space=pltpu.SMEM)]
-        + in_hbm(2 + len(weights))
+        + vmem(2)
+        + anywhere(len(weights))
         + vmem(len(carry)),
         out_specs=vmem(2),
         scratch_shapes=[
-            pltpu.VMEM((2, rows, depth), jnp.bfloat16),
             pltpu.VMEM((depth, width), jnp.bfloat16),
-            pltpu.SemaphoreType.DMA((len(steps), 4)),
+            pltpu.SemaphoreType.DMA((len(steps), 2)),
         ],
-        compiler_params=pltpu.CompilerParams(vmem_limit_bytes=48 * MIB),
+        compiler_params=pltpu.CompilerParams(vmem_limit_bytes=32 * MIB),
         cost_estimate=pl.CostEstimate(
             flops=4 * rows * width * depth,
             bytes_accessed=2 * depth * (2 * rows + width),
@@ -287,14 +284,16 @@
 
     pair_held = fetch((w_key, w_value), [{}, {}], [], [])
     far_tokens = swap(hidden, 1)
-    rows = [0, half] + ([begin, half + begin] if halved else [])
-    shapes = [(half, query_width)] * 2 + [(some, query_width)] * (len(rows) - 2)
-    places = jnp.stack([jnp.int32(row) for row in rows])
-    halves = copy_call(cut_kernel, places, [w_query], shapes, shapes)
+    places = [(me ^ (2 * chip)) * depth for chip in range(chips)] + [0, half]
+    shapes = [(half, query_width)] * 2
+    if halved:
+        places += [begin, half + begin]
+        shapes += [(some, query_width)] * 2
+    *halves, near_tokens = cut(places, w_query, hidden, shapes)
     parts = halves[2:]
 
     def term(arrays, chip, row):
-        return (arrays, (me ^ (2 * chip)) * depth + row)
+        return (arrays, places[chip] + row, chip * depth + row)
 
     direct = [pair_held[side][chip][0][1] for side in range(2) for chip in axes]
     gate = [*direct, cosine, sine, first]
@@ -309,7 +308,7 @@
     pair_terms = [
         term([pair_held[side][chip][0][1] for side in range(2)], chip, 0) for chip in range(chips)
     ]
-    far, near = project(pair_terms, hidden, far_tokens)
+    far, near = project(pair_terms, near_tokens, far_tokens)
     query_held = fetch(halves[:2], given, [*gate, *mine], [near, *other])
 
     pair = finish_pair(near, swap(far, 1), cosine, sine)
@@ -331,8 +330,8 @@
     everything = [(side, chip) for chip in range(chips) for side in range(2)]
     early = [(0, 0), (1, 0), (0, axes[0]), (1, axes[-1])]
     late = [wanted for wanted in everything if wanted not in early]
-    carry = project(query_terms(early, pair), hidden, far_tokens)
-    far, near = project(query_terms(late, blocks[-2]), hidden, far_tokens, carry)
+    carry = project(query_terms(early, pair), near_tokens, far_tokens)
+    far, near = project(query_terms(late, blocks[-2]), near_tokens, far_tokens, carry)
     return attend(near, swap(far, 1), cosine, sine, first, keys_values, back)[None]
 
 

time: 80.1 us -> 80 us (level)
  waiting for transfers between devices: 23.2 us -> 21.2 us
  local copies, waits for them, and re-layouts: 7.75 us -> 9.03 us
  Pallas kernels: 22.2 us -> 23.4 us
    pallas_call x3, Pallas kernels: 15.1 us -> 17.6 us  [project(): pl.pallas_call(functools.partial(project_kernel, steps), out_shape=[jax.S...]
    pallas_call x1, Pallas kernels: 3.31 us -> 1.03 us  [cut(): pl.pallas_call(functools.partial(cut_kernel, chips), out_shape=[jax.Shape...]
    ppermute x15, waiting for transfers between devices: 18 us -> 16.1 us  [swap(): return lax.ppermute(array, 'dp', [(i, i ^ mask) for i in range(dp_size)])]
    unnamed x32 -> x50, local copies, waits for them, and re-layouts: 7.53 us -> 8.64 us
    pallas_call x1, Pallas kernels: 0.12 us -> 1.14 us  [finish_pair(): pl.pallas_call(pair_kernel, out_shape=jax.ShapeDtypeStruct(near.shape, jn...]
  transfers between devices with their start and end apart: 19 -> 19, of which waited for: 6 -> 6; matrix products, arithmetic and copies ran while one was open for 6% -> 5% of each run, Pallas kernels for 18% -> 18%
where the time goes in v9:
time: 80 us; the launch traced here: 78.7 us
  Pallas kernels  23.4 us (29%)
  waiting for transfers between devices  21.2 us (26%)
  starting transfers between devices  20.8 us (26%)
  local copies, waits for them, and re-layouts  9.03 us (11%)
  other arithmetic  3.84 us (5%)
    pallas_call x3, Pallas kernels, project(): pl.pallas_call(functools.partial(project_kernel, steps), out_shape=[jax.S...  17.6 us
    ppermute x15, waiting for transfers between devices, swap(): return lax.ppermute(array, 'dp', [(i, i ^ mask) for i in range(dp_size)])  16.1 us
    ppermute x15, starting transfers between devices, swap(): return lax.ppermute(array, 'dp', [(i, i ^ mask) for i in range(dp_size)])  13 us
    unnamed x50, local copies, waits for them, and re-layouts  8.64 us
    ppermute x2, starting transfers between devices, shards(): lax.ppermute(blocks[0], 'ctx', [(i, i + 1) for i in range(ctx_size - 1)])  6.4 us
    ppermute x2, waiting for transfers between devices, shards(): lax.ppermute(blocks[0], 'ctx', [(i, i + 1) for i in range(ctx_size - 1)])  5.12 us
    pallas_call x1, Pallas kernels, attend(): pl.pallas_call(functools.partial(attend_kernel, back), out_shape=jax.Shap...  3.65 us
  transfers between devices with their start and end apart: 19, of which 6 were waited for; matrix products, arithmetic and copies ran while one was open for 5% of the time, Pallas kernels for 18%

profile of v9, /device:TPU:17, one launch (start us, length us, event | category | flops | bytes accessed | tf_op | source)
XLA Modules:
  0.0 78.7 jit_solution(13812990916589460518)
XLA Ops:
  0.0 0.7 collective-permute-start
  0.7 1.2 %collective-permute-start.5 = (bf16[1024,128]{1,0:T(8,128)(2,1)}, bf16[1024,128]{1,0:T(8,128)(2,1)S(1)}, u32[]{:S(2)}, u32[]{:S(2)}) collective-permute-start(bf16[1024,128]{1,0:T(8,128)(2,1)} %refs_1_.1), channel_id=1, source_target_pairs={{0,16},{4,20},{8,24},{12,28},{16,0},{20,4},{24,8},{28,12},{1,17},{... | collective-permute-start | bytes 786440 | tf_op jit(solution)/shard_map/ppermute | solution.py:257
  1.9 1.2 %collective-permute-start.3 = (bf16[1024,128]{1,0:T(8,128)(2,1)}, bf16[1024,128]{1,0:T(8,128)(2,1)}, u32[]{:S(2)}, u32[]{:S(2)}) collective-permute-start(bf16[1024,128]{1,0:T(8,128)(2,1)} %refs_1_.1), channel_id=1, source_target_pairs={{0,8},{4,12},{8,0},{12,4},{16,24},{20,28},{24,16},{28,20},{1,9},{5... | collective-permute-start | bytes 786440 | tf_op jit(solution)/shard_map/ppermute | solution.py:257
  3.6 0.8 %reduce-window_clone.1 = s32[1,16]{1,0:T(1,128)S(1)} reduce-window(s32[1,16]{1,0:T(1,128)} %param.9, s32[]{:T(128)} %constant.21.clone.1), window={size=1x16 pad=0_0x15_0}, to_apply=%region_0.0 | reduce-window | flops 240 | bytes 132 | tf_op jit(solution)/shard_map/reduce-window.clone
  5.3 2.8 %copy-done = bf16[1,384,8192]{2,1,0:T(8,128)(2,1)S(1)} copy-done((bf16[1,384,8192]{2,1,0:T(8,128)(2,1)S(1)}, bf16[1,384,8192]{2,1,0:T(8,128)(2,1)}, u32[]{:S(2)}) %copy-start) | copy-done | bytes 6291480
  8.1 1.2 %copy-done.1 = bf16[1024,512]{1,0:T(8,128)(2,1)S(1)} copy-done((bf16[1024,512]{1,0:T(8,128)(2,1)S(1)}, bf16[1024,512]{1,0:T(8,128)(2,1)}, u32[]{:S(2)}) %copy-start.1) | copy-done | bytes 1048600
  9.3 1.0 %shard_map.55 = (bf16[512,512]{1,0:T(8,128)(2,1)S(1)}, bf16[512,512]{1,0:T(8,128)(2,1)S(1)}, bf16[256,512]{1,0:T(8,128)(2,1)S(1)}, bf16[256,512]{1,0:T(8,128)(2,1)S(1)}, bf16[384,4096]{1,0:T(8,128)(2,1)S(1)}) custom-call(s32[8]{0:T(128)S(1)} %stack.114.places, bf16[1024,512]{1,0:T(8,128)(2,1)S(1)} %copy-done.1, bf16[384,8192]{1,0:T(8,128)(2,1)S(1)} %bitcast.28), custom_call_target="tpu_custom_call" | custom-call | bytes 9437184 | tf_op jit(solution)/shard_map/pallas_call | solution.py:68
  10.4 0.8 fusion
  11.2 4.3 %collective-permute-done.2.refs_2_ = bf16[1024,128]{1,0:T(8,128)(2,1)} collective-permute-done((bf16[1024,128]{1,0:T(8,128)(2,1)}, bf16[1024,128]{1,0:T(8,128)(2,1)}, u32[]{:S(2)}, u32[]{:S(2)}) %collective-permute-start.2) | collective-permute-done | bytes 262176 | tf_op jit(solution)/shard_map/ppermute | solution.py:257
  15.5 1.2 %collective-permute-start.1 = (bf16[256,512]{1,0:T(8,128)(2,1)S(1)}, bf16[256,512]{1,0:T(8,128)(2,1)S(1)}, u32[]{:S(2)}, u32[]{:S(2)}) collective-permute-start(bf16[256,512]{1,0:T(8,128)(2,1)S(1)} %get-tuple-element.31), channel_id=1, source_target_pairs={{0,8},{4,12},{8,0},{12,4},{16,24},{20,28},{24,16},{28,20},{1,9},{5... | collective-permute-start | bytes 786440 | tf_op jit(solution)/shard_map/ppermute | solution.py:257
  17.5 0.8 %collective-permute-start.6 = (bf16[1024,128]{1,0:T(8,128)(2,1)}, bf16[1024,128]{1,0:T(8,128)(2,1)S(1)}, u32[]{:S(2)}, u32[]{:S(2)}) collective-permute-start(bf16[1024,128]{1,0:T(8,128)(2,1)} %collective-permute-done.2.refs_2_), channel_id=1, source_target_pairs={{0,16},{4,20},{8,24},{12,28},{16,0},{20,4},{24,8},{28,12},{1,17},{... | collective-permute-start | bytes 786440 | tf_op jit(solution)/shard_map/ppermute | solution.py:257
  18.8 3.4 %collective-permute-done.1.refs_0_ = bf16[256,512]{1,0:T(8,128)(2,1)S(1)} collective-permute-done((bf16[256,512]{1,0:T(8,128)(2,1)S(1)}, bf16[256,512]{1,0:T(8,128)(2,1)S(1)}, u32[]{:S(2)}, u32[]{:S(2)}) %collective-permute-start.1) | collective-permute-done | bytes 262176 | tf_op jit(solution)/shard_map/ppermute | solution.py:257
  22.2 0.9 %collective-permute-done.11.refs_2_ = bf16[256,512]{1,0:T(8,128)(2,1)S(1)} collective-permute-done((bf16[256,512]{1,0:T(8,128)(2,1)S(1)}, bf16[256,512]{1,0:T(8,128)(2,1)S(1)}, u32[]{:S(2)}, u32[]{:S(2)}) %collective-permute-start.11) | collective-permute-done | bytes 262176 | tf_op jit(solution)/shard_map/ppermute | solution.py:257
  23.8 5.0 %collective-permute-done.6.refs_6_ = bf16[1024,128]{1,0:T(8,128)(2,1)S(1)} collective-permute-done((bf16[1024,128]{1,0:T(8,128)(2,1)}, bf16[1024,128]{1,0:T(8,128)(2,1)S(1)}, u32[]{:S(2)}, u32[]{:S(2)}) %collective-permute-start.6) | collective-permute-done | bytes 262176 | tf_op jit(solution)/shard_map/ppermute | solution.py:257
  28.7 1.3 %collective-permute-start.10 = (bf16[256,512]{1,0:T(8,128)(2,1)S(1)}, bf16[256,512]{1,0:T(8,128)(2,1)S(1)}, u32[]{:S(2)}, u32[]{:S(2)}) collective-permute-start(bf16[256,512]{1,0:T(8,128)(2,1)S(1)} %collective-permute-done.1.refs_0_), channel_id=1, source_target_pairs={{0,1},{1,0},{2,3},{3,2},{4,5},{5,4},{6,7},{7,6},{8,9},{9,8},{10,11... | collective-permute-start | bytes 786440 | tf_op jit(solution)/shard_map/ppermute | solution.py:303
  30.2 6.6 %shard_map.56 = (f32[384,256]{1,0:T(8,128)}, f32[384,256]{1,0:T(8,128)S(1)}) custom-call(s32[2,4]{1,0:T(2,128)S(1)} %pad_add_fusion.1.starts, bf16[384,4096]{1,0:T(8,128)(2,1)S(1)} %get-tuple-element.30.near, bf16[384,8192]{1,0:T(8,128)(2,1)} %collective-permute-done.far, bf16[1024,128]{1,0:T(8,128)(2,1)S(1)} %copy-done.11, ...), custom_call_target="tpu_custom_call" | custom-call | flops 1610612736 | bytes 8388608 | tf_op jit(solution)/shard_map/pallas_call | solution.py:132
  36.9 0.7 copy-done.9
  37.6 4.8 %collective-permute-start.8 = (f32[384,256]{1,0:T(8,128)}, f32[384,256]{1,0:T(8,128)}, u32[]{:S(2)}, u32[]{:S(2)}) collective-permute-start(f32[384,256]{1,0:T(8,128)} %get-tuple-element.33), channel_id=1, source_target_pairs={{0,4},{4,0},{8,12},{12,8},{16,20},{20,16},{24,28},{28,24},{1,5},{5... | collective-permute-start | bytes 1179656 | tf_op jit(solution)/shard_map/ppermute | solution.py:257
  42.4 0.7 copy-done.19
  43.1 0.7 copy-done.21
  44.6 1.1 %copy-done.10 = f32[384,256]{1,0:T(8,128)S(1)} copy-done((f32[384,256]{1,0:T(8,128)S(1)}, f32[384,256]{1,0:T(8,128)}, u32[]{:S(2)}) %copy-start.10) | copy-done | bytes 393240
  45.6 1.1 %shard_map.57 = bf16[384,256]{1,0:T(8,128)(2,1)S(1)} custom-call(f32[384,256]{1,0:T(8,128)S(1)} %copy-done.10, f32[384,256]{1,0:T(8,128)} %collective-permute-done.8.far, f32[384,128]{1,0:T(8,128)S(1)} %pad_maximum_fusion.1.cosine, f32[384,128]{1,0:T(8,128)S(1)} %pad_maximum_fusion.2.sine), custom_call_target="tpu_custom_call" | custom-call | flops 589824 | bytes 1376256 | tf_op jit(solution)/shard_map/pallas_call | solution.py:165
  46.8 3.2 %collective-permute-start.9 = (bf16[384,256]{1,0:T(8,128)(2,1)S(1)}, bf16[384,256]{1,0:T(8,128)(2,1)}, u32[]{:S(2)}, u32[]{:S(2)}) collective-permute-start(bf16[384,256]{1,0:T(8,128)(2,1)S(1)} %shard_map.57), channel_id=1, source_target_pairs={{0,1},{1,2},{2,3},{4,5},{5,6},{6,7},{8,9},{9,10},{10,11},{12,13},{... | collective-permute-start | bytes 589832 | tf_op jit(solution)/shard_map/ppermute | solution.py:320
  50.1 5.1 %shard_map.58 = (f32[384,512]{1,0:T(8,128)S(1)}, f32[384,512]{1,0:T(8,128)S(1)}) custom-call(s32[2,4]{1,0:T(2,128)S(1)} %pad_add_fusion.2.starts, bf16[384,4096]{1,0:T(8,128)(2,1)S(1)} %get-tuple-element.30.near, bf16[384,8192]{1,0:T(8,128)(2,1)} %collective-permute-done.far, bf16[512,512]{1,0:T(8,128)(2,1)S(1)} %copy-done.6, ...), custom_call_target="tpu_custom_call" | custom-call | flops 1610612736 | bytes 5242880 | tf_op jit(solution)/shard_map/pallas_call | solution.py:132
  55.2 2.5 %collective-permute-done.16.refs_5_ = bf16[512,512]{1,0:T(8,128)(2,1)} collective-permute-done((bf16[512,512]{1,0:T(8,128)(2,1)}, bf16[512,512]{1,0:T(8,128)(2,1)}, u32[]{:S(2)}, u32[]{:S(2)}) %collective-permute-start.16) | collective-permute-done | bytes 524320 | tf_op jit(solution)/shard_map/ppermute | solution.py:257
  57.7 5.8 %shard_map.59 = (f32[384,512]{1,0:T(8,128)}, f32[384,512]{1,0:T(8,128)S(1)}) custom-call(s32[2,6]{1,0:T(2,128)S(1)} %pad_add_fusion.starts, bf16[384,4096]{1,0:T(8,128)(2,1)S(1)} %get-tuple-element.30.near, bf16[384,8192]{1,0:T(8,128)(2,1)} %collective-permute-done.far, bf16[256,512]{1,0:T(8,128)(2,1)S(1)} %copy-done.16, bf16[256,512]{1,0:T(8,128)(2,1)S(1)} %copy-done.20, ...), custom_call_target="tpu_custom_call" | custom-call | flops 1610612736 | bytes 5242880 | tf_op jit(solution)/shard_map/pallas_call | solution.py:132
  63.6 0.9 %copy-done.2 = f32[384,512]{1,0:T(8,128)} copy-done((f32[384,512]{1,0:T(8,128)}, f32[384,512]{1,0:T(8,128)S(1)}, u32[]{:S(2)}) %copy-start.2) | copy-done | bytes 786456
  64.5 1.0 %collective-permute-start.17 = (f32[384,512]{1,0:T(8,128)}, f32[384,512]{1,0:T(8,128)S(1)}, u32[]{:S(2)}, u32[]{:S(2)}) collective-permute-start(f32[384,512]{1,0:T(8,128)} %get-tuple-element.54), channel_id=1, source_target_pairs={{0,4},{4,0},{8,12},{12,8},{16,20},{20,16},{24,28},{28,24},{1,5},{5... | collective-permute-start | bytes 2359304 | tf_op jit(solution)/shard_map/ppermute | solution.py:257
  65.5 3.2 %collective-permute-start.18 = (bf16[384,256]{1,0:T(8,128)(2,1)}, bf16[384,256]{1,0:T(8,128)(2,1)S(1)}, u32[]{:S(2)}, u32[]{:S(2)}) collective-permute-start(bf16[384,256]{1,0:T(8,128)(2,1)} %collective-permute-done.9), channel_id=1, source_target_pairs={{0,1},{1,2},{2,3},{4,5},{5,6},{6,7},{8,9},{9,10},{10,11},{12,13},{... | collective-permute-start | bytes 589832 | tf_op jit(solution)/shard_map/ppermute | solution.py:320
  68.8 5.1 %collective-permute-done.18 = bf16[384,256]{1,0:T(8,128)(2,1)S(1)} collective-permute-done((bf16[384,256]{1,0:T(8,128)(2,1)}, bf16[384,256]{1,0:T(8,128)(2,1)S(1)}, u32[]{:S(2)}, u32[]{:S(2)}) %collective-permute-start.18) | collective-permute-done | bytes 196640 | tf_op jit(solution)/shard_map/ppermute | solution.py:320
  74.0 1.1 %pad_maximum_fusion.keys_values = bf16[1152,256]{1,0:T(8,128)(2,1)S(1)} fusion(bf16[384,256]{1,0:T(8,128)(2,1)} %copy-done.4, bf16[384,256]{1,0:T(8,128)(2,1)} %collective-permute-done.9, bf16[384,256]{1,0:T(8,128)(2,1)S(1)} %collective-permute-done.18), kind=kLoop, calls=%fused_computation | loop fusion | flops 1769472 | bytes 1179648 | tf_op jit(solution)/shard_map/concatenate | solution.py:321
  75.0 3.6 %shard_map.60 = bf16[384,512]{1,0:T(8,128)(2,1)} custom-call(f32[384,512]{1,0:T(8,128)S(1)} %copy-done.3, f32[384,512]{1,0:T(8,128)S(1)} %collective-permute-done.17.far, f32[384,128]{1,0:T(8,128)S(1)} %pad_maximum_fusion.1.cosine, f32[384,128]{1,0:T(8,128)S(1)} %pad_maximum_fusion.2.sine, s32[384,1]{1,0:T(8,128)S(1)} %copy.7.first, ...), custom_call_target="tpu_custom_call" | custom-call | flops 704643072 | bytes 1572864 | tf_op jit(solution)/shard_map/pallas_call | solution.py:227
  (82 shorter events, 4.3 us)
Async XLA Ops:
  0.0 30.2 %collective-permute-start = (bf16[384,8192]{1,0:T(8,128)(2,1)}, bf16[384,8192]{1,0:T(8,128)(2,1)}, u32[]{:S(2)}, u32[]{:S(2)}) collective-permute-start(bf16[384,8192]{1,0:T(8,128)(2,1)} %bitcast.27), channel_id=1, source_target_pairs={{0,4},{4,0},{8,12},{12,8},{16,20},{20,16},{24,28},{28,24},{1,5},{5... | collective-permute-start | bytes 18874376 | tf_op jit(solution)/shard_map/ppermute | solution.py:257
  0.7 16.0 %collective-permute-start.5 = (bf16[1024,128]{1,0:T(8,128)(2,1)}, bf16[1024,128]{1,0:T(8,128)(2,1)S(1)}, u32[]{:S(2)}, u32[]{:S(2)}) collective-permute-start(bf16[1024,128]{1,0:T(8,128)(2,1)} %refs_1_.1), channel_id=1, source_target_pairs={{0,16},{4,20},{8,24},{12,28},{16,0},{20,4},{24,8},{28,12},{1,17},{... | collective-permute-start | bytes 786440 | tf_op jit(solution)/shard_map/ppermute | solution.py:257
  1.9 15.6 %collective-permute-start.3 = (bf16[1024,128]{1,0:T(8,128)(2,1)}, bf16[1024,128]{1,0:T(8,128)(2,1)}, u32[]{:S(2)}, u32[]{:S(2)}) collective-permute-start(bf16[1024,128]{1,0:T(8,128)(2,1)} %refs_1_.1), channel_id=1, source_target_pairs={{0,8},{4,12},{8,0},{12,4},{16,24},{20,28},{24,16},{28,20},{1,9},{5... | collective-permute-start | bytes 786440 | tf_op jit(solution)/shard_map/ppermute | solution.py:257
  3.1 12.3 %collective-permute-start.2 = (bf16[1024,128]{1,0:T(8,128)(2,1)}, bf16[1024,128]{1,0:T(8,128)(2,1)}, u32[]{:S(2)}, u32[]{:S(2)}) collective-permute-start(bf16[1024,128]{1,0:T(8,128)(2,1)} %refs_0_.1), channel_id=1, source_target_pairs={{0,8},{4,12},{8,0},{12,4},{16,24},{20,28},{24,16},{28,20},{1,9},{5... | collective-permute-start | bytes 786440 | tf_op jit(solution)/shard_map/ppermute | solution.py:257
  3.4 15.0 %collective-permute-start.4 = (bf16[1024,128]{1,0:T(8,128)(2,1)}, bf16[1024,128]{1,0:T(8,128)(2,1)}, u32[]{:S(2)}, u32[]{:S(2)}) collective-permute-start(bf16[1024,128]{1,0:T(8,128)(2,1)} %refs_0_.1), channel_id=1, source_target_pairs={{0,16},{4,20},{8,24},{12,28},{16,0},{20,4},{24,8},{28,12},{1,17},{... | collective-permute-start | bytes 786440 | tf_op jit(solution)/shard_map/ppermute | solution.py:257
  10.4 26.5 %copy-start.5 = (bf16[512,512]{1,0:T(8,128)(2,1)}, bf16[512,512]{1,0:T(8,128)(2,1)S(1)}, u32[]{:S(2)}) copy-start(bf16[512,512]{1,0:T(8,128)(2,1)S(1)} %get-tuple-element.47.refs_0_) | copy-start | bytes 1572868
  10.4 26.5 %copy-start.7 = (bf16[512,512]{1,0:T(8,128)(2,1)}, bf16[512,512]{1,0:T(8,128)(2,1)S(1)}, u32[]{:S(2)}) copy-start(bf16[512,512]{1,0:T(8,128)(2,1)S(1)} %get-tuple-element.48.refs_1_) | copy-start | bytes 1572868
  10.4 13.4 %copy-start.24 = (s32[1,4]{1,0:T(1,128)S(1)}, s32[1,4]{1,0:T(1,128)}, u32[]{:S(2)}) copy-start(s32[1,4]{1,0:T(1,128)} %constant.60.clone.1) | copy-start | bytes 52
  10.4 19.8 %copy-start.11 = (bf16[1024,128]{1,0:T(8,128)(2,1)S(1)}, bf16[1024,128]{1,0:T(8,128)(2,1)}, u32[]{:S(2)}) copy-start(bf16[1024,128]{1,0:T(8,128)(2,1)} %refs_0_.1) | copy-start | bytes 786436
  10.4 19.8 %copy-start.12 = (bf16[1024,128]{1,0:T(8,128)(2,1)S(1)}, bf16[1024,128]{1,0:T(8,128)(2,1)}, u32[]{:S(2)}) copy-start(bf16[1024,128]{1,0:T(8,128)(2,1)} %refs_1_.1) | copy-start | bytes 786436
  15.5 6.7 %collective-permute-start.1 = (bf16[256,512]{1,0:T(8,128)(2,1)S(1)}, bf16[256,512]{1,0:T(8,128)(2,1)S(1)}, u32[]{:S(2)}, u32[]{:S(2)}) collective-permute-start(bf16[256,512]{1,0:T(8,128)(2,1)S(1)} %get-tuple-element.31), channel_id=1, source_target_pairs={{0,8},{4,12},{8,0},{12,4},{16,24},{20,28},{24,16},{28,20},{1,9},{5... | collective-permute-start | bytes 786440 | tf_op jit(solution)/shard_map/ppermute | solution.py:257
  16.7 6.4 %collective-permute-start.11 = (bf16[256,512]{1,0:T(8,128)(2,1)S(1)}, bf16[256,512]{1,0:T(8,128)(2,1)S(1)}, u32[]{:S(2)}, u32[]{:S(2)}) collective-permute-start(bf16[256,512]{1,0:T(8,128)(2,1)S(1)} %get-tuple-element.36), channel_id=1, source_target_pairs={{0,16},{4,20},{8,24},{12,28},{16,0},{20,4},{24,8},{28,12},{1,17},{... | collective-permute-start | bytes 786440 | tf_op jit(solution)/shard_map/ppermute | solution.py:257
  17.4 12.8 %copy-start.14 = (bf16[1024,128]{1,0:T(8,128)(2,1)S(1)}, bf16[1024,128]{1,0:T(8,128)(2,1)}, u32[]{:S(2)}) copy-start(bf16[1024,128]{1,0:T(8,128)(2,1)} %copy-done.13) | copy-start | bytes 786436
  17.5 11.2 %collective-permute-start.6 = (bf16[1024,128]{1,0:T(8,128)(2,1)}, bf16[1024,128]{1,0:T(8,128)(2,1)S(1)}, u32[]{:S(2)}, u32[]{:S(2)}) collective-permute-start(bf16[1024,128]{1,0:T(8,128)(2,1)} %collective-permute-done.2.refs_2_), channel_id=1, source_target_pairs={{0,16},{4,20},{8,24},{12,28},{16,0},{20,4},{24,8},{28,12},{1,17},{... | collective-permute-start | bytes 786440 | tf_op jit(solution)/shard_map/ppermute | solution.py:257
  18.4 11.7 %collective-permute-start.7 = (bf16[1024,128]{1,0:T(8,128)(2,1)}, bf16[1024,128]{1,0:T(8,128)(2,1)S(1)}, u32[]{:S(2)}, u32[]{:S(2)}) collective-permute-start(bf16[1024,128]{1,0:T(8,128)(2,1)} %copy-done.13), channel_id=1, source_target_pairs={{0,8},{4,12},{8,0},{12,4},{16,24},{20,28},{24,16},{28,20},{1,9},{5... | collective-permute-start | bytes 786440 | tf_op jit(solution)/shard_map/ppermute | solution.py:257
  22.2 14.7 %copy-start.15 = (bf16[256,512]{1,0:T(8,128)(2,1)}, bf16[256,512]{1,0:T(8,128)(2,1)S(1)}, u32[]{:S(2)}) copy-start(bf16[256,512]{1,0:T(8,128)(2,1)S(1)} %collective-permute-done.1.refs_0_) | copy-start | bytes 786436
  23.1 13.8 %copy-start.17 = (bf16[256,512]{1,0:T(8,128)(2,1)}, bf16[256,512]{1,0:T(8,128)(2,1)S(1)}, u32[]{:S(2)}) copy-start(bf16[256,512]{1,0:T(8,128)(2,1)S(1)} %collective-permute-done.11.refs_2_) | copy-start | bytes 786436
  23.1 20.7 %collective-permute-start.15 = (bf16[512,512]{1,0:T(8,128)(2,1)S(1)}, bf16[512,512]{1,0:T(8,128)(2,1)}, u32[]{:S(2)}, u32[]{:S(2)}) collective-permute-start(bf16[512,512]{1,0:T(8,128)(2,1)S(1)} %get-tuple-element.48.refs_1_), channel_id=1, source_target_pairs={{0,16},{4,20},{8,24},{12,28},{16,0},{20,4},{24,8},{28,12},{1,17},{... | collective-permute-start | bytes 1572872 | tf_op jit(solution)/shard_map/ppermute | solution.py:257
  23.3 20.7 %collective-permute-start.13 = (bf16[512,512]{1,0:T(8,128)(2,1)S(1)}, bf16[512,512]{1,0:T(8,128)(2,1)}, u32[]{:S(2)}, u32[]{:S(2)}) collective-permute-start(bf16[512,512]{1,0:T(8,128)(2,1)S(1)} %get-tuple-element.47.refs_0_), channel_id=1, source_target_pairs={{0,8},{4,12},{8,0},{12,4},{16,24},{20,28},{24,16},{28,20},{1,9},{5... | collective-permute-start | bytes 1572872 | tf_op jit(solution)/shard_map/ppermute | solution.py:257
  28.7 13.7 %collective-permute-start.10 = (bf16[256,512]{1,0:T(8,128)(2,1)S(1)}, bf16[256,512]{1,0:T(8,128)(2,1)S(1)}, u32[]{:S(2)}, u32[]{:S(2)}) collective-permute-start(bf16[256,512]{1,0:T(8,128)(2,1)S(1)} %collective-permute-done.1.refs_0_), channel_id=1, source_target_pairs={{0,1},{1,0},{2,3},{3,2},{4,5},{5,4},{6,7},{7,6},{8,9},{9,8},{10,11... | collective-permute-start | bytes 786440 | tf_op jit(solution)/shard_map/ppermute | solution.py:303
  30.0 13.1 %collective-permute-start.12 = (bf16[256,512]{1,0:T(8,128)(2,1)S(1)}, bf16[256,512]{1,0:T(8,128)(2,1)S(1)}, u32[]{:S(2)}, u32[]{:S(2)}) collective-permute-start(bf16[256,512]{1,0:T(8,128)(2,1)S(1)} %collective-permute-done.11.refs_2_), channel_id=1, source_target_pairs={{0,1},{1,0},{2,3},{3,2},{4,5},{5,4},{6,7},{7,6},{8,9},{9,8},{10,11... | collective-permute-start | bytes 786440 | tf_op jit(solution)/shard_map/ppermute | solution.py:303
  30.2 14.3 %copy-start.23 = (s32[1,4]{1,0:T(1,128)S(1)}, s32[1,4]{1,0:T(1,128)}, u32[]{:S(2)}) copy-start(s32[1,4]{1,0:T(1,128)} %constant.65.clone.1) | copy-start | bytes 52
  37.6 6.9 %collective-permute-start.8 = (f32[384,256]{1,0:T(8,128)}, f32[384,256]{1,0:T(8,128)}, u32[]{:S(2)}, u32[]{:S(2)}) collective-permute-start(f32[384,256]{1,0:T(8,128)} %get-tuple-element.33), channel_id=1, source_target_pairs={{0,4},{4,0},{8,12},{12,8},{16,20},{20,16},{24,28},{28,24},{1,5},{5... | collective-permute-start | bytes 1179656 | tf_op jit(solution)/shard_map/ppermute | solution.py:257
  43.8 13.9 %collective-permute-start.16 = (bf16[512,512]{1,0:T(8,128)(2,1)}, bf16[512,512]{1,0:T(8,128)(2,1)}, u32[]{:S(2)}, u32[]{:S(2)}) collective-permute-start(bf16[512,512]{1,0:T(8,128)(2,1)} %collective-permute-done.15.refs_3_), channel_id=1, source_target_pairs={{0,8},{4,12},{8,0},{12,4},{16,24},{20,28},{24,16},{28,20},{1,9},{5... | collective-permute-start | bytes 1572872 | tf_op jit(solution)/shard_map/ppermute | solution.py:257
  44.1 13.6 %collective-permute-start.14 = (bf16[512,512]{1,0:T(8,128)(2,1)}, bf16[512,512]{1,0:T(8,128)(2,1)}, u32[]{:S(2)}, u32[]{:S(2)}) collective-permute-start(bf16[512,512]{1,0:T(8,128)(2,1)} %collective-permute-done.13.refs_2_), channel_id=1, source_target_pairs={{0,16},{4,20},{8,24},{12,28},{16,0},{20,4},{24,8},{28,12},{1,17},{... | collective-permute-start | bytes 1572872 | tf_op jit(solution)/shard_map/ppermute | solution.py:257
  46.8 8.4 %copy-start.4 = (bf16[384,256]{1,0:T(8,128)(2,1)}, bf16[384,256]{1,0:T(8,128)(2,1)S(1)}, u32[]{:S(2)}) copy-start(bf16[384,256]{1,0:T(8,128)(2,1)S(1)} %shard_map.57) | copy-start | bytes 589828
  46.8 10.9 %collective-permute-start.9 = (bf16[384,256]{1,0:T(8,128)(2,1)S(1)}, bf16[384,256]{1,0:T(8,128)(2,1)}, u32[]{:S(2)}, u32[]{:S(2)}) collective-permute-start(bf16[384,256]{1,0:T(8,128)(2,1)S(1)} %shard_map.57), channel_id=1, source_target_pairs={{0,1},{1,2},{2,3},{4,5},{5,6},{6,7},{8,9},{9,10},{10,11},{12,13},{... | collective-permute-start | bytes 589832 | tf_op jit(solution)/shard_map/ppermute | solution.py:320
  50.1 7.6 %copy-start.16 = (bf16[256,512]{1,0:T(8,128)(2,1)S(1)}, bf16[256,512]{1,0:T(8,128)(2,1)}, u32[]{:S(2)}) copy-start(bf16[256,512]{1,0:T(8,128)(2,1)} %copy-done.15) | copy-start | bytes 786436
  50.1 7.6 %copy-start.18 = (bf16[256,512]{1,0:T(8,128)(2,1)S(1)}, bf16[256,512]{1,0:T(8,128)(2,1)}, u32[]{:S(2)}) copy-start(bf16[256,512]{1,0:T(8,128)(2,1)} %copy-done.17) | copy-start | bytes 786436
  64.5 10.6 %copy-start.3 = (f32[384,512]{1,0:T(8,128)S(1)}, f32[384,512]{1,0:T(8,128)}, u32[]{:S(2)}) copy-start(f32[384,512]{1,0:T(8,128)} %copy-done.2) | copy-start | bytes 2359300
  64.5 10.5 %collective-permute-start.17 = (f32[384,512]{1,0:T(8,128)}, f32[384,512]{1,0:T(8,128)S(1)}, u32[]{:S(2)}, u32[]{:S(2)}) collective-permute-start(f32[384,512]{1,0:T(8,128)} %get-tuple-element.54), channel_id=1, source_target_pairs={{0,4},{4,0},{8,12},{12,8},{16,20},{20,16},{24,28},{28,24},{1,5},{5... | collective-permute-start | bytes 2359304 | tf_op jit(solution)/shard_map/ppermute | solution.py:257
  65.5 8.5 %collective-permute-start.18 = (bf16[384,256]{1,0:T(8,128)(2,1)}, bf16[384,256]{1,0:T(8,128)(2,1)S(1)}, u32[]{:S(2)}, u32[]{:S(2)}) collective-permute-start(bf16[384,256]{1,0:T(8,128)(2,1)} %collective-permute-done.9), channel_id=1, source_target_pairs={{0,1},{1,2},{2,3},{4,5},{5,6},{6,7},{8,9},{9,10},{10,11},{12,13},{... | collective-permute-start | bytes 589832 | tf_op jit(solution)/shard_map/ppermute | solution.py:320
  (12 other events, 35.2 us)

commit v10 on v9

--- a/solution.py
+++ b/solution.py
@@ -41,7 +41,8 @@
 
 
 def after(array, *earlier):
-    return lax.optimization_barrier((array, *earlier))[0]
+    corners = [other[:8, : min(128, other.shape[1])] for other in earlier]
+    return lax.optimization_barrier((array, *corners))[0]
 
 
 def cut_kernel(chips, places, query, tokens, *refs):
@@ -80,57 +81,51 @@
     )(jnp.stack([jnp.int32(place) for place in places]), query, tokens)
 
 
-def project_kernel(steps, starts, near, far, *refs):
-    count = sum(len(spots) for _, spots in steps)
-    weights, refs = refs[:count], refs[count:]
+def project_kernel(depth, chips, pieces, places, near, far, *refs):
+    weights, refs = refs[: len(pieces)], refs[len(pieces) :]
     *carry, far_out, near_out, held, sems = refs
-    batches = []
-    used = row = 0
-    for step, (depth, spots) in enumerate(steps):
-        batch = []
-        for index, columns in enumerate(spots):
-            batch.append(
-                pltpu.make_async_copy(
-                    weights[used], held.at[row : row + depth, columns], sems.at[step, index]
-                )
-            )
-            batch[-1].start()
-            used += 1
-        batches.append((row, depth, batch))
-        row += depth
-    totals = [ref[...] for ref in carry]
-    for step, (row, depth, batch) in enumerate(batches):
-        for copy in batch:
-            copy.wait()
-        terms = []
-        for side, ref in enumerate((far, near)):
-            window = pl.ds(pl.multiple_of(starts[side, step], 128), depth)
-            terms.append(
-                jnp.dot(
-                    ref[:, window],
-                    held[row : row + depth, :],
-                    preferred_element_type=jnp.float32,
-                )
-            )
-        totals = [total + term for total, term in zip(totals, terms)] if totals else terms
-    far_out[...], near_out[...] = totals
-
-
-def project(terms, near, far, carry=()):
+    copies = []
+    for index, (slot, column) in enumerate(pieces):
+        rows, width = weights[index].shape
+        row = pl.multiple_of(slot * depth + places[len(chips) + index], 16)
+        spot = held.at[pl.ds(row, rows), column : column + width]
+        copies.append(pltpu.make_async_copy(weights[index], spot, sems.at[index]))
+        copies[-1].start()
+    for copy in copies:
+        copy.wait()
+
+    def product(ref, window, rows):
+        return jnp.dot(ref[:, window], held[rows, :], preferred_element_type=jnp.float32)
+
+    total = carry[0][...] if carry else None
+    for slot in range(len(chips)):
+        window = pl.ds(pl.multiple_of(places[slot], 128), depth)
+        term = product(far, window, slice(slot * depth, (slot + 1) * depth))
+        total = term if total is None else total + term
+    far_out[...] = total
+    total = carry[1][...] if carry else None
+    slot = 0
+    while slot < len(chips):
+        end = slot + 1
+        while end < len(chips) and chips[end] == chips[end - 1] + 1:
+            end += 1
+        window = slice(chips[slot] * depth, (chips[end - 1] + 1) * depth)
+        term = product(near, window, slice(slot * depth, end * depth))
+        total = term if total is None else total + term
+        slot = end
+    near_out[...] = total
+
+
+def project(depth, width, terms, near, far, carry=()):
     rows = near.shape[0]
-    width = sum(array.shape[1] for array in terms[0][0])
-    steps = []
-    for arrays, *_ in terms:
-        edges = [sum(array.shape[1] for array in arrays[:i]) for i in range(len(arrays) + 1)]
-        spots = [slice(*edge) for edge in zip(edges[:-1], edges[1:])]
-        steps.append((arrays[0].shape[0], spots))
-    depth = sum(step[0] for step in steps)
-    starts = jnp.stack(
-        [jnp.stack([jnp.int32(term[1 + side]) for term in terms]) for side in range(2)]
-    )
-    weights = [array for arrays, *_ in terms for array in arrays]
+    chips = [term[0] for term in terms]
+    pieces = [(slot, *piece) for slot, term in enumerate(terms) for piece in term[2]]
+    places = [term[1] for term in terms] + [row for _, _, row, _ in pieces]
+    weights = [array for _, array, _, _ in pieces]
     return pl.pallas_call(
-        functools.partial(project_kernel, steps),
+        functools.partial(
+            project_kernel, depth, chips, [(slot, column) for slot, _, _, column in pieces]
+        ),
         out_shape=[jax.ShapeDtypeStruct((rows, width), jnp.float32)] * 2,
         in_specs=[pl.BlockSpec(memory_space=pltpu.SMEM)]
         + vmem(2)
@@ -138,16 +133,16 @@
         + vmem(len(carry)),
         out_specs=vmem(2),
         scratch_shapes=[
-            pltpu.VMEM((depth, width), jnp.bfloat16),
-            pltpu.SemaphoreType.DMA((len(steps), 2)),
+            pltpu.VMEM((len(chips) * depth, width), jnp.bfloat16),
+            pltpu.SemaphoreType.DMA((len(pieces),)),
         ],
         compiler_params=pltpu.CompilerParams(vmem_limit_bytes=32 * MIB),
         cost_estimate=pl.CostEstimate(
-            flops=4 * rows * width * depth,
-            bytes_accessed=2 * depth * (2 * rows + width),
+            flops=4 * rows * width * depth * len(chips),
+            bytes_accessed=2 * depth * len(chips) * (2 * rows + width),
             transcendentals=0,
         ),
-    )(starts, near, far, *weights, *carry)
+    )(jnp.stack([jnp.int32(place) for place in places]), near, far, *weights, *carry)
 
 
 def turn(vectors, cosine, sine):
@@ -292,9 +287,6 @@
     *halves, near_tokens = cut(places, w_query, hidden, shapes)
     parts = halves[2:]
 
-    def term(arrays, chip, row):
-        return (arrays, places[chip] + row, chip * depth + row)
-
     direct = [pair_held[side][chip][0][1] for side in range(2) for chip in axes]
     gate = [*direct, cosine, sine, first]
     given, other = [{}, {}], []
@@ -306,32 +298,45 @@
             for side, axis in enumerate((bits - 1, 0))
         ]
     pair_terms = [
-        term([pair_held[side][chip][0][1] for side in range(2)], chip, 0) for chip in range(chips)
+        (
+            chip,
+            places[chip],
+            [(pair_held[side][chip][0][1], 0, side * head_size) for side in range(2)],
+        )
+        for chip in range(chips)
     ]
-    far, near = project(pair_terms, near_tokens, far_tokens)
+    far, near = project(depth, 2 * head_size, pair_terms, near_tokens, far_tokens)
     query_held = fetch(halves[:2], given, [*gate, *mine], [near, *other])
 
     pair = finish_pair(near, swap(far, 1), cosine, sine)
     longest = ctx_size * row_count // 2
     back = -(-(longest - 1) // ROW_TILE) * ROW_TILE
     hops = min(ctx_size - 1, -(-back // row_count))
-    blocks = [pair]
-    for _ in range(hops):
-        blocks.insert(0, lax.ppermute(blocks[0], "ctx", [(i, i + 1) for i in range(ctx_size - 1)]))
-    keys_values = jnp.concatenate(blocks, axis=0)
+    blocks = [
+        lax.ppermute(pair, "ctx", [(i, i + hop) for i in range(ctx_size - hop)])
+        for hop in range(hops, 0, -1)
+    ]
+    keys_values = jnp.concatenate(blocks + [pair], axis=0)
 
     def query_terms(wanted, *gate):
         return [
-            term([after(array, *gate)], chip, side * half + row)
-            for side, chip in wanted
-            for row, array in query_held[side][chip]
+            (
+                chip,
+                places[chip],
+                [
+                    (after(array, *gate), side * half + row, 0)
+                    for side in range(2)
+                    for row, array in query_held[side][chip]
+                ],
+            )
+            for chip in wanted
         ]
 
-    everything = [(side, chip) for chip in range(chips) for side in range(2)]
-    early = [(0, 0), (1, 0), (0, axes[0]), (1, axes[-1])]
-    late = [wanted for wanted in everything if wanted not in early]
-    carry = project(query_terms(early, pair), near_tokens, far_tokens)
-    far, near = project(query_terms(late, blocks[-2]), near_tokens, far_tokens, carry)
+    early = [0] + axes
+    late = [chip for chip in range(chips) if chip not in early]
+    carry = project(depth, query_width, query_terms(early, pair), near_tokens, far_tokens)
+    terms = query_terms(late, *blocks)
+    far, near = project(depth, query_width, terms, near_tokens, far_tokens, carry)
     return attend(near, swap(far, 1), cosine, sine, first, keys_values, back)[None]
 
 

time: 80 us -> 77.9 us (0.974)
  the two profiles are of different devices: /device:TPU:17 before, /device:TPU:25 now
where the time goes in v10:
time: 77.9 us; the launch traced here: 77.3 us
  Pallas kernels  24.7 us (32%)
  starting transfers between devices  22.4 us (29%)
  waiting for transfers between devices  13.2 us (17%)
  local copies, waits for them, and re-layouts  11.2 us (14%)
  other arithmetic  5.61 us (7%)
    ppermute x15, starting transfers between devices, swap(): return lax.ppermute(array, 'dp', [(i, i ^ mask) for i in range(dp_size)])  18.9 us
    pallas_call x3, Pallas kernels, project(): pl.pallas_call(functools.partial(project_kernel, depth, chips, [(slot, co...  17.8 us
    unnamed x20, local copies, waits for them, and re-layouts  10.9 us
    ppermute x15, waiting for transfers between devices, swap(): return lax.ppermute(array, 'dp', [(i, i ^ mask) for i in range(dp_size)])  7.04 us
    ppermute x2, waiting for transfers between devices, shards(): lax.ppermute(pair, 'ctx', [(i, i + hop) for i in range(ctx_size - hop)])  6.16 us
    pallas_call x1, Pallas kernels, attend(): pl.pallas_call(functools.partial(attend_kernel, back), out_shape=jax.Shap...  3.67 us
    ppermute x2, starting transfers between devices, shards(): lax.ppermute(pair, 'ctx', [(i, i + hop) for i in range(ctx_size - hop)])  2.58 us
    pallas_call x1, Pallas kernels, cut(): pl.pallas_call(functools.partial(cut_kernel, chips), out_shape=[jax.Shape...  2.07 us
  transfers between devices with their start and end apart: 19, of which 7 were waited for; matrix products, arithmetic and copies ran while one was open for 8% of the time, Pallas kernels for 22%

profile of v10, /device:TPU:25, one launch (start us, length us, event | category | flops | bytes accessed | tf_op | source)
XLA Modules:
  0.0 77.3 jit_solution(10977666035715848634)
XLA Ops:
  0.7 1.2 %collective-permute-start.2 = (bf16[1024,128]{1,0:T(8,128)(2,1)}, bf16[1024,128]{1,0:T(8,128)(2,1)S(1)}, u32[]{:S(2)}, u32[]{:S(2)}) collective-permute-start(bf16[1024,128]{1,0:T(8,128)(2,1)} %refs_0_.1), channel_id=1, source_target_pairs={{0,16},{4,20},{8,24},{12,28},{16,0},{20,4},{24,8},{28,12},{1,17},{... | collective-permute-start | bytes 786440 | tf_op jit(solution)/shard_map/ppermute | solution.py:252
  1.9 1.2 %collective-permute-start.1 = (bf16[1024,128]{1,0:T(8,128)(2,1)}, bf16[1024,128]{1,0:T(8,128)(2,1)}, u32[]{:S(2)}, u32[]{:S(2)}) collective-permute-start(bf16[1024,128]{1,0:T(8,128)(2,1)} %refs_0_.1), channel_id=1, source_target_pairs={{0,8},{4,12},{8,0},{12,4},{16,24},{20,28},{24,16},{28,20},{1,9},{5... | collective-permute-start | bytes 786440 | tf_op jit(solution)/shard_map/ppermute | solution.py:252
  5.2 1.6 %multiply_sine_fusion = (f32[384,64]{1,0:T(8,128)}, f32[384,64]{1,0:T(8,128)}, f32[384,64]{1,0:T(8,128)}) fusion(f32[64]{0:T(128)S(1)} %negate_power_fusion, f32[384]{0:T(512)S(1)} %get-tuple-element.59), kind=kLoop, calls=%fused_computation.1 | loop fusion | flops 49152 | bytes 296704 | tf_op jit(solution)/shard_map/sin | solution.py:21
  6.9 2.8 %copy-done = bf16[1,384,8192]{2,1,0:T(8,128)(2,1)S(1)} copy-done((bf16[1,384,8192]{2,1,0:T(8,128)(2,1)S(1)}, bf16[1,384,8192]{2,1,0:T(8,128)(2,1)}, u32[]{:S(2)}) %copy-start) | copy-done | bytes 6291480
  9.7 1.2 %copy-done.1 = bf16[1024,512]{1,0:T(8,128)(2,1)S(1)} copy-done((bf16[1024,512]{1,0:T(8,128)(2,1)S(1)}, bf16[1024,512]{1,0:T(8,128)(2,1)}, u32[]{:S(2)}) %copy-start.1) | copy-done | bytes 1048600
  10.9 2.1 %shard_map.55 = (bf16[512,512]{1,0:T(8,128)(2,1)}, bf16[512,512]{1,0:T(8,128)(2,1)}, bf16[256,512]{1,0:T(8,128)(2,1)S(1)}, bf16[256,512]{1,0:T(8,128)(2,1)S(1)}, bf16[384,4096]{1,0:T(8,128)(2,1)S(1)}) custom-call(s32[8]{0:T(128)S(1)} %stack.53.places, bf16[1024,512]{1,0:T(8,128)(2,1)S(1)} %copy-done.1, bf16[384,8192]{1,0:T(8,128)(2,1)S(1)} %bitcast.15), custom_call_target="tpu_custom_call" | custom-call | bytes 9437184 | tf_op jit(solution)/shard_map/pallas_call | solution.py:69
  13.0 1.3 %collective-permute-start.5 = (bf16[256,512]{1,0:T(8,128)(2,1)S(1)}, bf16[256,512]{1,0:T(8,128)(2,1)}, u32[]{:S(2)}, u32[]{:S(2)}) collective-permute-start(bf16[256,512]{1,0:T(8,128)(2,1)S(1)} %get-tuple-element.32), channel_id=1, source_target_pairs={{0,16},{4,20},{8,24},{12,28},{16,0},{20,4},{24,8},{28,12},{1,17},{... | collective-permute-start | bytes 786440 | tf_op jit(solution)/shard_map/ppermute | solution.py:252
  14.5 1.2 %collective-permute-start.6 = (bf16[256,512]{1,0:T(8,128)(2,1)S(1)}, bf16[256,512]{1,0:T(8,128)(2,1)}, u32[]{:S(2)}, u32[]{:S(2)}) collective-permute-start(bf16[256,512]{1,0:T(8,128)(2,1)S(1)} %get-tuple-element.33), channel_id=1, source_target_pairs={{0,8},{4,12},{8,0},{12,4},{16,24},{20,28},{24,16},{28,20},{1,9},{5... | collective-permute-start | bytes 786440 | tf_op jit(solution)/shard_map/ppermute | solution.py:252
  16.5 1.2 %collective-permute-start.8 = (bf16[1024,128]{1,0:T(8,128)(2,1)}, bf16[1024,128]{1,0:T(8,128)(2,1)S(1)}, u32[]{:S(2)}, u32[]{:S(2)}) collective-permute-start(bf16[1024,128]{1,0:T(8,128)(2,1)} %collective-permute-done.1.refs_2_), channel_id=1, source_target_pairs={{0,16},{4,20},{8,24},{12,28},{16,0},{20,4},{24,8},{28,12},{1,17},{... | collective-permute-start | bytes 786440 | tf_op jit(solution)/shard_map/ppermute | solution.py:252
  18.0 1.9 %collective-permute-done.5.refs_5_ = bf16[256,512]{1,0:T(8,128)(2,1)} collective-permute-done((bf16[256,512]{1,0:T(8,128)(2,1)S(1)}, bf16[256,512]{1,0:T(8,128)(2,1)}, u32[]{:S(2)}, u32[]{:S(2)}) %collective-permute-start.5) | collective-permute-done | bytes 262176 | tf_op jit(solution)/shard_map/ppermute | solution.py:252
  19.9 1.4 %collective-permute-done.6.refs_3_ = bf16[256,512]{1,0:T(8,128)(2,1)} collective-permute-done((bf16[256,512]{1,0:T(8,128)(2,1)S(1)}, bf16[256,512]{1,0:T(8,128)(2,1)}, u32[]{:S(2)}, u32[]{:S(2)}) %collective-permute-start.6) | collective-permute-done | bytes 262176 | tf_op jit(solution)/shard_map/ppermute | solution.py:252
  21.3 1.7 %collective-permute-start.16 = (bf16[512,512]{1,0:T(8,128)(2,1)}, bf16[512,512]{1,0:T(8,128)(2,1)}, u32[]{:S(2)}, u32[]{:S(2)}) collective-permute-start(bf16[512,512]{1,0:T(8,128)(2,1)} %get-tuple-element.44.refs_1_), channel_id=1, source_target_pairs={{0,16},{4,20},{8,24},{12,28},{16,0},{20,4},{24,8},{28,12},{1,17},{... | collective-permute-start | bytes 1572872 | tf_op jit(solution)/shard_map/ppermute | solution.py:252
  22.9 1.2 %collective-permute-start.7 = (bf16[512,512]{1,0:T(8,128)(2,1)}, bf16[512,512]{1,0:T(8,128)(2,1)}, u32[]{:S(2)}, u32[]{:S(2)}) collective-permute-start(bf16[512,512]{1,0:T(8,128)(2,1)} %get-tuple-element.43.refs_0_), channel_id=1, source_target_pairs={{0,8},{4,12},{8,0},{12,4},{16,24},{20,28},{24,16},{28,20},{1,9},{5... | collective-permute-start | bytes 1572872 | tf_op jit(solution)/shard_map/ppermute | solution.py:252
  24.2 1.2 %collective-permute-done.8.refs_6_ = bf16[1024,128]{1,0:T(8,128)(2,1)S(1)} collective-permute-done((bf16[1024,128]{1,0:T(8,128)(2,1)}, bf16[1024,128]{1,0:T(8,128)(2,1)S(1)}, u32[]{:S(2)}, u32[]{:S(2)}) %collective-permute-start.8) | collective-permute-done | bytes 262176 | tf_op jit(solution)/shard_map/ppermute | solution.py:252
  28.4 0.9 %copy-done.2 = bf16[1024,128]{1,0:T(8,128)(2,1)S(1)} copy-done((bf16[1024,128]{1,0:T(8,128)(2,1)S(1)}, bf16[1024,128]{1,0:T(8,128)(2,1)}, u32[]{:S(2)}) %copy-start.2) | copy-done | bytes 262168
  30.3 0.9 %copy-done.5 = bf16[1024,128]{1,0:T(8,128)(2,1)S(1)} copy-done((bf16[1024,128]{1,0:T(8,128)(2,1)S(1)}, bf16[1024,128]{1,0:T(8,128)(2,1)}, u32[]{:S(2)}) %copy-start.5) | copy-done | bytes 262168
  31.2 0.9 %copy-done.7 = bf16[1024,128]{1,0:T(8,128)(2,1)S(1)} copy-done((bf16[1024,128]{1,0:T(8,128)(2,1)S(1)}, bf16[1024,128]{1,0:T(8,128)(2,1)}, u32[]{:S(2)}) %copy-start.7) | copy-done | bytes 262168
  33.1 6.6 %shard_map.56 = (f32[384,256]{1,0:T(8,128)}, f32[384,256]{1,0:T(8,128)S(1)}) custom-call(s32[12]{0:T(128)S(1)} %stack.54.places, bf16[384,4096]{1,0:T(8,128)(2,1)S(1)} %get-tuple-element.30.near, bf16[384,8192]{1,0:T(8,128)(2,1)} %collective-permute-done.far, bf16[1024,128]{1,0:T(8,128)(2,1)S(1)} %copy-done.2, bf16[1024,128]{1,0:T(8,128)(2,1)S(1)} %copy-done.3, ...), custom_call_target="tpu_custom_call" | custom-call | flops 1610612736 | bytes 8388608 | tf_op jit(solution)/shard_map/pallas_call | solution.py:125
  39.7 4.3 %collective-permute-start.13 = (f32[384,256]{1,0:T(8,128)}, f32[384,256]{1,0:T(8,128)}, u32[]{:S(2)}, u32[]{:S(2)}) collective-permute-start(f32[384,256]{1,0:T(8,128)} %get-tuple-element.37), channel_id=1, source_target_pairs={{0,4},{4,0},{8,12},{12,8},{16,20},{20,16},{24,28},{28,24},{1,5},{5... | collective-permute-start | bytes 1179656 | tf_op jit(solution)/shard_map/ppermute | solution.py:252
  44.2 1.3 %collective-permute-start.12 = (bf16[512,512]{1,0:T(8,128)(2,1)}, bf16[512,512]{1,0:T(8,128)(2,1)S(1)}, u32[]{:S(2)}, u32[]{:S(2)}) collective-permute-start(bf16[512,512]{1,0:T(8,128)(2,1)} %collective-permute-done.7.refs_2_), channel_id=1, source_target_pairs={{0,16},{4,20},{8,24},{12,28},{16,0},{20,4},{24,8},{28,12},{1,17},{... | collective-permute-start | bytes 1572872 | tf_op jit(solution)/shard_map/ppermute | solution.py:252
  45.5 1.2 %collective-permute-start.17 = (bf16[512,512]{1,0:T(8,128)(2,1)}, bf16[512,512]{1,0:T(8,128)(2,1)S(1)}, u32[]{:S(2)}, u32[]{:S(2)}) collective-permute-start(bf16[512,512]{1,0:T(8,128)(2,1)} %collective-permute-done.16.refs_7_), channel_id=1, source_target_pairs={{0,8},{4,12},{8,0},{12,4},{16,24},{20,28},{24,16},{28,20},{1,9},{5... | collective-permute-start | bytes 1572872 | tf_op jit(solution)/shard_map/ppermute | solution.py:252
  46.8 1.1 %pad_maximum_fusion.2.sine = f32[384,128]{1,0:T(8,128)S(1)} fusion(f32[384,64]{1,0:T(8,128)} %get-tuple-element.55, f32[384,64]{1,0:T(8,128)} %get-tuple-element.56), kind=kLoop, calls=%fused_computation.7 | loop fusion | flops 49152 | bytes 393216 | tf_op jit(solution)/shard_map/concatenate | solution.py:24
  47.9 1.1 %pad_maximum_fusion.1.cosine = f32[384,128]{1,0:T(8,128)S(1)} fusion(f32[384,64]{1,0:T(8,128)} %get-tuple-element.57), kind=kLoop, calls=%fused_computation.4 | loop fusion | flops 49152 | bytes 294912 | tf_op jit(solution)/shard_map/concatenate | solution.py:23
  49.1 1.1 %shard_map.57 = bf16[384,256]{1,0:T(8,128)(2,1)S(1)} custom-call(f32[384,256]{1,0:T(8,128)S(1)} %get-tuple-element.35.near, f32[384,256]{1,0:T(8,128)} %collective-permute-done.13.far, f32[384,128]{1,0:T(8,128)S(1)} %pad_maximum_fusion.1.cosine, f32[384,128]{1,0:T(8,128)S(1)} %pad_maximum_fusion.2.sine), custom_call_target="tpu_custom_call" | custom-call | flops 589824 | bytes 1376256 | tf_op jit(solution)/shard_map/pallas_call | solution.py:160
  50.2 1.3 %collective-permute-start.15 = (bf16[384,256]{1,0:T(8,128)(2,1)S(1)}, bf16[384,256]{1,0:T(8,128)(2,1)S(1)}, u32[]{:S(2)}, u32[]{:S(2)}) collective-permute-start(bf16[384,256]{1,0:T(8,128)(2,1)S(1)} %shard_map.57), channel_id=1, source_target_pairs={{0,1},{1,2},{2,3},{4,5},{5,6},{6,7},{8,9},{9,10},{10,11},{12,13},{... | collective-permute-start | bytes 589832 | tf_op jit(solution)/shard_map/ppermute | solution.py:316
  51.5 1.3 %collective-permute-start.14 = (bf16[384,256]{1,0:T(8,128)(2,1)S(1)}, bf16[384,256]{1,0:T(8,128)(2,1)S(1)}, u32[]{:S(2)}, u32[]{:S(2)}) collective-permute-start(bf16[384,256]{1,0:T(8,128)(2,1)S(1)} %shard_map.57), channel_id=1, source_target_pairs={{0,2},{1,3},{4,6},{5,7},{8,10},{9,11},{12,14},{13,15},{16,18},{17,... | collective-permute-start | bytes 589832 | tf_op jit(solution)/shard_map/ppermute | solution.py:316
  52.8 7.3 %shard_map.58 = (f32[384,512]{1,0:T(8,128)S(1)}, f32[384,512]{1,0:T(8,128)S(1)}) custom-call(s32[11]{0:T(128)S(1)} %stack.57.places, bf16[384,4096]{1,0:T(8,128)(2,1)S(1)} %get-tuple-element.30.near, bf16[384,8192]{1,0:T(8,128)(2,1)} %collective-permute-done.far, bf16[512,512]{1,0:T(8,128)(2,1)} %get-tuple-element.43.refs_0_, ...), custom_call_target="tpu_custom_call" | custom-call | flops 2415919104 | bytes 7864320 | tf_op jit(solution)/shard_map/pallas_call | solution.py:125
  60.1 6.2 %collective-permute-done.14 = bf16[384,256]{1,0:T(8,128)(2,1)S(1)} collective-permute-done((bf16[384,256]{1,0:T(8,128)(2,1)S(1)}, bf16[384,256]{1,0:T(8,128)(2,1)S(1)}, u32[]{:S(2)}, u32[]{:S(2)}) %collective-permute-start.14) | collective-permute-done | bytes 196640 | tf_op jit(solution)/shard_map/ppermute | solution.py:316
  66.3 3.9 %shard_map.59 = (f32[384,512]{1,0:T(8,128)S(1)}, f32[384,512]{1,0:T(8,128)S(1)}) custom-call(s32[3]{0:T(128)S(1)} %pad_add_fusion.places, bf16[384,4096]{1,0:T(8,128)(2,1)S(1)} %get-tuple-element.30.near, bf16[384,8192]{1,0:T(8,128)(2,1)} %collective-permute-done.far, bf16[512,512]{1,0:T(8,128)(2,1)S(1)} %collective-permute-done.12.refs_0_, ...), custom_call_target="tpu_custom_call" | custom-call | flops 805306368 | bytes 2621440 | tf_op jit(solution)/shard_map/pallas_call | solution.py:125
  70.2 1.5 %collective-permute-start.18 = (f32[384,512]{1,0:T(8,128)S(1)}, f32[384,512]{1,0:T(8,128)S(1)}, u32[]{:S(2)}, u32[]{:S(2)}) collective-permute-start(f32[384,512]{1,0:T(8,128)S(1)} %get-tuple-element.54), channel_id=1, source_target_pairs={{0,4},{4,0},{8,12},{12,8},{16,20},{20,16},{24,28},{28,24},{1,5},{5... | collective-permute-start | bytes 2359304 | tf_op jit(solution)/shard_map/ppermute | solution.py:252
  71.9 1.8 %collective-permute-done.18.far = f32[384,512]{1,0:T(8,128)S(1)} collective-permute-done((f32[384,512]{1,0:T(8,128)S(1)}, f32[384,512]{1,0:T(8,128)S(1)}, u32[]{:S(2)}, u32[]{:S(2)}) %collective-permute-start.18) | collective-permute-done | bytes 786464 | tf_op jit(solution)/shard_map/ppermute | solution.py:252
  73.6 3.7 %shard_map.60 = bf16[384,512]{1,0:T(8,128)(2,1)} custom-call(f32[384,512]{1,0:T(8,128)S(1)} %get-tuple-element.53.near, f32[384,512]{1,0:T(8,128)S(1)} %collective-permute-done.18.far, f32[384,128]{1,0:T(8,128)S(1)} %pad_maximum_fusion.1.cosine, f32[384,128]{1,0:T(8,128)S(1)} %pad_maximum_fusion.2.sine, s32[384,1]{1,0:T(8,128)S(1)} %sub.26.first, ...), custom_call_target="tpu_custom_call" | custom-call | flops 704643072 | bytes 1572864 | tf_op jit(solution)/shard_map/pallas_call | solution.py:222
  (48 shorter events, 9.2 us)
Async XLA Ops:
  0.0 28.4 %collective-permute-start = (bf16[384,8192]{1,0:T(8,128)(2,1)}, bf16[384,8192]{1,0:T(8,128)(2,1)}, u32[]{:S(2)}, u32[]{:S(2)}) collective-permute-start(bf16[384,8192]{1,0:T(8,128)(2,1)} %bitcast.14), channel_id=1, source_target_pairs={{0,4},{4,0},{8,12},{12,8},{16,20},{20,16},{24,28},{28,24},{1,5},{5... | collective-permute-start | bytes 18874376 | tf_op jit(solution)/shard_map/ppermute | solution.py:252
  0.7 15.1 %collective-permute-start.2 = (bf16[1024,128]{1,0:T(8,128)(2,1)}, bf16[1024,128]{1,0:T(8,128)(2,1)S(1)}, u32[]{:S(2)}, u32[]{:S(2)}) collective-permute-start(bf16[1024,128]{1,0:T(8,128)(2,1)} %refs_0_.1), channel_id=1, source_target_pairs={{0,16},{4,20},{8,24},{12,28},{16,0},{20,4},{24,8},{28,12},{1,17},{... | collective-permute-start | bytes 786440 | tf_op jit(solution)/shard_map/ppermute | solution.py:252
  1.9 11.1 %collective-permute-start.1 = (bf16[1024,128]{1,0:T(8,128)(2,1)}, bf16[1024,128]{1,0:T(8,128)(2,1)}, u32[]{:S(2)}, u32[]{:S(2)}) collective-permute-start(bf16[1024,128]{1,0:T(8,128)(2,1)} %refs_0_.1), channel_id=1, source_target_pairs={{0,8},{4,12},{8,0},{12,4},{16,24},{20,28},{24,16},{28,20},{1,9},{5... | collective-permute-start | bytes 786440 | tf_op jit(solution)/shard_map/ppermute | solution.py:252
  3.1 11.4 %collective-permute-start.4 = (bf16[1024,128]{1,0:T(8,128)(2,1)}, bf16[1024,128]{1,0:T(8,128)(2,1)}, u32[]{:S(2)}, u32[]{:S(2)}) collective-permute-start(bf16[1024,128]{1,0:T(8,128)(2,1)} %refs_1_.1), channel_id=1, source_target_pairs={{0,16},{4,20},{8,24},{12,28},{16,0},{20,4},{24,8},{28,12},{1,17},{... | collective-permute-start | bytes 786440 | tf_op jit(solution)/shard_map/ppermute | solution.py:252
  3.4 14.4 %collective-permute-start.3 = (bf16[1024,128]{1,0:T(8,128)(2,1)}, bf16[1024,128]{1,0:T(8,128)(2,1)}, u32[]{:S(2)}, u32[]{:S(2)}) collective-permute-start(bf16[1024,128]{1,0:T(8,128)(2,1)} %refs_1_.1), channel_id=1, source_target_pairs={{0,8},{4,12},{8,0},{12,4},{16,24},{20,28},{24,16},{28,20},{1,9},{5... | collective-permute-start | bytes 786440 | tf_op jit(solution)/shard_map/ppermute | solution.py:252
  6.9 2.8 %copy-start = (bf16[1,384,8192]{2,1,0:T(8,128)(2,1)S(1)}, bf16[1,384,8192]{2,1,0:T(8,128)(2,1)}, u32[]{:S(2)}) copy-start(bf16[1,384,8192]{2,1,0:T(8,128)(2,1)} %param.5) | copy-start | bytes 18874372
  9.7 1.2 %copy-start.1 = (bf16[1024,512]{1,0:T(8,128)(2,1)S(1)}, bf16[1024,512]{1,0:T(8,128)(2,1)}, u32[]{:S(2)}) copy-start(bf16[1024,512]{1,0:T(8,128)(2,1)} %query.1) | copy-start | bytes 3145732
  13.0 6.8 %collective-permute-start.5 = (bf16[256,512]{1,0:T(8,128)(2,1)S(1)}, bf16[256,512]{1,0:T(8,128)(2,1)}, u32[]{:S(2)}, u32[]{:S(2)}) collective-permute-start(bf16[256,512]{1,0:T(8,128)(2,1)S(1)} %get-tuple-element.32), channel_id=1, source_target_pairs={{0,16},{4,20},{8,24},{12,28},{16,0},{20,4},{24,8},{28,12},{1,17},{... | collective-permute-start | bytes 786440 | tf_op jit(solution)/shard_map/ppermute | solution.py:252
  14.5 6.7 %collective-permute-start.6 = (bf16[256,512]{1,0:T(8,128)(2,1)S(1)}, bf16[256,512]{1,0:T(8,128)(2,1)}, u32[]{:S(2)}, u32[]{:S(2)}) collective-permute-start(bf16[256,512]{1,0:T(8,128)(2,1)S(1)} %get-tuple-element.33), channel_id=1, source_target_pairs={{0,8},{4,12},{8,0},{12,4},{16,24},{20,28},{24,16},{28,20},{1,9},{5... | collective-permute-start | bytes 786440 | tf_op jit(solution)/shard_map/ppermute | solution.py:252
  15.8 0.7 copy-start.4
  16.5 8.9 %collective-permute-start.8 = (bf16[1024,128]{1,0:T(8,128)(2,1)}, bf16[1024,128]{1,0:T(8,128)(2,1)S(1)}, u32[]{:S(2)}, u32[]{:S(2)}) collective-permute-start(bf16[1024,128]{1,0:T(8,128)(2,1)} %collective-permute-done.1.refs_2_), channel_id=1, source_target_pairs={{0,16},{4,20},{8,24},{12,28},{16,0},{20,4},{24,8},{28,12},{1,17},{... | collective-permute-start | bytes 786440 | tf_op jit(solution)/shard_map/ppermute | solution.py:252
  17.7 9.1 %collective-permute-start.9 = (bf16[1024,128]{1,0:T(8,128)(2,1)}, bf16[1024,128]{1,0:T(8,128)(2,1)S(1)}, u32[]{:S(2)}, u32[]{:S(2)}) collective-permute-start(bf16[1024,128]{1,0:T(8,128)(2,1)} %collective-permute-done.4.refs_5_), channel_id=1, source_target_pairs={{0,8},{4,12},{8,0},{12,4},{16,24},{20,28},{24,16},{28,20},{1,9},{5... | collective-permute-start | bytes 786440 | tf_op jit(solution)/shard_map/ppermute | solution.py:252
  21.3 22.9 %collective-permute-start.16 = (bf16[512,512]{1,0:T(8,128)(2,1)}, bf16[512,512]{1,0:T(8,128)(2,1)}, u32[]{:S(2)}, u32[]{:S(2)}) collective-permute-start(bf16[512,512]{1,0:T(8,128)(2,1)} %get-tuple-element.44.refs_1_), channel_id=1, source_target_pairs={{0,16},{4,20},{8,24},{12,28},{16,0},{20,4},{24,8},{28,12},{1,17},{... | collective-permute-start | bytes 1572872 | tf_op jit(solution)/shard_map/ppermute | solution.py:252
  22.9 21.2 %collective-permute-start.7 = (bf16[512,512]{1,0:T(8,128)(2,1)}, bf16[512,512]{1,0:T(8,128)(2,1)}, u32[]{:S(2)}, u32[]{:S(2)}) collective-permute-start(bf16[512,512]{1,0:T(8,128)(2,1)} %get-tuple-element.43.refs_0_), channel_id=1, source_target_pairs={{0,8},{4,12},{8,0},{12,4},{16,24},{20,28},{24,16},{28,20},{1,9},{5... | collective-permute-start | bytes 1572872 | tf_op jit(solution)/shard_map/ppermute | solution.py:252
  25.4 0.7 copy-start.6
  26.1 18.0 %collective-permute-start.10 = (bf16[256,512]{1,0:T(8,128)(2,1)}, bf16[256,512]{1,0:T(8,128)(2,1)}, u32[]{:S(2)}, u32[]{:S(2)}) collective-permute-start(bf16[256,512]{1,0:T(8,128)(2,1)} %collective-permute-done.5.refs_5_), channel_id=1, source_target_pairs={{0,1},{1,0},{2,3},{3,2},{4,5},{5,4},{6,7},{7,6},{8,9},{9,8},{10,11... | collective-permute-start | bytes 786440 | tf_op jit(solution)/shard_map/ppermute | solution.py:295
  26.8 0.7 copy-start.8
  27.5 16.7 %collective-permute-start.11 = (bf16[256,512]{1,0:T(8,128)(2,1)}, bf16[256,512]{1,0:T(8,128)(2,1)}, u32[]{:S(2)}, u32[]{:S(2)}) collective-permute-start(bf16[256,512]{1,0:T(8,128)(2,1)} %collective-permute-done.6.refs_3_), channel_id=1, source_target_pairs={{0,1},{1,0},{2,3},{3,2},{4,5},{5,4},{6,7},{7,6},{8,9},{9,8},{10,11... | collective-permute-start | bytes 786440 | tf_op jit(solution)/shard_map/ppermute | solution.py:295
  28.4 1.0 %copy-start.2 = (bf16[1024,128]{1,0:T(8,128)(2,1)S(1)}, bf16[1024,128]{1,0:T(8,128)(2,1)}, u32[]{:S(2)}) copy-start(bf16[1024,128]{1,0:T(8,128)(2,1)} %refs_0_.1) | copy-start | bytes 786436
  29.3 0.9 %copy-start.3 = (bf16[1024,128]{1,0:T(8,128)(2,1)S(1)}, bf16[1024,128]{1,0:T(8,128)(2,1)}, u32[]{:S(2)}) copy-start(bf16[1024,128]{1,0:T(8,128)(2,1)} %refs_1_.1) | copy-start | bytes 786436
  30.3 0.9 %copy-start.5 = (bf16[1024,128]{1,0:T(8,128)(2,1)S(1)}, bf16[1024,128]{1,0:T(8,128)(2,1)}, u32[]{:S(2)}) copy-start(bf16[1024,128]{1,0:T(8,128)(2,1)} %copy-done.4) | copy-start | bytes 786436
  31.2 0.9 %copy-start.7 = (bf16[1024,128]{1,0:T(8,128)(2,1)S(1)}, bf16[1024,128]{1,0:T(8,128)(2,1)}, u32[]{:S(2)}) copy-start(bf16[1024,128]{1,0:T(8,128)(2,1)} %copy-done.6) | copy-start | bytes 786436
  32.2 0.9 %copy-start.9 = (bf16[1024,128]{1,0:T(8,128)(2,1)S(1)}, bf16[1024,128]{1,0:T(8,128)(2,1)}, u32[]{:S(2)}) copy-start(bf16[1024,128]{1,0:T(8,128)(2,1)} %copy-done.8) | copy-start | bytes 786436
  39.7 9.3 %collective-permute-start.13 = (f32[384,256]{1,0:T(8,128)}, f32[384,256]{1,0:T(8,128)}, u32[]{:S(2)}, u32[]{:S(2)}) collective-permute-start(f32[384,256]{1,0:T(8,128)} %get-tuple-element.37), channel_id=1, source_target_pairs={{0,4},{4,0},{8,12},{12,8},{16,20},{20,16},{24,28},{28,24},{1,5},{5... | collective-permute-start | bytes 1179656 | tf_op jit(solution)/shard_map/ppermute | solution.py:252
  44.2 22.1 %collective-permute-start.12 = (bf16[512,512]{1,0:T(8,128)(2,1)}, bf16[512,512]{1,0:T(8,128)(2,1)S(1)}, u32[]{:S(2)}, u32[]{:S(2)}) collective-permute-start(bf16[512,512]{1,0:T(8,128)(2,1)} %collective-permute-done.7.refs_2_), channel_id=1, source_target_pairs={{0,16},{4,20},{8,24},{12,28},{16,0},{20,4},{24,8},{28,12},{1,17},{... | collective-permute-start | bytes 1572872 | tf_op jit(solution)/shard_map/ppermute | solution.py:252
  45.5 20.8 %collective-permute-start.17 = (bf16[512,512]{1,0:T(8,128)(2,1)}, bf16[512,512]{1,0:T(8,128)(2,1)S(1)}, u32[]{:S(2)}, u32[]{:S(2)}) collective-permute-start(bf16[512,512]{1,0:T(8,128)(2,1)} %collective-permute-done.16.refs_7_), channel_id=1, source_target_pairs={{0,8},{4,12},{8,0},{12,4},{16,24},{20,28},{24,16},{28,20},{1,9},{5... | collective-permute-start | bytes 1572872 | tf_op jit(solution)/shard_map/ppermute | solution.py:252
  50.2 9.9 %collective-permute-start.15 = (bf16[384,256]{1,0:T(8,128)(2,1)S(1)}, bf16[384,256]{1,0:T(8,128)(2,1)S(1)}, u32[]{:S(2)}, u32[]{:S(2)}) collective-permute-start(bf16[384,256]{1,0:T(8,128)(2,1)S(1)} %shard_map.57), channel_id=1, source_target_pairs={{0,1},{1,2},{2,3},{4,5},{5,6},{6,7},{8,9},{9,10},{10,11},{12,13},{... | collective-permute-start | bytes 589832 | tf_op jit(solution)/shard_map/ppermute | solution.py:316
  51.5 14.8 %collective-permute-start.14 = (bf16[384,256]{1,0:T(8,128)(2,1)S(1)}, bf16[384,256]{1,0:T(8,128)(2,1)S(1)}, u32[]{:S(2)}, u32[]{:S(2)}) collective-permute-start(bf16[384,256]{1,0:T(8,128)(2,1)S(1)} %shard_map.57), channel_id=1, source_target_pairs={{0,2},{1,3},{4,6},{5,7},{8,10},{9,11},{12,14},{13,15},{16,18},{17,... | collective-permute-start | bytes 589832 | tf_op jit(solution)/shard_map/ppermute | solution.py:316
  70.2 3.4 %collective-permute-start.18 = (f32[384,512]{1,0:T(8,128)S(1)}, f32[384,512]{1,0:T(8,128)S(1)}, u32[]{:S(2)}, u32[]{:S(2)}) collective-permute-start(f32[384,512]{1,0:T(8,128)S(1)} %get-tuple-element.54), channel_id=1, source_target_pairs={{0,4},{4,0},{8,12},{12,8},{16,20},{20,16},{24,28},{28,24},{1,5},{5... | collective-permute-start | bytes 2359304 | tf_op jit(solution)/shard_map/ppermute | solution.py:252

commit v11 on v4

--- a/solution.py
+++ b/solution.py
@@ -44,8 +44,12 @@
     return lax.optimization_barrier((array, *earlier))[0]
 
 
+def corner(array):
+    return array[:8, :128]
+
+
 def project_kernel(steps, carried, final, starts, near, far, *refs):
-    count = sum(len(spots) for _, spots in steps)
+    count = sum(len(spots) for _, spots, _ in steps)
     weights, refs = refs[:count], refs[count:]
     if carried:
         carry, refs = refs[0], refs[1:]
@@ -53,14 +57,16 @@
     rows = near.shape[0]
     batches = ([], [], [])
     used = row = 0
-    for step, (depth, spots) in enumerate(steps):
+    for step, (depth, spots, source) in enumerate(steps):
         here = slice(row, row + depth)
         row += depth
         window = pl.ds(pl.multiple_of(starts[step], 128), depth)
         for index, columns in enumerate(spots):
             batches[0].append(
                 pltpu.make_async_copy(
-                    weights[used], held.at[here, columns], sems.at[step, 2 + index]
+                    weights[used].at[source : source + depth],
+                    held.at[here, columns],
+                    sems.at[step, 2 + index],
                 )
             )
             used += 1
@@ -92,13 +98,13 @@
     rows = near.shape[0]
     width = sum(array.shape[1] for array in terms[0][1])
     steps = []
-    for _, arrays in terms:
+    for _, arrays, source, depth in terms:
         edges = [sum(array.shape[1] for array in arrays[:i]) for i in range(len(arrays) + 1)]
         spots = [slice(*edge) for edge in zip(edges[:-1], edges[1:])]
-        steps.append((arrays[0].shape[0], spots))
+        steps.append((depth, spots, source))
     depth = sum(step[0] for step in steps)
-    starts = jnp.stack([start for start, _ in terms]).astype(jnp.int32)
-    weights = [array for _, arrays in terms for array in arrays]
+    starts = jnp.stack([start for start, *_ in terms]).astype(jnp.int32)
+    weights = [array for _, arrays, *_ in terms for array in arrays]
     whole = jax.ShapeDtypeStruct((2 * rows, width), jnp.float32)
     part = jax.ShapeDtypeStruct((rows, width), jnp.float32)
     carries = [] if carry is None else [carry]
@@ -229,20 +235,19 @@
     def swap(array, mask):
         return lax.ppermute(array, "dp", [(i, i ^ mask) for i in range(dp_size)])
 
-    def fetch(pair, gate, later, seconds):
-        held = [{0: [(0, array)]} for array in pair]
-        for step in range(bits):
-            axes = (step, bits - 1 - step)
-            for sources in zip(*[sorted(side) for side in held]):
-                for side, source in enumerate(sources):
-                    array = held[side][source][0][1]
-                    mask = 2 << axes[side]
-                    if source == 0 and step == bits - 1 and seconds:
-                        got = seconds[side]
-                    else:
-                        array = after(array, *(gate if source == 0 else later))
-                        got = [(0, swap(array, mask))]
-                    held[side][source | (1 << axes[side])] = got
+    def fetch(pair, given, gate, later):
+        held = []
+        for side, array in enumerate(pair):
+            pieces = {0: array, **given[side]}
+            reached = [0]
+            for axis in list(range(bits))[:: 1 - 2 * side]:
+                for source in list(reached):
+                    target = source | (1 << axis)
+                    reached.append(target)
+                    if target not in pieces:
+                        sent = after(pieces[source], *(later if source else gate))
+                        pieces[target] = swap(sent, 2 << axis)
+            held.append(pieces)
         return held
 
     sibling_hidden = swap(hidden, 1)
@@ -255,55 +260,78 @@
     def begins(chip):
         return (me ^ (2 * chip)) * depth
 
-    first_axis, last_axis = 1, 1 << (bits - 1)
-    last = chips - 1
-
+    axes = [1 << axis for axis in range(bits)]
     half = depth // 2
+    some = half // 2
+    halved = ctx_size % 2 == 0 and bits > 1
+    begin = (place % 2) * some
     halves = [w_query[:half], w_query[half:]]
-    parts = []
-    if ctx_size % 2 == 0:
-        begin = (place % 2) * (half // 2)
-        parts = [
-            lax.dynamic_slice_in_dim(w_query, side * half + begin, half // 2, 0)
-            for side in range(2)
-        ]
-
-    pair_held = fetch((w_key, w_value), [], [], [])
+
+    pair_held = fetch((w_key, w_value), [{}, {}], [], [])
     pair_terms = [
-        (begins(chip), [pair_held[side][chip][0][1] for side in range(2)]) for chip in range(chips)
+        (begins(chip), [pair_held[side][chip] for side in range(2)], 0, depth)
+        for chip in range(chips)
     ]
-    carry = project(pair_terms[:-1], hidden, sibling_hidden)
-    near, far = project(pair_terms[-1:], hidden, sibling_hidden, carry, True)
-    gate = [pair_held[0][last_axis][0][1], pair_held[1][first_axis][0][1]]
-    gate += [cosine, sine, first, *halves, *parts]
-    mine = [swap(after(part, *gate), 2 << axis) for part, axis in zip(parts, (bits - 1, 0))]
-    other = [lax.ppermute(part, "ctx", [(i, i ^ 1) for i in range(ctx_size)]) for part in mine]
-    seconds = [
-        [(begin, here), (half // 2 - begin, there)] for here, there in zip(mine, other)
-    ]
-    query_held = fetch(halves, gate, [near, *mine], seconds)
-
+    early_chips = [0] + axes
+    late_chips = [chip for chip in range(chips) if chip not in early_chips]
+    carry = project([pair_terms[chip] for chip in early_chips], hidden, sibling_hidden)
+    terms = [pair_terms[chip] for chip in late_chips]
+    near, far = project(terms, hidden, sibling_hidden, carry, True)
     pair = finish_pair(near, swap(far, 1), cosine, sine)
     longest = ctx_size * row_count // 2
     back = -(-(longest - 1) // ROW_TILE) * ROW_TILE
-    hops = min(ctx_size - 1, -(-back // row_count))
-    blocks = [
-        lax.ppermute(after(pair, *other), "ctx", [(i, i + hop) for i in range(ctx_size - hop)])
-        for hop in range(hops, 0, -1)
-    ]
-    keys_values = jnp.concatenate(blocks + [pair], axis=0)
-
-    def query_terms(wanted, *gate):
-        return [
-            (begins(chip) + side * half + begin, [after(array, *gate)])
-            for side, chip in wanted
-            for begin, array in query_held[side][chip]
+    blocks = [pair]
+    for _ in range(min(ctx_size - 1, -(-back // row_count))):
+        blocks.insert(0, lax.ppermute(blocks[0], "ctx", [(i, i + 1) for i in range(ctx_size - 1)]))
+    keys_values = jnp.concatenate(blocks, axis=0)
+    direct = [corner(pair_held[side][chip]) for side in range(2) for chip in axes]
+    gate = [*direct, cosine, sine, first]
+    later = [corner(blocks[-2])]
+
+    early, late = [], []
+    given = [{}, {}]
+    if halved:
+        ends = (0, bits - 1)
+        joined = [
+            jnp.concatenate(
+                [
+                    halves[side],
+                    lax.dynamic_slice_in_dim(w_query, (1 - side) * half + begin, some, 0),
+                ],
+                axis=0,
+            )
+            for side in range(2)
         ]
-
-    late = [(0, last), (1, last)]
-    early = [(side, chip) for chip in range(last) for side in range(2)]
-    carry = project(query_terms(early, pair), hidden, sibling_hidden)
-    near, far = project(query_terms(late, keys_values), hidden, sibling_hidden, carry, True)
+        got = [swap(after(joined[side], *gate), 2 << ends[side]) for side in range(2)]
+        both = jnp.concatenate([after(got[1 - side], *later)[half:] for side in range(2)], axis=0)
+        both = lax.ppermute(both, "ctx", [(i, i ^ 1) for i in range(ctx_size)])
+        for side in range(2):
+            chip = 1 << ends[side]
+            given[side][chip] = after(got[side], *later)[:half]
+            given[1 - side][chip] = None
+            early.append((begins(chip) + side * half, [got[side]], 0, half))
+            early.append((begins(chip) + (1 - side) * half + begin, [got[side]], half, some))
+            late.append(
+                (
+                    begins(chip) + (1 - side) * half + some - begin,
+                    [both],
+                    (1 - side) * some,
+                    some,
+                )
+            )
+    query_held = fetch(halves, given, gate, later)
+    for side in range(2):
+        for chip in range(chips):
+            if chip == 0 or chip in late_chips or chip not in given[side]:
+                term = (begins(chip) + side * half, [query_held[side][chip]], 0, half)
+                (late if chip in late_chips else early).append(term)
+
+    def gated(terms, *gate):
+        return [(start, [after(array, *gate) for array in arrays], *rest) for start, arrays, *rest in terms]
+
+    carry = project(gated(early, *later), hidden, sibling_hidden)
+    terms = gated(late, corner(blocks[0]))
+    near, far = project(terms, hidden, sibling_hidden, carry, True)
     return attend(near, swap(far, 1), cosine, sine, first, keys_values, back)[None]
 
 

time: 78.1 us -> 74.9 us (0.959)
  waiting for transfers between devices: 23.4 us -> 19.6 us
  other arithmetic: 2.79 us -> 5.83 us
  Pallas kernels: 21.7 us -> 20.3 us
  starting transfers between devices: 21.7 us -> 20.3 us
    ppermute x15 -> x13, waiting for transfers between devices: 11.5 us -> 7.94 us  [swap(): return lax.ppermute(array, 'dp', [(i, i ^ mask) for i in range(dp_size)])]
    concatenate x1 -> x3, other arithmetic: 0.04 us -> 3.07 us  [the longest x1 1.24 us: shards(): jnp.concatenate([halves[side], lax.dynamic_slice_in_dim(w_query, (1 - sid...]
    slice x0 -> x4, local copies, waits for them, and re-layouts: none -> 1.74 us  [the longest x2 1.71 us: shards(): given[side][chip] = after(got[side], *later)[:half]]
    slice x1, local copies, waits for them, and re-layouts: 1.27 us -> 0.07 us  [shards(): halves = [w_query[:half], w_query[half:]]]
    pallas_call x1, Pallas kernels: 1.14 us -> 0.12 us  [finish_pair(): pl.pallas_call(pair_kernel, out_shape=jax.ShapeDtypeStruct(near.shape, jn...]
    ppermute x15 -> x13, starting transfers between devices: 14.7 us -> 13.7 us  [swap(): return lax.ppermute(array, 'dp', [(i, i ^ mask) for i in range(dp_size)])]
    dynamic_slice x1, local copies, waits for them, and re-layouts: 1.95 us -> 1.07 us  [shards(): lax.dynamic_slice_in_dim(w_query, (1 - side) * half + begin, some, 0)]
    unnamed x12 -> x22, local copies, waits for them, and re-layouts: 3.41 us -> 4.02 us
  transfers between devices with their start and end apart: 19 -> 16, of which waited for: 8 -> 6; matrix products, arithmetic and copies ran while one was open for 8% -> 11% of each run, Pallas kernels for 19% -> 17%
where the time goes in v11:
time: 74.9 us; the launch traced here: 73.4 us
  starting transfers between devices  20.3 us (27%)
  Pallas kernels  20.3 us (27%)
  waiting for transfers between devices  19.6 us (26%)
  local copies, waits for them, and re-layouts  7.12 us (10%)
  other arithmetic  5.83 us (8%)
    pallas_call x4, Pallas kernels, project(): pl.pallas_call(functools.partial(project_kernel, steps, carry is not None...  16.5 us
    ppermute x13, starting transfers between devices, swap(): return lax.ppermute(array, 'dp', [(i, i ^ mask) for i in range(dp_size)])  13.7 us
    ppermute x2, waiting for transfers between devices, shards(): lax.ppermute(blocks[0], 'ctx', [(i, i + 1) for i in range(ctx_size - 1)])  11.7 us
    ppermute x13, waiting for transfers between devices, swap(): return lax.ppermute(array, 'dp', [(i, i ^ mask) for i in range(dp_size)])  7.94 us
    ppermute x2, starting transfers between devices, shards(): lax.ppermute(blocks[0], 'ctx', [(i, i + 1) for i in range(ctx_size - 1)])  5.27 us
    unnamed x22, local copies, waits for them, and re-layouts  4.02 us
    pallas_call x1, Pallas kernels, attend(): pl.pallas_call(functools.partial(attend_kernel, back), out_shape=jax.Shap...  3.65 us
    slice x2, local copies, waits for them, and re-layouts, shards(): given[side][chip] = after(got[side], *later)[:half]  1.71 us
  transfers between devices with their start and end apart: 16, of which 6 were waited for; matrix products, arithmetic and copies ran while one was open for 11% of the time, Pallas kernels for 17%

profile of v11, /device:TPU:17, one launch (start us, length us, event | category | flops | bytes accessed | tf_op | source)
XLA Modules:
  0.0 73.4 jit_solution(6880706684624226404)
XLA Ops:
  0.7 1.2 %collective-permute-start.1 = (bf16[1024,128]{1,0:T(8,128)(2,1)}, bf16[1024,128]{1,0:T(8,128)(2,1)}, u32[]{:S(2)}, u32[]{:S(2)}) collective-permute-start(bf16[1024,128]{1,0:T(8,128)(2,1)} %refs_0_.1), channel_id=1, source_target_pairs={{0,8},{4,12},{8,0},{12,4},{16,24},{20,28},{24,16},{28,20},{1,9},{5... | collective-permute-start | bytes 786440 | tf_op jit(solution)/shard_map/ppermute | solution.py:236
  1.9 1.2 %collective-permute-start.2 = (bf16[1024,128]{1,0:T(8,128)(2,1)}, bf16[1024,128]{1,0:T(8,128)(2,1)S(1)}, u32[]{:S(2)}, u32[]{:S(2)}) collective-permute-start(bf16[1024,128]{1,0:T(8,128)(2,1)} %refs_0_.1), channel_id=1, source_target_pairs={{0,16},{4,20},{8,24},{12,28},{16,0},{20,4},{24,8},{28,12},{1,17},{... | collective-permute-start | bytes 786440 | tf_op jit(solution)/shard_map/ppermute | solution.py:236
  3.6 0.8 %reduce-window_clone.1 = s32[1,16]{1,0:T(1,128)S(1)} reduce-window(s32[1,16]{1,0:T(1,128)} %param.9, s32[]{:T(128)} %constant.37.clone.1), window={size=1x16 pad=0_0x15_0}, to_apply=%region_0.0 | reduce-window | flops 240 | bytes 132 | tf_op jit(solution)/shard_map/reduce-window.clone
  5.2 1.1 %constant_dynamic-slice_fusion.1 = (bf16[256,512]{1,0:T(8,128)(2,1)S(1)}, bf16[256,512]{1,0:T(8,128)(2,1)S(1)}) fusion(bf16[1024,512]{1,0:T(8,128)(2,1)} %param.6, s32[]{:T(128)S(6)} %select_n.18, s32[]{:T(128)S(6)} %select_n.20), kind=kLoop, calls=%fused_computation.18 | loop fusion | bytes 1048584 | tf_op jit(solution)/shard_map/dynamic_slice | solution.py:299
  6.3 0.8 %fusion = (f32[384,64]{1,0:T(8,128)S(1)}, f32[384,64]{1,0:T(8,128)S(1)}, f32[384,64]{1,0:T(8,128)S(1)}) fusion(f32[64]{0:T(128)S(1)} %negate_power_fusion, f32[384]{0:T(512)S(1)} %get-tuple-element.45), kind=kLoop, calls=%fused_computation.8 | loop fusion | flops 49152 | bytes 296704 | tf_op jit(solution)/shard_map/neg | solution.py:24
  7.3 1.2 %pad_maximum_fusion = (bf16[768,512]{1,0:T(8,128)(2,1)}, bf16[768,512]{1,0:T(8,128)(2,1)}) fusion(bf16[256,512]{1,0:T(8,128)(2,1)S(1)} %get-tuple-element.37, bf16[512,512]{1,0:T(8,128)(2,1)S(1)} %get-tuple-element.32.refs_5_, bf16[256,512]{1,0:T(8,128)(2,1)S(1)} %get-tuple-element.38, bf16[512,512]{1,0:T(8,128)(2,1)S(1)} %get-tuple-element.31.refs_4_), kind=kLoop, calls=%fused_computation | loop fusion | flops 3145728 | bytes 3145728 | tf_op jit(solution)/shard_map/concatenate | solution.py:296
  8.9 1.2 %collective-permute-start.6 = (bf16[1024,128]{1,0:T(8,128)(2,1)}, bf16[1024,128]{1,0:T(8,128)(2,1)}, u32[]{:S(2)}, u32[]{:S(2)}) collective-permute-start(bf16[1024,128]{1,0:T(8,128)(2,1)} %collective-permute-done.1.refs_2_), channel_id=1, source_target_pairs={{0,16},{4,20},{8,24},{12,28},{16,0},{20,4},{24,8},{28,12},{1,17},{... | collective-permute-start | bytes 786440 | tf_op jit(solution)/shard_map/ppermute | solution.py:236
  10.1 5.3 %collective-permute-done.4.refs_5_ = bf16[1024,128]{1,0:T(8,128)(2,1)} collective-permute-done((bf16[1024,128]{1,0:T(8,128)(2,1)}, bf16[1024,128]{1,0:T(8,128)(2,1)}, u32[]{:S(2)}, u32[]{:S(2)}) %collective-permute-start.4) | collective-permute-done | bytes 262176 | tf_op jit(solution)/shard_map/ppermute | solution.py:236
  15.8 0.7 copy-done.4
  16.5 0.7 copy-done.6
  17.2 1.2 %collective-permute-start.5 = (bf16[768,512]{1,0:T(8,128)(2,1)}, bf16[768,512]{1,0:T(8,128)(2,1)S(1)}, u32[]{:S(2)}, u32[]{:S(2)}) collective-permute-start(bf16[768,512]{1,0:T(8,128)(2,1)} %get-tuple-element.20), channel_id=1, source_target_pairs={{0,16},{4,20},{8,24},{12,28},{16,0},{20,4},{24,8},{28,12},{1,17},{... | collective-permute-start | bytes 2359304 | tf_op jit(solution)/shard_map/ppermute | solution.py:236
  18.4 1.2 %collective-permute-start.10 = (bf16[768,512]{1,0:T(8,128)(2,1)}, bf16[768,512]{1,0:T(8,128)(2,1)S(1)}, u32[]{:S(2)}, u32[]{:S(2)}) collective-permute-start(bf16[768,512]{1,0:T(8,128)(2,1)} %get-tuple-element.24), channel_id=1, source_target_pairs={{0,8},{4,12},{8,0},{12,4},{16,24},{20,28},{24,16},{28,20},{1,9},{5... | collective-permute-start | bytes 2359304 | tf_op jit(solution)/shard_map/ppermute | solution.py:236
  19.7 0.9 %copy-done.5 = bf16[1024,128]{1,0:T(8,128)(2,1)S(1)} copy-done((bf16[1024,128]{1,0:T(8,128)(2,1)S(1)}, bf16[1024,128]{1,0:T(8,128)(2,1)}, u32[]{:S(2)}) %copy-start.5) | copy-done | bytes 262168
  20.7 0.9 %copy-done.7 = bf16[1024,128]{1,0:T(8,128)(2,1)S(1)} copy-done((bf16[1024,128]{1,0:T(8,128)(2,1)S(1)}, bf16[1024,128]{1,0:T(8,128)(2,1)}, u32[]{:S(2)}) %copy-start.7) | copy-done | bytes 262168
  21.6 5.3 %shard_map.55.refs_2_ = f32[768,256]{1,0:T(8,128)S(1)} custom-call(s32[3]{0:T(128)S(1)} %pad_add_fusion.1.starts, bf16[384,8192]{1,0:T(8,128)(2,1)} %bitcast.16, bf16[384,8192]{1,0:T(8,128)(2,1)} %collective-permute-done.far, bf16[1024,128]{1,0:T(8,128)(2,1)S(1)} %copy-done.2, bf16[1024,128]{1,0:T(8,128)(2,1)S(1)} %copy-done.3, ...), custom_call_target="tpu_custom_call" | custom-call | flops 1207959552 | bytes 6291456 | tf_op jit(solution)/shard_map/pallas_call | solution.py:111
  26.9 2.4 %shard_map.56 = (f32[384,256]{1,0:T(8,128)S(1)}, f32[384,256]{1,0:T(8,128)S(1)}) custom-call(s32[1]{0:T(128)} %bitcast.2.starts, bf16[384,8192]{1,0:T(8,128)(2,1)} %bitcast.17, bf16[384,8192]{1,0:T(8,128)(2,1)} %collective-permute-done.far, bf16[1024,128]{1,0:T(8,128)(2,1)} %collective-permute-done.6.refs_0_, ...), custom_call_target="tpu_custom_call" | custom-call | flops 402653184 | bytes 2097152 | tf_op jit(solution)/shard_map/pallas_call | solution.py:111
  29.4 2.9 %collective-permute-start.8 = (f32[384,256]{1,0:T(8,128)S(1)}, f32[384,256]{1,0:T(8,128)S(1)}, u32[]{:S(2)}, u32[]{:S(2)}) collective-permute-start(f32[384,256]{1,0:T(8,128)S(1)} %get-tuple-element.22), channel_id=1, source_target_pairs={{0,4},{4,0},{8,12},{12,8},{16,20},{20,16},{24,28},{28,24},{1,5},{5... | collective-permute-start | bytes 1179656 | tf_op jit(solution)/shard_map/ppermute | solution.py:236
  32.3 1.3 %collective-permute-done.8.far = f32[384,256]{1,0:T(8,128)S(1)} collective-permute-done((f32[384,256]{1,0:T(8,128)S(1)}, f32[384,256]{1,0:T(8,128)S(1)}, u32[]{:S(2)}, u32[]{:S(2)}) %collective-permute-start.8) | collective-permute-done | bytes 393248 | tf_op jit(solution)/shard_map/ppermute | solution.py:236
  33.8 3.2 %collective-permute-start.9 = (bf16[384,256]{1,0:T(8,128)(2,1)S(1)}, bf16[384,256]{1,0:T(8,128)(2,1)S(1)}, u32[]{:S(2)}, u32[]{:S(2)}) collective-permute-start(bf16[384,256]{1,0:T(8,128)(2,1)S(1)} %shard_map.57), channel_id=1, source_target_pairs={{0,1},{1,2},{2,3},{4,5},{5,6},{6,7},{8,9},{9,10},{10,11},{12,13},{... | collective-permute-start | bytes 589832 | tf_op jit(solution)/shard_map/ppermute | solution.py:285
  37.0 4.8 %collective-permute-done.9 = bf16[384,256]{1,0:T(8,128)(2,1)S(1)} collective-permute-done((bf16[384,256]{1,0:T(8,128)(2,1)S(1)}, bf16[384,256]{1,0:T(8,128)(2,1)S(1)}, u32[]{:S(2)}, u32[]{:S(2)}) %collective-permute-start.9) | collective-permute-done | bytes 196640 | tf_op jit(solution)/shard_map/ppermute | solution.py:285
  42.5 0.9 %slice.47 = bf16[512,512]{1,0:T(8,128)(2,1)} slice(bf16[768,512]{1,0:T(8,128)(2,1)S(1)} %collective-permute-done.5.refs_2_.refs_3_), slice={[0:512], [0:512]} | slice | bytes 1048576 | tf_op jit(solution)/shard_map/slice | solution.py:310
  43.4 0.9 %slice.46 = bf16[512,512]{1,0:T(8,128)(2,1)} slice(bf16[768,512]{1,0:T(8,128)(2,1)S(1)} %collective-permute-done.10.refs_0_.refs_1_), slice={[0:512], [0:512]} | slice | bytes 1048576 | tf_op jit(solution)/shard_map/slice | solution.py:310
  44.8 0.9 %pad_maximum_fusion.3 = bf16[512,512]{1,0:T(8,128)(2,1)} fusion(bf16[256,512]{1,0:T(8,128)(2,1)S(1)} %slice.44, bf16[256,512]{1,0:T(8,128)(2,1)S(1)} %slice.42), kind=kLoop, calls=%fused_computation.3 | loop fusion | flops 1048576 | bytes 1048576 | tf_op jit(solution)/shard_map/concatenate | solution.py:306
  45.6 1.3 %collective-permute-start.11 = (bf16[512,512]{1,0:T(8,128)(2,1)}, bf16[512,512]{1,0:T(8,128)(2,1)S(1)}, u32[]{:S(2)}, u32[]{:S(2)}) collective-permute-start(bf16[512,512]{1,0:T(8,128)(2,1)} %pad_maximum_fusion.3), channel_id=1, source_target_pairs={{0,1},{1,0},{2,3},{3,2},{4,5},{5,4},{6,7},{7,6},{8,9},{9,8},{10,11... | collective-permute-start | bytes 1572872 | tf_op jit(solution)/shard_map/ppermute | solution.py:307
  46.9 2.1 %collective-permute-start.12 = (bf16[384,256]{1,0:T(8,128)(2,1)}, bf16[384,256]{1,0:T(8,128)(2,1)}, u32[]{:S(2)}, u32[]{:S(2)}) collective-permute-start(bf16[384,256]{1,0:T(8,128)(2,1)} %copy-done.9), channel_id=1, source_target_pairs={{0,1},{1,2},{2,3},{4,5},{5,6},{6,7},{8,9},{9,10},{10,11},{12,13},{... | collective-permute-start | bytes 589832 | tf_op jit(solution)/shard_map/ppermute | solution.py:285
  49.1 4.8 %shard_map.58.refs_4_ = f32[768,512]{1,0:T(8,128)S(1)} custom-call(s32[6]{0:T(128)S(1)} %stack.58.starts, bf16[384,8192]{1,0:T(8,128)(2,1)} %bitcast.18, bf16[384,8192]{1,0:T(8,128)(2,1)} %collective-permute-done.far, bf16[768,512]{1,0:T(8,128)(2,1)S(1)} %collective-permute-done.10.refs_0_.refs_1_, ...), custom_call_target="tpu_custom_call" | custom-call | flops 2013265920 | bytes 6553600 | tf_op jit(solution)/shard_map/pallas_call | solution.py:111
  54.0 6.9 %collective-permute-done.12 = bf16[384,256]{1,0:T(8,128)(2,1)} collective-permute-done((bf16[384,256]{1,0:T(8,128)(2,1)}, bf16[384,256]{1,0:T(8,128)(2,1)}, u32[]{:S(2)}, u32[]{:S(2)}) %collective-permute-start.12) | collective-permute-done | bytes 196640 | tf_op jit(solution)/shard_map/ppermute | solution.py:285
  60.9 4.0 %shard_map.59 = (f32[384,512]{1,0:T(8,128)S(1)}, f32[384,512]{1,0:T(8,128)}) custom-call(s32[4]{0:T(128)S(1)} %pad_add_fusion.starts, bf16[384,8192]{1,0:T(8,128)(2,1)} %bitcast.19, bf16[384,8192]{1,0:T(8,128)(2,1)} %collective-permute-done.far, bf16[512,512]{1,0:T(8,128)(2,1)S(1)} %collective-permute-done.11.refs_0_.refs_1_, ...), custom_call_target="tpu_custom_call" | custom-call | flops 1207959552 | bytes 3932160 | tf_op jit(solution)/shard_map/pallas_call | solution.py:111
  64.9 2.7 %collective-permute-start.15 = (f32[384,512]{1,0:T(8,128)}, f32[384,512]{1,0:T(8,128)S(1)}, u32[]{:S(2)}, u32[]{:S(2)}) collective-permute-start(f32[384,512]{1,0:T(8,128)} %get-tuple-element.34), channel_id=1, source_target_pairs={{0,4},{4,0},{8,12},{12,8},{16,20},{20,16},{24,28},{28,24},{1,5},{5... | collective-permute-start | bytes 2359304 | tf_op jit(solution)/shard_map/ppermute | solution.py:236
  67.8 1.0 %pad_maximum_fusion.2.keys_values = bf16[1152,256]{1,0:T(8,128)(2,1)S(1)} fusion(bf16[384,256]{1,0:T(8,128)(2,1)S(1)} %copy-done.1, bf16[384,256]{1,0:T(8,128)(2,1)S(1)} %copy-done.10, bf16[384,256]{1,0:T(8,128)(2,1)} %collective-permute-done.12), kind=kLoop, calls=%fused_computation.2 | loop fusion | flops 1769472 | bytes 1179648 | tf_op jit(solution)/shard_map/concatenate | solution.py:286
  68.8 1.0 %collective-permute-done.15.far = f32[384,512]{1,0:T(8,128)S(1)} collective-permute-done((f32[384,512]{1,0:T(8,128)}, f32[384,512]{1,0:T(8,128)S(1)}, u32[]{:S(2)}, u32[]{:S(2)}) %collective-permute-start.15) | collective-permute-done | bytes 786464 | tf_op jit(solution)/shard_map/ppermute | solution.py:236
  69.8 3.6 %shard_map.60 = bf16[384,512]{1,0:T(8,128)(2,1)} custom-call(f32[384,512]{1,0:T(8,128)S(1)} %get-tuple-element.33.near, f32[384,512]{1,0:T(8,128)S(1)} %collective-permute-done.15.far, f32[384,128]{1,0:T(8,128)S(1)} %pad_maximum_fusion.4.cosine, f32[384,128]{1,0:T(8,128)S(1)} %pad_maximum_fusion.5.sine, s32[384,1]{1,0:T(8,128)S(1)} %copy.7.first, ...), custom_call_target="tpu_custom_call" | custom-call | flops 704643072 | bytes 1572864 | tf_op jit(solution)/shard_map/pallas_call | solution.py:206
  (51 shorter events, 4.6 us)
Async XLA Ops:
  0.0 7.1 %copy-start.8 = (bf16[1024,512]{1,0:T(8,128)(2,1)S(1)}, bf16[1024,512]{1,0:T(8,128)(2,1)}, u32[]{:S(2)}) copy-start(bf16[1024,512]{1,0:T(8,128)(2,1)} %param.6) | copy-start | bytes 3145732
  0.0 19.7 %collective-permute-start = (bf16[384,8192]{1,0:T(8,128)(2,1)}, bf16[384,8192]{1,0:T(8,128)(2,1)}, u32[]{:S(2)}, u32[]{:S(2)}) collective-permute-start(bf16[384,8192]{1,0:T(8,128)(2,1)} %bitcast.15), channel_id=1, source_target_pairs={{0,4},{4,0},{8,12},{12,8},{16,20},{20,16},{24,28},{28,24},{1,5},{5... | collective-permute-start | bytes 18874376 | tf_op jit(solution)/shard_map/ppermute | solution.py:236
  0.7 8.2 %collective-permute-start.1 = (bf16[1024,128]{1,0:T(8,128)(2,1)}, bf16[1024,128]{1,0:T(8,128)(2,1)}, u32[]{:S(2)}, u32[]{:S(2)}) collective-permute-start(bf16[1024,128]{1,0:T(8,128)(2,1)} %refs_0_.1), channel_id=1, source_target_pairs={{0,8},{4,12},{8,0},{12,4},{16,24},{20,28},{24,16},{28,20},{1,9},{5... | collective-permute-start | bytes 786440 | tf_op jit(solution)/shard_map/ppermute | solution.py:236
  1.9 13.9 %collective-permute-start.2 = (bf16[1024,128]{1,0:T(8,128)(2,1)}, bf16[1024,128]{1,0:T(8,128)(2,1)S(1)}, u32[]{:S(2)}, u32[]{:S(2)}) collective-permute-start(bf16[1024,128]{1,0:T(8,128)(2,1)} %refs_0_.1), channel_id=1, source_target_pairs={{0,16},{4,20},{8,24},{12,28},{16,0},{20,4},{24,8},{28,12},{1,17},{... | collective-permute-start | bytes 786440 | tf_op jit(solution)/shard_map/ppermute | solution.py:236
  3.1 12.2 %collective-permute-start.4 = (bf16[1024,128]{1,0:T(8,128)(2,1)}, bf16[1024,128]{1,0:T(8,128)(2,1)}, u32[]{:S(2)}, u32[]{:S(2)}) collective-permute-start(bf16[1024,128]{1,0:T(8,128)(2,1)} %refs_1_.1), channel_id=1, source_target_pairs={{0,16},{4,20},{8,24},{12,28},{16,0},{20,4},{24,8},{28,12},{1,17},{... | collective-permute-start | bytes 786440 | tf_op jit(solution)/shard_map/ppermute | solution.py:236
  3.4 13.1 %collective-permute-start.3 = (bf16[1024,128]{1,0:T(8,128)(2,1)}, bf16[1024,128]{1,0:T(8,128)(2,1)S(1)}, u32[]{:S(2)}, u32[]{:S(2)}) collective-permute-start(bf16[1024,128]{1,0:T(8,128)(2,1)} %refs_1_.1), channel_id=1, source_target_pairs={{0,8},{4,12},{8,0},{12,4},{16,24},{20,28},{24,16},{28,20},{1,9},{5... | collective-permute-start | bytes 786440 | tf_op jit(solution)/shard_map/ppermute | solution.py:236
  7.3 12.4 %copy-start.2 = (bf16[1024,128]{1,0:T(8,128)(2,1)S(1)}, bf16[1024,128]{1,0:T(8,128)(2,1)}, u32[]{:S(2)}) copy-start(bf16[1024,128]{1,0:T(8,128)(2,1)} %refs_0_.1) | copy-start | bytes 786436
  7.3 12.4 %copy-start.3 = (bf16[1024,128]{1,0:T(8,128)(2,1)S(1)}, bf16[1024,128]{1,0:T(8,128)(2,1)}, u32[]{:S(2)}) copy-start(bf16[1024,128]{1,0:T(8,128)(2,1)} %refs_1_.1) | copy-start | bytes 786436
  8.9 18.0 %collective-permute-start.6 = (bf16[1024,128]{1,0:T(8,128)(2,1)}, bf16[1024,128]{1,0:T(8,128)(2,1)}, u32[]{:S(2)}, u32[]{:S(2)}) collective-permute-start(bf16[1024,128]{1,0:T(8,128)(2,1)} %collective-permute-done.1.refs_2_), channel_id=1, source_target_pairs={{0,16},{4,20},{8,24},{12,28},{16,0},{20,4},{24,8},{28,12},{1,17},{... | collective-permute-start | bytes 786440 | tf_op jit(solution)/shard_map/ppermute | solution.py:236
  15.4 11.5 %collective-permute-start.7 = (bf16[1024,128]{1,0:T(8,128)(2,1)}, bf16[1024,128]{1,0:T(8,128)(2,1)}, u32[]{:S(2)}, u32[]{:S(2)}) collective-permute-start(bf16[1024,128]{1,0:T(8,128)(2,1)} %collective-permute-done.4.refs_5_), channel_id=1, source_target_pairs={{0,8},{4,12},{8,0},{12,4},{16,24},{20,28},{24,16},{28,20},{1,9},{5... | collective-permute-start | bytes 786440 | tf_op jit(solution)/shard_map/ppermute | solution.py:236
  15.8 0.7 copy-start.4
  16.5 0.7 copy-start.6
  17.2 25.3 %collective-permute-start.5 = (bf16[768,512]{1,0:T(8,128)(2,1)}, bf16[768,512]{1,0:T(8,128)(2,1)S(1)}, u32[]{:S(2)}, u32[]{:S(2)}) collective-permute-start(bf16[768,512]{1,0:T(8,128)(2,1)} %get-tuple-element.20), channel_id=1, source_target_pairs={{0,16},{4,20},{8,24},{12,28},{16,0},{20,4},{24,8},{28,12},{1,17},{... | collective-permute-start | bytes 2359304 | tf_op jit(solution)/shard_map/ppermute | solution.py:236
  18.4 24.9 %collective-permute-start.10 = (bf16[768,512]{1,0:T(8,128)(2,1)}, bf16[768,512]{1,0:T(8,128)(2,1)S(1)}, u32[]{:S(2)}, u32[]{:S(2)}) collective-permute-start(bf16[768,512]{1,0:T(8,128)(2,1)} %get-tuple-element.24), channel_id=1, source_target_pairs={{0,8},{4,12},{8,0},{12,4},{16,24},{20,28},{24,16},{28,20},{1,9},{5... | collective-permute-start | bytes 2359304 | tf_op jit(solution)/shard_map/ppermute | solution.py:236
  19.7 1.0 %copy-start.5 = (bf16[1024,128]{1,0:T(8,128)(2,1)S(1)}, bf16[1024,128]{1,0:T(8,128)(2,1)}, u32[]{:S(2)}) copy-start(bf16[1024,128]{1,0:T(8,128)(2,1)} %copy-done.4) | copy-start | bytes 786436
  20.7 0.9 %copy-start.7 = (bf16[1024,128]{1,0:T(8,128)(2,1)S(1)}, bf16[1024,128]{1,0:T(8,128)(2,1)}, u32[]{:S(2)}) copy-start(bf16[1024,128]{1,0:T(8,128)(2,1)} %copy-done.6) | copy-start | bytes 786436
  29.4 4.3 %collective-permute-start.8 = (f32[384,256]{1,0:T(8,128)S(1)}, f32[384,256]{1,0:T(8,128)S(1)}, u32[]{:S(2)}, u32[]{:S(2)}) collective-permute-start(f32[384,256]{1,0:T(8,128)S(1)} %get-tuple-element.22), channel_id=1, source_target_pairs={{0,4},{4,0},{8,12},{12,8},{16,20},{20,16},{24,28},{28,24},{1,5},{5... | collective-permute-start | bytes 1179656 | tf_op jit(solution)/shard_map/ppermute | solution.py:236
  33.8 10.5 %copy-start = (bf16[384,256]{1,0:T(8,128)(2,1)}, bf16[384,256]{1,0:T(8,128)(2,1)S(1)}, u32[]{:S(2)}) copy-start(bf16[384,256]{1,0:T(8,128)(2,1)S(1)} %shard_map.57) | copy-start | bytes 589828
  33.8 8.0 %collective-permute-start.9 = (bf16[384,256]{1,0:T(8,128)(2,1)S(1)}, bf16[384,256]{1,0:T(8,128)(2,1)S(1)}, u32[]{:S(2)}, u32[]{:S(2)}) collective-permute-start(bf16[384,256]{1,0:T(8,128)(2,1)S(1)} %shard_map.57), channel_id=1, source_target_pairs={{0,1},{1,2},{2,3},{4,5},{5,6},{6,7},{8,9},{9,10},{10,11},{12,13},{... | collective-permute-start | bytes 589832 | tf_op jit(solution)/shard_map/ppermute | solution.py:285
  41.8 0.7 copy-start.9
  44.2 16.7 %collective-permute-start.14 = (bf16[512,512]{1,0:T(8,128)(2,1)}, bf16[512,512]{1,0:T(8,128)(2,1)}, u32[]{:S(2)}, u32[]{:S(2)}) collective-permute-start(bf16[512,512]{1,0:T(8,128)(2,1)} %slice.47), channel_id=1, source_target_pairs={{0,8},{4,12},{8,0},{12,4},{16,24},{20,28},{24,16},{28,20},{1,9},{5... | collective-permute-start | bytes 1572872 | tf_op jit(solution)/shard_map/ppermute | solution.py:236
  44.6 16.3 %collective-permute-start.13 = (bf16[512,512]{1,0:T(8,128)(2,1)}, bf16[512,512]{1,0:T(8,128)(2,1)}, u32[]{:S(2)}, u32[]{:S(2)}) collective-permute-start(bf16[512,512]{1,0:T(8,128)(2,1)} %slice.46), channel_id=1, source_target_pairs={{0,16},{4,20},{8,24},{12,28},{16,0},{20,4},{24,8},{28,12},{1,17},{... | collective-permute-start | bytes 1572872 | tf_op jit(solution)/shard_map/ppermute | solution.py:236
  45.6 15.3 %collective-permute-start.11 = (bf16[512,512]{1,0:T(8,128)(2,1)}, bf16[512,512]{1,0:T(8,128)(2,1)S(1)}, u32[]{:S(2)}, u32[]{:S(2)}) collective-permute-start(bf16[512,512]{1,0:T(8,128)(2,1)} %pad_maximum_fusion.3), channel_id=1, source_target_pairs={{0,1},{1,0},{2,3},{3,2},{4,5},{5,4},{6,7},{7,6},{8,9},{9,8},{10,11... | collective-permute-start | bytes 1572872 | tf_op jit(solution)/shard_map/ppermute | solution.py:307
  46.9 14.0 %collective-permute-start.12 = (bf16[384,256]{1,0:T(8,128)(2,1)}, bf16[384,256]{1,0:T(8,128)(2,1)}, u32[]{:S(2)}, u32[]{:S(2)}) collective-permute-start(bf16[384,256]{1,0:T(8,128)(2,1)} %copy-done.9), channel_id=1, source_target_pairs={{0,1},{1,2},{2,3},{4,5},{5,6},{6,7},{8,9},{9,10},{10,11},{12,13},{... | collective-permute-start | bytes 589832 | tf_op jit(solution)/shard_map/ppermute | solution.py:285
  54.0 13.8 %copy-start.1 = (bf16[384,256]{1,0:T(8,128)(2,1)S(1)}, bf16[384,256]{1,0:T(8,128)(2,1)}, u32[]{:S(2)}) copy-start(bf16[384,256]{1,0:T(8,128)(2,1)} %copy-done) | copy-start | bytes 589828
  54.0 13.8 %copy-start.10 = (bf16[384,256]{1,0:T(8,128)(2,1)S(1)}, bf16[384,256]{1,0:T(8,128)(2,1)}, u32[]{:S(2)}) copy-start(bf16[384,256]{1,0:T(8,128)(2,1)} %copy-done.9) | copy-start | bytes 589828
  64.9 4.9 %collective-permute-start.15 = (f32[384,512]{1,0:T(8,128)}, f32[384,512]{1,0:T(8,128)S(1)}, u32[]{:S(2)}, u32[]{:S(2)}) collective-permute-start(f32[384,512]{1,0:T(8,128)} %get-tuple-element.34), channel_id=1, source_target_pairs={{0,4},{4,0},{8,12},{12,8},{16,20},{20,16},{24,28},{28,24},{1,5},{5... | collective-permute-start | bytes 2359304 | tf_op jit(solution)/shard_map/ppermute | solution.py:236

commit v12 on v11

--- a/solution.py
+++ b/solution.py
@@ -262,9 +262,10 @@
 
     axes = [1 << axis for axis in range(bits)]
     half = depth // 2
-    some = half // 2
-    halved = ctx_size % 2 == 0 and bits > 1
-    begin = (place % 2) * some
+    lack = 128
+    keep = half - lack
+    halved = ctx_size % 2 == 0 and bits > 1 and keep > 0
+    odd = place % 2
     halves = [w_query[:half], w_query[half:]]
 
     pair_held = fetch((w_key, w_value), [{}, {}], [], [])
@@ -284,7 +285,7 @@
     for _ in range(min(ctx_size - 1, -(-back // row_count))):
         blocks.insert(0, lax.ppermute(blocks[0], "ctx", [(i, i + 1) for i in range(ctx_size - 1)]))
     keys_values = jnp.concatenate(blocks, axis=0)
-    direct = [corner(pair_held[side][chip]) for side in range(2) for chip in axes]
+    direct = [pair_held[0][axes[-1]], pair_held[1][axes[0]]]
     gate = [*direct, cosine, sine, first]
     later = [corner(blocks[-2])]
 
@@ -296,29 +297,28 @@
             jnp.concatenate(
                 [
                     halves[side],
-                    lax.dynamic_slice_in_dim(w_query, (1 - side) * half + begin, some, 0),
+                    lax.dynamic_slice_in_dim(w_query, (1 - side) * half + odd * lack, keep, 0),
                 ],
                 axis=0,
             )
             for side in range(2)
         ]
         got = [swap(after(joined[side], *gate), 2 << ends[side]) for side in range(2)]
-        both = jnp.concatenate([after(got[1 - side], *later)[half:] for side in range(2)], axis=0)
+        row = half + odd * (keep - lack)
+        both = [
+            lax.dynamic_slice_in_dim(after(got[1 - side], *later), row, lack, 0)
+            for side in range(2)
+        ]
+        both = jnp.concatenate(both, axis=0)
         both = lax.ppermute(both, "ctx", [(i, i ^ 1) for i in range(ctx_size)])
         for side in range(2):
             chip = 1 << ends[side]
             given[side][chip] = after(got[side], *later)[:half]
             given[1 - side][chip] = None
             early.append((begins(chip) + side * half, [got[side]], 0, half))
-            early.append((begins(chip) + (1 - side) * half + begin, [got[side]], half, some))
-            late.append(
-                (
-                    begins(chip) + (1 - side) * half + some - begin,
-                    [both],
-                    (1 - side) * some,
-                    some,
-                )
-            )
+            first_row = begins(chip) + (1 - side) * half
+            early.append((first_row + odd * lack, [got[side]], half, keep))
+            late.append((first_row + (1 - odd) * keep, [both], (1 - side) * lack, lack))
     query_held = fetch(halves, given, gate, later)
     for side in range(2):
         for chip in range(chips):

time: 74.9 us -> 85.2 us (1.14)
  waiting for transfers between devices: 19.6 us -> 30 us
  starting transfers between devices: 20.3 us -> 19.4 us
    ppermute x13, waiting for transfers between devices: 7.94 us -> 24.4 us  [swap(): return lax.ppermute(array, 'dp', [(i, i ^ mask) for i in range(dp_size)])]
    ppermute x2, waiting for transfers between devices: 11.7 us -> 5.62 us  [shards(): lax.ppermute(blocks[0], 'ctx', [(i, i + 1) for i in range(ctx_size - 1)])]
    ppermute x13, starting transfers between devices: 13.7 us -> 12.8 us  [swap(): return lax.ppermute(array, 'dp', [(i, i ^ mask) for i in range(dp_size)])]
    unnamed x22 -> x20, local copies, waits for them, and re-layouts: 4.02 us -> 4.33 us
  transfers between devices with their start and end apart: 16 -> 16, of which waited for: 6 -> 8; matrix products, arithmetic and copies ran while one was open for 11% -> 9% of each run, Pallas kernels for 17% -> 16%
where the time goes in v12:
time: 85.2 us; the launch traced here: 83.7 us
  waiting for transfers between devices  30 us (35%)
  Pallas kernels  20.7 us (24%)
  starting transfers between devices  19.4 us (23%)
  local copies, waits for them, and re-layouts  7.53 us (9%)
  other arithmetic  5.91 us (7%)
    ppermute x13, waiting for transfers between devices, swap(): return lax.ppermute(array, 'dp', [(i, i ^ mask) for i in range(dp_size)])  24.4 us
    pallas_call x4, Pallas kernels, project(): pl.pallas_call(functools.partial(project_kernel, steps, carry is not None...  17 us
    ppermute x13, starting transfers between devices, swap(): return lax.ppermute(array, 'dp', [(i, i ^ mask) for i in range(dp_size)])  12.8 us
    ppermute x2, waiting for transfers between devices, shards(): lax.ppermute(blocks[0], 'ctx', [(i, i + 1) for i in range(ctx_size - 1)])  5.62 us
    ppermute x2, starting transfers between devices, shards(): lax.ppermute(blocks[0], 'ctx', [(i, i + 1) for i in range(ctx_size - 1)])  5.27 us
    unnamed x20, local copies, waits for them, and re-layouts  4.33 us
    pallas_call x1, Pallas kernels, attend(): pl.pallas_call(functools.partial(attend_kernel, back), out_shape=jax.Shap...  3.65 us
    slice x2, local copies, waits for them, and re-layouts, shards(): given[side][chip] = after(got[side], *later)[:half]  1.72 us
  transfers between devices with their start and end apart: 16, of which 8 were waited for; matrix products, arithmetic and copies ran while one was open for 9% of the time, Pallas kernels for 16%

profile of v12, /device:TPU:17, one launch (start us, length us, event | category | flops | bytes accessed | tf_op | source)
XLA Modules:
  0.0 83.7 jit_solution(1986507576354289576)
XLA Ops:
  0.7 1.2 %collective-permute-start.4 = (bf16[1024,128]{1,0:T(8,128)(2,1)}, bf16[1024,128]{1,0:T(8,128)(2,1)}, u32[]{:S(2)}, u32[]{:S(2)}) collective-permute-start(bf16[1024,128]{1,0:T(8,128)(2,1)} %refs_0_.1), channel_id=1, source_target_pairs={{0,8},{4,12},{8,0},{12,4},{16,24},{20,28},{24,16},{28,20},{1,9},{5... | collective-permute-start | bytes 786440 | tf_op jit(solution)/shard_map/ppermute | solution.py:236
  1.9 1.2 %collective-permute-start.1 = (bf16[1024,128]{1,0:T(8,128)(2,1)}, bf16[1024,128]{1,0:T(8,128)(2,1)S(1)}, u32[]{:S(2)}, u32[]{:S(2)}) collective-permute-start(bf16[1024,128]{1,0:T(8,128)(2,1)} %refs_0_.1), channel_id=1, source_target_pairs={{0,16},{4,20},{8,24},{12,28},{16,0},{20,4},{24,8},{28,12},{1,17},{... | collective-permute-start | bytes 786440 | tf_op jit(solution)/shard_map/ppermute | solution.py:236
  3.6 0.8 %reduce-window_clone.1 = s32[1,16]{1,0:T(1,128)S(1)} reduce-window(s32[1,16]{1,0:T(1,128)} %param.9, s32[]{:T(128)} %constant.41.clone.1), window={size=1x16 pad=0_0x15_0}, to_apply=%region_0.0 | reduce-window | flops 240 | bytes 132 | tf_op jit(solution)/shard_map/reduce-window.clone
  5.2 0.8 fusion
  6.1 1.2 %constant_dynamic-slice_fusion.3 = (bf16[384,512]{1,0:T(8,128)(2,1)S(1)}, bf16[384,512]{1,0:T(8,128)(2,1)S(1)}) fusion(bf16[1024,512]{1,0:T(8,128)(2,1)} %param.6, s32[]{:T(128)S(6)} %select_n.22, s32[]{:T(128)S(6)} %select_n.25), kind=kLoop, calls=%fused_computation.15 | loop fusion | bytes 1572872 | tf_op jit(solution)/shard_map/dynamic_slice | solution.py:300
  7.5 1.4 %pad_maximum_fusion = (bf16[896,512]{1,0:T(8,128)(2,1)}, bf16[896,512]{1,0:T(8,128)(2,1)}) fusion(bf16[384,512]{1,0:T(8,128)(2,1)S(1)} %get-tuple-element.37, bf16[512,512]{1,0:T(8,128)(2,1)S(1)} %get-tuple-element.32.refs_5_, bf16[384,512]{1,0:T(8,128)(2,1)S(1)} %get-tuple-element.38, bf16[512,512]{1,0:T(8,128)(2,1)S(1)} %get-tuple-element.31.refs_4_), kind=kLoop, calls=%fused_computation | loop fusion | flops 3670016 | bytes 3670016 | tf_op jit(solution)/shard_map/concatenate | solution.py:297
  8.9 0.8 %collective-permute-done.1.refs_4_ = bf16[1024,128]{1,0:T(8,128)(2,1)S(1)} collective-permute-done((bf16[1024,128]{1,0:T(8,128)(2,1)}, bf16[1024,128]{1,0:T(8,128)(2,1)S(1)}, u32[]{:S(2)}, u32[]{:S(2)}) %collective-permute-start.1) | collective-permute-done | bytes 262176 | tf_op jit(solution)/shard_map/ppermute | solution.py:236
  10.5 4.0 %collective-permute-done.2.refs_3_ = bf16[1024,128]{1,0:T(8,128)(2,1)S(1)} collective-permute-done((bf16[1024,128]{1,0:T(8,128)(2,1)}, bf16[1024,128]{1,0:T(8,128)(2,1)S(1)}, u32[]{:S(2)}, u32[]{:S(2)}) %collective-permute-start.2) | collective-permute-done | bytes 262176 | tf_op jit(solution)/shard_map/ppermute | solution.py:236
  15.2 1.2 %collective-permute-start.10 = (bf16[896,512]{1,0:T(8,128)(2,1)}, bf16[896,512]{1,0:T(8,128)(2,1)S(1)}, u32[]{:S(2)}, u32[]{:S(2)}) collective-permute-start(bf16[896,512]{1,0:T(8,128)(2,1)} %get-tuple-element.24), channel_id=1, source_target_pairs={{0,8},{4,12},{8,0},{12,4},{16,24},{20,28},{24,16},{28,20},{1,9},{5... | collective-permute-start | bytes 2752520 | tf_op jit(solution)/shard_map/ppermute | solution.py:236
  16.4 1.2 %collective-permute-start.3 = (bf16[896,512]{1,0:T(8,128)(2,1)}, bf16[896,512]{1,0:T(8,128)(2,1)S(1)}, u32[]{:S(2)}, u32[]{:S(2)}) collective-permute-start(bf16[896,512]{1,0:T(8,128)(2,1)} %get-tuple-element.20), channel_id=1, source_target_pairs={{0,16},{4,20},{8,24},{12,28},{16,0},{20,4},{24,8},{28,12},{1,17},{... | collective-permute-start | bytes 2752520 | tf_op jit(solution)/shard_map/ppermute | solution.py:236
  18.2 0.9 %copy-done.3 = bf16[1024,128]{1,0:T(8,128)(2,1)S(1)} copy-done((bf16[1024,128]{1,0:T(8,128)(2,1)S(1)}, bf16[1024,128]{1,0:T(8,128)(2,1)}, u32[]{:S(2)}) %copy-start.3) | copy-done | bytes 262168
  19.2 0.9 %copy-done.5 = bf16[1024,128]{1,0:T(8,128)(2,1)S(1)} copy-done((bf16[1024,128]{1,0:T(8,128)(2,1)S(1)}, bf16[1024,128]{1,0:T(8,128)(2,1)}, u32[]{:S(2)}) %copy-start.5) | copy-done | bytes 262168
  20.1 0.9 %copy-done.7 = bf16[1024,128]{1,0:T(8,128)(2,1)S(1)} copy-done((bf16[1024,128]{1,0:T(8,128)(2,1)S(1)}, bf16[1024,128]{1,0:T(8,128)(2,1)}, u32[]{:S(2)}) %copy-start.7) | copy-done | bytes 262168
  21.1 5.3 %shard_map.55.refs_2_ = f32[768,256]{1,0:T(8,128)S(1)} custom-call(s32[3]{0:T(128)S(1)} %pad_add_fusion.1.starts, bf16[384,8192]{1,0:T(8,128)(2,1)} %bitcast.16, bf16[384,8192]{1,0:T(8,128)(2,1)} %collective-permute-done.far, bf16[1024,128]{1,0:T(8,128)(2,1)S(1)} %copy-done.2, bf16[1024,128]{1,0:T(8,128)(2,1)S(1)} %copy-done.3, ...), custom_call_target="tpu_custom_call" | custom-call | flops 1207959552 | bytes 6291456 | tf_op jit(solution)/shard_map/pallas_call | solution.py:111
  26.3 16.8 %collective-permute-done.5.refs_0_ = bf16[1024,128]{1,0:T(8,128)(2,1)} collective-permute-done((bf16[1024,128]{1,0:T(8,128)(2,1)}, bf16[1024,128]{1,0:T(8,128)(2,1)}, u32[]{:S(2)}, u32[]{:S(2)}) %collective-permute-start.5) | collective-permute-done | bytes 262176 | tf_op jit(solution)/shard_map/ppermute | solution.py:236
  43.2 2.4 %shard_map.56 = (f32[384,256]{1,0:T(8,128)S(1)}, f32[384,256]{1,0:T(8,128)S(1)}) custom-call(s32[1]{0:T(128)} %bitcast.2.starts, bf16[384,8192]{1,0:T(8,128)(2,1)} %bitcast.17, bf16[384,8192]{1,0:T(8,128)(2,1)} %collective-permute-done.far, bf16[1024,128]{1,0:T(8,128)(2,1)} %collective-permute-done.5.refs_0_, ...), custom_call_target="tpu_custom_call" | custom-call | flops 402653184 | bytes 2097152 | tf_op jit(solution)/shard_map/pallas_call | solution.py:111
  45.6 2.0 %collective-permute-start.8 = (f32[384,256]{1,0:T(8,128)S(1)}, f32[384,256]{1,0:T(8,128)S(1)}, u32[]{:S(2)}, u32[]{:S(2)}) collective-permute-start(f32[384,256]{1,0:T(8,128)S(1)} %get-tuple-element.22), channel_id=1, source_target_pairs={{0,4},{4,0},{8,12},{12,8},{16,20},{20,16},{24,28},{28,24},{1,5},{5... | collective-permute-start | bytes 1179656 | tf_op jit(solution)/shard_map/ppermute | solution.py:236
  47.6 1.3 %collective-permute-done.8.far = f32[384,256]{1,0:T(8,128)S(1)} collective-permute-done((f32[384,256]{1,0:T(8,128)S(1)}, f32[384,256]{1,0:T(8,128)S(1)}, u32[]{:S(2)}, u32[]{:S(2)}) %collective-permute-start.8) | collective-permute-done | bytes 393248 | tf_op jit(solution)/shard_map/ppermute | solution.py:236
  49.1 3.2 %collective-permute-start.9 = (bf16[384,256]{1,0:T(8,128)(2,1)S(1)}, bf16[384,256]{1,0:T(8,128)(2,1)}, u32[]{:S(2)}, u32[]{:S(2)}) collective-permute-start(bf16[384,256]{1,0:T(8,128)(2,1)S(1)} %shard_map.57), channel_id=1, source_target_pairs={{0,1},{1,2},{2,3},{4,5},{5,6},{6,7},{8,9},{9,10},{10,11},{12,13},{... | collective-permute-start | bytes 589832 | tf_op jit(solution)/shard_map/ppermute | solution.py:286
  52.3 4.9 %collective-permute-done.9 = bf16[384,256]{1,0:T(8,128)(2,1)} collective-permute-done((bf16[384,256]{1,0:T(8,128)(2,1)S(1)}, bf16[384,256]{1,0:T(8,128)(2,1)}, u32[]{:S(2)}, u32[]{:S(2)}) %collective-permute-start.9) | collective-permute-done | bytes 196640 | tf_op jit(solution)/shard_map/ppermute | solution.py:286
  57.2 0.9 %slice.23 = bf16[512,512]{1,0:T(8,128)(2,1)} slice(bf16[896,512]{1,0:T(8,128)(2,1)S(1)} %collective-permute-done.3.refs_2_.refs_3_), slice={[0:512], [0:512]} | slice | bytes 1048576 | tf_op jit(solution)/shard_map/slice | solution.py:316
  58.1 0.8 slice.22
  59.2 1.2 %collective-permute-start.13 = (bf16[512,512]{1,0:T(8,128)(2,1)}, bf16[512,512]{1,0:T(8,128)(2,1)}, u32[]{:S(2)}, u32[]{:S(2)}) collective-permute-start(bf16[512,512]{1,0:T(8,128)(2,1)} %slice.22), channel_id=1, source_target_pairs={{0,16},{4,20},{8,24},{12,28},{16,0},{20,4},{24,8},{28,12},{1,17},{... | collective-permute-start | bytes 1572872 | tf_op jit(solution)/shard_map/ppermute | solution.py:236
  60.5 0.7 pad_maximum_fusion.3
  61.2 1.3 %collective-permute-start.11 = (bf16[256,512]{1,0:T(8,128)(2,1)}, bf16[256,512]{1,0:T(8,128)(2,1)S(1)}, u32[]{:S(2)}, u32[]{:S(2)}) collective-permute-start(bf16[256,512]{1,0:T(8,128)(2,1)} %pad_maximum_fusion.3), channel_id=1, source_target_pairs={{0,1},{1,0},{2,3},{3,2},{4,5},{5,4},{6,7},{7,6},{8,9},{9,8},{10,11... | collective-permute-start | bytes 786440 | tf_op jit(solution)/shard_map/ppermute | solution.py:313
  62.6 2.1 %collective-permute-start.12 = (bf16[384,256]{1,0:T(8,128)(2,1)}, bf16[384,256]{1,0:T(8,128)(2,1)S(1)}, u32[]{:S(2)}, u32[]{:S(2)}) collective-permute-start(bf16[384,256]{1,0:T(8,128)(2,1)} %collective-permute-done.9), channel_id=1, source_target_pairs={{0,1},{1,2},{2,3},{4,5},{5,6},{6,7},{8,9},{9,10},{10,11},{12,13},{... | collective-permute-start | bytes 589832 | tf_op jit(solution)/shard_map/ppermute | solution.py:286
  64.7 5.4 %shard_map.58.refs_4_ = f32[768,512]{1,0:T(8,128)S(1)} custom-call(s32[6]{0:T(128)S(1)} %stack.58.starts, bf16[384,8192]{1,0:T(8,128)(2,1)} %bitcast.18, bf16[384,8192]{1,0:T(8,128)(2,1)} %collective-permute-done.far, bf16[896,512]{1,0:T(8,128)(2,1)S(1)} %collective-permute-done.10.refs_0_.refs_1_, ...), custom_call_target="tpu_custom_call" | custom-call | flops 2214592512 | bytes 7208960 | tf_op jit(solution)/shard_map/pallas_call | solution.py:111
  70.1 0.7 collective-permute-done.12
  71.5 3.9 %shard_map.59 = (f32[384,512]{1,0:T(8,128)S(1)}, f32[384,512]{1,0:T(8,128)S(1)}) custom-call(s32[4]{0:T(128)S(1)} %pad_add_fusion.starts, bf16[384,8192]{1,0:T(8,128)(2,1)} %bitcast.19, bf16[384,8192]{1,0:T(8,128)(2,1)} %collective-permute-done.far, bf16[256,512]{1,0:T(8,128)(2,1)S(1)} %collective-permute-done.11.refs_0_.refs_1_, ...), custom_call_target="tpu_custom_call" | custom-call | flops 1006632960 | bytes 3276800 | tf_op jit(solution)/shard_map/pallas_call | solution.py:111
  75.4 2.7 %collective-permute-start.15 = (f32[384,512]{1,0:T(8,128)S(1)}, f32[384,512]{1,0:T(8,128)S(1)}, u32[]{:S(2)}, u32[]{:S(2)}) collective-permute-start(f32[384,512]{1,0:T(8,128)S(1)} %get-tuple-element.34), channel_id=1, source_target_pairs={{0,4},{4,0},{8,12},{12,8},{16,20},{20,16},{24,28},{28,24},{1,5},{5... | collective-permute-start | bytes 2359304 | tf_op jit(solution)/shard_map/ppermute | solution.py:236
  78.3 1.1 %pad_maximum_fusion.2.keys_values = bf16[1152,256]{1,0:T(8,128)(2,1)S(1)} fusion(bf16[384,256]{1,0:T(8,128)(2,1)S(1)} %copy-done.1, bf16[384,256]{1,0:T(8,128)(2,1)} %collective-permute-done.9, bf16[384,256]{1,0:T(8,128)(2,1)} %copy-done.9), kind=kLoop, calls=%fused_computation.2 | loop fusion | flops 1769472 | bytes 1179648 | tf_op jit(solution)/shard_map/concatenate | solution.py:287
  80.1 3.6 %shard_map.60 = bf16[384,512]{1,0:T(8,128)(2,1)} custom-call(f32[384,512]{1,0:T(8,128)S(1)} %get-tuple-element.33.near, f32[384,512]{1,0:T(8,128)S(1)} %collective-permute-done.15.far, f32[384,128]{1,0:T(8,128)S(1)} %pad_maximum_fusion.4.cosine, f32[384,128]{1,0:T(8,128)S(1)} %pad_maximum_fusion.5.sine, s32[384,1]{1,0:T(8,128)S(1)} %copy.7.first, ...), custom_call_target="tpu_custom_call" | custom-call | flops 704643072 | bytes 1572864 | tf_op jit(solution)/shard_map/pallas_call | solution.py:206
  (49 shorter events, 6.3 us)
Async XLA Ops:
  0.0 7.3 %copy-start.8 = (bf16[1024,512]{1,0:T(8,128)(2,1)S(1)}, bf16[1024,512]{1,0:T(8,128)(2,1)}, u32[]{:S(2)}) copy-start(bf16[1024,512]{1,0:T(8,128)(2,1)} %param.6) | copy-start | bytes 3145732
  0.0 18.2 %collective-permute-start = (bf16[384,8192]{1,0:T(8,128)(2,1)}, bf16[384,8192]{1,0:T(8,128)(2,1)}, u32[]{:S(2)}, u32[]{:S(2)}) collective-permute-start(bf16[384,8192]{1,0:T(8,128)(2,1)} %bitcast.15), channel_id=1, source_target_pairs={{0,4},{4,0},{8,12},{12,8},{16,20},{20,16},{24,28},{28,24},{1,5},{5... | collective-permute-start | bytes 18874376 | tf_op jit(solution)/shard_map/ppermute | solution.py:236
  0.7 17.0 %collective-permute-start.4 = (bf16[1024,128]{1,0:T(8,128)(2,1)}, bf16[1024,128]{1,0:T(8,128)(2,1)}, u32[]{:S(2)}, u32[]{:S(2)}) collective-permute-start(bf16[1024,128]{1,0:T(8,128)(2,1)} %refs_0_.1), channel_id=1, source_target_pairs={{0,8},{4,12},{8,0},{12,4},{16,24},{20,28},{24,16},{28,20},{1,9},{5... | collective-permute-start | bytes 786440 | tf_op jit(solution)/shard_map/ppermute | solution.py:236
  1.9 7.9 %collective-permute-start.1 = (bf16[1024,128]{1,0:T(8,128)(2,1)}, bf16[1024,128]{1,0:T(8,128)(2,1)S(1)}, u32[]{:S(2)}, u32[]{:S(2)}) collective-permute-start(bf16[1024,128]{1,0:T(8,128)(2,1)} %refs_0_.1), channel_id=1, source_target_pairs={{0,16},{4,20},{8,24},{12,28},{16,0},{20,4},{24,8},{28,12},{1,17},{... | collective-permute-start | bytes 786440 | tf_op jit(solution)/shard_map/ppermute | solution.py:236
  3.1 14.7 %collective-permute-start.6 = (bf16[1024,128]{1,0:T(8,128)(2,1)}, bf16[1024,128]{1,0:T(8,128)(2,1)}, u32[]{:S(2)}, u32[]{:S(2)}) collective-permute-start(bf16[1024,128]{1,0:T(8,128)(2,1)} %refs_1_.1), channel_id=1, source_target_pairs={{0,16},{4,20},{8,24},{12,28},{16,0},{20,4},{24,8},{28,12},{1,17},{... | collective-permute-start | bytes 786440 | tf_op jit(solution)/shard_map/ppermute | solution.py:236
  3.4 11.1 %collective-permute-start.2 = (bf16[1024,128]{1,0:T(8,128)(2,1)}, bf16[1024,128]{1,0:T(8,128)(2,1)S(1)}, u32[]{:S(2)}, u32[]{:S(2)}) collective-permute-start(bf16[1024,128]{1,0:T(8,128)(2,1)} %refs_1_.1), channel_id=1, source_target_pairs={{0,8},{4,12},{8,0},{12,4},{16,24},{20,28},{24,16},{28,20},{1,9},{5... | collective-permute-start | bytes 786440 | tf_op jit(solution)/shard_map/ppermute | solution.py:236
  7.5 10.7 %copy-start.2 = (bf16[1024,128]{1,0:T(8,128)(2,1)S(1)}, bf16[1024,128]{1,0:T(8,128)(2,1)}, u32[]{:S(2)}) copy-start(bf16[1024,128]{1,0:T(8,128)(2,1)} %refs_0_.1) | copy-start | bytes 786436
  9.8 0.7 copy-start.4
  14.5 0.7 copy-start.6
  15.2 42.0 %collective-permute-start.10 = (bf16[896,512]{1,0:T(8,128)(2,1)}, bf16[896,512]{1,0:T(8,128)(2,1)S(1)}, u32[]{:S(2)}, u32[]{:S(2)}) collective-permute-start(bf16[896,512]{1,0:T(8,128)(2,1)} %get-tuple-element.24), channel_id=1, source_target_pairs={{0,8},{4,12},{8,0},{12,4},{16,24},{20,28},{24,16},{28,20},{1,9},{5... | collective-permute-start | bytes 2752520 | tf_op jit(solution)/shard_map/ppermute | solution.py:236
  16.4 40.8 %collective-permute-start.3 = (bf16[896,512]{1,0:T(8,128)(2,1)}, bf16[896,512]{1,0:T(8,128)(2,1)S(1)}, u32[]{:S(2)}, u32[]{:S(2)}) collective-permute-start(bf16[896,512]{1,0:T(8,128)(2,1)} %get-tuple-element.20), channel_id=1, source_target_pairs={{0,16},{4,20},{8,24},{12,28},{16,0},{20,4},{24,8},{28,12},{1,17},{... | collective-permute-start | bytes 2752520 | tf_op jit(solution)/shard_map/ppermute | solution.py:236
  17.6 25.5 %collective-permute-start.5 = (bf16[1024,128]{1,0:T(8,128)(2,1)}, bf16[1024,128]{1,0:T(8,128)(2,1)}, u32[]{:S(2)}, u32[]{:S(2)}) collective-permute-start(bf16[1024,128]{1,0:T(8,128)(2,1)} %collective-permute-done.4.refs_2_), channel_id=1, source_target_pairs={{0,16},{4,20},{8,24},{12,28},{16,0},{20,4},{24,8},{28,12},{1,17},{... | collective-permute-start | bytes 786440 | tf_op jit(solution)/shard_map/ppermute | solution.py:236
  17.9 25.3 %collective-permute-start.7 = (bf16[1024,128]{1,0:T(8,128)(2,1)}, bf16[1024,128]{1,0:T(8,128)(2,1)}, u32[]{:S(2)}, u32[]{:S(2)}) collective-permute-start(bf16[1024,128]{1,0:T(8,128)(2,1)} %collective-permute-done.6.refs_5_), channel_id=1, source_target_pairs={{0,8},{4,12},{8,0},{12,4},{16,24},{20,28},{24,16},{28,20},{1,9},{5... | collective-permute-start | bytes 786440 | tf_op jit(solution)/shard_map/ppermute | solution.py:236
  18.2 1.0 %copy-start.3 = (bf16[1024,128]{1,0:T(8,128)(2,1)S(1)}, bf16[1024,128]{1,0:T(8,128)(2,1)}, u32[]{:S(2)}) copy-start(bf16[1024,128]{1,0:T(8,128)(2,1)} %refs_1_.1) | copy-start | bytes 786436
  19.2 0.9 %copy-start.5 = (bf16[1024,128]{1,0:T(8,128)(2,1)S(1)}, bf16[1024,128]{1,0:T(8,128)(2,1)}, u32[]{:S(2)}) copy-start(bf16[1024,128]{1,0:T(8,128)(2,1)} %copy-done.4) | copy-start | bytes 786436
  20.1 0.9 %copy-start.7 = (bf16[1024,128]{1,0:T(8,128)(2,1)S(1)}, bf16[1024,128]{1,0:T(8,128)(2,1)}, u32[]{:S(2)}) copy-start(bf16[1024,128]{1,0:T(8,128)(2,1)} %copy-done.6) | copy-start | bytes 786436
  45.6 3.4 %collective-permute-start.8 = (f32[384,256]{1,0:T(8,128)S(1)}, f32[384,256]{1,0:T(8,128)S(1)}, u32[]{:S(2)}, u32[]{:S(2)}) collective-permute-start(f32[384,256]{1,0:T(8,128)S(1)} %get-tuple-element.22), channel_id=1, source_target_pairs={{0,4},{4,0},{8,12},{12,8},{16,20},{20,16},{24,28},{28,24},{1,5},{5... | collective-permute-start | bytes 1179656 | tf_op jit(solution)/shard_map/ppermute | solution.py:236
  49.1 11.4 %copy-start = (bf16[384,256]{1,0:T(8,128)(2,1)}, bf16[384,256]{1,0:T(8,128)(2,1)S(1)}, u32[]{:S(2)}) copy-start(bf16[384,256]{1,0:T(8,128)(2,1)S(1)} %shard_map.57) | copy-start | bytes 589828
  49.1 8.1 %collective-permute-start.9 = (bf16[384,256]{1,0:T(8,128)(2,1)S(1)}, bf16[384,256]{1,0:T(8,128)(2,1)}, u32[]{:S(2)}, u32[]{:S(2)}) collective-permute-start(bf16[384,256]{1,0:T(8,128)(2,1)S(1)} %shard_map.57), channel_id=1, source_target_pairs={{0,1},{1,2},{2,3},{4,5},{5,6},{6,7},{8,9},{9,10},{10,11},{12,13},{... | collective-permute-start | bytes 589832 | tf_op jit(solution)/shard_map/ppermute | solution.py:286
  59.0 12.5 %collective-permute-start.14 = (bf16[512,512]{1,0:T(8,128)(2,1)}, bf16[512,512]{1,0:T(8,128)(2,1)}, u32[]{:S(2)}, u32[]{:S(2)}) collective-permute-start(bf16[512,512]{1,0:T(8,128)(2,1)} %slice.23), channel_id=1, source_target_pairs={{0,8},{4,12},{8,0},{12,4},{16,24},{20,28},{24,16},{28,20},{1,9},{5... | collective-permute-start | bytes 1572872 | tf_op jit(solution)/shard_map/ppermute | solution.py:236
  59.2 12.3 %collective-permute-start.13 = (bf16[512,512]{1,0:T(8,128)(2,1)}, bf16[512,512]{1,0:T(8,128)(2,1)}, u32[]{:S(2)}, u32[]{:S(2)}) collective-permute-start(bf16[512,512]{1,0:T(8,128)(2,1)} %slice.22), channel_id=1, source_target_pairs={{0,16},{4,20},{8,24},{12,28},{16,0},{20,4},{24,8},{28,12},{1,17},{... | collective-permute-start | bytes 1572872 | tf_op jit(solution)/shard_map/ppermute | solution.py:236
  61.2 9.7 %collective-permute-start.11 = (bf16[256,512]{1,0:T(8,128)(2,1)}, bf16[256,512]{1,0:T(8,128)(2,1)S(1)}, u32[]{:S(2)}, u32[]{:S(2)}) collective-permute-start(bf16[256,512]{1,0:T(8,128)(2,1)} %pad_maximum_fusion.3), channel_id=1, source_target_pairs={{0,1},{1,0},{2,3},{3,2},{4,5},{5,4},{6,7},{7,6},{8,9},{9,8},{10,11... | collective-permute-start | bytes 786440 | tf_op jit(solution)/shard_map/ppermute | solution.py:313
  62.6 8.2 %collective-permute-start.12 = (bf16[384,256]{1,0:T(8,128)(2,1)}, bf16[384,256]{1,0:T(8,128)(2,1)S(1)}, u32[]{:S(2)}, u32[]{:S(2)}) collective-permute-start(bf16[384,256]{1,0:T(8,128)(2,1)} %collective-permute-done.9), channel_id=1, source_target_pairs={{0,1},{1,2},{2,3},{4,5},{5,6},{6,7},{8,9},{9,10},{10,11},{12,13},{... | collective-permute-start | bytes 589832 | tf_op jit(solution)/shard_map/ppermute | solution.py:286
  70.1 8.2 %copy-start.1 = (bf16[384,256]{1,0:T(8,128)(2,1)S(1)}, bf16[384,256]{1,0:T(8,128)(2,1)}, u32[]{:S(2)}) copy-start(bf16[384,256]{1,0:T(8,128)(2,1)} %copy-done) | copy-start | bytes 589828
  70.9 0.7 copy-start.9
  75.4 4.7 %collective-permute-start.15 = (f32[384,512]{1,0:T(8,128)S(1)}, f32[384,512]{1,0:T(8,128)S(1)}, u32[]{:S(2)}, u32[]{:S(2)}) collective-permute-start(f32[384,512]{1,0:T(8,128)S(1)} %get-tuple-element.34), channel_id=1, source_target_pairs={{0,4},{4,0},{8,12},{12,8},{16,20},{20,16},{24,28},{28,24},{1,5},{5... | collective-permute-start | bytes 2359304 | tf_op jit(solution)/shard_map/ppermute | solution.py:236

commit v13 on v12

--- a/solution.py
+++ b/solution.py
@@ -262,10 +262,12 @@
 
     axes = [1 << axis for axis in range(bits)]
     half = depth // 2
-    lack = 128
-    keep = half - lack
-    halved = ctx_size % 2 == 0 and bits > 1 and keep > 0
+    some = half // 2
+    halved = ctx_size % 2 == 0 and bits > 1
     odd = place % 2
+    begin = odd * some
+    lack = some // 2 if some % 256 == 0 else some
+    more = some - lack
     halves = [w_query[:half], w_query[half:]]
 
     pair_held = fetch((w_key, w_value), [{}, {}], [], [])
@@ -285,7 +287,7 @@
     for _ in range(min(ctx_size - 1, -(-back // row_count))):
         blocks.insert(0, lax.ppermute(blocks[0], "ctx", [(i, i + 1) for i in range(ctx_size - 1)]))
     keys_values = jnp.concatenate(blocks, axis=0)
-    direct = [pair_held[0][axes[-1]], pair_held[1][axes[0]]]
+    direct = [corner(pair_held[side][chip]) for side in range(2) for chip in axes]
     gate = [*direct, cosine, sine, first]
     later = [corner(blocks[-2])]
 
@@ -297,16 +299,15 @@
             jnp.concatenate(
                 [
                     halves[side],
-                    lax.dynamic_slice_in_dim(w_query, (1 - side) * half + odd * lack, keep, 0),
+                    lax.dynamic_slice_in_dim(w_query, (1 - side) * half + begin, some, 0),
                 ],
                 axis=0,
             )
             for side in range(2)
         ]
         got = [swap(after(joined[side], *gate), 2 << ends[side]) for side in range(2)]
-        row = half + odd * (keep - lack)
         both = [
-            lax.dynamic_slice_in_dim(after(got[1 - side], *later), row, lack, 0)
+            lax.dynamic_slice_in_dim(after(got[1 - side], *later), half + odd * more, lack, 0)
             for side in range(2)
         ]
         both = jnp.concatenate(both, axis=0)
@@ -316,9 +317,14 @@
             given[side][chip] = after(got[side], *later)[:half]
             given[1 - side][chip] = None
             early.append((begins(chip) + side * half, [got[side]], 0, half))
+            early.append((begins(chip) + (1 - side) * half + begin, [got[side]], half, some))
             first_row = begins(chip) + (1 - side) * half
-            early.append((first_row + odd * lack, [got[side]], half, keep))
-            late.append((first_row + (1 - odd) * keep, [both], (1 - side) * lack, lack))
+            if more:
+                row = some - odd * more
+                part = lax.dynamic_slice_in_dim(w_query, (1 - side) * half + row, more, 0)
+                part = swap(after(part, corner(near)), 2 << ends[side])
+                early.append((first_row + row, [part], 0, more))
+            late.append((first_row + (1 - odd) * (half - lack), [both], (1 - side) * lack, lack))
     query_held = fetch(halves, given, gate, later)
     for side in range(2):
         for chip in range(chips):

time: 85.2 us -> 68.8 us (0.81)
  waiting for transfers between devices: 30 us -> 12.7 us
  starting transfers between devices: 19.4 us -> 20.4 us
    ppermute x13 -> x15, waiting for transfers between devices: 24.4 us -> 8.94 us  [swap(): return lax.ppermute(array, 'dp', [(i, i ^ mask) for i in range(dp_size)])]
    ppermute x2, waiting for transfers between devices: 5.62 us -> 3.74 us  [shards(): lax.ppermute(blocks[0], 'ctx', [(i, i + 1) for i in range(ctx_size - 1)])]
    dynamic_slice x3 -> x4, local copies, waits for them, and re-layouts: 1.19 us -> 2.81 us  [the longest x1 1.71 us: shards(): part = lax.dynamic_slice_in_dim(w_query, (1 - side) * half + row, more, 0)]
    ppermute x13 -> x15, starting transfers between devices: 12.8 us -> 13.8 us  [swap(): return lax.ppermute(array, 'dp', [(i, i ^ mask) for i in range(dp_size)])]
    unnamed x20 -> x18, local copies, waits for them, and re-layouts: 4.33 us -> 3.45 us
  transfers between devices with their start and end apart: 16 -> 18, of which waited for: 8 -> 8; matrix products, arithmetic and copies ran while one was open for 9% -> 16% of each run, Pallas kernels for 16% -> 19%
where the time goes in v13:
time: 68.8 us; the launch traced here: 67.9 us
  Pallas kernels  20.5 us (30%)
  starting transfers between devices  20.4 us (30%)
  waiting for transfers between devices  12.7 us (18%)
  local copies, waits for them, and re-layouts  8.3 us (12%)
  other arithmetic  5.8 us (8%)
    pallas_call x4, Pallas kernels, project(): pl.pallas_call(functools.partial(project_kernel, steps, carry is not None...  16.7 us
    ppermute x15, starting transfers between devices, swap(): return lax.ppermute(array, 'dp', [(i, i ^ mask) for i in range(dp_size)])  13.8 us
    ppermute x15, waiting for transfers between devices, swap(): return lax.ppermute(array, 'dp', [(i, i ^ mask) for i in range(dp_size)])  8.94 us
    ppermute x2, starting transfers between devices, shards(): lax.ppermute(blocks[0], 'ctx', [(i, i + 1) for i in range(ctx_size - 1)])  5.17 us
    ppermute x2, waiting for transfers between devices, shards(): lax.ppermute(blocks[0], 'ctx', [(i, i + 1) for i in range(ctx_size - 1)])  3.74 us
    pallas_call x1, Pallas kernels, attend(): pl.pallas_call(functools.partial(attend_kernel, back), out_shape=jax.Shap...  3.65 us
    unnamed x18, local copies, waits for them, and re-layouts  3.45 us
    slice x2, local copies, waits for them, and re-layouts, shards(): given[side][chip] = after(got[side], *later)[:half]  1.74 us
  transfers between devices with their start and end apart: 18, of which 8 were waited for; matrix products, arithmetic and copies ran while one was open for 16% of the time, Pallas kernels for 19%

profile of v13, /device:TPU:17, one launch (start us, length us, event | category | flops | bytes accessed | tf_op | source)
XLA Modules:
  0.0 67.9 jit_solution(12889285357566270376)
XLA Ops:
  0.7 1.2 %collective-permute-start.1 = (bf16[1024,128]{1,0:T(8,128)(2,1)}, bf16[1024,128]{1,0:T(8,128)(2,1)}, u32[]{:S(2)}, u32[]{:S(2)}) collective-permute-start(bf16[1024,128]{1,0:T(8,128)(2,1)} %refs_0_.1), channel_id=1, source_target_pairs={{0,8},{4,12},{8,0},{12,4},{16,24},{20,28},{24,16},{28,20},{1,9},{5... | collective-permute-start | bytes 786440 | tf_op jit(solution)/shard_map/ppermute | solution.py:236
  1.9 1.2 %collective-permute-start.2 = (bf16[1024,128]{1,0:T(8,128)(2,1)}, bf16[1024,128]{1,0:T(8,128)(2,1)S(1)}, u32[]{:S(2)}, u32[]{:S(2)}) collective-permute-start(bf16[1024,128]{1,0:T(8,128)(2,1)} %refs_0_.1), channel_id=1, source_target_pairs={{0,16},{4,20},{8,24},{12,28},{16,0},{20,4},{24,8},{28,12},{1,17},{... | collective-permute-start | bytes 786440 | tf_op jit(solution)/shard_map/ppermute | solution.py:236
  3.6 0.8 %reduce-window_clone.1 = s32[1,16]{1,0:T(1,128)S(1)} reduce-window(s32[1,16]{1,0:T(1,128)} %param.9, s32[]{:T(128)} %constant.44.clone.1), window={size=1x16 pad=0_0x15_0}, to_apply=%region_0.0 | reduce-window | flops 240 | bytes 132 | tf_op jit(solution)/shard_map/reduce-window.clone
  5.2 1.1 %constant_dynamic-slice_fusion.5 = (bf16[256,512]{1,0:T(8,128)(2,1)S(1)}, bf16[256,512]{1,0:T(8,128)(2,1)S(1)}) fusion(bf16[1024,512]{1,0:T(8,128)(2,1)} %param.6, s32[]{:T(128)S(6)} %select_n.28, s32[]{:T(128)S(6)} %select_n.31), kind=kLoop, calls=%fused_computation.16 | loop fusion | bytes 1048584 | tf_op jit(solution)/shard_map/dynamic_slice | solution.py:302
  6.3 0.8 %fusion = (f32[384,64]{1,0:T(8,128)S(1)}, f32[384,64]{1,0:T(8,128)S(1)}, f32[384,64]{1,0:T(8,128)S(1)}) fusion(f32[64]{0:T(128)S(1)} %negate_power_fusion, f32[384]{0:T(512)S(1)} %get-tuple-element.55), kind=kLoop, calls=%fused_computation.8 | loop fusion | flops 49152 | bytes 296704 | tf_op jit(solution)/shard_map/neg | solution.py:24
  7.3 1.3 %pad_maximum_fusion = (bf16[768,512]{1,0:T(8,128)(2,1)}, bf16[768,512]{1,0:T(8,128)(2,1)}) fusion(bf16[256,512]{1,0:T(8,128)(2,1)S(1)} %get-tuple-element.47, bf16[512,512]{1,0:T(8,128)(2,1)S(1)} %get-tuple-element.40.refs_7_, bf16[256,512]{1,0:T(8,128)(2,1)S(1)} %get-tuple-element.48, bf16[512,512]{1,0:T(8,128)(2,1)S(1)} %get-tuple-element.39.refs_6_), kind=kLoop, calls=%fused_computation | loop fusion | flops 3145728 | bytes 3145728 | tf_op jit(solution)/shard_map/concatenate | solution.py:299
  8.9 1.2 %collective-permute-start.6 = (bf16[1024,128]{1,0:T(8,128)(2,1)}, bf16[1024,128]{1,0:T(8,128)(2,1)}, u32[]{:S(2)}, u32[]{:S(2)}) collective-permute-start(bf16[1024,128]{1,0:T(8,128)(2,1)} %collective-permute-done.1.refs_2_), channel_id=1, source_target_pairs={{0,16},{4,20},{8,24},{12,28},{16,0},{20,4},{24,8},{28,12},{1,17},{... | collective-permute-start | bytes 786440 | tf_op jit(solution)/shard_map/ppermute | solution.py:236
  10.1 5.3 %collective-permute-done.4.refs_5_ = bf16[1024,128]{1,0:T(8,128)(2,1)} collective-permute-done((bf16[1024,128]{1,0:T(8,128)(2,1)}, bf16[1024,128]{1,0:T(8,128)(2,1)}, u32[]{:S(2)}, u32[]{:S(2)}) %collective-permute-start.4) | collective-permute-done | bytes 262176 | tf_op jit(solution)/shard_map/ppermute | solution.py:236
  15.8 0.7 %copy-done.2 = bf16[1024,128]{1,0:T(8,128)(2,1)} copy-done((bf16[1024,128]{1,0:T(8,128)(2,1)}, bf16[1024,128]{1,0:T(8,128)(2,1)S(1)}, u32[]{:S(2)}) %copy-start.2) | copy-done | bytes 262168
  17.2 1.2 %collective-permute-start.5 = (bf16[768,512]{1,0:T(8,128)(2,1)}, bf16[768,512]{1,0:T(8,128)(2,1)S(1)}, u32[]{:S(2)}, u32[]{:S(2)}) collective-permute-start(bf16[768,512]{1,0:T(8,128)(2,1)} %get-tuple-element.24), channel_id=1, source_target_pairs={{0,16},{4,20},{8,24},{12,28},{16,0},{20,4},{24,8},{28,12},{1,17},{... | collective-permute-start | bytes 2359304 | tf_op jit(solution)/shard_map/ppermute | solution.py:236
  18.4 1.2 %collective-permute-start.10 = (bf16[768,512]{1,0:T(8,128)(2,1)}, bf16[768,512]{1,0:T(8,128)(2,1)S(1)}, u32[]{:S(2)}, u32[]{:S(2)}) collective-permute-start(bf16[768,512]{1,0:T(8,128)(2,1)} %get-tuple-element.28), channel_id=1, source_target_pairs={{0,8},{4,12},{8,0},{12,4},{16,24},{20,28},{24,16},{28,20},{1,9},{5... | collective-permute-start | bytes 2359304 | tf_op jit(solution)/shard_map/ppermute | solution.py:236
  19.7 0.9 %copy-done.3 = bf16[1024,128]{1,0:T(8,128)(2,1)S(1)} copy-done((bf16[1024,128]{1,0:T(8,128)(2,1)S(1)}, bf16[1024,128]{1,0:T(8,128)(2,1)}, u32[]{:S(2)}) %copy-start.3) | copy-done | bytes 262168
  20.7 0.9 %copy-done.5 = bf16[1024,128]{1,0:T(8,128)(2,1)S(1)} copy-done((bf16[1024,128]{1,0:T(8,128)(2,1)S(1)}, bf16[1024,128]{1,0:T(8,128)(2,1)}, u32[]{:S(2)}) %copy-start.5) | copy-done | bytes 262168
  21.6 5.3 %shard_map.55.refs_2_ = f32[768,256]{1,0:T(8,128)S(1)} custom-call(s32[3]{0:T(128)S(1)} %pad_add_fusion.1.starts, bf16[384,8192]{1,0:T(8,128)(2,1)} %bitcast.18, bf16[384,8192]{1,0:T(8,128)(2,1)} %collective-permute-done.far, bf16[1024,128]{1,0:T(8,128)(2,1)S(1)} %copy-done, bf16[1024,128]{1,0:T(8,128)(2,1)S(1)} %copy-done.1, ...), custom_call_target="tpu_custom_call" | custom-call | flops 1207959552 | bytes 6291456 | tf_op jit(solution)/shard_map/pallas_call | solution.py:111
  26.9 2.4 %shard_map.56 = (f32[384,256]{1,0:T(8,128)S(1)}, f32[384,256]{1,0:T(8,128)S(1)}) custom-call(s32[1]{0:T(128)} %bitcast.2.starts, bf16[384,8192]{1,0:T(8,128)(2,1)} %bitcast.19, bf16[384,8192]{1,0:T(8,128)(2,1)} %collective-permute-done.far, bf16[1024,128]{1,0:T(8,128)(2,1)} %collective-permute-done.6.refs_0_, ...), custom_call_target="tpu_custom_call" | custom-call | flops 402653184 | bytes 2097152 | tf_op jit(solution)/shard_map/pallas_call | solution.py:111
  29.4 2.9 %collective-permute-start.8 = (f32[384,256]{1,0:T(8,128)S(1)}, f32[384,256]{1,0:T(8,128)S(1)}, u32[]{:S(2)}, u32[]{:S(2)}) collective-permute-start(f32[384,256]{1,0:T(8,128)S(1)} %get-tuple-element.26), channel_id=1, source_target_pairs={{0,4},{4,0},{8,12},{12,8},{16,20},{20,16},{24,28},{28,24},{1,5},{5... | collective-permute-start | bytes 1179656 | tf_op jit(solution)/shard_map/ppermute | solution.py:236
  32.3 1.3 %collective-permute-done.8.far = f32[384,256]{1,0:T(8,128)S(1)} collective-permute-done((f32[384,256]{1,0:T(8,128)S(1)}, f32[384,256]{1,0:T(8,128)S(1)}, u32[]{:S(2)}, u32[]{:S(2)}) %collective-permute-start.8) | collective-permute-done | bytes 393248 | tf_op jit(solution)/shard_map/ppermute | solution.py:236
  33.8 3.2 %collective-permute-start.9 = (bf16[384,256]{1,0:T(8,128)(2,1)S(1)}, bf16[384,256]{1,0:T(8,128)(2,1)S(1)}, u32[]{:S(2)}, u32[]{:S(2)}) collective-permute-start(bf16[384,256]{1,0:T(8,128)(2,1)S(1)} %shard_map.57), channel_id=1, source_target_pairs={{0,1},{1,2},{2,3},{4,5},{5,6},{6,7},{8,9},{9,10},{10,11},{12,13},{... | collective-permute-start | bytes 589832 | tf_op jit(solution)/shard_map/ppermute | solution.py:288
  37.0 1.7 %constant_dynamic-slice_fusion = (bf16[128,512]{1,0:T(8,128)(2,1)}, bf16[128,512]{1,0:T(8,128)(2,1)}) fusion(bf16[1024,512]{1,0:T(8,128)(2,1)} %param.6, s32[]{:T(128)S(6)} %select_n.33, s32[]{:T(128)S(6)} %select_n.32), kind=kLoop, calls=%fused_computation.11 | loop fusion | bytes 524296 | tf_op jit(solution)/shard_map/dynamic_slice | solution.py:324
  39.2 2.6 %collective-permute-done.9 = bf16[384,256]{1,0:T(8,128)(2,1)S(1)} collective-permute-done((bf16[384,256]{1,0:T(8,128)(2,1)S(1)}, bf16[384,256]{1,0:T(8,128)(2,1)S(1)}, u32[]{:S(2)}, u32[]{:S(2)}) %collective-permute-start.9) | collective-permute-done | bytes 196640 | tf_op jit(solution)/shard_map/ppermute | solution.py:288
  41.8 0.9 %slice.43 = bf16[512,512]{1,0:T(8,128)(2,1)} slice(bf16[768,512]{1,0:T(8,128)(2,1)S(1)} %collective-permute-done.5.refs_3_.refs_4_), slice={[0:512], [0:512]} | slice | bytes 1048576 | tf_op jit(solution)/shard_map/slice | solution.py:317
  42.9 0.9 %slice.42 = bf16[512,512]{1,0:T(8,128)(2,1)} slice(bf16[768,512]{1,0:T(8,128)(2,1)S(1)} %collective-permute-done.10.refs_0_.refs_1_), slice={[0:512], [0:512]} | slice | bytes 1048576 | tf_op jit(solution)/shard_map/slice | solution.py:317
  44.0 0.7 %pad_maximum_fusion.3 = bf16[256,512]{1,0:T(8,128)(2,1)} fusion(bf16[128,512]{1,0:T(8,128)(2,1)S(1)} %constant_dynamic-slice_fusion.2, bf16[128,512]{1,0:T(8,128)(2,1)S(1)} %constant_dynamic-slice_fusion.4), kind=kLoop, calls=%fused_computation.5 | loop fusion | flops 524288 | bytes 524288 | tf_op jit(solution)/shard_map/concatenate | solution.py:313
  44.7 1.4 %collective-permute-start.11 = (bf16[256,512]{1,0:T(8,128)(2,1)}, bf16[256,512]{1,0:T(8,128)(2,1)S(1)}, u32[]{:S(2)}, u32[]{:S(2)}) collective-permute-start(bf16[256,512]{1,0:T(8,128)(2,1)} %pad_maximum_fusion.3), channel_id=1, source_target_pairs={{0,1},{1,0},{2,3},{3,2},{4,5},{5,4},{6,7},{7,6},{8,9},{9,8},{10,11... | collective-permute-start | bytes 786440 | tf_op jit(solution)/shard_map/ppermute | solution.py:314
  46.3 2.0 %collective-permute-start.12 = (bf16[384,256]{1,0:T(8,128)(2,1)}, bf16[384,256]{1,0:T(8,128)(2,1)S(1)}, u32[]{:S(2)}, u32[]{:S(2)}) collective-permute-start(bf16[384,256]{1,0:T(8,128)(2,1)} %copy-done.7), channel_id=1, source_target_pairs={{0,1},{1,2},{2,3},{4,5},{5,6},{6,7},{8,9},{9,10},{10,11},{12,13},{... | collective-permute-start | bytes 589832 | tf_op jit(solution)/shard_map/ppermute | solution.py:288
  48.3 5.2 %shard_map.58.refs_4_ = f32[768,512]{1,0:T(8,128)S(1)} custom-call(s32[8]{0:T(128)S(1)} %stack.66.starts, bf16[384,8192]{1,0:T(8,128)(2,1)} %bitcast.20, bf16[384,8192]{1,0:T(8,128)(2,1)} %collective-permute-done.far, bf16[768,512]{1,0:T(8,128)(2,1)S(1)} %collective-permute-done.10.refs_0_.refs_1_, ...), custom_call_target="tpu_custom_call" | custom-call | flops 2214592512 | bytes 7208960 | tf_op jit(solution)/shard_map/pallas_call | solution.py:111
  53.5 1.1 %collective-permute-done.12 = bf16[384,256]{1,0:T(8,128)(2,1)S(1)} collective-permute-done((bf16[384,256]{1,0:T(8,128)(2,1)}, bf16[384,256]{1,0:T(8,128)(2,1)S(1)}, u32[]{:S(2)}, u32[]{:S(2)}) %collective-permute-start.12) | collective-permute-done | bytes 196640 | tf_op jit(solution)/shard_map/ppermute | solution.py:288
  55.3 0.7 %collective-permute-done.13.refs_2_ = bf16[512,512]{1,0:T(8,128)(2,1)} collective-permute-done((bf16[512,512]{1,0:T(8,128)(2,1)}, bf16[512,512]{1,0:T(8,128)(2,1)}, u32[]{:S(2)}, u32[]{:S(2)}) %collective-permute-start.13) | collective-permute-done | bytes 524320 | tf_op jit(solution)/shard_map/ppermute | solution.py:236
  56.0 3.9 %shard_map.59 = (f32[384,512]{1,0:T(8,128)S(1)}, f32[384,512]{1,0:T(8,128)S(1)}) custom-call(s32[4]{0:T(128)S(1)} %pad_add_fusion.starts, bf16[384,8192]{1,0:T(8,128)(2,1)} %bitcast.21, bf16[384,8192]{1,0:T(8,128)(2,1)} %collective-permute-done.far, bf16[256,512]{1,0:T(8,128)(2,1)S(1)} %collective-permute-done.11.refs_0_.refs_1_, ...), custom_call_target="tpu_custom_call" | custom-call | flops 1006632960 | bytes 3276800 | tf_op jit(solution)/shard_map/pallas_call | solution.py:111
  59.9 2.5 %collective-permute-start.17 = (f32[384,512]{1,0:T(8,128)S(1)}, f32[384,512]{1,0:T(8,128)S(1)}, u32[]{:S(2)}, u32[]{:S(2)}) collective-permute-start(f32[384,512]{1,0:T(8,128)S(1)} %get-tuple-element.42), channel_id=1, source_target_pairs={{0,4},{4,0},{8,12},{12,8},{16,20},{20,16},{24,28},{28,24},{1,5},{5... | collective-permute-start | bytes 2359304 | tf_op jit(solution)/shard_map/ppermute | solution.py:236
  62.5 1.1 %pad_maximum_fusion.2.keys_values = bf16[1152,256]{1,0:T(8,128)(2,1)S(1)} fusion(bf16[384,256]{1,0:T(8,128)(2,1)S(1)} %shard_map.57, bf16[384,256]{1,0:T(8,128)(2,1)} %copy-done.7, bf16[384,256]{1,0:T(8,128)(2,1)} %copy-done.8), kind=kLoop, calls=%fused_computation.2 | loop fusion | flops 1769472 | bytes 1179648 | tf_op jit(solution)/shard_map/concatenate | solution.py:289
  64.3 3.6 %shard_map.60 = bf16[384,512]{1,0:T(8,128)(2,1)} custom-call(f32[384,512]{1,0:T(8,128)S(1)} %get-tuple-element.41.near, f32[384,512]{1,0:T(8,128)S(1)} %collective-permute-done.17.far, f32[384,128]{1,0:T(8,128)S(1)} %pad_maximum_fusion.4.cosine, f32[384,128]{1,0:T(8,128)S(1)} %pad_maximum_fusion.5.sine, s32[384,1]{1,0:T(8,128)S(1)} %copy.7.first, ...), custom_call_target="tpu_custom_call" | custom-call | flops 704643072 | bytes 1572864 | tf_op jit(solution)/shard_map/pallas_call | solution.py:206
  (52 shorter events, 6.3 us)
Async XLA Ops:
  0.0 7.1 %copy-start.6 = (bf16[1024,512]{1,0:T(8,128)(2,1)S(1)}, bf16[1024,512]{1,0:T(8,128)(2,1)}, u32[]{:S(2)}) copy-start(bf16[1024,512]{1,0:T(8,128)(2,1)} %param.6) | copy-start | bytes 3145732
  0.0 19.7 %collective-permute-start = (bf16[384,8192]{1,0:T(8,128)(2,1)}, bf16[384,8192]{1,0:T(8,128)(2,1)}, u32[]{:S(2)}, u32[]{:S(2)}) collective-permute-start(bf16[384,8192]{1,0:T(8,128)(2,1)} %bitcast.17), channel_id=1, source_target_pairs={{0,4},{4,0},{8,12},{12,8},{16,20},{20,16},{24,28},{28,24},{1,5},{5... | collective-permute-start | bytes 18874376 | tf_op jit(solution)/shard_map/ppermute | solution.py:236
  0.7 8.2 %collective-permute-start.1 = (bf16[1024,128]{1,0:T(8,128)(2,1)}, bf16[1024,128]{1,0:T(8,128)(2,1)}, u32[]{:S(2)}, u32[]{:S(2)}) collective-permute-start(bf16[1024,128]{1,0:T(8,128)(2,1)} %refs_0_.1), channel_id=1, source_target_pairs={{0,8},{4,12},{8,0},{12,4},{16,24},{20,28},{24,16},{28,20},{1,9},{5... | collective-permute-start | bytes 786440 | tf_op jit(solution)/shard_map/ppermute | solution.py:236
  1.9 13.9 %collective-permute-start.2 = (bf16[1024,128]{1,0:T(8,128)(2,1)}, bf16[1024,128]{1,0:T(8,128)(2,1)S(1)}, u32[]{:S(2)}, u32[]{:S(2)}) collective-permute-start(bf16[1024,128]{1,0:T(8,128)(2,1)} %refs_0_.1), channel_id=1, source_target_pairs={{0,16},{4,20},{8,24},{12,28},{16,0},{20,4},{24,8},{28,12},{1,17},{... | collective-permute-start | bytes 786440 | tf_op jit(solution)/shard_map/ppermute | solution.py:236
  3.1 12.2 %collective-permute-start.4 = (bf16[1024,128]{1,0:T(8,128)(2,1)}, bf16[1024,128]{1,0:T(8,128)(2,1)}, u32[]{:S(2)}, u32[]{:S(2)}) collective-permute-start(bf16[1024,128]{1,0:T(8,128)(2,1)} %refs_1_.1), channel_id=1, source_target_pairs={{0,16},{4,20},{8,24},{12,28},{16,0},{20,4},{24,8},{28,12},{1,17},{... | collective-permute-start | bytes 786440 | tf_op jit(solution)/shard_map/ppermute | solution.py:236
  3.4 13.1 %collective-permute-start.3 = (bf16[1024,128]{1,0:T(8,128)(2,1)}, bf16[1024,128]{1,0:T(8,128)(2,1)S(1)}, u32[]{:S(2)}, u32[]{:S(2)}) collective-permute-start(bf16[1024,128]{1,0:T(8,128)(2,1)} %refs_1_.1), channel_id=1, source_target_pairs={{0,8},{4,12},{8,0},{12,4},{16,24},{20,28},{24,16},{28,20},{1,9},{5... | collective-permute-start | bytes 786440 | tf_op jit(solution)/shard_map/ppermute | solution.py:236
  7.3 12.4 %copy-start = (bf16[1024,128]{1,0:T(8,128)(2,1)S(1)}, bf16[1024,128]{1,0:T(8,128)(2,1)}, u32[]{:S(2)}) copy-start(bf16[1024,128]{1,0:T(8,128)(2,1)} %refs_0_.1) | copy-start | bytes 786436
  7.3 12.4 %copy-start.1 = (bf16[1024,128]{1,0:T(8,128)(2,1)S(1)}, bf16[1024,128]{1,0:T(8,128)(2,1)}, u32[]{:S(2)}) copy-start(bf16[1024,128]{1,0:T(8,128)(2,1)} %refs_1_.1) | copy-start | bytes 786436
  8.9 18.0 %collective-permute-start.6 = (bf16[1024,128]{1,0:T(8,128)(2,1)}, bf16[1024,128]{1,0:T(8,128)(2,1)}, u32[]{:S(2)}, u32[]{:S(2)}) collective-permute-start(bf16[1024,128]{1,0:T(8,128)(2,1)} %collective-permute-done.1.refs_2_), channel_id=1, source_target_pairs={{0,16},{4,20},{8,24},{12,28},{16,0},{20,4},{24,8},{28,12},{1,17},{... | collective-permute-start | bytes 786440 | tf_op jit(solution)/shard_map/ppermute | solution.py:236
  15.4 11.5 %collective-permute-start.7 = (bf16[1024,128]{1,0:T(8,128)(2,1)}, bf16[1024,128]{1,0:T(8,128)(2,1)}, u32[]{:S(2)}, u32[]{:S(2)}) collective-permute-start(bf16[1024,128]{1,0:T(8,128)(2,1)} %collective-permute-done.4.refs_5_), channel_id=1, source_target_pairs={{0,8},{4,12},{8,0},{12,4},{16,24},{20,28},{24,16},{28,20},{1,9},{5... | collective-permute-start | bytes 786440 | tf_op jit(solution)/shard_map/ppermute | solution.py:236
  15.8 0.7 %copy-start.2 = (bf16[1024,128]{1,0:T(8,128)(2,1)}, bf16[1024,128]{1,0:T(8,128)(2,1)S(1)}, u32[]{:S(2)}) copy-start(bf16[1024,128]{1,0:T(8,128)(2,1)S(1)} %collective-permute-done.2.refs_4_) | copy-start | bytes 786436
  16.5 0.7 %copy-start.4 = (bf16[1024,128]{1,0:T(8,128)(2,1)}, bf16[1024,128]{1,0:T(8,128)(2,1)S(1)}, u32[]{:S(2)}) copy-start(bf16[1024,128]{1,0:T(8,128)(2,1)S(1)} %collective-permute-done.3.refs_3_) | copy-start | bytes 786436
  17.2 24.6 %collective-permute-start.5 = (bf16[768,512]{1,0:T(8,128)(2,1)}, bf16[768,512]{1,0:T(8,128)(2,1)S(1)}, u32[]{:S(2)}, u32[]{:S(2)}) collective-permute-start(bf16[768,512]{1,0:T(8,128)(2,1)} %get-tuple-element.24), channel_id=1, source_target_pairs={{0,16},{4,20},{8,24},{12,28},{16,0},{20,4},{24,8},{28,12},{1,17},{... | collective-permute-start | bytes 2359304 | tf_op jit(solution)/shard_map/ppermute | solution.py:236
  18.4 23.4 %collective-permute-start.10 = (bf16[768,512]{1,0:T(8,128)(2,1)}, bf16[768,512]{1,0:T(8,128)(2,1)S(1)}, u32[]{:S(2)}, u32[]{:S(2)}) collective-permute-start(bf16[768,512]{1,0:T(8,128)(2,1)} %get-tuple-element.28), channel_id=1, source_target_pairs={{0,8},{4,12},{8,0},{12,4},{16,24},{20,28},{24,16},{28,20},{1,9},{5... | collective-permute-start | bytes 2359304 | tf_op jit(solution)/shard_map/ppermute | solution.py:236
  19.7 1.0 %copy-start.3 = (bf16[1024,128]{1,0:T(8,128)(2,1)S(1)}, bf16[1024,128]{1,0:T(8,128)(2,1)}, u32[]{:S(2)}) copy-start(bf16[1024,128]{1,0:T(8,128)(2,1)} %copy-done.2) | copy-start | bytes 786436
  20.7 0.9 %copy-start.5 = (bf16[1024,128]{1,0:T(8,128)(2,1)S(1)}, bf16[1024,128]{1,0:T(8,128)(2,1)}, u32[]{:S(2)}) copy-start(bf16[1024,128]{1,0:T(8,128)(2,1)} %copy-done.4) | copy-start | bytes 786436
  29.4 4.3 %collective-permute-start.8 = (f32[384,256]{1,0:T(8,128)S(1)}, f32[384,256]{1,0:T(8,128)S(1)}, u32[]{:S(2)}, u32[]{:S(2)}) collective-permute-start(f32[384,256]{1,0:T(8,128)S(1)} %get-tuple-element.26), channel_id=1, source_target_pairs={{0,4},{4,0},{8,12},{12,8},{16,20},{20,16},{24,28},{28,24},{1,5},{5... | collective-permute-start | bytes 1179656 | tf_op jit(solution)/shard_map/ppermute | solution.py:236
  33.8 8.0 %collective-permute-start.9 = (bf16[384,256]{1,0:T(8,128)(2,1)S(1)}, bf16[384,256]{1,0:T(8,128)(2,1)S(1)}, u32[]{:S(2)}, u32[]{:S(2)}) collective-permute-start(bf16[384,256]{1,0:T(8,128)(2,1)S(1)} %shard_map.57), channel_id=1, source_target_pairs={{0,1},{1,2},{2,3},{4,5},{5,6},{6,7},{8,9},{9,10},{10,11},{12,13},{... | collective-permute-start | bytes 589832 | tf_op jit(solution)/shard_map/ppermute | solution.py:288
  38.7 7.6 %collective-permute-start.16 = (bf16[128,512]{1,0:T(8,128)(2,1)}, bf16[128,512]{1,0:T(8,128)(2,1)}, u32[]{:S(2)}, u32[]{:S(2)}) collective-permute-start(bf16[128,512]{1,0:T(8,128)(2,1)} %get-tuple-element.37), channel_id=1, source_target_pairs={{0,16},{4,20},{8,24},{12,28},{16,0},{20,4},{24,8},{28,12},{1,17},{... | collective-permute-start | bytes 393224 | tf_op jit(solution)/shard_map/ppermute | solution.py:236
  38.9 7.4 %collective-permute-start.15 = (bf16[128,512]{1,0:T(8,128)(2,1)}, bf16[128,512]{1,0:T(8,128)(2,1)}, u32[]{:S(2)}, u32[]{:S(2)}) collective-permute-start(bf16[128,512]{1,0:T(8,128)(2,1)} %get-tuple-element.35), channel_id=1, source_target_pairs={{0,8},{4,12},{8,0},{12,4},{16,24},{20,28},{24,16},{28,20},{1,9},{5... | collective-permute-start | bytes 393224 | tf_op jit(solution)/shard_map/ppermute | solution.py:236
  41.8 2.2 %copy-start.7 = (bf16[384,256]{1,0:T(8,128)(2,1)}, bf16[384,256]{1,0:T(8,128)(2,1)S(1)}, u32[]{:S(2)}) copy-start(bf16[384,256]{1,0:T(8,128)(2,1)S(1)} %collective-permute-done.9) | copy-start | bytes 589828
  42.6 12.5 %collective-permute-start.14 = (bf16[512,512]{1,0:T(8,128)(2,1)}, bf16[512,512]{1,0:T(8,128)(2,1)}, u32[]{:S(2)}, u32[]{:S(2)}) collective-permute-start(bf16[512,512]{1,0:T(8,128)(2,1)} %slice.43), channel_id=1, source_target_pairs={{0,8},{4,12},{8,0},{12,4},{16,24},{20,28},{24,16},{28,20},{1,9},{5... | collective-permute-start | bytes 1572872 | tf_op jit(solution)/shard_map/ppermute | solution.py:236
  43.8 12.3 %collective-permute-start.13 = (bf16[512,512]{1,0:T(8,128)(2,1)}, bf16[512,512]{1,0:T(8,128)(2,1)}, u32[]{:S(2)}, u32[]{:S(2)}) collective-permute-start(bf16[512,512]{1,0:T(8,128)(2,1)} %slice.42), channel_id=1, source_target_pairs={{0,16},{4,20},{8,24},{12,28},{16,0},{20,4},{24,8},{28,12},{1,17},{... | collective-permute-start | bytes 1572872 | tf_op jit(solution)/shard_map/ppermute | solution.py:236
  44.7 9.9 %collective-permute-start.11 = (bf16[256,512]{1,0:T(8,128)(2,1)}, bf16[256,512]{1,0:T(8,128)(2,1)S(1)}, u32[]{:S(2)}, u32[]{:S(2)}) collective-permute-start(bf16[256,512]{1,0:T(8,128)(2,1)} %pad_maximum_fusion.3), channel_id=1, source_target_pairs={{0,1},{1,0},{2,3},{3,2},{4,5},{5,4},{6,7},{7,6},{8,9},{9,8},{10,11... | collective-permute-start | bytes 786440 | tf_op jit(solution)/shard_map/ppermute | solution.py:314
  46.3 8.3 %collective-permute-start.12 = (bf16[384,256]{1,0:T(8,128)(2,1)}, bf16[384,256]{1,0:T(8,128)(2,1)S(1)}, u32[]{:S(2)}, u32[]{:S(2)}) collective-permute-start(bf16[384,256]{1,0:T(8,128)(2,1)} %copy-done.7), channel_id=1, source_target_pairs={{0,1},{1,2},{2,3},{4,5},{5,6},{6,7},{8,9},{9,10},{10,11},{12,13},{... | collective-permute-start | bytes 589832 | tf_op jit(solution)/shard_map/ppermute | solution.py:288
  54.6 0.7 %copy-start.8 = (bf16[384,256]{1,0:T(8,128)(2,1)}, bf16[384,256]{1,0:T(8,128)(2,1)S(1)}, u32[]{:S(2)}) copy-start(bf16[384,256]{1,0:T(8,128)(2,1)S(1)} %collective-permute-done.12) | copy-start | bytes 589828
  59.9 4.4 %collective-permute-start.17 = (f32[384,512]{1,0:T(8,128)S(1)}, f32[384,512]{1,0:T(8,128)S(1)}, u32[]{:S(2)}, u32[]{:S(2)}) collective-permute-start(f32[384,512]{1,0:T(8,128)S(1)} %get-tuple-element.42), channel_id=1, source_target_pairs={{0,4},{4,0},{8,12},{12,8},{16,20},{20,16},{24,28},{28,24},{1,5},{5... | collective-permute-start | bytes 2359304 | tf_op jit(solution)/shard_map/ppermute | solution.py:236

commit v14 on v13

--- a/solution.py
+++ b/solution.py
@@ -287,7 +287,7 @@
     for _ in range(min(ctx_size - 1, -(-back // row_count))):
         blocks.insert(0, lax.ppermute(blocks[0], "ctx", [(i, i + 1) for i in range(ctx_size - 1)]))
     keys_values = jnp.concatenate(blocks, axis=0)
-    direct = [corner(pair_held[side][chip]) for side in range(2) for chip in axes]
+    direct = [corner(pair_held[0][axes[0]]), corner(pair_held[1][axes[-1]])]
     gate = [*direct, cosine, sine, first]
     later = [corner(blocks[-2])]
 

time: 68.8 us -> 69.5 us (1.010)
    ppermute x15, waiting for transfers between devices: 8.94 us -> 11.4 us  [swap(): return lax.ppermute(array, 'dp', [(i, i ^ mask) for i in range(dp_size)])]
    ppermute x2, waiting for transfers between devices: 3.74 us -> 1.63 us  [shards(): lax.ppermute(blocks[0], 'ctx', [(i, i + 1) for i in range(ctx_size - 1)])]
  transfers between devices with their start and end apart: 18 -> 18, of which waited for: 8 -> 6; matrix products, arithmetic and copies ran while one was open for 16% -> 16% of each run, Pallas kernels for 19% -> 19%
where the time goes in v14:
time: 69.5 us; the launch traced here: 68.6 us
  starting transfers between devices  20.8 us (30%)
  Pallas kernels  20.5 us (29%)
  waiting for transfers between devices  13 us (19%)
  local copies, waits for them, and re-layouts  8.18 us (12%)
  other arithmetic  5.8 us (8%)
    pallas_call x4, Pallas kernels, project(): pl.pallas_call(functools.partial(project_kernel, steps, carry is not None...  16.7 us
    ppermute x15, starting transfers between devices, swap(): return lax.ppermute(array, 'dp', [(i, i ^ mask) for i in range(dp_size)])  14.3 us
    ppermute x15, waiting for transfers between devices, swap(): return lax.ppermute(array, 'dp', [(i, i ^ mask) for i in range(dp_size)])  11.4 us
    ppermute x2, starting transfers between devices, shards(): lax.ppermute(blocks[0], 'ctx', [(i, i + 1) for i in range(ctx_size - 1)])  5.28 us
    pallas_call x1, Pallas kernels, attend(): pl.pallas_call(functools.partial(attend_kernel, back), out_shape=jax.Shap...  3.65 us
    unnamed x18, local copies, waits for them, and re-layouts  3.34 us
    slice x2, local copies, waits for them, and re-layouts, shards(): given[side][chip] = after(got[side], *later)[:half]  1.74 us
    dynamic_slice x1, local copies, waits for them, and re-layouts, shards(): part = lax.dynamic_slice_in_dim(w_query, (1 - side) * half + row, more, 0)  1.71 us
  transfers between devices with their start and end apart: 18, of which 6 were waited for; matrix products, arithmetic and copies ran while one was open for 16% of the time, Pallas kernels for 19%

profile of v14, /device:TPU:17, one launch (start us, length us, event | category | flops | bytes accessed | tf_op | source)
XLA Modules:
  0.0 68.6 jit_solution(9511516178326531686)
XLA Ops:
  0.7 1.2 %collective-permute-start.2 = (bf16[1024,128]{1,0:T(8,128)(2,1)}, bf16[1024,128]{1,0:T(8,128)(2,1)}, u32[]{:S(2)}, u32[]{:S(2)}) collective-permute-start(bf16[1024,128]{1,0:T(8,128)(2,1)} %refs_1_.1), channel_id=1, source_target_pairs={{0,16},{4,20},{8,24},{12,28},{16,0},{20,4},{24,8},{28,12},{1,17},{... | collective-permute-start | bytes 786440 | tf_op jit(solution)/shard_map/ppermute | solution.py:236
  1.9 1.2 %collective-permute-start.6 = (bf16[1024,128]{1,0:T(8,128)(2,1)}, bf16[1024,128]{1,0:T(8,128)(2,1)S(1)}, u32[]{:S(2)}, u32[]{:S(2)}) collective-permute-start(bf16[1024,128]{1,0:T(8,128)(2,1)} %refs_1_.1), channel_id=1, source_target_pairs={{0,8},{4,12},{8,0},{12,4},{16,24},{20,28},{24,16},{28,20},{1,9},{5... | collective-permute-start | bytes 786440 | tf_op jit(solution)/shard_map/ppermute | solution.py:236
  3.6 0.8 %reduce-window_clone.1 = s32[1,16]{1,0:T(1,128)S(1)} reduce-window(s32[1,16]{1,0:T(1,128)} %param.9, s32[]{:T(128)} %constant.44.clone.1), window={size=1x16 pad=0_0x15_0}, to_apply=%region_0.0 | reduce-window | flops 240 | bytes 132 | tf_op jit(solution)/shard_map/reduce-window.clone
  5.2 1.1 %constant_dynamic-slice_fusion.5 = (bf16[256,512]{1,0:T(8,128)(2,1)S(1)}, bf16[256,512]{1,0:T(8,128)(2,1)S(1)}) fusion(bf16[1024,512]{1,0:T(8,128)(2,1)} %param.6, s32[]{:T(128)S(6)} %select_n.28, s32[]{:T(128)S(6)} %select_n.31), kind=kLoop, calls=%fused_computation.16 | loop fusion | bytes 1048584 | tf_op jit(solution)/shard_map/dynamic_slice | solution.py:302
  6.3 0.8 %fusion = (f32[384,64]{1,0:T(8,128)S(1)}, f32[384,64]{1,0:T(8,128)S(1)}, f32[384,64]{1,0:T(8,128)S(1)}) fusion(f32[64]{0:T(128)S(1)} %negate_power_fusion, f32[384]{0:T(512)S(1)} %get-tuple-element.55), kind=kLoop, calls=%fused_computation.8 | loop fusion | flops 49152 | bytes 296704 | tf_op jit(solution)/shard_map/neg | solution.py:24
  7.3 1.3 %pad_maximum_fusion = (bf16[768,512]{1,0:T(8,128)(2,1)}, bf16[768,512]{1,0:T(8,128)(2,1)}) fusion(bf16[256,512]{1,0:T(8,128)(2,1)S(1)} %get-tuple-element.47, bf16[512,512]{1,0:T(8,128)(2,1)S(1)} %get-tuple-element.40.refs_7_, bf16[256,512]{1,0:T(8,128)(2,1)S(1)} %get-tuple-element.48, bf16[512,512]{1,0:T(8,128)(2,1)S(1)} %get-tuple-element.39.refs_6_), kind=kLoop, calls=%fused_computation | loop fusion | flops 3145728 | bytes 3145728 | tf_op jit(solution)/shard_map/concatenate | solution.py:299
  8.6 6.8 %collective-permute-done.1.refs_2_ = bf16[1024,128]{1,0:T(8,128)(2,1)} collective-permute-done((bf16[1024,128]{1,0:T(8,128)(2,1)}, bf16[1024,128]{1,0:T(8,128)(2,1)}, u32[]{:S(2)}, u32[]{:S(2)}) %collective-permute-start.1) | collective-permute-done | bytes 262176 | tf_op jit(solution)/shard_map/ppermute | solution.py:236
  15.6 1.2 %collective-permute-start.5 = (bf16[1024,128]{1,0:T(8,128)(2,1)}, bf16[1024,128]{1,0:T(8,128)(2,1)}, u32[]{:S(2)}, u32[]{:S(2)}) collective-permute-start(bf16[1024,128]{1,0:T(8,128)(2,1)} %collective-permute-done.2.refs_5_), channel_id=1, source_target_pairs={{0,8},{4,12},{8,0},{12,4},{16,24},{20,28},{24,16},{28,20},{1,9},{5... | collective-permute-start | bytes 786440 | tf_op jit(solution)/shard_map/ppermute | solution.py:236
  17.7 1.2 %collective-permute-start.3 = (bf16[768,512]{1,0:T(8,128)(2,1)}, bf16[768,512]{1,0:T(8,128)(2,1)S(1)}, u32[]{:S(2)}, u32[]{:S(2)}) collective-permute-start(bf16[768,512]{1,0:T(8,128)(2,1)} %get-tuple-element.24), channel_id=1, source_target_pairs={{0,16},{4,20},{8,24},{12,28},{16,0},{20,4},{24,8},{28,12},{1,17},{... | collective-permute-start | bytes 2359304 | tf_op jit(solution)/shard_map/ppermute | solution.py:236
  18.9 0.7 %copy-done.4 = bf16[1024,128]{1,0:T(8,128)(2,1)} copy-done((bf16[1024,128]{1,0:T(8,128)(2,1)}, bf16[1024,128]{1,0:T(8,128)(2,1)S(1)}, u32[]{:S(2)}) %copy-start.4) | copy-done | bytes 262168
  20.0 0.9 %copy-done.3 = bf16[1024,128]{1,0:T(8,128)(2,1)S(1)} copy-done((bf16[1024,128]{1,0:T(8,128)(2,1)S(1)}, bf16[1024,128]{1,0:T(8,128)(2,1)}, u32[]{:S(2)}) %copy-start.3) | copy-done | bytes 262168
  21.0 0.9 %copy-done.5 = bf16[1024,128]{1,0:T(8,128)(2,1)S(1)} copy-done((bf16[1024,128]{1,0:T(8,128)(2,1)S(1)}, bf16[1024,128]{1,0:T(8,128)(2,1)}, u32[]{:S(2)}) %copy-start.5) | copy-done | bytes 262168
  21.9 5.3 %shard_map.55.refs_2_ = f32[768,256]{1,0:T(8,128)S(1)} custom-call(s32[3]{0:T(128)S(1)} %pad_add_fusion.1.starts, bf16[384,8192]{1,0:T(8,128)(2,1)} %bitcast.18, bf16[384,8192]{1,0:T(8,128)(2,1)} %collective-permute-done.far, bf16[1024,128]{1,0:T(8,128)(2,1)S(1)} %copy-done, bf16[1024,128]{1,0:T(8,128)(2,1)S(1)} %copy-done.1, ...), custom_call_target="tpu_custom_call" | custom-call | flops 1207959552 | bytes 6291456 | tf_op jit(solution)/shard_map/pallas_call | solution.py:111
  27.2 2.4 %shard_map.56 = (f32[384,256]{1,0:T(8,128)S(1)}, f32[384,256]{1,0:T(8,128)S(1)}) custom-call(s32[1]{0:T(128)} %bitcast.2.starts, bf16[384,8192]{1,0:T(8,128)(2,1)} %bitcast.19, bf16[384,8192]{1,0:T(8,128)(2,1)} %collective-permute-done.far, bf16[1024,128]{1,0:T(8,128)(2,1)} %collective-permute-done.4.refs_0_, ...), custom_call_target="tpu_custom_call" | custom-call | flops 402653184 | bytes 2097152 | tf_op jit(solution)/shard_map/pallas_call | solution.py:111
  29.7 2.4 %collective-permute-start.8 = (f32[384,256]{1,0:T(8,128)S(1)}, f32[384,256]{1,0:T(8,128)S(1)}, u32[]{:S(2)}, u32[]{:S(2)}) collective-permute-start(f32[384,256]{1,0:T(8,128)S(1)} %get-tuple-element.26), channel_id=1, source_target_pairs={{0,4},{4,0},{8,12},{12,8},{16,20},{20,16},{24,28},{28,24},{1,5},{5... | collective-permute-start | bytes 1179656 | tf_op jit(solution)/shard_map/ppermute | solution.py:236
  32.0 1.3 %collective-permute-done.8.far = f32[384,256]{1,0:T(8,128)S(1)} collective-permute-done((f32[384,256]{1,0:T(8,128)S(1)}, f32[384,256]{1,0:T(8,128)S(1)}, u32[]{:S(2)}, u32[]{:S(2)}) %collective-permute-start.8) | collective-permute-done | bytes 393248 | tf_op jit(solution)/shard_map/ppermute | solution.py:236
  33.5 3.2 %collective-permute-start.9 = (bf16[384,256]{1,0:T(8,128)(2,1)S(1)}, bf16[384,256]{1,0:T(8,128)(2,1)S(1)}, u32[]{:S(2)}, u32[]{:S(2)}) collective-permute-start(bf16[384,256]{1,0:T(8,128)(2,1)S(1)} %shard_map.57), channel_id=1, source_target_pairs={{0,1},{1,2},{2,3},{4,5},{5,6},{6,7},{8,9},{9,10},{10,11},{12,13},{... | collective-permute-start | bytes 589832 | tf_op jit(solution)/shard_map/ppermute | solution.py:288
  36.7 1.7 %constant_dynamic-slice_fusion = (bf16[128,512]{1,0:T(8,128)(2,1)}, bf16[128,512]{1,0:T(8,128)(2,1)}) fusion(bf16[1024,512]{1,0:T(8,128)(2,1)} %param.6, s32[]{:T(128)S(6)} %select_n.33, s32[]{:T(128)S(6)} %select_n.32), kind=kLoop, calls=%fused_computation.11 | loop fusion | bytes 524296 | tf_op jit(solution)/shard_map/dynamic_slice | solution.py:324
  38.7 1.2 %collective-permute-start.15 = (bf16[128,512]{1,0:T(8,128)(2,1)}, bf16[128,512]{1,0:T(8,128)(2,1)}, u32[]{:S(2)}, u32[]{:S(2)}) collective-permute-start(bf16[128,512]{1,0:T(8,128)(2,1)} %get-tuple-element.35), channel_id=1, source_target_pairs={{0,8},{4,12},{8,0},{12,4},{16,24},{20,28},{24,16},{28,20},{1,9},{5... | collective-permute-start | bytes 393224 | tf_op jit(solution)/shard_map/ppermute | solution.py:236
  39.9 1.6 %collective-permute-done.9 = bf16[384,256]{1,0:T(8,128)(2,1)S(1)} collective-permute-done((bf16[384,256]{1,0:T(8,128)(2,1)S(1)}, bf16[384,256]{1,0:T(8,128)(2,1)S(1)}, u32[]{:S(2)}, u32[]{:S(2)}) %collective-permute-start.9) | collective-permute-done | bytes 196640 | tf_op jit(solution)/shard_map/ppermute | solution.py:288
  41.5 0.9 %slice.35 = bf16[512,512]{1,0:T(8,128)(2,1)} slice(bf16[768,512]{1,0:T(8,128)(2,1)S(1)} %collective-permute-done.3.refs_3_.refs_4_), slice={[0:512], [0:512]} | slice | bytes 1048576 | tf_op jit(solution)/shard_map/slice | solution.py:317
  42.4 1.2 %collective-permute-start.14 = (bf16[512,512]{1,0:T(8,128)(2,1)}, bf16[512,512]{1,0:T(8,128)(2,1)}, u32[]{:S(2)}, u32[]{:S(2)}) collective-permute-start(bf16[512,512]{1,0:T(8,128)(2,1)} %slice.35), channel_id=1, source_target_pairs={{0,8},{4,12},{8,0},{12,4},{16,24},{20,28},{24,16},{28,20},{1,9},{5... | collective-permute-start | bytes 1572872 | tf_op jit(solution)/shard_map/ppermute | solution.py:236
  43.6 0.9 %slice.34 = bf16[512,512]{1,0:T(8,128)(2,1)} slice(bf16[768,512]{1,0:T(8,128)(2,1)S(1)} %collective-permute-done.10.refs_0_.refs_1_), slice={[0:512], [0:512]} | slice | bytes 1048576 | tf_op jit(solution)/shard_map/slice | solution.py:317
  44.8 0.7 %pad_maximum_fusion.3 = bf16[256,512]{1,0:T(8,128)(2,1)} fusion(bf16[128,512]{1,0:T(8,128)(2,1)S(1)} %constant_dynamic-slice_fusion.2, bf16[128,512]{1,0:T(8,128)(2,1)S(1)} %constant_dynamic-slice_fusion.4), kind=kLoop, calls=%fused_computation.5 | loop fusion | flops 524288 | bytes 524288 | tf_op jit(solution)/shard_map/concatenate | solution.py:313
  45.5 1.3 %collective-permute-start.11 = (bf16[256,512]{1,0:T(8,128)(2,1)}, bf16[256,512]{1,0:T(8,128)(2,1)S(1)}, u32[]{:S(2)}, u32[]{:S(2)}) collective-permute-start(bf16[256,512]{1,0:T(8,128)(2,1)} %pad_maximum_fusion.3), channel_id=1, source_target_pairs={{0,1},{1,0},{2,3},{3,2},{4,5},{5,4},{6,7},{7,6},{8,9},{9,8},{10,11... | collective-permute-start | bytes 786440 | tf_op jit(solution)/shard_map/ppermute | solution.py:314
  46.9 2.1 %collective-permute-start.12 = (bf16[384,256]{1,0:T(8,128)(2,1)}, bf16[384,256]{1,0:T(8,128)(2,1)S(1)}, u32[]{:S(2)}, u32[]{:S(2)}) collective-permute-start(bf16[384,256]{1,0:T(8,128)(2,1)} %copy-done.7), channel_id=1, source_target_pairs={{0,1},{1,2},{2,3},{4,5},{5,6},{6,7},{8,9},{9,10},{10,11},{12,13},{... | collective-permute-start | bytes 589832 | tf_op jit(solution)/shard_map/ppermute | solution.py:288
  49.0 5.2 %shard_map.58.refs_4_ = f32[768,512]{1,0:T(8,128)S(1)} custom-call(s32[8]{0:T(128)S(1)} %stack.66.starts, bf16[384,8192]{1,0:T(8,128)(2,1)} %bitcast.20, bf16[384,8192]{1,0:T(8,128)(2,1)} %collective-permute-done.far, bf16[768,512]{1,0:T(8,128)(2,1)S(1)} %collective-permute-done.10.refs_0_.refs_1_, ...), custom_call_target="tpu_custom_call" | custom-call | flops 2214592512 | bytes 7208960 | tf_op jit(solution)/shard_map/pallas_call | solution.py:111
  54.9 1.8 %collective-permute-done.13.refs_2_ = bf16[512,512]{1,0:T(8,128)(2,1)} collective-permute-done((bf16[512,512]{1,0:T(8,128)(2,1)}, bf16[512,512]{1,0:T(8,128)(2,1)}, u32[]{:S(2)}, u32[]{:S(2)}) %collective-permute-start.13) | collective-permute-done | bytes 524320 | tf_op jit(solution)/shard_map/ppermute | solution.py:236
  56.7 3.9 %shard_map.59 = (f32[384,512]{1,0:T(8,128)S(1)}, f32[384,512]{1,0:T(8,128)S(1)}) custom-call(s32[4]{0:T(128)S(1)} %pad_add_fusion.starts, bf16[384,8192]{1,0:T(8,128)(2,1)} %bitcast.21, bf16[384,8192]{1,0:T(8,128)(2,1)} %collective-permute-done.far, bf16[256,512]{1,0:T(8,128)(2,1)S(1)} %collective-permute-done.11.refs_0_.refs_1_, ...), custom_call_target="tpu_custom_call" | custom-call | flops 1006632960 | bytes 3276800 | tf_op jit(solution)/shard_map/pallas_call | solution.py:111
  60.6 2.5 %collective-permute-start.17 = (f32[384,512]{1,0:T(8,128)S(1)}, f32[384,512]{1,0:T(8,128)S(1)}, u32[]{:S(2)}, u32[]{:S(2)}) collective-permute-start(f32[384,512]{1,0:T(8,128)S(1)} %get-tuple-element.42), channel_id=1, source_target_pairs={{0,4},{4,0},{8,12},{12,8},{16,20},{20,16},{24,28},{28,24},{1,5},{5... | collective-permute-start | bytes 2359304 | tf_op jit(solution)/shard_map/ppermute | solution.py:236
  63.2 1.1 %pad_maximum_fusion.2.keys_values = bf16[1152,256]{1,0:T(8,128)(2,1)S(1)} fusion(bf16[384,256]{1,0:T(8,128)(2,1)S(1)} %shard_map.57, bf16[384,256]{1,0:T(8,128)(2,1)} %copy-done.7, bf16[384,256]{1,0:T(8,128)(2,1)} %copy-done.8), kind=kLoop, calls=%fused_computation.2 | loop fusion | flops 1769472 | bytes 1179648 | tf_op jit(solution)/shard_map/concatenate | solution.py:289
  65.0 3.6 %shard_map.60 = bf16[384,512]{1,0:T(8,128)(2,1)} custom-call(f32[384,512]{1,0:T(8,128)S(1)} %get-tuple-element.41.near, f32[384,512]{1,0:T(8,128)S(1)} %collective-permute-done.17.far, f32[384,128]{1,0:T(8,128)S(1)} %pad_maximum_fusion.4.cosine, f32[384,128]{1,0:T(8,128)S(1)} %pad_maximum_fusion.5.sine, s32[384,1]{1,0:T(8,128)S(1)} %copy.7.first, ...), custom_call_target="tpu_custom_call" | custom-call | flops 704643072 | bytes 1572864 | tf_op jit(solution)/shard_map/pallas_call | solution.py:206
  (52 shorter events, 5.8 us)
Async XLA Ops:
  0.0 7.1 %copy-start.6 = (bf16[1024,512]{1,0:T(8,128)(2,1)S(1)}, bf16[1024,512]{1,0:T(8,128)(2,1)}, u32[]{:S(2)}) copy-start(bf16[1024,512]{1,0:T(8,128)(2,1)} %param.6) | copy-start | bytes 3145732
  0.0 20.0 %collective-permute-start = (bf16[384,8192]{1,0:T(8,128)(2,1)}, bf16[384,8192]{1,0:T(8,128)(2,1)}, u32[]{:S(2)}, u32[]{:S(2)}) collective-permute-start(bf16[384,8192]{1,0:T(8,128)(2,1)} %bitcast.17), channel_id=1, source_target_pairs={{0,4},{4,0},{8,12},{12,8},{16,20},{20,16},{24,28},{28,24},{1,5},{5... | collective-permute-start | bytes 18874376 | tf_op jit(solution)/shard_map/ppermute | solution.py:236
  0.7 15.0 %collective-permute-start.2 = (bf16[1024,128]{1,0:T(8,128)(2,1)}, bf16[1024,128]{1,0:T(8,128)(2,1)}, u32[]{:S(2)}, u32[]{:S(2)}) collective-permute-start(bf16[1024,128]{1,0:T(8,128)(2,1)} %refs_1_.1), channel_id=1, source_target_pairs={{0,16},{4,20},{8,24},{12,28},{16,0},{20,4},{24,8},{28,12},{1,17},{... | collective-permute-start | bytes 786440 | tf_op jit(solution)/shard_map/ppermute | solution.py:236
  1.9 15.1 %collective-permute-start.6 = (bf16[1024,128]{1,0:T(8,128)(2,1)}, bf16[1024,128]{1,0:T(8,128)(2,1)S(1)}, u32[]{:S(2)}, u32[]{:S(2)}) collective-permute-start(bf16[1024,128]{1,0:T(8,128)(2,1)} %refs_1_.1), channel_id=1, source_target_pairs={{0,8},{4,12},{8,0},{12,4},{16,24},{20,28},{24,16},{28,20},{1,9},{5... | collective-permute-start | bytes 786440 | tf_op jit(solution)/shard_map/ppermute | solution.py:236
  3.1 12.3 %collective-permute-start.1 = (bf16[1024,128]{1,0:T(8,128)(2,1)}, bf16[1024,128]{1,0:T(8,128)(2,1)}, u32[]{:S(2)}, u32[]{:S(2)}) collective-permute-start(bf16[1024,128]{1,0:T(8,128)(2,1)} %refs_0_.1), channel_id=1, source_target_pairs={{0,8},{4,12},{8,0},{12,4},{16,24},{20,28},{24,16},{28,20},{1,9},{5... | collective-permute-start | bytes 786440 | tf_op jit(solution)/shard_map/ppermute | solution.py:236
  3.4 15.5 %collective-permute-start.7 = (bf16[1024,128]{1,0:T(8,128)(2,1)}, bf16[1024,128]{1,0:T(8,128)(2,1)S(1)}, u32[]{:S(2)}, u32[]{:S(2)}) collective-permute-start(bf16[1024,128]{1,0:T(8,128)(2,1)} %refs_0_.1), channel_id=1, source_target_pairs={{0,16},{4,20},{8,24},{12,28},{16,0},{20,4},{24,8},{28,12},{1,17},{... | collective-permute-start | bytes 786440 | tf_op jit(solution)/shard_map/ppermute | solution.py:236
  7.3 12.7 %copy-start = (bf16[1024,128]{1,0:T(8,128)(2,1)S(1)}, bf16[1024,128]{1,0:T(8,128)(2,1)}, u32[]{:S(2)}) copy-start(bf16[1024,128]{1,0:T(8,128)(2,1)} %refs_0_.1) | copy-start | bytes 786436
  7.3 12.7 %copy-start.1 = (bf16[1024,128]{1,0:T(8,128)(2,1)S(1)}, bf16[1024,128]{1,0:T(8,128)(2,1)}, u32[]{:S(2)}) copy-start(bf16[1024,128]{1,0:T(8,128)(2,1)} %refs_1_.1) | copy-start | bytes 786436
  15.4 11.8 %collective-permute-start.4 = (bf16[1024,128]{1,0:T(8,128)(2,1)}, bf16[1024,128]{1,0:T(8,128)(2,1)}, u32[]{:S(2)}, u32[]{:S(2)}) collective-permute-start(bf16[1024,128]{1,0:T(8,128)(2,1)} %collective-permute-done.1.refs_2_), channel_id=1, source_target_pairs={{0,16},{4,20},{8,24},{12,28},{16,0},{20,4},{24,8},{28,12},{1,17},{... | collective-permute-start | bytes 786440 | tf_op jit(solution)/shard_map/ppermute | solution.py:236
  15.6 11.6 %collective-permute-start.5 = (bf16[1024,128]{1,0:T(8,128)(2,1)}, bf16[1024,128]{1,0:T(8,128)(2,1)}, u32[]{:S(2)}, u32[]{:S(2)}) collective-permute-start(bf16[1024,128]{1,0:T(8,128)(2,1)} %collective-permute-done.2.refs_5_), channel_id=1, source_target_pairs={{0,8},{4,12},{8,0},{12,4},{16,24},{20,28},{24,16},{28,20},{1,9},{5... | collective-permute-start | bytes 786440 | tf_op jit(solution)/shard_map/ppermute | solution.py:236
  17.0 0.7 %copy-start.2 = (bf16[1024,128]{1,0:T(8,128)(2,1)}, bf16[1024,128]{1,0:T(8,128)(2,1)S(1)}, u32[]{:S(2)}) copy-start(bf16[1024,128]{1,0:T(8,128)(2,1)S(1)} %collective-permute-done.6.refs_3_) | copy-start | bytes 786436
  17.7 23.8 %collective-permute-start.3 = (bf16[768,512]{1,0:T(8,128)(2,1)}, bf16[768,512]{1,0:T(8,128)(2,1)S(1)}, u32[]{:S(2)}, u32[]{:S(2)}) collective-permute-start(bf16[768,512]{1,0:T(8,128)(2,1)} %get-tuple-element.24), channel_id=1, source_target_pairs={{0,16},{4,20},{8,24},{12,28},{16,0},{20,4},{24,8},{28,12},{1,17},{... | collective-permute-start | bytes 2359304 | tf_op jit(solution)/shard_map/ppermute | solution.py:236
  18.9 0.7 %copy-start.4 = (bf16[1024,128]{1,0:T(8,128)(2,1)}, bf16[1024,128]{1,0:T(8,128)(2,1)S(1)}, u32[]{:S(2)}) copy-start(bf16[1024,128]{1,0:T(8,128)(2,1)S(1)} %collective-permute-done.7.refs_4_) | copy-start | bytes 786436
  19.7 21.9 %collective-permute-start.10 = (bf16[768,512]{1,0:T(8,128)(2,1)}, bf16[768,512]{1,0:T(8,128)(2,1)S(1)}, u32[]{:S(2)}, u32[]{:S(2)}) collective-permute-start(bf16[768,512]{1,0:T(8,128)(2,1)} %get-tuple-element.28), channel_id=1, source_target_pairs={{0,8},{4,12},{8,0},{12,4},{16,24},{20,28},{24,16},{28,20},{1,9},{5... | collective-permute-start | bytes 2359304 | tf_op jit(solution)/shard_map/ppermute | solution.py:236
  20.0 1.0 %copy-start.3 = (bf16[1024,128]{1,0:T(8,128)(2,1)S(1)}, bf16[1024,128]{1,0:T(8,128)(2,1)}, u32[]{:S(2)}) copy-start(bf16[1024,128]{1,0:T(8,128)(2,1)} %copy-done.2) | copy-start | bytes 786436
  21.0 0.9 %copy-start.5 = (bf16[1024,128]{1,0:T(8,128)(2,1)S(1)}, bf16[1024,128]{1,0:T(8,128)(2,1)}, u32[]{:S(2)}) copy-start(bf16[1024,128]{1,0:T(8,128)(2,1)} %copy-done.4) | copy-start | bytes 786436
  29.7 3.7 %collective-permute-start.8 = (f32[384,256]{1,0:T(8,128)S(1)}, f32[384,256]{1,0:T(8,128)S(1)}, u32[]{:S(2)}, u32[]{:S(2)}) collective-permute-start(f32[384,256]{1,0:T(8,128)S(1)} %get-tuple-element.26), channel_id=1, source_target_pairs={{0,4},{4,0},{8,12},{12,8},{16,20},{20,16},{24,28},{28,24},{1,5},{5... | collective-permute-start | bytes 1179656 | tf_op jit(solution)/shard_map/ppermute | solution.py:236
  33.5 8.0 %collective-permute-start.9 = (bf16[384,256]{1,0:T(8,128)(2,1)S(1)}, bf16[384,256]{1,0:T(8,128)(2,1)S(1)}, u32[]{:S(2)}, u32[]{:S(2)}) collective-permute-start(bf16[384,256]{1,0:T(8,128)(2,1)S(1)} %shard_map.57), channel_id=1, source_target_pairs={{0,1},{1,2},{2,3},{4,5},{5,6},{6,7},{8,9},{9,10},{10,11},{12,13},{... | collective-permute-start | bytes 589832 | tf_op jit(solution)/shard_map/ppermute | solution.py:288
  38.4 8.5 %collective-permute-start.16 = (bf16[128,512]{1,0:T(8,128)(2,1)}, bf16[128,512]{1,0:T(8,128)(2,1)}, u32[]{:S(2)}, u32[]{:S(2)}) collective-permute-start(bf16[128,512]{1,0:T(8,128)(2,1)} %get-tuple-element.37), channel_id=1, source_target_pairs={{0,16},{4,20},{8,24},{12,28},{16,0},{20,4},{24,8},{28,12},{1,17},{... | collective-permute-start | bytes 393224 | tf_op jit(solution)/shard_map/ppermute | solution.py:236
  38.7 8.3 %collective-permute-start.15 = (bf16[128,512]{1,0:T(8,128)(2,1)}, bf16[128,512]{1,0:T(8,128)(2,1)}, u32[]{:S(2)}, u32[]{:S(2)}) collective-permute-start(bf16[128,512]{1,0:T(8,128)(2,1)} %get-tuple-element.35), channel_id=1, source_target_pairs={{0,8},{4,12},{8,0},{12,4},{16,24},{20,28},{24,16},{28,20},{1,9},{5... | collective-permute-start | bytes 393224 | tf_op jit(solution)/shard_map/ppermute | solution.py:236
  41.5 3.2 %copy-start.7 = (bf16[384,256]{1,0:T(8,128)(2,1)}, bf16[384,256]{1,0:T(8,128)(2,1)S(1)}, u32[]{:S(2)}) copy-start(bf16[384,256]{1,0:T(8,128)(2,1)S(1)} %collective-permute-done.9) | copy-start | bytes 589828
  42.4 12.5 %collective-permute-start.14 = (bf16[512,512]{1,0:T(8,128)(2,1)}, bf16[512,512]{1,0:T(8,128)(2,1)}, u32[]{:S(2)}, u32[]{:S(2)}) collective-permute-start(bf16[512,512]{1,0:T(8,128)(2,1)} %slice.35), channel_id=1, source_target_pairs={{0,8},{4,12},{8,0},{12,4},{16,24},{20,28},{24,16},{28,20},{1,9},{5... | collective-permute-start | bytes 1572872 | tf_op jit(solution)/shard_map/ppermute | solution.py:236
  44.5 12.3 %collective-permute-start.13 = (bf16[512,512]{1,0:T(8,128)(2,1)}, bf16[512,512]{1,0:T(8,128)(2,1)}, u32[]{:S(2)}, u32[]{:S(2)}) collective-permute-start(bf16[512,512]{1,0:T(8,128)(2,1)} %slice.34), channel_id=1, source_target_pairs={{0,16},{4,20},{8,24},{12,28},{16,0},{20,4},{24,8},{28,12},{1,17},{... | collective-permute-start | bytes 1572872 | tf_op jit(solution)/shard_map/ppermute | solution.py:236
  45.5 8.8 %collective-permute-start.11 = (bf16[256,512]{1,0:T(8,128)(2,1)}, bf16[256,512]{1,0:T(8,128)(2,1)S(1)}, u32[]{:S(2)}, u32[]{:S(2)}) collective-permute-start(bf16[256,512]{1,0:T(8,128)(2,1)} %pad_maximum_fusion.3), channel_id=1, source_target_pairs={{0,1},{1,0},{2,3},{3,2},{4,5},{5,4},{6,7},{7,6},{8,9},{9,8},{10,11... | collective-permute-start | bytes 786440 | tf_op jit(solution)/shard_map/ppermute | solution.py:314
  46.9 7.3 %collective-permute-start.12 = (bf16[384,256]{1,0:T(8,128)(2,1)}, bf16[384,256]{1,0:T(8,128)(2,1)S(1)}, u32[]{:S(2)}, u32[]{:S(2)}) collective-permute-start(bf16[384,256]{1,0:T(8,128)(2,1)} %copy-done.7), channel_id=1, source_target_pairs={{0,1},{1,2},{2,3},{4,5},{5,6},{6,7},{8,9},{9,10},{10,11},{12,13},{... | collective-permute-start | bytes 589832 | tf_op jit(solution)/shard_map/ppermute | solution.py:288
  54.2 0.7 %copy-start.8 = (bf16[384,256]{1,0:T(8,128)(2,1)}, bf16[384,256]{1,0:T(8,128)(2,1)S(1)}, u32[]{:S(2)}) copy-start(bf16[384,256]{1,0:T(8,128)(2,1)S(1)} %collective-permute-done.12) | copy-start | bytes 589828
  60.6 4.4 %collective-permute-start.17 = (f32[384,512]{1,0:T(8,128)S(1)}, f32[384,512]{1,0:T(8,128)S(1)}, u32[]{:S(2)}, u32[]{:S(2)}) collective-permute-start(f32[384,512]{1,0:T(8,128)S(1)} %get-tuple-element.42), channel_id=1, source_target_pairs={{0,4},{4,0},{8,12},{12,8},{16,20},{20,16},{24,28},{28,24},{1,5},{5... | collective-permute-start | bytes 2359304 | tf_op jit(solution)/shard_map/ppermute | solution.py:236

commit v15 on v13

--- a/solution.py
+++ b/solution.py
@@ -277,9 +277,7 @@
     ]
     early_chips = [0] + axes
     late_chips = [chip for chip in range(chips) if chip not in early_chips]
-    carry = project([pair_terms[chip] for chip in early_chips], hidden, sibling_hidden)
-    terms = [pair_terms[chip] for chip in late_chips]
-    near, far = project(terms, hidden, sibling_hidden, carry, True)
+    near, far = project(pair_terms, hidden, sibling_hidden, None, True)
     pair = finish_pair(near, swap(far, 1), cosine, sine)
     longest = ctx_size * row_count // 2
     back = -(-(longest - 1) // ROW_TILE) * ROW_TILE

time: 68.8 us -> 71.6 us (1.041)
  starting transfers between devices: 20.4 us -> 24.9 us
  other arithmetic: 5.8 us -> 7.32 us
  waiting for transfers between devices: 12.7 us -> 11.2 us
  Pallas kernels: 20.5 us -> 19.2 us
  local copies, waits for them, and re-layouts: 8.3 us -> 7.34 us
    ppermute x15, starting transfers between devices: 13.8 us -> 18.3 us  [swap(): return lax.ppermute(array, 'dp', [(i, i ^ mask) for i in range(dp_size)])]
    pallas_call x4 -> x3, Pallas kernels: 16.7 us -> 15.4 us  [project(): pl.pallas_call(functools.partial(project_kernel, steps, carry is not None...]
    slice x1, local copies, waits for them, and re-layouts: 0.07 us -> 1.27 us  [shards(): halves = [w_query[:half], w_query[half:]]]
    unnamed x18 -> x16, local copies, waits for them, and re-layouts: 3.45 us -> 2.28 us
    ppermute x2, waiting for transfers between devices: 3.74 us -> 2.61 us  [shards(): lax.ppermute(blocks[0], 'ctx', [(i, i + 1) for i in range(ctx_size - 1)])]
    dynamic_slice x1, local copies, waits for them, and re-layouts: 1.07 us -> 0.04 us  [shards(): lax.dynamic_slice_in_dim(w_query, (1 - side) * half + begin, some, 0)]
    concatenate x1, other arithmetic: 0.12 us -> 1.05 us  [rope_tables(): jnp.concatenate([-sine_part, sine_part], axis=-1)]
  transfers between devices with their start and end apart: 18 -> 18, of which waited for: 8 -> 8; matrix products, arithmetic and copies ran while one was open for 16% -> 18% of each run, Pallas kernels for 19% -> 17%
where the time goes in v15:
time: 71.6 us; the launch traced here: 70.2 us
  starting transfers between devices  24.9 us (35%)
  Pallas kernels  19.2 us (27%)
  waiting for transfers between devices  11.2 us (16%)
  local copies, waits for them, and re-layouts  7.34 us (10%)
  other arithmetic  7.32 us (10%)
    ppermute x15, starting transfers between devices, swap(): return lax.ppermute(array, 'dp', [(i, i ^ mask) for i in range(dp_size)])  18.3 us
    pallas_call x3, Pallas kernels, project(): pl.pallas_call(functools.partial(project_kernel, steps, carry is not None...  15.4 us
    ppermute x15, waiting for transfers between devices, swap(): return lax.ppermute(array, 'dp', [(i, i ^ mask) for i in range(dp_size)])  8.59 us
    ppermute x2, starting transfers between devices, shards(): lax.ppermute(blocks[0], 'ctx', [(i, i + 1) for i in range(ctx_size - 1)])  5.18 us
    pallas_call x1, Pallas kernels, attend(): pl.pallas_call(functools.partial(attend_kernel, back), out_shape=jax.Shap...  3.65 us
    ppermute x2, waiting for transfers between devices, shards(): lax.ppermute(blocks[0], 'ctx', [(i, i + 1) for i in range(ctx_size - 1)])  2.61 us
    unnamed x16, local copies, waits for them, and re-layouts  2.28 us
    slice x2, local copies, waits for them, and re-layouts, shards(): given[side][chip] = after(got[side], *later)[:half]  1.77 us
  transfers between devices with their start and end apart: 18, of which 8 were waited for; matrix products, arithmetic and copies ran while one was open for 18% of the time, Pallas kernels for 17%

profile of v15, /device:TPU:17, one launch (start us, length us, event | category | flops | bytes accessed | tf_op | source)
XLA Modules:
  0.0 70.2 jit_solution(1499151162670554914)
XLA Ops:
  0.7 1.2 %collective-permute-start.1 = (bf16[1024,128]{1,0:T(8,128)(2,1)}, bf16[1024,128]{1,0:T(8,128)(2,1)S(1)}, u32[]{:S(2)}, u32[]{:S(2)}) collective-permute-start(bf16[1024,128]{1,0:T(8,128)(2,1)} %refs_0_.1), channel_id=1, source_target_pairs={{0,8},{4,12},{8,0},{12,4},{16,24},{20,28},{24,16},{28,20},{1,9},{5... | collective-permute-start | bytes 786440 | tf_op jit(solution)/shard_map/ppermute | solution.py:236
  1.9 1.2 %collective-permute-start.2 = (bf16[1024,128]{1,0:T(8,128)(2,1)}, bf16[1024,128]{1,0:T(8,128)(2,1)S(1)}, u32[]{:S(2)}, u32[]{:S(2)}) collective-permute-start(bf16[1024,128]{1,0:T(8,128)(2,1)} %refs_0_.1), channel_id=1, source_target_pairs={{0,16},{4,20},{8,24},{12,28},{16,0},{20,4},{24,8},{28,12},{1,17},{... | collective-permute-start | bytes 786440 | tf_op jit(solution)/shard_map/ppermute | solution.py:236
  3.6 0.8 %reduce-window_clone.1 = s32[1,16]{1,0:T(1,128)S(1)} reduce-window(s32[1,16]{1,0:T(1,128)} %param.9, s32[]{:T(128)} %constant.44.clone.1), window={size=1x16 pad=0_0x15_0}, to_apply=%region_0.0 | reduce-window | flops 240 | bytes 132 | tf_op jit(solution)/shard_map/reduce-window.clone
  5.2 1.4 %fusion = (f32[384,64]{1,0:T(8,128)S(1)}, f32[384,64]{1,0:T(8,128)}, f32[384,64]{1,0:T(8,128)S(1)}) fusion(f32[64]{0:T(128)S(1)} %negate_power_fusion, f32[384]{0:T(512)S(1)} %get-tuple-element.55), kind=kLoop, calls=%fused_computation.8 | loop fusion | flops 49152 | bytes 296704 | tf_op jit(solution)/shard_map/neg | solution.py:24
  6.7 1.3 %fusion.2 = (bf16[512,512]{1,0:T(8,128)(2,1)S(1)}, bf16[512,512]{1,0:T(8,128)(2,1)S(1)}) fusion(bf16[1024,512]{1,0:T(8,128)(2,1)} %param.6), kind=kLoop, calls=%fused_computation.23 | loop fusion | bytes 2097152 | tf_op jit(solution)/shard_map/slice | solution.py:271
  8.2 1.0 %pad_maximum_fusion.5.sine = f32[384,128]{1,0:T(8,128)S(1)} fusion(f32[384,64]{1,0:T(8,128)} %get-tuple-element.50, f32[384,64]{1,0:T(8,128)S(1)} %get-tuple-element.49), kind=kLoop, calls=%fused_computation.7 | loop fusion | flops 49152 | bytes 393216 | tf_op jit(solution)/shard_map/concatenate | solution.py:24
  9.2 1.3 %collective-permute-start.6 = (bf16[1024,128]{1,0:T(8,128)(2,1)S(1)}, bf16[1024,128]{1,0:T(8,128)(2,1)S(1)}, u32[]{:S(2)}, u32[]{:S(2)}) collective-permute-start(bf16[1024,128]{1,0:T(8,128)(2,1)S(1)} %collective-permute-done.1.refs_2_), channel_id=1, source_target_pairs={{0,16},{4,20},{8,24},{12,28},{16,0},{20,4},{24,8},{28,12},{1,17},{... | collective-permute-start | bytes 786440 | tf_op jit(solution)/shard_map/ppermute | solution.py:236
  10.5 4.9 %collective-permute-done.4.refs_5_ = bf16[1024,128]{1,0:T(8,128)(2,1)} collective-permute-done((bf16[1024,128]{1,0:T(8,128)(2,1)}, bf16[1024,128]{1,0:T(8,128)(2,1)}, u32[]{:S(2)}, u32[]{:S(2)}) %collective-permute-start.4) | collective-permute-done | bytes 262176 | tf_op jit(solution)/shard_map/ppermute | solution.py:236
  15.7 1.3 %pad_maximum_fusion = (bf16[768,512]{1,0:T(8,128)(2,1)}, bf16[768,512]{1,0:T(8,128)(2,1)}) fusion(bf16[256,512]{1,0:T(8,128)(2,1)S(1)} %get-tuple-element.47, bf16[512,512]{1,0:T(8,128)(2,1)S(1)} %get-tuple-element.40.refs_7_, bf16[256,512]{1,0:T(8,128)(2,1)S(1)} %get-tuple-element.48, bf16[512,512]{1,0:T(8,128)(2,1)S(1)} %get-tuple-element.39.refs_6_), kind=kLoop, calls=%fused_computation | loop fusion | flops 3145728 | bytes 3145728 | tf_op jit(solution)/shard_map/concatenate | solution.py:297
  17.7 1.2 %collective-permute-start.5 = (bf16[768,512]{1,0:T(8,128)(2,1)}, bf16[768,512]{1,0:T(8,128)(2,1)S(1)}, u32[]{:S(2)}, u32[]{:S(2)}) collective-permute-start(bf16[768,512]{1,0:T(8,128)(2,1)} %get-tuple-element.24), channel_id=1, source_target_pairs={{0,16},{4,20},{8,24},{12,28},{16,0},{20,4},{24,8},{28,12},{1,17},{... | collective-permute-start | bytes 2359304 | tf_op jit(solution)/shard_map/ppermute | solution.py:236
  18.9 1.2 %collective-permute-start.10 = (bf16[768,512]{1,0:T(8,128)(2,1)}, bf16[768,512]{1,0:T(8,128)(2,1)S(1)}, u32[]{:S(2)}, u32[]{:S(2)}) collective-permute-start(bf16[768,512]{1,0:T(8,128)(2,1)} %get-tuple-element.28), channel_id=1, source_target_pairs={{0,8},{4,12},{8,0},{12,4},{16,24},{20,28},{24,16},{28,20},{1,9},{5... | collective-permute-start | bytes 2359304 | tf_op jit(solution)/shard_map/ppermute | solution.py:236
  20.2 0.8 %collective-permute-done.6.refs_6_ = bf16[1024,128]{1,0:T(8,128)(2,1)S(1)} collective-permute-done((bf16[1024,128]{1,0:T(8,128)(2,1)S(1)}, bf16[1024,128]{1,0:T(8,128)(2,1)S(1)}, u32[]{:S(2)}, u32[]{:S(2)}) %collective-permute-start.6) | collective-permute-done | bytes 262176 | tf_op jit(solution)/shard_map/ppermute | solution.py:236
  21.7 0.9 %copy-done.3 = bf16[1024,128]{1,0:T(8,128)(2,1)S(1)} copy-done((bf16[1024,128]{1,0:T(8,128)(2,1)S(1)}, bf16[1024,128]{1,0:T(8,128)(2,1)}, u32[]{:S(2)}) %copy-start.3) | copy-done | bytes 262168
  22.6 6.4 %shard_map.55 = (f32[384,256]{1,0:T(8,128)S(1)}, f32[384,256]{1,0:T(8,128)S(1)}) custom-call(s32[4]{0:T(128)S(1)} %pad_add_fusion.1.starts, bf16[384,8192]{1,0:T(8,128)(2,1)} %bitcast.18, bf16[384,8192]{1,0:T(8,128)(2,1)} %collective-permute-done.far, bf16[1024,128]{1,0:T(8,128)(2,1)S(1)} %copy-done, bf16[1024,128]{1,0:T(8,128)(2,1)S(1)} %copy-done.1, ...), custom_call_target="tpu_custom_call" | custom-call | flops 1610612736 | bytes 8388608 | tf_op jit(solution)/shard_map/pallas_call | solution.py:111
  29.0 4.9 %collective-permute-start.8 = (f32[384,256]{1,0:T(8,128)S(1)}, f32[384,256]{1,0:T(8,128)S(1)}, u32[]{:S(2)}, u32[]{:S(2)}) collective-permute-start(f32[384,256]{1,0:T(8,128)S(1)} %get-tuple-element.26), channel_id=1, source_target_pairs={{0,4},{4,0},{8,12},{12,8},{16,20},{20,16},{24,28},{28,24},{1,5},{5... | collective-permute-start | bytes 1179656 | tf_op jit(solution)/shard_map/ppermute | solution.py:236
  33.9 1.3 %collective-permute-done.8.far = f32[384,256]{1,0:T(8,128)S(1)} collective-permute-done((f32[384,256]{1,0:T(8,128)S(1)}, f32[384,256]{1,0:T(8,128)S(1)}, u32[]{:S(2)}, u32[]{:S(2)}) %collective-permute-start.8) | collective-permute-done | bytes 393248 | tf_op jit(solution)/shard_map/ppermute | solution.py:236
  35.4 3.2 %collective-permute-start.9 = (bf16[384,256]{1,0:T(8,128)(2,1)S(1)}, bf16[384,256]{1,0:T(8,128)(2,1)S(1)}, u32[]{:S(2)}, u32[]{:S(2)}) collective-permute-start(bf16[384,256]{1,0:T(8,128)(2,1)S(1)} %shard_map.56), channel_id=1, source_target_pairs={{0,1},{1,2},{2,3},{4,5},{5,6},{6,7},{8,9},{9,10},{10,11},{12,13},{... | collective-permute-start | bytes 589832 | tf_op jit(solution)/shard_map/ppermute | solution.py:286
  38.6 1.7 %constant_dynamic-slice_fusion = (bf16[128,512]{1,0:T(8,128)(2,1)}, bf16[128,512]{1,0:T(8,128)(2,1)}) fusion(bf16[1024,512]{1,0:T(8,128)(2,1)} %param.6, s32[]{:T(128)S(6)} %select_n.33, s32[]{:T(128)S(6)} %select_n.32), kind=kLoop, calls=%fused_computation.11 | loop fusion | bytes 524296 | tf_op jit(solution)/shard_map/dynamic_slice | solution.py:322
  40.4 1.4 %collective-permute-start.16 = (bf16[128,512]{1,0:T(8,128)(2,1)}, bf16[128,512]{1,0:T(8,128)(2,1)}, u32[]{:S(2)}, u32[]{:S(2)}) collective-permute-start(bf16[128,512]{1,0:T(8,128)(2,1)} %get-tuple-element.37), channel_id=1, source_target_pairs={{0,16},{4,20},{8,24},{12,28},{16,0},{20,4},{24,8},{28,12},{1,17},{... | collective-permute-start | bytes 393224 | tf_op jit(solution)/shard_map/ppermute | solution.py:236
  41.9 1.5 %collective-permute-done.9 = bf16[384,256]{1,0:T(8,128)(2,1)S(1)} collective-permute-done((bf16[384,256]{1,0:T(8,128)(2,1)S(1)}, bf16[384,256]{1,0:T(8,128)(2,1)S(1)}, u32[]{:S(2)}, u32[]{:S(2)}) %collective-permute-start.9) | collective-permute-done | bytes 196640 | tf_op jit(solution)/shard_map/ppermute | solution.py:286
  43.4 0.9 %slice.43 = bf16[512,512]{1,0:T(8,128)(2,1)} slice(bf16[768,512]{1,0:T(8,128)(2,1)S(1)} %collective-permute-done.5.refs_3_.refs_4_), slice={[0:512], [0:512]} | slice | bytes 1048576 | tf_op jit(solution)/shard_map/slice | solution.py:315
  44.3 0.9 %slice.42 = bf16[512,512]{1,0:T(8,128)(2,1)} slice(bf16[768,512]{1,0:T(8,128)(2,1)S(1)} %collective-permute-done.10.refs_0_.refs_1_), slice={[0:512], [0:512]} | slice | bytes 1048576 | tf_op jit(solution)/shard_map/slice | solution.py:315
  45.2 1.6 %collective-permute-start.13 = (bf16[512,512]{1,0:T(8,128)(2,1)}, bf16[512,512]{1,0:T(8,128)(2,1)}, u32[]{:S(2)}, u32[]{:S(2)}) collective-permute-start(bf16[512,512]{1,0:T(8,128)(2,1)} %slice.42), channel_id=1, source_target_pairs={{0,16},{4,20},{8,24},{12,28},{16,0},{20,4},{24,8},{28,12},{1,17},{... | collective-permute-start | bytes 1572872 | tf_op jit(solution)/shard_map/ppermute | solution.py:236
  47.5 1.4 %collective-permute-start.11 = (bf16[256,512]{1,0:T(8,128)(2,1)}, bf16[256,512]{1,0:T(8,128)(2,1)S(1)}, u32[]{:S(2)}, u32[]{:S(2)}) collective-permute-start(bf16[256,512]{1,0:T(8,128)(2,1)} %pad_maximum_fusion.3), channel_id=1, source_target_pairs={{0,1},{1,0},{2,3},{3,2},{4,5},{5,4},{6,7},{7,6},{8,9},{9,8},{10,11... | collective-permute-start | bytes 786440 | tf_op jit(solution)/shard_map/ppermute | solution.py:312
  49.1 2.0 %collective-permute-start.12 = (bf16[384,256]{1,0:T(8,128)(2,1)}, bf16[384,256]{1,0:T(8,128)(2,1)S(1)}, u32[]{:S(2)}, u32[]{:S(2)}) collective-permute-start(bf16[384,256]{1,0:T(8,128)(2,1)} %copy-done.5), channel_id=1, source_target_pairs={{0,1},{1,2},{2,3},{4,5},{5,6},{6,7},{8,9},{9,10},{10,11},{12,13},{... | collective-permute-start | bytes 589832 | tf_op jit(solution)/shard_map/ppermute | solution.py:286
  51.1 5.2 %shard_map.57.refs_4_ = f32[768,512]{1,0:T(8,128)S(1)} custom-call(s32[8]{0:T(128)S(1)} %stack.66.starts, bf16[384,8192]{1,0:T(8,128)(2,1)} %bitcast.19, bf16[384,8192]{1,0:T(8,128)(2,1)} %collective-permute-done.far, bf16[768,512]{1,0:T(8,128)(2,1)S(1)} %collective-permute-done.10.refs_0_.refs_1_, ...), custom_call_target="tpu_custom_call" | custom-call | flops 2214592512 | bytes 7208960 | tf_op jit(solution)/shard_map/pallas_call | solution.py:111
  56.3 1.1 %collective-permute-done.12 = bf16[384,256]{1,0:T(8,128)(2,1)S(1)} collective-permute-done((bf16[384,256]{1,0:T(8,128)(2,1)}, bf16[384,256]{1,0:T(8,128)(2,1)S(1)}, u32[]{:S(2)}, u32[]{:S(2)}) %collective-permute-start.12) | collective-permute-done | bytes 196640 | tf_op jit(solution)/shard_map/ppermute | solution.py:286
  58.1 3.9 %shard_map.58 = (f32[384,512]{1,0:T(8,128)S(1)}, f32[384,512]{1,0:T(8,128)S(1)}) custom-call(s32[4]{0:T(128)S(1)} %pad_add_fusion.starts, bf16[384,8192]{1,0:T(8,128)(2,1)} %bitcast.20, bf16[384,8192]{1,0:T(8,128)(2,1)} %collective-permute-done.far, bf16[256,512]{1,0:T(8,128)(2,1)S(1)} %collective-permute-done.11.refs_0_.refs_1_, ...), custom_call_target="tpu_custom_call" | custom-call | flops 1006632960 | bytes 3276800 | tf_op jit(solution)/shard_map/pallas_call | solution.py:111
  62.0 2.7 %collective-permute-start.17 = (f32[384,512]{1,0:T(8,128)S(1)}, f32[384,512]{1,0:T(8,128)S(1)}, u32[]{:S(2)}, u32[]{:S(2)}) collective-permute-start(f32[384,512]{1,0:T(8,128)S(1)} %get-tuple-element.42), channel_id=1, source_target_pairs={{0,4},{4,0},{8,12},{12,8},{16,20},{20,16},{24,28},{28,24},{1,5},{5... | collective-permute-start | bytes 2359304 | tf_op jit(solution)/shard_map/ppermute | solution.py:236
  64.8 1.0 %pad_maximum_fusion.2.keys_values = bf16[1152,256]{1,0:T(8,128)(2,1)S(1)} fusion(bf16[384,256]{1,0:T(8,128)(2,1)S(1)} %shard_map.56, bf16[384,256]{1,0:T(8,128)(2,1)S(1)} %copy-done.6, bf16[384,256]{1,0:T(8,128)(2,1)} %copy-done.7), kind=kLoop, calls=%fused_computation.2 | loop fusion | flops 1769472 | bytes 1179648 | tf_op jit(solution)/shard_map/concatenate | solution.py:287
  65.8 0.8 %collective-permute-done.17.far = f32[384,512]{1,0:T(8,128)S(1)} collective-permute-done((f32[384,512]{1,0:T(8,128)S(1)}, f32[384,512]{1,0:T(8,128)S(1)}, u32[]{:S(2)}, u32[]{:S(2)}) %collective-permute-start.17) | collective-permute-done | bytes 786464 | tf_op jit(solution)/shard_map/ppermute | solution.py:236
  66.5 3.6 %shard_map.59 = bf16[384,512]{1,0:T(8,128)(2,1)} custom-call(f32[384,512]{1,0:T(8,128)S(1)} %get-tuple-element.41.near, f32[384,512]{1,0:T(8,128)S(1)} %collective-permute-done.17.far, f32[384,128]{1,0:T(8,128)S(1)} %pad_maximum_fusion.4.cosine, f32[384,128]{1,0:T(8,128)S(1)} %pad_maximum_fusion.5.sine, s32[384,1]{1,0:T(8,128)S(1)} %copy.7.first, ...), custom_call_target="tpu_custom_call" | custom-call | flops 704643072 | bytes 1572864 | tf_op jit(solution)/shard_map/pallas_call | solution.py:206
  (49 shorter events, 5.8 us)
Async XLA Ops:
  0.0 21.6 %collective-permute-start = (bf16[384,8192]{1,0:T(8,128)(2,1)}, bf16[384,8192]{1,0:T(8,128)(2,1)}, u32[]{:S(2)}, u32[]{:S(2)}) collective-permute-start(bf16[384,8192]{1,0:T(8,128)(2,1)} %bitcast.17), channel_id=1, source_target_pairs={{0,4},{4,0},{8,12},{12,8},{16,20},{20,16},{24,28},{28,24},{1,5},{5... | collective-permute-start | bytes 18874376 | tf_op jit(solution)/shard_map/ppermute | solution.py:236
  0.7 8.6 %collective-permute-start.1 = (bf16[1024,128]{1,0:T(8,128)(2,1)}, bf16[1024,128]{1,0:T(8,128)(2,1)S(1)}, u32[]{:S(2)}, u32[]{:S(2)}) collective-permute-start(bf16[1024,128]{1,0:T(8,128)(2,1)} %refs_0_.1), channel_id=1, source_target_pairs={{0,8},{4,12},{8,0},{12,4},{16,24},{20,28},{24,16},{28,20},{1,9},{5... | collective-permute-start | bytes 786440 | tf_op jit(solution)/shard_map/ppermute | solution.py:236
  1.9 15.1 %collective-permute-start.2 = (bf16[1024,128]{1,0:T(8,128)(2,1)}, bf16[1024,128]{1,0:T(8,128)(2,1)S(1)}, u32[]{:S(2)}, u32[]{:S(2)}) collective-permute-start(bf16[1024,128]{1,0:T(8,128)(2,1)} %refs_0_.1), channel_id=1, source_target_pairs={{0,16},{4,20},{8,24},{12,28},{16,0},{20,4},{24,8},{28,12},{1,17},{... | collective-permute-start | bytes 786440 | tf_op jit(solution)/shard_map/ppermute | solution.py:236
  3.1 12.3 %collective-permute-start.4 = (bf16[1024,128]{1,0:T(8,128)(2,1)}, bf16[1024,128]{1,0:T(8,128)(2,1)}, u32[]{:S(2)}, u32[]{:S(2)}) collective-permute-start(bf16[1024,128]{1,0:T(8,128)(2,1)} %refs_1_.1), channel_id=1, source_target_pairs={{0,16},{4,20},{8,24},{12,28},{16,0},{20,4},{24,8},{28,12},{1,17},{... | collective-permute-start | bytes 786440 | tf_op jit(solution)/shard_map/ppermute | solution.py:236
  3.4 13.6 %collective-permute-start.3 = (bf16[1024,128]{1,0:T(8,128)(2,1)}, bf16[1024,128]{1,0:T(8,128)(2,1)S(1)}, u32[]{:S(2)}, u32[]{:S(2)}) collective-permute-start(bf16[1024,128]{1,0:T(8,128)(2,1)} %refs_1_.1), channel_id=1, source_target_pairs={{0,8},{4,12},{8,0},{12,4},{16,24},{20,28},{24,16},{28,20},{1,9},{5... | collective-permute-start | bytes 786440 | tf_op jit(solution)/shard_map/ppermute | solution.py:236
  5.2 2.9 %copy-start.4 = (bf16[1024,512]{1,0:T(8,128)(2,1)S(1)}, bf16[1024,512]{1,0:T(8,128)(2,1)}, u32[]{:S(2)}) copy-start(bf16[1024,512]{1,0:T(8,128)(2,1)} %param.6) | copy-start | bytes 3145732
  9.2 11.7 %collective-permute-start.6 = (bf16[1024,128]{1,0:T(8,128)(2,1)S(1)}, bf16[1024,128]{1,0:T(8,128)(2,1)S(1)}, u32[]{:S(2)}, u32[]{:S(2)}) collective-permute-start(bf16[1024,128]{1,0:T(8,128)(2,1)S(1)} %collective-permute-done.1.refs_2_), channel_id=1, source_target_pairs={{0,16},{4,20},{8,24},{12,28},{16,0},{20,4},{24,8},{28,12},{1,17},{... | collective-permute-start | bytes 786440 | tf_op jit(solution)/shard_map/ppermute | solution.py:236
  15.4 6.2 %collective-permute-start.7 = (bf16[1024,128]{1,0:T(8,128)(2,1)}, bf16[1024,128]{1,0:T(8,128)(2,1)S(1)}, u32[]{:S(2)}, u32[]{:S(2)}) collective-permute-start(bf16[1024,128]{1,0:T(8,128)(2,1)} %collective-permute-done.4.refs_5_), channel_id=1, source_target_pairs={{0,8},{4,12},{8,0},{12,4},{16,24},{20,28},{24,16},{28,20},{1,9},{5... | collective-permute-start | bytes 786440 | tf_op jit(solution)/shard_map/ppermute | solution.py:236
  15.7 6.0 %copy-start = (bf16[1024,128]{1,0:T(8,128)(2,1)S(1)}, bf16[1024,128]{1,0:T(8,128)(2,1)}, u32[]{:S(2)}) copy-start(bf16[1024,128]{1,0:T(8,128)(2,1)} %refs_0_.1) | copy-start | bytes 786436
  15.7 6.0 %copy-start.1 = (bf16[1024,128]{1,0:T(8,128)(2,1)S(1)}, bf16[1024,128]{1,0:T(8,128)(2,1)}, u32[]{:S(2)}) copy-start(bf16[1024,128]{1,0:T(8,128)(2,1)} %refs_1_.1) | copy-start | bytes 786436
  17.0 0.7 %copy-start.2 = (bf16[1024,128]{1,0:T(8,128)(2,1)}, bf16[1024,128]{1,0:T(8,128)(2,1)S(1)}, u32[]{:S(2)}) copy-start(bf16[1024,128]{1,0:T(8,128)(2,1)S(1)} %collective-permute-done.3.refs_3_) | copy-start | bytes 786436
  17.7 25.8 %collective-permute-start.5 = (bf16[768,512]{1,0:T(8,128)(2,1)}, bf16[768,512]{1,0:T(8,128)(2,1)S(1)}, u32[]{:S(2)}, u32[]{:S(2)}) collective-permute-start(bf16[768,512]{1,0:T(8,128)(2,1)} %get-tuple-element.24), channel_id=1, source_target_pairs={{0,16},{4,20},{8,24},{12,28},{16,0},{20,4},{24,8},{28,12},{1,17},{... | collective-permute-start | bytes 2359304 | tf_op jit(solution)/shard_map/ppermute | solution.py:236
  18.9 24.5 %collective-permute-start.10 = (bf16[768,512]{1,0:T(8,128)(2,1)}, bf16[768,512]{1,0:T(8,128)(2,1)S(1)}, u32[]{:S(2)}, u32[]{:S(2)}) collective-permute-start(bf16[768,512]{1,0:T(8,128)(2,1)} %get-tuple-element.28), channel_id=1, source_target_pairs={{0,8},{4,12},{8,0},{12,4},{16,24},{20,28},{24,16},{28,20},{1,9},{5... | collective-permute-start | bytes 2359304 | tf_op jit(solution)/shard_map/ppermute | solution.py:236
  21.7 1.0 %copy-start.3 = (bf16[1024,128]{1,0:T(8,128)(2,1)S(1)}, bf16[1024,128]{1,0:T(8,128)(2,1)}, u32[]{:S(2)}) copy-start(bf16[1024,128]{1,0:T(8,128)(2,1)} %copy-done.2) | copy-start | bytes 786436
  29.0 6.3 %collective-permute-start.8 = (f32[384,256]{1,0:T(8,128)S(1)}, f32[384,256]{1,0:T(8,128)S(1)}, u32[]{:S(2)}, u32[]{:S(2)}) collective-permute-start(f32[384,256]{1,0:T(8,128)S(1)} %get-tuple-element.26), channel_id=1, source_target_pairs={{0,4},{4,0},{8,12},{12,8},{16,20},{20,16},{24,28},{28,24},{1,5},{5... | collective-permute-start | bytes 1179656 | tf_op jit(solution)/shard_map/ppermute | solution.py:236
  35.4 8.0 %collective-permute-start.9 = (bf16[384,256]{1,0:T(8,128)(2,1)S(1)}, bf16[384,256]{1,0:T(8,128)(2,1)S(1)}, u32[]{:S(2)}, u32[]{:S(2)}) collective-permute-start(bf16[384,256]{1,0:T(8,128)(2,1)S(1)} %shard_map.56), channel_id=1, source_target_pairs={{0,1},{1,2},{2,3},{4,5},{5,6},{6,7},{8,9},{9,10},{10,11},{12,13},{... | collective-permute-start | bytes 589832 | tf_op jit(solution)/shard_map/ppermute | solution.py:286
  40.4 8.7 %collective-permute-start.16 = (bf16[128,512]{1,0:T(8,128)(2,1)}, bf16[128,512]{1,0:T(8,128)(2,1)}, u32[]{:S(2)}, u32[]{:S(2)}) collective-permute-start(bf16[128,512]{1,0:T(8,128)(2,1)} %get-tuple-element.37), channel_id=1, source_target_pairs={{0,16},{4,20},{8,24},{12,28},{16,0},{20,4},{24,8},{28,12},{1,17},{... | collective-permute-start | bytes 393224 | tf_op jit(solution)/shard_map/ppermute | solution.py:236
  41.8 7.3 %collective-permute-start.15 = (bf16[128,512]{1,0:T(8,128)(2,1)}, bf16[128,512]{1,0:T(8,128)(2,1)}, u32[]{:S(2)}, u32[]{:S(2)}) collective-permute-start(bf16[128,512]{1,0:T(8,128)(2,1)} %get-tuple-element.35), channel_id=1, source_target_pairs={{0,8},{4,12},{8,0},{12,4},{16,24},{20,28},{24,16},{28,20},{1,9},{5... | collective-permute-start | bytes 393224 | tf_op jit(solution)/shard_map/ppermute | solution.py:236
  43.4 1.8 %copy-start.5 = (bf16[384,256]{1,0:T(8,128)(2,1)}, bf16[384,256]{1,0:T(8,128)(2,1)S(1)}, u32[]{:S(2)}) copy-start(bf16[384,256]{1,0:T(8,128)(2,1)S(1)} %collective-permute-done.9) | copy-start | bytes 589828
  44.3 13.2 %collective-permute-start.14 = (bf16[512,512]{1,0:T(8,128)(2,1)}, bf16[512,512]{1,0:T(8,128)(2,1)}, u32[]{:S(2)}, u32[]{:S(2)}) collective-permute-start(bf16[512,512]{1,0:T(8,128)(2,1)} %slice.43), channel_id=1, source_target_pairs={{0,8},{4,12},{8,0},{12,4},{16,24},{20,28},{24,16},{28,20},{1,9},{5... | collective-permute-start | bytes 1572872 | tf_op jit(solution)/shard_map/ppermute | solution.py:236
  45.2 12.9 %collective-permute-start.13 = (bf16[512,512]{1,0:T(8,128)(2,1)}, bf16[512,512]{1,0:T(8,128)(2,1)}, u32[]{:S(2)}, u32[]{:S(2)}) collective-permute-start(bf16[512,512]{1,0:T(8,128)(2,1)} %slice.42), channel_id=1, source_target_pairs={{0,16},{4,20},{8,24},{12,28},{16,0},{20,4},{24,8},{28,12},{1,17},{... | collective-permute-start | bytes 1572872 | tf_op jit(solution)/shard_map/ppermute | solution.py:236
  47.5 9.9 %collective-permute-start.11 = (bf16[256,512]{1,0:T(8,128)(2,1)}, bf16[256,512]{1,0:T(8,128)(2,1)S(1)}, u32[]{:S(2)}, u32[]{:S(2)}) collective-permute-start(bf16[256,512]{1,0:T(8,128)(2,1)} %pad_maximum_fusion.3), channel_id=1, source_target_pairs={{0,1},{1,0},{2,3},{3,2},{4,5},{5,4},{6,7},{7,6},{8,9},{9,8},{10,11... | collective-permute-start | bytes 786440 | tf_op jit(solution)/shard_map/ppermute | solution.py:312
  49.1 8.3 %collective-permute-start.12 = (bf16[384,256]{1,0:T(8,128)(2,1)}, bf16[384,256]{1,0:T(8,128)(2,1)S(1)}, u32[]{:S(2)}, u32[]{:S(2)}) collective-permute-start(bf16[384,256]{1,0:T(8,128)(2,1)} %copy-done.5), channel_id=1, source_target_pairs={{0,1},{1,2},{2,3},{4,5},{5,6},{6,7},{8,9},{9,10},{10,11},{12,13},{... | collective-permute-start | bytes 589832 | tf_op jit(solution)/shard_map/ppermute | solution.py:286
  56.3 8.5 %copy-start.6 = (bf16[384,256]{1,0:T(8,128)(2,1)S(1)}, bf16[384,256]{1,0:T(8,128)(2,1)}, u32[]{:S(2)}) copy-start(bf16[384,256]{1,0:T(8,128)(2,1)} %copy-done.5) | copy-start | bytes 589828
  57.4 0.7 copy-start.7
  62.0 4.6 %collective-permute-start.17 = (f32[384,512]{1,0:T(8,128)S(1)}, f32[384,512]{1,0:T(8,128)S(1)}, u32[]{:S(2)}, u32[]{:S(2)}) collective-permute-start(f32[384,512]{1,0:T(8,128)S(1)} %get-tuple-element.42), channel_id=1, source_target_pairs={{0,4},{4,0},{8,12},{12,8},{16,20},{20,16},{24,28},{28,24},{1,5},{5... | collective-permute-start | bytes 2359304 | tf_op jit(solution)/shard_map/ppermute | solution.py:236

commit v16 on v13

--- a/solution.py
+++ b/solution.py
@@ -89,12 +89,12 @@
         if carried:
             total = total + carry[place, :]
         if final:
-            outs[1 - side][...] = total
+            outs[1 - side][...] = total.astype(outs[1 - side].dtype)
         else:
             outs[0][place, :] = total
 
 
-def project(terms, near, far, carry=None, final=False):
+def project(terms, near, far, carry=None, final=None):
     rows = near.shape[0]
     width = sum(array.shape[1] for array in terms[0][1])
     steps = []
@@ -107,10 +107,11 @@
     weights = [array for _, arrays, *_ in terms for array in arrays]
     whole = jax.ShapeDtypeStruct((2 * rows, width), jnp.float32)
     part = jax.ShapeDtypeStruct((rows, width), jnp.float32)
+    sent = jax.ShapeDtypeStruct((rows, width), final or jnp.float32)
     carries = [] if carry is None else [carry]
     return pl.pallas_call(
         functools.partial(project_kernel, steps, carry is not None, final),
-        out_shape=(part, part) if final else whole,
+        out_shape=(part, sent) if final else whole,
         in_specs=[pl.BlockSpec(memory_space=pltpu.SMEM)]
         + anywhere(2 + len(weights))
         + vmem(len(carries)),
@@ -135,7 +136,7 @@
 
 def pair_kernel(near, far, cosine, sine, out):
     head_size = cosine.shape[1]
-    pair = near[...] + far[...]
+    pair = near[...] + far[...].astype(jnp.float32)
     out[:, :head_size] = turn(pair[:, :head_size], cosine[...], sine[...]).astype(out.dtype)
     out[:, head_size:] = pair[:, head_size:].astype(out.dtype)
 
@@ -160,7 +161,7 @@
     tiles = rows // ROW_TILE
     for head in range(head_count):
         columns = slice(head * head_size, (head + 1) * head_size)
-        turned = turn(near[:, columns] + far[:, columns], cosine[...], sine[...])
+        turned = turn(near[:, columns] + far[:, columns].astype(jnp.float32), cosine[...], sine[...])
         turned = turned.astype(jnp.bfloat16)
         for tile in range(tiles):
             rotated[tile, head * ROW_TILE : (head + 1) * ROW_TILE, :] = turned[
@@ -279,7 +280,7 @@
     late_chips = [chip for chip in range(chips) if chip not in early_chips]
     carry = project([pair_terms[chip] for chip in early_chips], hidden, sibling_hidden)
     terms = [pair_terms[chip] for chip in late_chips]
-    near, far = project(terms, hidden, sibling_hidden, carry, True)
+    near, far = project(terms, hidden, sibling_hidden, carry, jnp.float32)
     pair = finish_pair(near, swap(far, 1), cosine, sine)
     longest = ctx_size * row_count // 2
     back = -(-(longest - 1) // ROW_TILE) * ROW_TILE
@@ -337,7 +338,7 @@
 
     carry = project(gated(early, *later), hidden, sibling_hidden)
     terms = gated(late, corner(blocks[0]))
-    near, far = project(terms, hidden, sibling_hidden, carry, True)
+    near, far = project(terms, hidden, sibling_hidden, carry, jnp.bfloat16)
     return attend(near, swap(far, 1), cosine, sine, first, keys_values, back)[None]
 
 

time: 68.8 us -> 68.3 us (level)
    unnamed x18 -> x20, local copies, waits for them, and re-layouts: 3.45 us -> 3.46 us
where the time goes in v16:
time: 68.3 us; the launch traced here: 67.4 us
  Pallas kernels  20.5 us (30%)
  starting transfers between devices  20.4 us (30%)
  waiting for transfers between devices  12.2 us (18%)
  local copies, waits for them, and re-layouts  8.31 us (12%)
  other arithmetic  5.7 us (8%)
    pallas_call x4, Pallas kernels, project(): pl.pallas_call(functools.partial(project_kernel, steps, carry is not None...  16.7 us
    ppermute x15, starting transfers between devices, swap(): return lax.ppermute(array, 'dp', [(i, i ^ mask) for i in range(dp_size)])  13.8 us
    ppermute x15, waiting for transfers between devices, swap(): return lax.ppermute(array, 'dp', [(i, i ^ mask) for i in range(dp_size)])  8.46 us
    ppermute x2, starting transfers between devices, shards(): lax.ppermute(blocks[0], 'ctx', [(i, i + 1) for i in range(ctx_size - 1)])  5.18 us
    ppermute x2, waiting for transfers between devices, shards(): lax.ppermute(blocks[0], 'ctx', [(i, i + 1) for i in range(ctx_size - 1)])  3.73 us
    pallas_call x1, Pallas kernels, attend(): pl.pallas_call(functools.partial(attend_kernel, back), out_shape=jax.Shap...  3.66 us
    unnamed x20, local copies, waits for them, and re-layouts  3.46 us
    slice x2, local copies, waits for them, and re-layouts, shards(): given[side][chip] = after(got[side], *later)[:half]  1.75 us
  transfers between devices with their start and end apart: 18, of which 8 were waited for; matrix products, arithmetic and copies ran while one was open for 16% of the time, Pallas kernels for 19%

profile of v16, /device:TPU:17, one launch (start us, length us, event | category | flops | bytes accessed | tf_op | source)
XLA Modules:
  0.0 67.4 jit_solution(7242422300828382043)
XLA Ops:
  0.7 1.2 %collective-permute-start.1 = (bf16[1024,128]{1,0:T(8,128)(2,1)}, bf16[1024,128]{1,0:T(8,128)(2,1)}, u32[]{:S(2)}, u32[]{:S(2)}) collective-permute-start(bf16[1024,128]{1,0:T(8,128)(2,1)} %refs_0_.1), channel_id=1, source_target_pairs={{0,8},{4,12},{8,0},{12,4},{16,24},{20,28},{24,16},{28,20},{1,9},{5... | collective-permute-start | bytes 786440 | tf_op jit(solution)/shard_map/ppermute | solution.py:237
  1.9 1.2 %collective-permute-start.2 = (bf16[1024,128]{1,0:T(8,128)(2,1)}, bf16[1024,128]{1,0:T(8,128)(2,1)S(1)}, u32[]{:S(2)}, u32[]{:S(2)}) collective-permute-start(bf16[1024,128]{1,0:T(8,128)(2,1)} %refs_0_.1), channel_id=1, source_target_pairs={{0,16},{4,20},{8,24},{12,28},{16,0},{20,4},{24,8},{28,12},{1,17},{... | collective-permute-start | bytes 786440 | tf_op jit(solution)/shard_map/ppermute | solution.py:237
  3.6 0.8 %reduce-window_clone.1 = s32[1,16]{1,0:T(1,128)S(1)} reduce-window(s32[1,16]{1,0:T(1,128)} %param.9, s32[]{:T(128)} %constant.44.clone.1), window={size=1x16 pad=0_0x15_0}, to_apply=%region_0.0 | reduce-window | flops 240 | bytes 132 | tf_op jit(solution)/shard_map/reduce-window.clone
  5.2 1.1 %constant_dynamic-slice_fusion.5 = (bf16[256,512]{1,0:T(8,128)(2,1)S(1)}, bf16[256,512]{1,0:T(8,128)(2,1)S(1)}) fusion(bf16[1024,512]{1,0:T(8,128)(2,1)} %param.6, s32[]{:T(128)S(6)} %select_n.28, s32[]{:T(128)S(6)} %select_n.31), kind=kLoop, calls=%fused_computation.16 | loop fusion | bytes 1048584 | tf_op jit(solution)/shard_map/dynamic_slice | solution.py:303
  6.3 0.8 %fusion = (f32[384,64]{1,0:T(8,128)S(1)}, f32[384,64]{1,0:T(8,128)S(1)}, f32[384,64]{1,0:T(8,128)S(1)}) fusion(f32[64]{0:T(128)S(1)} %negate_power_fusion, f32[384]{0:T(512)S(1)} %get-tuple-element.55), kind=kLoop, calls=%fused_computation.8 | loop fusion | flops 49152 | bytes 296704 | tf_op jit(solution)/shard_map/neg | solution.py:24
  7.3 1.3 %pad_maximum_fusion = (bf16[768,512]{1,0:T(8,128)(2,1)}, bf16[768,512]{1,0:T(8,128)(2,1)}) fusion(bf16[256,512]{1,0:T(8,128)(2,1)S(1)} %get-tuple-element.47, bf16[512,512]{1,0:T(8,128)(2,1)S(1)} %get-tuple-element.40.refs_7_, bf16[256,512]{1,0:T(8,128)(2,1)S(1)} %get-tuple-element.48, bf16[512,512]{1,0:T(8,128)(2,1)S(1)} %get-tuple-element.39.refs_6_), kind=kLoop, calls=%fused_computation | loop fusion | flops 3145728 | bytes 3145728 | tf_op jit(solution)/shard_map/concatenate | solution.py:300
  8.9 1.2 %collective-permute-start.6 = (bf16[1024,128]{1,0:T(8,128)(2,1)}, bf16[1024,128]{1,0:T(8,128)(2,1)}, u32[]{:S(2)}, u32[]{:S(2)}) collective-permute-start(bf16[1024,128]{1,0:T(8,128)(2,1)} %collective-permute-done.1.refs_2_), channel_id=1, source_target_pairs={{0,16},{4,20},{8,24},{12,28},{16,0},{20,4},{24,8},{28,12},{1,17},{... | collective-permute-start | bytes 786440 | tf_op jit(solution)/shard_map/ppermute | solution.py:237
  10.1 5.3 %collective-permute-done.4.refs_5_ = bf16[1024,128]{1,0:T(8,128)(2,1)} collective-permute-done((bf16[1024,128]{1,0:T(8,128)(2,1)}, bf16[1024,128]{1,0:T(8,128)(2,1)}, u32[]{:S(2)}, u32[]{:S(2)}) %collective-permute-start.4) | collective-permute-done | bytes 262176 | tf_op jit(solution)/shard_map/ppermute | solution.py:237
  16.5 0.7 %copy-done.4 = bf16[1024,128]{1,0:T(8,128)(2,1)} copy-done((bf16[1024,128]{1,0:T(8,128)(2,1)}, bf16[1024,128]{1,0:T(8,128)(2,1)S(1)}, u32[]{:S(2)}) %copy-start.4) | copy-done | bytes 262168
  17.2 1.2 %collective-permute-start.5 = (bf16[768,512]{1,0:T(8,128)(2,1)}, bf16[768,512]{1,0:T(8,128)(2,1)S(1)}, u32[]{:S(2)}, u32[]{:S(2)}) collective-permute-start(bf16[768,512]{1,0:T(8,128)(2,1)} %get-tuple-element.24), channel_id=1, source_target_pairs={{0,16},{4,20},{8,24},{12,28},{16,0},{20,4},{24,8},{28,12},{1,17},{... | collective-permute-start | bytes 2359304 | tf_op jit(solution)/shard_map/ppermute | solution.py:237
  18.4 1.2 %collective-permute-start.10 = (bf16[768,512]{1,0:T(8,128)(2,1)}, bf16[768,512]{1,0:T(8,128)(2,1)S(1)}, u32[]{:S(2)}, u32[]{:S(2)}) collective-permute-start(bf16[768,512]{1,0:T(8,128)(2,1)} %get-tuple-element.28), channel_id=1, source_target_pairs={{0,8},{4,12},{8,0},{12,4},{16,24},{20,28},{24,16},{28,20},{1,9},{5... | collective-permute-start | bytes 2359304 | tf_op jit(solution)/shard_map/ppermute | solution.py:237
  19.7 0.9 %copy-done.3 = bf16[1024,128]{1,0:T(8,128)(2,1)S(1)} copy-done((bf16[1024,128]{1,0:T(8,128)(2,1)S(1)}, bf16[1024,128]{1,0:T(8,128)(2,1)}, u32[]{:S(2)}) %copy-start.3) | copy-done | bytes 262168
  20.7 0.9 %copy-done.5 = bf16[1024,128]{1,0:T(8,128)(2,1)S(1)} copy-done((bf16[1024,128]{1,0:T(8,128)(2,1)S(1)}, bf16[1024,128]{1,0:T(8,128)(2,1)}, u32[]{:S(2)}) %copy-start.5) | copy-done | bytes 262168
  21.6 5.3 %shard_map.55.refs_2_ = f32[768,256]{1,0:T(8,128)S(1)} custom-call(s32[3]{0:T(128)S(1)} %pad_add_fusion.1.starts, bf16[384,8192]{1,0:T(8,128)(2,1)} %bitcast.18, bf16[384,8192]{1,0:T(8,128)(2,1)} %collective-permute-done.far, bf16[1024,128]{1,0:T(8,128)(2,1)S(1)} %copy-done, bf16[1024,128]{1,0:T(8,128)(2,1)S(1)} %copy-done.1, ...), custom_call_target="tpu_custom_call" | custom-call | flops 1207959552 | bytes 6291456 | tf_op jit(solution)/shard_map/pallas_call | solution.py:112
  26.9 2.4 %shard_map.56 = (f32[384,256]{1,0:T(8,128)S(1)}, f32[384,256]{1,0:T(8,128)S(1)}) custom-call(s32[1]{0:T(128)} %bitcast.2.starts, bf16[384,8192]{1,0:T(8,128)(2,1)} %bitcast.19, bf16[384,8192]{1,0:T(8,128)(2,1)} %collective-permute-done.far, bf16[1024,128]{1,0:T(8,128)(2,1)} %collective-permute-done.6.refs_0_, ...), custom_call_target="tpu_custom_call" | custom-call | flops 402653184 | bytes 2097152 | tf_op jit(solution)/shard_map/pallas_call | solution.py:112
  29.4 2.9 %collective-permute-start.8 = (f32[384,256]{1,0:T(8,128)S(1)}, f32[384,256]{1,0:T(8,128)S(1)}, u32[]{:S(2)}, u32[]{:S(2)}) collective-permute-start(f32[384,256]{1,0:T(8,128)S(1)} %get-tuple-element.26), channel_id=1, source_target_pairs={{0,4},{4,0},{8,12},{12,8},{16,20},{20,16},{24,28},{28,24},{1,5},{5... | collective-permute-start | bytes 1179656 | tf_op jit(solution)/shard_map/ppermute | solution.py:237
  32.3 1.3 %collective-permute-done.8.far = f32[384,256]{1,0:T(8,128)S(1)} collective-permute-done((f32[384,256]{1,0:T(8,128)S(1)}, f32[384,256]{1,0:T(8,128)S(1)}, u32[]{:S(2)}, u32[]{:S(2)}) %collective-permute-start.8) | collective-permute-done | bytes 393248 | tf_op jit(solution)/shard_map/ppermute | solution.py:237
  33.8 3.2 %collective-permute-start.9 = (bf16[384,256]{1,0:T(8,128)(2,1)S(1)}, bf16[384,256]{1,0:T(8,128)(2,1)S(1)}, u32[]{:S(2)}, u32[]{:S(2)}) collective-permute-start(bf16[384,256]{1,0:T(8,128)(2,1)S(1)} %shard_map.57), channel_id=1, source_target_pairs={{0,1},{1,2},{2,3},{4,5},{5,6},{6,7},{8,9},{9,10},{10,11},{12,13},{... | collective-permute-start | bytes 589832 | tf_op jit(solution)/shard_map/ppermute | solution.py:289
  37.0 1.7 %constant_dynamic-slice_fusion = (bf16[128,512]{1,0:T(8,128)(2,1)}, bf16[128,512]{1,0:T(8,128)(2,1)}) fusion(bf16[1024,512]{1,0:T(8,128)(2,1)} %param.6, s32[]{:T(128)S(6)} %select_n.33, s32[]{:T(128)S(6)} %select_n.32), kind=kLoop, calls=%fused_computation.11 | loop fusion | bytes 524296 | tf_op jit(solution)/shard_map/dynamic_slice | solution.py:325
  39.1 2.6 %collective-permute-done.9 = bf16[384,256]{1,0:T(8,128)(2,1)S(1)} collective-permute-done((bf16[384,256]{1,0:T(8,128)(2,1)S(1)}, bf16[384,256]{1,0:T(8,128)(2,1)S(1)}, u32[]{:S(2)}, u32[]{:S(2)}) %collective-permute-start.9) | collective-permute-done | bytes 196640 | tf_op jit(solution)/shard_map/ppermute | solution.py:289
  41.8 0.9 %slice.43 = bf16[512,512]{1,0:T(8,128)(2,1)} slice(bf16[768,512]{1,0:T(8,128)(2,1)S(1)} %collective-permute-done.5.refs_3_.refs_4_), slice={[0:512], [0:512]} | slice | bytes 1048576 | tf_op jit(solution)/shard_map/slice | solution.py:318
  42.9 0.9 %slice.42 = bf16[512,512]{1,0:T(8,128)(2,1)} slice(bf16[768,512]{1,0:T(8,128)(2,1)S(1)} %collective-permute-done.10.refs_0_.refs_1_), slice={[0:512], [0:512]} | slice | bytes 1048576 | tf_op jit(solution)/shard_map/slice | solution.py:318
  44.0 0.7 %pad_maximum_fusion.3 = bf16[256,512]{1,0:T(8,128)(2,1)} fusion(bf16[128,512]{1,0:T(8,128)(2,1)S(1)} %constant_dynamic-slice_fusion.2, bf16[128,512]{1,0:T(8,128)(2,1)S(1)} %constant_dynamic-slice_fusion.4), kind=kLoop, calls=%fused_computation.5 | loop fusion | flops 524288 | bytes 524288 | tf_op jit(solution)/shard_map/concatenate | solution.py:314
  44.7 1.4 %collective-permute-start.11 = (bf16[256,512]{1,0:T(8,128)(2,1)}, bf16[256,512]{1,0:T(8,128)(2,1)S(1)}, u32[]{:S(2)}, u32[]{:S(2)}) collective-permute-start(bf16[256,512]{1,0:T(8,128)(2,1)} %pad_maximum_fusion.3), channel_id=1, source_target_pairs={{0,1},{1,0},{2,3},{3,2},{4,5},{5,4},{6,7},{7,6},{8,9},{9,8},{10,11... | collective-permute-start | bytes 786440 | tf_op jit(solution)/shard_map/ppermute | solution.py:315
  46.3 2.0 %collective-permute-start.12 = (bf16[384,256]{1,0:T(8,128)(2,1)}, bf16[384,256]{1,0:T(8,128)(2,1)S(1)}, u32[]{:S(2)}, u32[]{:S(2)}) collective-permute-start(bf16[384,256]{1,0:T(8,128)(2,1)} %copy-done.7), channel_id=1, source_target_pairs={{0,1},{1,2},{2,3},{4,5},{5,6},{6,7},{8,9},{9,10},{10,11},{12,13},{... | collective-permute-start | bytes 589832 | tf_op jit(solution)/shard_map/ppermute | solution.py:289
  48.3 5.2 %shard_map.58.refs_4_ = f32[768,512]{1,0:T(8,128)S(1)} custom-call(s32[8]{0:T(128)S(1)} %stack.66.starts, bf16[384,8192]{1,0:T(8,128)(2,1)} %bitcast.20, bf16[384,8192]{1,0:T(8,128)(2,1)} %collective-permute-done.far, bf16[768,512]{1,0:T(8,128)(2,1)S(1)} %collective-permute-done.10.refs_0_.refs_1_, ...), custom_call_target="tpu_custom_call" | custom-call | flops 2214592512 | bytes 7208960 | tf_op jit(solution)/shard_map/pallas_call | solution.py:112
  53.5 1.1 %collective-permute-done.12 = bf16[384,256]{1,0:T(8,128)(2,1)S(1)} collective-permute-done((bf16[384,256]{1,0:T(8,128)(2,1)}, bf16[384,256]{1,0:T(8,128)(2,1)S(1)}, u32[]{:S(2)}, u32[]{:S(2)}) %collective-permute-start.12) | collective-permute-done | bytes 196640 | tf_op jit(solution)/shard_map/ppermute | solution.py:289
  55.3 0.7 %collective-permute-done.13.refs_2_ = bf16[512,512]{1,0:T(8,128)(2,1)} collective-permute-done((bf16[512,512]{1,0:T(8,128)(2,1)}, bf16[512,512]{1,0:T(8,128)(2,1)}, u32[]{:S(2)}, u32[]{:S(2)}) %collective-permute-start.13) | collective-permute-done | bytes 524320 | tf_op jit(solution)/shard_map/ppermute | solution.py:237
  56.0 3.9 %shard_map.59 = (f32[384,512]{1,0:T(8,128)S(1)}, bf16[384,512]{1,0:T(8,128)(2,1)S(1)}) custom-call(s32[4]{0:T(128)S(1)} %pad_add_fusion.starts, bf16[384,8192]{1,0:T(8,128)(2,1)} %bitcast.21, bf16[384,8192]{1,0:T(8,128)(2,1)} %collective-permute-done.far, bf16[256,512]{1,0:T(8,128)(2,1)S(1)} %collective-permute-done.11.refs_0_.refs_1_, ...), custom_call_target="tpu_custom_call" | custom-call | flops 1006632960 | bytes 3276800 | tf_op jit(solution)/shard_map/pallas_call | solution.py:112
  59.9 2.5 %collective-permute-start.17 = (bf16[384,512]{1,0:T(8,128)(2,1)S(1)}, bf16[384,512]{1,0:T(8,128)(2,1)S(1)}, u32[]{:S(2)}, u32[]{:S(2)}) collective-permute-start(bf16[384,512]{1,0:T(8,128)(2,1)S(1)} %get-tuple-element.42), channel_id=1, source_target_pairs={{0,4},{4,0},{8,12},{12,8},{16,20},{20,16},{24,28},{28,24},{1,5},{5... | collective-permute-start | bytes 1179656 | tf_op jit(solution)/shard_map/ppermute | solution.py:237
  62.5 1.0 %pad_maximum_fusion.2.keys_values = bf16[1152,256]{1,0:T(8,128)(2,1)S(1)} fusion(bf16[384,256]{1,0:T(8,128)(2,1)S(1)} %shard_map.57, bf16[384,256]{1,0:T(8,128)(2,1)S(1)} %copy-done.8, bf16[384,256]{1,0:T(8,128)(2,1)} %copy-done.9), kind=kLoop, calls=%fused_computation.2 | loop fusion | flops 1769472 | bytes 1179648 | tf_op jit(solution)/shard_map/concatenate | solution.py:290
  63.7 3.7 %shard_map.60 = bf16[384,512]{1,0:T(8,128)(2,1)} custom-call(f32[384,512]{1,0:T(8,128)S(1)} %get-tuple-element.41.near, bf16[384,512]{1,0:T(8,128)(2,1)S(1)} %collective-permute-done.17.far, f32[384,128]{1,0:T(8,128)S(1)} %pad_maximum_fusion.4.cosine, f32[384,128]{1,0:T(8,128)S(1)} %pad_maximum_fusion.5.sine, s32[384,1]{1,0:T(8,128)S(1)} %copy.7.first, ...), custom_call_target="tpu_custom_call" | custom-call | flops 704643072 | bytes 1572864 | tf_op jit(solution)/shard_map/pallas_call | solution.py:207
  (54 shorter events, 5.9 us)
Async XLA Ops:
  0.0 7.1 %copy-start.6 = (bf16[1024,512]{1,0:T(8,128)(2,1)S(1)}, bf16[1024,512]{1,0:T(8,128)(2,1)}, u32[]{:S(2)}) copy-start(bf16[1024,512]{1,0:T(8,128)(2,1)} %param.6) | copy-start | bytes 3145732
  0.0 19.7 %collective-permute-start = (bf16[384,8192]{1,0:T(8,128)(2,1)}, bf16[384,8192]{1,0:T(8,128)(2,1)}, u32[]{:S(2)}, u32[]{:S(2)}) collective-permute-start(bf16[384,8192]{1,0:T(8,128)(2,1)} %bitcast.17), channel_id=1, source_target_pairs={{0,4},{4,0},{8,12},{12,8},{16,20},{20,16},{24,28},{28,24},{1,5},{5... | collective-permute-start | bytes 18874376 | tf_op jit(solution)/shard_map/ppermute | solution.py:237
  0.7 8.2 %collective-permute-start.1 = (bf16[1024,128]{1,0:T(8,128)(2,1)}, bf16[1024,128]{1,0:T(8,128)(2,1)}, u32[]{:S(2)}, u32[]{:S(2)}) collective-permute-start(bf16[1024,128]{1,0:T(8,128)(2,1)} %refs_0_.1), channel_id=1, source_target_pairs={{0,8},{4,12},{8,0},{12,4},{16,24},{20,28},{24,16},{28,20},{1,9},{5... | collective-permute-start | bytes 786440 | tf_op jit(solution)/shard_map/ppermute | solution.py:237
  1.9 13.9 %collective-permute-start.2 = (bf16[1024,128]{1,0:T(8,128)(2,1)}, bf16[1024,128]{1,0:T(8,128)(2,1)S(1)}, u32[]{:S(2)}, u32[]{:S(2)}) collective-permute-start(bf16[1024,128]{1,0:T(8,128)(2,1)} %refs_0_.1), channel_id=1, source_target_pairs={{0,16},{4,20},{8,24},{12,28},{16,0},{20,4},{24,8},{28,12},{1,17},{... | collective-permute-start | bytes 786440 | tf_op jit(solution)/shard_map/ppermute | solution.py:237
  3.1 12.2 %collective-permute-start.4 = (bf16[1024,128]{1,0:T(8,128)(2,1)}, bf16[1024,128]{1,0:T(8,128)(2,1)}, u32[]{:S(2)}, u32[]{:S(2)}) collective-permute-start(bf16[1024,128]{1,0:T(8,128)(2,1)} %refs_1_.1), channel_id=1, source_target_pairs={{0,16},{4,20},{8,24},{12,28},{16,0},{20,4},{24,8},{28,12},{1,17},{... | collective-permute-start | bytes 786440 | tf_op jit(solution)/shard_map/ppermute | solution.py:237
  3.4 13.1 %collective-permute-start.3 = (bf16[1024,128]{1,0:T(8,128)(2,1)}, bf16[1024,128]{1,0:T(8,128)(2,1)S(1)}, u32[]{:S(2)}, u32[]{:S(2)}) collective-permute-start(bf16[1024,128]{1,0:T(8,128)(2,1)} %refs_1_.1), channel_id=1, source_target_pairs={{0,8},{4,12},{8,0},{12,4},{16,24},{20,28},{24,16},{28,20},{1,9},{5... | collective-permute-start | bytes 786440 | tf_op jit(solution)/shard_map/ppermute | solution.py:237
  7.3 12.4 %copy-start = (bf16[1024,128]{1,0:T(8,128)(2,1)S(1)}, bf16[1024,128]{1,0:T(8,128)(2,1)}, u32[]{:S(2)}) copy-start(bf16[1024,128]{1,0:T(8,128)(2,1)} %refs_0_.1) | copy-start | bytes 786436
  7.3 12.4 %copy-start.1 = (bf16[1024,128]{1,0:T(8,128)(2,1)S(1)}, bf16[1024,128]{1,0:T(8,128)(2,1)}, u32[]{:S(2)}) copy-start(bf16[1024,128]{1,0:T(8,128)(2,1)} %refs_1_.1) | copy-start | bytes 786436
  8.9 18.0 %collective-permute-start.6 = (bf16[1024,128]{1,0:T(8,128)(2,1)}, bf16[1024,128]{1,0:T(8,128)(2,1)}, u32[]{:S(2)}, u32[]{:S(2)}) collective-permute-start(bf16[1024,128]{1,0:T(8,128)(2,1)} %collective-permute-done.1.refs_2_), channel_id=1, source_target_pairs={{0,16},{4,20},{8,24},{12,28},{16,0},{20,4},{24,8},{28,12},{1,17},{... | collective-permute-start | bytes 786440 | tf_op jit(solution)/shard_map/ppermute | solution.py:237
  15.4 11.5 %collective-permute-start.7 = (bf16[1024,128]{1,0:T(8,128)(2,1)}, bf16[1024,128]{1,0:T(8,128)(2,1)}, u32[]{:S(2)}, u32[]{:S(2)}) collective-permute-start(bf16[1024,128]{1,0:T(8,128)(2,1)} %collective-permute-done.4.refs_5_), channel_id=1, source_target_pairs={{0,8},{4,12},{8,0},{12,4},{16,24},{20,28},{24,16},{28,20},{1,9},{5... | collective-permute-start | bytes 786440 | tf_op jit(solution)/shard_map/ppermute | solution.py:237
  15.8 0.7 %copy-start.2 = (bf16[1024,128]{1,0:T(8,128)(2,1)}, bf16[1024,128]{1,0:T(8,128)(2,1)S(1)}, u32[]{:S(2)}) copy-start(bf16[1024,128]{1,0:T(8,128)(2,1)S(1)} %collective-permute-done.2.refs_4_) | copy-start | bytes 786436
  16.5 0.7 %copy-start.4 = (bf16[1024,128]{1,0:T(8,128)(2,1)}, bf16[1024,128]{1,0:T(8,128)(2,1)S(1)}, u32[]{:S(2)}) copy-start(bf16[1024,128]{1,0:T(8,128)(2,1)S(1)} %collective-permute-done.3.refs_3_) | copy-start | bytes 786436
  17.2 24.6 %collective-permute-start.5 = (bf16[768,512]{1,0:T(8,128)(2,1)}, bf16[768,512]{1,0:T(8,128)(2,1)S(1)}, u32[]{:S(2)}, u32[]{:S(2)}) collective-permute-start(bf16[768,512]{1,0:T(8,128)(2,1)} %get-tuple-element.24), channel_id=1, source_target_pairs={{0,16},{4,20},{8,24},{12,28},{16,0},{20,4},{24,8},{28,12},{1,17},{... | collective-permute-start | bytes 2359304 | tf_op jit(solution)/shard_map/ppermute | solution.py:237
  18.4 23.4 %collective-permute-start.10 = (bf16[768,512]{1,0:T(8,128)(2,1)}, bf16[768,512]{1,0:T(8,128)(2,1)S(1)}, u32[]{:S(2)}, u32[]{:S(2)}) collective-permute-start(bf16[768,512]{1,0:T(8,128)(2,1)} %get-tuple-element.28), channel_id=1, source_target_pairs={{0,8},{4,12},{8,0},{12,4},{16,24},{20,28},{24,16},{28,20},{1,9},{5... | collective-permute-start | bytes 2359304 | tf_op jit(solution)/shard_map/ppermute | solution.py:237
  19.7 1.0 %copy-start.3 = (bf16[1024,128]{1,0:T(8,128)(2,1)S(1)}, bf16[1024,128]{1,0:T(8,128)(2,1)}, u32[]{:S(2)}) copy-start(bf16[1024,128]{1,0:T(8,128)(2,1)} %copy-done.2) | copy-start | bytes 786436
  20.7 0.9 %copy-start.5 = (bf16[1024,128]{1,0:T(8,128)(2,1)S(1)}, bf16[1024,128]{1,0:T(8,128)(2,1)}, u32[]{:S(2)}) copy-start(bf16[1024,128]{1,0:T(8,128)(2,1)} %copy-done.4) | copy-start | bytes 786436
  29.4 4.3 %collective-permute-start.8 = (f32[384,256]{1,0:T(8,128)S(1)}, f32[384,256]{1,0:T(8,128)S(1)}, u32[]{:S(2)}, u32[]{:S(2)}) collective-permute-start(f32[384,256]{1,0:T(8,128)S(1)} %get-tuple-element.26), channel_id=1, source_target_pairs={{0,4},{4,0},{8,12},{12,8},{16,20},{20,16},{24,28},{28,24},{1,5},{5... | collective-permute-start | bytes 1179656 | tf_op jit(solution)/shard_map/ppermute | solution.py:237
  33.8 8.0 %collective-permute-start.9 = (bf16[384,256]{1,0:T(8,128)(2,1)S(1)}, bf16[384,256]{1,0:T(8,128)(2,1)S(1)}, u32[]{:S(2)}, u32[]{:S(2)}) collective-permute-start(bf16[384,256]{1,0:T(8,128)(2,1)S(1)} %shard_map.57), channel_id=1, source_target_pairs={{0,1},{1,2},{2,3},{4,5},{5,6},{6,7},{8,9},{9,10},{10,11},{12,13},{... | collective-permute-start | bytes 589832 | tf_op jit(solution)/shard_map/ppermute | solution.py:289
  38.7 7.6 %collective-permute-start.16 = (bf16[128,512]{1,0:T(8,128)(2,1)}, bf16[128,512]{1,0:T(8,128)(2,1)}, u32[]{:S(2)}, u32[]{:S(2)}) collective-permute-start(bf16[128,512]{1,0:T(8,128)(2,1)} %get-tuple-element.37), channel_id=1, source_target_pairs={{0,16},{4,20},{8,24},{12,28},{16,0},{20,4},{24,8},{28,12},{1,17},{... | collective-permute-start | bytes 393224 | tf_op jit(solution)/shard_map/ppermute | solution.py:237
  38.9 7.4 %collective-permute-start.15 = (bf16[128,512]{1,0:T(8,128)(2,1)}, bf16[128,512]{1,0:T(8,128)(2,1)}, u32[]{:S(2)}, u32[]{:S(2)}) collective-permute-start(bf16[128,512]{1,0:T(8,128)(2,1)} %get-tuple-element.35), channel_id=1, source_target_pairs={{0,8},{4,12},{8,0},{12,4},{16,24},{20,28},{24,16},{28,20},{1,9},{5... | collective-permute-start | bytes 393224 | tf_op jit(solution)/shard_map/ppermute | solution.py:237
  41.8 2.3 %copy-start.7 = (bf16[384,256]{1,0:T(8,128)(2,1)}, bf16[384,256]{1,0:T(8,128)(2,1)S(1)}, u32[]{:S(2)}) copy-start(bf16[384,256]{1,0:T(8,128)(2,1)S(1)} %collective-permute-done.9) | copy-start | bytes 589828
  42.6 12.5 %collective-permute-start.14 = (bf16[512,512]{1,0:T(8,128)(2,1)}, bf16[512,512]{1,0:T(8,128)(2,1)}, u32[]{:S(2)}, u32[]{:S(2)}) collective-permute-start(bf16[512,512]{1,0:T(8,128)(2,1)} %slice.43), channel_id=1, source_target_pairs={{0,8},{4,12},{8,0},{12,4},{16,24},{20,28},{24,16},{28,20},{1,9},{5... | collective-permute-start | bytes 1572872 | tf_op jit(solution)/shard_map/ppermute | solution.py:237
  43.8 12.3 %collective-permute-start.13 = (bf16[512,512]{1,0:T(8,128)(2,1)}, bf16[512,512]{1,0:T(8,128)(2,1)}, u32[]{:S(2)}, u32[]{:S(2)}) collective-permute-start(bf16[512,512]{1,0:T(8,128)(2,1)} %slice.42), channel_id=1, source_target_pairs={{0,16},{4,20},{8,24},{12,28},{16,0},{20,4},{24,8},{28,12},{1,17},{... | collective-permute-start | bytes 1572872 | tf_op jit(solution)/shard_map/ppermute | solution.py:237
  44.7 9.9 %collective-permute-start.11 = (bf16[256,512]{1,0:T(8,128)(2,1)}, bf16[256,512]{1,0:T(8,128)(2,1)S(1)}, u32[]{:S(2)}, u32[]{:S(2)}) collective-permute-start(bf16[256,512]{1,0:T(8,128)(2,1)} %pad_maximum_fusion.3), channel_id=1, source_target_pairs={{0,1},{1,0},{2,3},{3,2},{4,5},{5,4},{6,7},{7,6},{8,9},{9,8},{10,11... | collective-permute-start | bytes 786440 | tf_op jit(solution)/shard_map/ppermute | solution.py:315
  46.3 8.3 %collective-permute-start.12 = (bf16[384,256]{1,0:T(8,128)(2,1)}, bf16[384,256]{1,0:T(8,128)(2,1)S(1)}, u32[]{:S(2)}, u32[]{:S(2)}) collective-permute-start(bf16[384,256]{1,0:T(8,128)(2,1)} %copy-done.7), channel_id=1, source_target_pairs={{0,1},{1,2},{2,3},{4,5},{5,6},{6,7},{8,9},{9,10},{10,11},{12,13},{... | collective-permute-start | bytes 589832 | tf_op jit(solution)/shard_map/ppermute | solution.py:289
  53.5 9.0 %copy-start.8 = (bf16[384,256]{1,0:T(8,128)(2,1)S(1)}, bf16[384,256]{1,0:T(8,128)(2,1)}, u32[]{:S(2)}) copy-start(bf16[384,256]{1,0:T(8,128)(2,1)} %copy-done.7) | copy-start | bytes 589828
  54.6 0.7 %copy-start.9 = (bf16[384,256]{1,0:T(8,128)(2,1)}, bf16[384,256]{1,0:T(8,128)(2,1)S(1)}, u32[]{:S(2)}) copy-start(bf16[384,256]{1,0:T(8,128)(2,1)S(1)} %collective-permute-done.12) | copy-start | bytes 589828
  59.9 3.8 %collective-permute-start.17 = (bf16[384,512]{1,0:T(8,128)(2,1)S(1)}, bf16[384,512]{1,0:T(8,128)(2,1)S(1)}, u32[]{:S(2)}, u32[]{:S(2)}) collective-permute-start(bf16[384,512]{1,0:T(8,128)(2,1)S(1)} %get-tuple-element.42), channel_id=1, source_target_pairs={{0,4},{4,0},{8,12},{12,8},{16,20},{20,16},{24,28},{28,24},{1,5},{5... | collective-permute-start | bytes 1179656 | tf_op jit(solution)/shard_map/ppermute | solution.py:237
